TPU v7x, 512 devices: a whole 4x8x8 slice. The times are simulated.
512 devices in a mesh: cam: 8 (over x, y_hi), slab: 64 (over y_lo, z, core).
Axes of the slice: x: 4, y: 8 (y_hi: 2, y_lo: 4; y = y_hi * 4 + y_lo), z: 8, core: 2. Of those that a mesh axis runs over, the one named last changes fastest.
Arguments:
- frames_in: bfloat16 [8, 16384, 1152], P('cam', 'slab'), may hold values from -6 to 6
- cam_embed: float32 [8, 1152], replicated, may hold values from -6 to 6
- norm_gain: float32 [1152], replicated, may hold values from 0.1 to 1.9
- q_gain: float32 [1152], replicated, may hold values from 0.1 to 1.9
- k_gain: float32 [1152], replicated, may hold values from 0.1 to 1.9
- w_qkv: bfloat16 [1152, 3456], P('slab'), may hold values from -0.1875 to 0.1875
- w_out: bfloat16 [1152, 1152], P('slab'), may hold values from -0.1875 to 0.1875
Outputs:
- frames_out: bfloat16 [8, 16384, 1152], P('cam', 'slab')
All inputs are finite; a program needn't handle non-finite values.
Results may differ from a plain program's by a relative error of at most 0.0033.
Values may be sent and summed in bfloat16 or wider, within the bound.
No kernel may reach another device: no remote copies, remote signals or barrier semaphores. Data moves between devices by JAX's collectives and lax.ppermute only.
A program may use at most 128 MiB of HBM per device.

v0:
```python
import jax
import jax.numpy as jnp
from jax import lax
from jax.sharding import PartitionSpec as P

HEADS = 16
HD = 72
SH = 8
XH = 4
TH = 4


def partner_2(block, axis, distance):
    count = lax.axis_size(axis)
    route = []
    for low in range(count):
        high = low | 1 << distance
        if high != low and high < count:
            route += [(low, high), (high, low)]
    return lax.ppermute(block, axis, route)


def from_behind(block, axis, distance):
    devices = range(lax.axis_size(axis))
    route = [((i - distance) % len(devices), i) for i in devices]
    return lax.ppermute(block, axis, route)


def layer_norm(hidden, gain):
    mean = jnp.mean(hidden, -1, keepdims=True)
    centred = hidden - mean
    variance = jnp.mean(centred * centred, -1, keepdims=True)
    return centred * lax.rsqrt(variance + 1e-06) * gain


def head_norm(part, gain):
    shaped = part.reshape(part.shape[0], HEADS, HD)
    mean_sq = jnp.mean(shaped * shaped, -1, keepdims=True)
    return (shaped * lax.rsqrt(mean_sq + 1e-06)).reshape(part.shape) * gain


def softmax_rows(scores):
    expd = jnp.exp(scores)
    return (expd / jnp.sum(expd, -1, keepdims=True)).astype(jnp.bfloat16)


def attend(query, keys, values, heads):
    scale = 1.0 / HD**0.5
    q_three = query.reshape(query.shape[0], heads, HD)
    k_three = keys.reshape(keys.shape[0], heads, HD)
    v_three = values.reshape(values.shape[0], heads, HD)
    scores = (
        jnp.einsum("rnd,knd->nrk", q_three, k_three, preferred_element_type=jnp.float32) * scale
    )
    weights = softmax_rows(scores)
    result = jnp.einsum("nrk,knd->rnd", weights, v_three, preferred_element_type=jnp.float32)
    return result.reshape(query.shape[0], heads * HD).astype(jnp.bfloat16)


def local(frames_in, cam_embed, norm_gain, q_gain, k_gain, w_qkv, w_out):
    tokens = frames_in[0]
    rows = tokens.shape[0]
    width = tokens.shape[1]
    n_sp = SH * HD
    n_cr = XH * HD
    n_tm = TH * HD
    count = cam_embed.shape[0]
    here = lax.axis_index("cam")
    picker = (jnp.arange(count) == here).astype(jnp.float32)
    embed = jnp.dot(picker[None, :], cam_embed, precision=lax.Precision.HIGHEST)
    hidden = tokens.astype(jnp.float32) + embed
    normed = layer_norm(hidden, norm_gain).astype(jnp.bfloat16)
    columns = normed
    projected = jnp.dot(
        columns,
        lax.all_gather(w_qkv, "slab", axis=0, tiled=True),
        preferred_element_type=jnp.float32,
    )
    query = head_norm(projected[:, :width], q_gain).astype(jnp.bfloat16)
    keys = head_norm(projected[:, width : 2 * width], k_gain).astype(jnp.bfloat16)
    values = projected[:, 2 * width :].astype(jnp.bfloat16)
    own_space = jnp.concatenate([keys[:, :n_sp], values[:, :n_sp]], 1)
    own_cross = jnp.concatenate([keys[:, n_sp : n_sp + n_cr], values[:, n_sp : n_sp + n_cr]], 1)
    partner = partner_2(jnp.concatenate([own_space, own_cross], 1), "slab", 0)
    space_kv = jnp.concatenate([own_space, partner[:, : 2 * n_sp]], 0)
    frame_cross = jnp.concatenate([own_cross, partner[:, 2 * n_sp :]], 0)
    from_left = from_behind(frame_cross, "cam", 1)
    from_right = from_behind(frame_cross, "cam", -1)
    cross_kv = jnp.concatenate([from_left, from_right], 0)
    space_out = attend(query[:, :n_sp], space_kv[:, :n_sp], space_kv[:, n_sp:], SH)
    cross_out = attend(query[:, n_sp : n_sp + n_cr], cross_kv[:, :n_cr], cross_kv[:, n_cr:], XH)
    slabs = lax.axis_size("slab")
    piece = rows // slabs
    start_tm = n_sp + n_cr
    packed = jnp.concatenate([query[:, start_tm:], keys[:, start_tm:], values[:, start_tm:]], 1)
    packed = packed.reshape(slabs, piece * 3 * n_tm)
    moved = lax.all_to_all(packed, "slab", split_axis=0, concat_axis=0, tiled=True)
    grid = moved.reshape(slabs // 2, 2, piece, 3, TH, HD)
    scale = 1.0 / HD**0.5
    time_scores = (
        jnp.einsum(
            "fhpnd,ghpnd->hpnfg",
            grid[:, :, :, 0],
            grid[:, :, :, 1],
            preferred_element_type=jnp.float32,
        )
        * scale
    )
    time_weights = softmax_rows(time_scores)
    time_res = jnp.einsum(
        "hpnfg,ghpnd->fhpnd", time_weights, grid[:, :, :, 2], preferred_element_type=jnp.float32
    )
    time_res = time_res.astype(jnp.bfloat16).reshape(slabs, piece * n_tm)
    returned = lax.all_to_all(time_res, "slab", split_axis=0, concat_axis=0, tiled=True).reshape(
        rows, n_tm
    )
    mixed = jnp.concatenate([space_out, cross_out, returned], 1)
    columns = mixed
    update = jnp.dot(
        columns,
        lax.all_gather(w_out, "slab", axis=0, tiled=True),
        preferred_element_type=jnp.float32,
    )
    return (hidden + update).astype(jnp.bfloat16)[None]


def solution(mesh):
    placed = (P("cam", "slab", None), P(), P(), P(), P(), P("slab", None), P("slab", None))
    return jax.shard_map(
        local, mesh=mesh, in_specs=placed, out_specs=P("cam", "slab", None), check_vma=False
    )
```

profile of v0, /device:TPU:17, one launch (start us, length us, event | category | flops | bytes accessed | tf_op | source)
XLA Modules:
  0.0 372.3 jit_solution(18082256980128589137)
XLA Ops:
  6.5 0.7 all-gather.5.cloned.1.call-update
  7.3 0.7 all-gather.7.cloned.1.call-update
  8.2 1.3 fusion.10
  9.8 130.7 %all-gather.5.cloned.1.call-done = bf16[64,18,3456]{2,1,0:T(8,128)(2,1)} async-done(((bf16[1,18,3456]{2,1,0:T(8,128)(2,1)}), bf16[64,18,3456]{2,1,0:T(8,128)(2,1)}) %all-gather.5.cloned.1.call-update) | async-done | bytes 7962640 | tf_op jit(solution)/shard_map/all_gather | solution.py:76
  140.5 13.2 %reshape.96 = bf16[1152,3456]{1,0:T(8,128)(2,1)} reshape(bf16[64,18,3456]{2,1,0:T(8,128)(2,1)} %all-gather.5.cloned.1.call-done) | data formatting | bytes 15925248
  153.7 7.2 %fusion.48 = (bf16[256,3456]{1,0:T(8,128)(2,1)}, f32[256,3456]{1,0:T(8,128)S(1)}) fusion(bf16[1152,3456]{1,0:T(8,128)(2,1)} %reshape.96, bf16[1,256,1152]{2,1,0:T(8,128)(2,1)S(1)} %copy-done.4, f32[1152]{0:T(1024)S(1)} %copy-done.11, f32[256]{0:T(256)S(1)} %add_rsqrt_fusion.2, f32[256]{0:T(256)S(1)} %broadcast_multiply_fusion, ...), kind=kOutput, calls=%fused_computation.72 | convolution fusion | flops 2041085952 | bytes 13872128 | tf_op jit(solution)/shard_map/dot_general | solution.py:74
  160.9 1.3 slice_multiply_fusion
  162.2 0.8 copy-done.2
  164.0 1.6 copy.31
  165.9 1.4 copy.32
  167.3 1.9 fusion.42
  169.1 2.4 multiply_convert_fusion
  171.5 1.1 fusion.46
  172.8 0.9 all_to_all.16
  173.7 0.5 broadcast.71
  174.2 3.3 reduce.4
  177.5 1.3 reshape.104
  178.8 9.1 %all-to-all-start = ((bf16[64,2,1728]{2,1,0:T(2,128)(2,1)}), bf16[64,2,1728]{2,1,0:T(2,128)(2,1)}, u32[]{:S(2)}, u32[]{:S(2)}) async-start(bf16[64,2,1728]{2,1,0:T(2,128)(2,1)} %reshape.104), calls=%async_computation | async-start | bytes 917504 | tf_op jit(solution)/shard_map/all_to_all | solution.py:97
  187.9 1.0 slice.87
  189.0 1.4 concatenate.26
  190.4 1.3 copy.33
  191.7 2.4 collective-permute-start
  194.1 72.3 %all-gather.7.cloned.1.call-done = bf16[64,18,1152]{2,1,0:T(8,128)(2,1)} async-done(((bf16[1,18,1152]{2,1,0:T(8,128)(2,1)}), bf16[64,18,1152]{2,1,0:T(8,128)(2,1)}) %all-gather.7.cloned.1.call-update) | async-done | bytes 2654224 | tf_op jit(solution)/shard_map/all_gather | solution.py:121
  266.4 5.4 %reshape.98 = bf16[1152,1152]{1,0:T(8,128)(2,1)} reshape(bf16[64,18,1152]{2,1,0:T(8,128)(2,1)} %all-gather.7.cloned.1.call-done) | data formatting | bytes 5308416
  271.8 0.9 copy.38
  272.8 3.1 reshape.105
  276.0 2.8 reduce.1
  278.7 1.4 reshape.92
  280.1 1.0 fusion.45
  281.4 1.2 fusion.16
  283.3 1.5 reduce.5
  284.8 0.8 reshape.106
  285.6 9.3 %all-to-all-start.1 = ((bf16[64,2,576]{2,1,0:T(2,128)(2,1)}), bf16[64,2,576]{2,1,0:T(2,128)(2,1)S(1)}, u32[]{:S(2)}, u32[]{:S(2)}) async-start(bf16[64,2,576]{2,1,0:T(2,128)(2,1)} %reshape.106), calls=%async_computation.1 | async-start | bytes 327680 | tf_op jit(solution)/shard_map/all_to_all | solution.py:114
  294.9 1.0 slice.95
  296.3 1.1 copy.41
  297.4 7.6 %collective-permute-start.2 = (bf16[512,576]{0,1:T(8,128)(2,1)}, bf16[512,576]{0,1:T(8,128)(2,1)}, u32[]{:S(2)}, u32[]{:S(2)}) collective-permute-start(bf16[512,576]{0,1:T(8,128)(2,1)} %copy.41), channel_id=1, source_target_pairs={{64,0},{128,64},{192,128},{256,192},{320,256},{384,320},{448,384},... | collective-permute-start | bytes 1769480 | tf_op jit(solution)/shard_map/ppermute | solution.py:26
  305.0 2.1 collective-permute-start.1
  307.2 1.1 slice.90
  310.1 1.0 fusion
  311.1 1.0 fusion.7
  312.4 0.9 reduce.2
  313.6 44.9 %collective-permute-done.1 = bf16[512,576]{0,1:T(8,128)(2,1)} collective-permute-done((bf16[512,576]{0,1:T(8,128)(2,1)}, bf16[512,576]{0,1:T(8,128)(2,1)}, u32[]{:S(2)}, u32[]{:S(2)}) %collective-permute-start.1) | collective-permute-done | bytes 589856 | tf_op jit(solution)/shard_map/ppermute | solution.py:26
  358.5 1.1 constant_dynamic-update-slice_fusion.1
  359.7 1.1 constant_dynamic-update-slice_fusion
  360.9 1.0 fusion.1
  361.9 1.0 fusion.17
  362.8 0.8 copy-done.3
  363.6 1.9 fusion.3
  (58 shorter events, 5.8 us)
Async XLA Ops:
  6.5 1.5 copy-start
  6.5 2.9 copy-start.4
  6.5 134.0 %all-gather.5.cloned.1.call-start = ((), (), s32[]{:S(2)}) async-start(), calls=%async_computation.2 | async-start | bytes 10782720 | tf_op jit(solution)/shard_map/all_gather | solution.py:76
  7.3 259.1 %all-gather.7.cloned.1.call-start = ((), (), s32[]{:S(2)}) async-start(), calls=%async_computation.3 | async-start | bytes 3594240 | tf_op jit(solution)/shard_map/all_gather | solution.py:121
  9.8 143.9 %copy-start.11 = (f32[1152]{0:T(1024)S(1)}, f32[1152]{0:T(1024)}, u32[]{:S(2)}) copy-start(f32[1152]{0:T(1024)} %param.9) | copy-start | bytes 13828
  160.9 2.1 copy-start.2
  165.8 3.3 copy-start.9
  165.9 3.3 copy-start.10
  178.8 94.1 %all-to-all-start = ((bf16[64,2,1728]{2,1,0:T(2,128)(2,1)}), bf16[64,2,1728]{2,1,0:T(2,128)(2,1)}, u32[]{:S(2)}, u32[]{:S(2)}) async-start(bf16[64,2,1728]{2,1,0:T(2,128)(2,1)} %reshape.104), calls=%async_computation | async-start | bytes 917504 | tf_op jit(solution)/shard_map/all_to_all | solution.py:97
  191.7 103.2 %collective-permute-start = (bf16[256,1728]{0,1:T(8,128)(2,1)}, bf16[256,1728]{0,1:T(8,128)(2,1)}, u32[]{:S(2)}, u32[]{:S(2)}) collective-permute-start(bf16[256,1728]{0,1:T(8,128)(2,1)} %copy.33), channel_id=1, source_target_pairs={{0,1},{1,0},{2,3},{3,2},{4,5},{5,4},{6,7},{7,6},{8,9},{9,8},{10,11... | collective-permute-start | bytes 2654216 | tf_op jit(solution)/shard_map/ppermute | solution.py:20
  271.8 0.9 copy-start.8
  283.3 12.9 %copy-start.5 = (bf16[256,288]{1,0:T(8,128)(2,1)S(1)}, bf16[256,288]{1,0:T(8,128)(2,1)}, u32[]{:S(2)}) copy-start(bf16[256,288]{1,0:T(8,128)(2,1)} %get-tuple-element.29) | copy-start | bytes 442372
  283.3 12.9 %copy-start.6 = (bf16[256,288]{1,0:T(8,128)(2,1)S(1)}, bf16[256,288]{1,0:T(8,128)(2,1)}, u32[]{:S(2)}) copy-start(bf16[256,288]{1,0:T(8,128)(2,1)} %get-tuple-element.9) | copy-start | bytes 442372
  285.6 26.5 %all-to-all-start.1 = ((bf16[64,2,576]{2,1,0:T(2,128)(2,1)}), bf16[64,2,576]{2,1,0:T(2,128)(2,1)S(1)}, u32[]{:S(2)}, u32[]{:S(2)}) async-start(bf16[64,2,576]{2,1,0:T(2,128)(2,1)} %reshape.106), calls=%async_computation.1 | async-start | bytes 327680 | tf_op jit(solution)/shard_map/all_to_all | solution.py:114
  297.4 62.3 %collective-permute-start.2 = (bf16[512,576]{0,1:T(8,128)(2,1)}, bf16[512,576]{0,1:T(8,128)(2,1)}, u32[]{:S(2)}, u32[]{:S(2)}) collective-permute-start(bf16[512,576]{0,1:T(8,128)(2,1)} %copy.41), channel_id=1, source_target_pairs={{64,0},{128,64},{192,128},{256,192},{320,256},{384,320},{448,384},... | collective-permute-start | bytes 1769480 | tf_op jit(solution)/shard_map/ppermute | solution.py:26
  305.0 53.5 %collective-permute-start.1 = (bf16[512,576]{0,1:T(8,128)(2,1)}, bf16[512,576]{0,1:T(8,128)(2,1)}, u32[]{:S(2)}, u32[]{:S(2)}) collective-permute-start(bf16[512,576]{0,1:T(8,128)(2,1)} %copy.41), channel_id=1, source_target_pairs={{448,0},{0,64},{64,128},{128,192},{192,256},{256,320},{320,384},{3... | collective-permute-start | bytes 1769480 | tf_op jit(solution)/shard_map/ppermute | solution.py:26
  309.1 1.0 copy-start.7
  361.9 1.8 copy-start.3
  363.6 1.9 copy-start.1
Sparse Core Ops, SparseCore 0:
  9.5 130.9 all-gather.4
  142.6 123.6 all-gather.6
where the time goes:
time: 374 us; the launch traced here: 372 us
  waiting for transfers between devices  249 us (67%)
  local copies, waits for them, and re-layouts  49.4 us (13%)
  starting transfers between devices  30.7 us (8%)
  matrix products  14.7 us (4%)
  other arithmetic  14.5 us (4%)
  between operations  13.8 us (4%)
    all_gather x1, waiting for transfers between devices, local(): lax.all_gather(w_qkv, 'slab', axis=0, tiled=True)  131 us
    all_gather x1, waiting for transfers between devices, local(): lax.all_gather(w_out, 'slab', axis=0, tiled=True)  72.3 us
    ppermute x2, waiting for transfers between devices, from_behind(): return lax.ppermute(block, axis, route)  44.9 us
    unnamed x33, local copies, waits for them, and re-layouts  27.8 us
    ppermute x2, starting transfers between devices, from_behind(): return lax.ppermute(block, axis, route)  9.79 us
    all_to_all x1, starting transfers between devices, local(): lax.all_to_all(time_res, 'slab', split_axis=0, concat_axis=0, tiled=True)  9.29 us
    all_to_all x1, starting transfers between devices, local(): lax.all_to_all(packed, 'slab', split_axis=0, concat_axis=0, tiled=True)  9.15 us
  transfers between devices with their start and end apart: 7, of which 3 were waited for; matrix products, arithmetic and copies ran while one was open for 19% of the time, Pallas kernels for 0%

commit v1 on v0

v1 whole, which is shorter than its diff:
```python
import jax
import jax.numpy as jnp
from jax import lax
from jax.experimental import pallas as pl
from jax.experimental.pallas import tpu as pltpu
from jax.sharding import Mesh
from jax.sharding import PartitionSpec as P

HEADS = 16
HD = 72
D = HEADS * HD
PAIR = 2 * HD
GROUP = 3 * PAIR
HALF = 256
CAM = ("x", "yh")
CHIP = ("yl", "z")
SLAB = ("yl", "z", "core")
EVERY = ("x", "yh", "yl", "z", "core")
SCALE = 1.4426950408889634 / HD**0.5
F32 = jnp.float32
BF16 = jnp.bfloat16
VMEM_LIMIT = 50 * 1024 * 1024


def route(move):
    pairs = []
    for x in range(4):
        for y in range(8):
            for z in range(8):
                for core in range(2):
                    a, b, c = move(x, y, z, core)
                    source = ((x * 8 + y) * 8 + z) * 2 + core
                    pairs.append((source, ((a % 4 * 8 + b % 8) * 8 + c % 8) * 2 + core))
    return pairs


def towards(core):
    return 1 if core else -1


ROUTES = (
    route(lambda x, y, z, core: (x + towards(core), y, z)),
    route(lambda x, y, z, core: (x, y + towards(core), z)),
    route(lambda x, y, z, core: (x, y, z + towards(core))),
)


def shift_cam(block, distance):
    return lax.ppermute(block, CAM, [(i, (i + distance) % 8) for i in range(8)])


def swap_core(block):
    return lax.ppermute(block, "core", [(0, 1), (1, 0)])


def mm(a, b):
    return jnp.dot(a, b, preferred_element_type=F32)


def split_mm(a, b):
    high = a.astype(BF16)
    low = (a - high.astype(F32)).astype(BF16)
    return mm(high, b) + mm(low, b)


def normalise(tokens, embed, gain):
    hidden = tokens.astype(F32) + embed
    centred = hidden - jnp.mean(hidden, -1, keepdims=True)
    variance = jnp.mean(centred * centred, -1, keepdims=True)
    return (centred * lax.rsqrt(variance + 1e-06) * gain).astype(BF16)


def head_parts(normed, weight, gains):
    projected = mm(normed, weight)
    lane = lax.broadcasted_iota(jnp.int32, (GROUP, 128), 0) // HD
    head = lax.broadcasted_iota(jnp.int32, (GROUP, 128), 1)
    member = ((lane == head) & (head < 4)).astype(BF16)
    lane_t = lax.broadcasted_iota(jnp.int32, (128, GROUP), 1) // HD
    head_t = lax.broadcasted_iota(jnp.int32, (128, GROUP), 0)
    member_t = ((lane_t == head_t) & (head_t < 4)).astype(BF16)
    mean_sq = split_mm(projected * projected, member) * (1.0 / HD)
    factor = split_mm(lax.rsqrt(mean_sq + 1e-06), member_t)
    column = lax.broadcasted_iota(jnp.int32, projected.shape, 1)
    factor = jnp.where(column < 2 * PAIR, factor, 1.0)
    scaled = (projected * factor * gains).astype(BF16)
    return scaled[:, :PAIR], scaled[:, PAIR : 2 * PAIR], scaled[:, 2 * PAIR :]


def attend(query, pairs_kv, mask=None):
    rows = query.shape[0]
    column = lax.broadcasted_iota(jnp.int32, (rows, PAIR), 1)
    result = None
    for head in range(2):
        own = (column >= head * HD) & (column < (head + 1) * HD)
        picked = jnp.where(own, query, jnp.zeros_like(query))
        total = None
        for keys, values in pairs_kv:
            scores = lax.dot_general(picked, keys, (((1,), (1,)), ((), ())), preferred_element_type=F32)
            expd = jnp.exp2(scores * SCALE)
            if mask is not None:
                expd = jnp.where(mask, expd, 0.0)
            wide = jnp.concatenate([values, jnp.ones((values.shape[0], 256 - PAIR), BF16)], 1)
            part = mm(expd.astype(BF16), wide)
            total = part if total is None else total + part
        head_out = total[:, :PAIR] / total[:, PAIR : PAIR + 1]
        result = head_out if head == 0 else jnp.where(own, head_out, result)
    return result


def start_fetch(order, blocks, group, slot, sem):
    for j, block in enumerate(blocks):
        @pl.when(order[group] == j)
        def _(block=block):
            pltpu.make_async_copy(block, slot, sem).start()


def wait_fetch(blocks, slot, sem):
    pltpu.make_async_copy(blocks[0], slot, sem).wait()


def cross_project_kernel(order, own, other, embed, gain, gains, b0, b1, b2, b3, query, kv, normed, weight, sem):
    blocks = (b0, b1, b2, b3)
    start_fetch(order, blocks, 2, weight, sem)
    normed[:HALF] = normalise(own[...], embed[...], gain[...])
    normed[HALF:] = normalise(other[...], embed[...], gain[...])
    wait_fetch(blocks, weight, sem)
    q, k, v = head_parts(normed[...], weight[...], gains[2:3])
    query[...] = q
    kv[...] = jnp.concatenate([k, v], 1)


def space_kernel(order, normed, gains, b0, b1, b2, b3, out, weight, sem):
    blocks = (b0, b1, b2, b3)
    for group in range(2):
        start_fetch(order, blocks, group, weight.at[group], sem.at[group])
    outs = []
    for group in range(2):
        wait_fetch(blocks, weight.at[group], sem.at[group])
        q, k, v = head_parts(normed[...], weight[group], gains[group : group + 1])
        outs.append(attend(q, [(k, v)]).astype(BF16))
    out[...] = jnp.concatenate(outs, 1)


def time_kernel(order, own, other, embed, gain, gains, b0, b1, b2, b3, out, weight, sem):
    blocks = (b0, b1, b2, b3)
    start_fetch(order, blocks, 3, weight, sem)
    parts = [normalise(ref[...], embed[...], gain[...]) for ref in (own, other)]
    wait_fetch(blocks, weight, sem)
    row = lax.broadcasted_iota(jnp.int32, (HALF, HALF), 0) % 8
    col = lax.broadcasted_iota(jnp.int32, (HALF, HALF), 1) % 8
    core = order[4]
    for i, part in enumerate(parts):
        q, k, v = head_parts(part, weight[...], gains[3:4])
        result = attend(q, [(k, v)], row == col)
        place = core if i == 0 else 1 - core
        out[place] = result.astype(BF16)


def cross_kernel(query, left, right, out):
    sides = [(ref[:, :PAIR], ref[:, PAIR:]) for ref in (left, right)]
    out[...] = attend(query[...], sides).astype(BF16)


def out_kernel(order, tokens, embed, own_sc, other_sc, timed, w_out, out):
    core = order[4]
    total = tokens[...].astype(F32) + embed[...]
    for who, ref in ((core, own_sc), (1 - core, other_sc)):
        total += mm(ref[:, : 2 * PAIR], w_out[pl.ds(pl.multiple_of(who * 2 * PAIR, 16), 2 * PAIR)])
        start = pl.multiple_of(8 * HD + who * PAIR, 16)
        total += mm(ref[:, 2 * PAIR :], w_out[pl.ds(start, PAIR)])
    for who in range(2):
        start = 12 * HD + who * PAIR
        total += mm(timed[who], w_out[start : start + PAIR])
    out[...] = total.astype(BF16)


def call(kernel, out_shapes, args, scratch=(), flops=0, anys=0):
    smem = pl.BlockSpec(memory_space=pltpu.SMEM)
    vmem = pl.BlockSpec(memory_space=pltpu.VMEM)
    hbm = pl.BlockSpec(memory_space=pl.ANY)
    specs = []
    for i, arg in enumerate(args):
        if arg.dtype == jnp.int32:
            specs.append(smem)
        else:
            specs.append(hbm if i >= len(args) - anys else vmem)
    moved = sum(a.size * a.dtype.itemsize for a in args)
    single = not isinstance(out_shapes, tuple)
    return pl.pallas_call(
        kernel,
        out_shape=out_shapes,
        in_specs=specs,
        out_specs=vmem if single else (vmem,) * len(out_shapes),
        scratch_shapes=list(scratch),
        compiler_params=pltpu.CompilerParams(vmem_limit_bytes=VMEM_LIMIT),
        cost_estimate=pl.CostEstimate(flops=flops, bytes_accessed=moved, transcendentals=0),
    )(*args)


def by_group(array, rows):
    shaped = array.reshape(rows, -1, HEADS, HD)
    kinds = shaped.shape[1]

    def arranged(low, high, groups):
        part = shaped[:, :, low:high].reshape(rows, kinds, 2, groups, 2, HD)
        return part.transpose(2, 3, 0, 1, 4, 5).reshape(2, groups, rows, kinds * PAIR)

    return jnp.concatenate([arranged(0, 8, 2), arranged(8, 12, 1), arranged(12, 16, 1)], 1)


def local(frames_in, cam_embed, norm_gain, q_gain, k_gain, w_qkv, w_out):
    tokens = frames_in[0]
    core = lax.axis_index("core")
    x, yl, z = lax.axis_index("x"), lax.axis_index("yl"), lax.axis_index("z")
    colour = (x + 2 * yl + 3 * z) % 4
    groups = jnp.arange(4, dtype=jnp.int32)
    order = jnp.where(core == 0, groups - colour, colour - groups) % 4
    order = jnp.concatenate([order, core[None]]).astype(jnp.int32)
    embed = lax.dynamic_slice_in_dim(cam_embed, lax.axis_index(CAM), 1, 0)
    gain = norm_gain[None]
    gains = jnp.concatenate([q_gain, k_gain, jnp.ones_like(q_gain)])[None]
    gains = lax.dynamic_index_in_dim(by_group(gains, 1), core, 0, False).reshape(4, GROUP)

    w_out_all = lax.all_gather(w_out, SLAB, axis=0, tiled=True)

    mine = by_group(w_qkv, 18)
    received = swap_core(lax.dynamic_index_in_dim(mine, 1 - core, 0, False))
    kept = lax.dynamic_index_in_dim(mine, core, 0, False)
    first = jnp.where(core == 0, kept, received)
    second = jnp.where(core == 0, received, kept)
    pair = jnp.concatenate([first, second], 1)
    rolled = lax.dynamic_slice_in_dim(jnp.concatenate([pair, pair[:3]], 0), x, 4, 0)
    pieces = jnp.stack([rolled[(2 * (i // 8) + 3 * (i % 8)) % 4] for i in range(32)])
    time_own = lax.all_to_all(tokens.reshape(32, 8, D), CHIP, 0, 0, tiled=True).reshape(HALF, D)
    b0 = lax.all_to_all(pieces, CHIP, 0, 0, tiled=True).reshape(D, GROUP)
    other = swap_core(tokens)
    time_other = swap_core(time_own)
    blocks = (b0,) + tuple(lax.ppermute(b0, EVERY, r) for r in ROUTES)

    one = [pltpu.VMEM((D, GROUP), BF16), pltpu.SemaphoreType.DMA]
    two = [pltpu.VMEM((2, D, GROUP), BF16), pltpu.SemaphoreType.DMA((2,))]
    rows = 2 * HALF
    query, kv, normed = call(
        cross_project_kernel,
        (
            jax.ShapeDtypeStruct((rows, PAIR), BF16),
            jax.ShapeDtypeStruct((rows, 2 * PAIR), BF16),
            jax.ShapeDtypeStruct((rows, D), BF16),
        ),
        (order, tokens, other, embed, gain, gains) + blocks,
        one,
        2 * rows * D * GROUP,
        4,
    )
    left, right = shift_cam(kv, 1), shift_cam(kv, -1)
    timed = call(
        time_kernel,
        jax.ShapeDtypeStruct((2, HALF, PAIR), BF16),
        (order, time_own, time_other, embed, gain, gains) + blocks,
        one,
        2 * rows * D * GROUP,
        4,
    )
    timed = timed.reshape(2, 32, 8, PAIR).transpose(1, 0, 2, 3).reshape(64, 8, PAIR)
    timed = lax.all_to_all(timed, SLAB, 0, 0, tiled=True)
    timed = timed.reshape(32, 2, 8, PAIR).transpose(1, 0, 2, 3).reshape(2, HALF, PAIR)
    space = call(
        space_kernel,
        jax.ShapeDtypeStruct((rows, 2 * PAIR), BF16),
        (order, normed, gains) + blocks,
        two,
        4 * rows * D * GROUP,
        4,
    )
    cross = call(cross_kernel, jax.ShapeDtypeStruct((rows, PAIR), BF16), (query, left, right), (), 8 * rows * rows * 256)
    mixed = jnp.concatenate([space, cross], 1)
    arrived = swap_core(mixed[HALF:])
    return call(
        out_kernel,
        jax.ShapeDtypeStruct((HALF, D), BF16),
        (order, tokens, embed, mixed[:HALF], arrived, timed, w_out_all),
        (),
        2 * HALF * D * D,
    )[None]


def solution(mesh):
    fine = Mesh(mesh.devices.reshape(4, 2, 4, 8, 2), EVERY)
    placed = (P(CAM, SLAB, None), P(), P(), P(), P(), P(SLAB, None), P(SLAB, None))
    return jax.shard_map(local, mesh=fine, in_specs=placed, out_specs=P(CAM, SLAB, None), check_vma=False)
```

time: 374 us -> 205 us (0.55)
  the two profiles are of different devices: /device:TPU:17 before, /device:TPU:1 now
where the time goes in v1:
time: 205 us; the launch traced here: 203 us
  starting transfers between devices  62.5 us (30%)
  blocking collectives  44 us (21%)
  waiting for transfers between devices  30.9 us (15%)
  local copies, waits for them, and re-layouts  26.8 us (13%)
  Pallas kernels  22.6 us (11%)
  between operations  13.9 us (7%)
    all_to_all x1, blocking collectives, local(): b0 = lax.all_to_all(pieces, CHIP, 0, 0, tiled=True).reshape(D, GROUP)  44 us
    pallas_call x5, Pallas kernels, call(): pl.pallas_call(kernel, out_shape=out_shapes, in_specs=specs, out_specs=vm...  22.6 us
    ppermute x4, starting transfers between devices, swap_core(): return lax.ppermute(block, 'core', [(0, 1), (1, 0)])  22.4 us
    all_gather x1, waiting for transfers between devices, local(): w_out_all = lax.all_gather(w_out, SLAB, axis=0, tiled=True)  15.7 us
    all_to_all x1, starting transfers between devices, local(): timed = lax.all_to_all(timed, SLAB, 0, 0, tiled=True)  13.6 us
    all_to_all x1, waiting for transfers between devices, local(): timed = lax.all_to_all(timed, SLAB, 0, 0, tiled=True)  13 us
    ppermute x2, starting transfers between devices, shift_cam(): return lax.ppermute(block, CAM, [(i, (i + distance) % 8) for i in range(8)])  11.3 us
    ppermute x3, starting transfers between devices, local(): blocks = (b0,) + tuple((lax.ppermute(b0, EVERY, r) for r in ROUTES))  9.49 us
  transfers between devices with their start and end apart: 12, of which 4 were waited for; matrix products, arithmetic and copies ran while one was open for 13% of the time, Pallas kernels for 9%

profile of v1, /device:TPU:1, one launch (start us, length us, event | category | flops | bytes accessed | tf_op | source)
XLA Modules:
  0.0 202.8 jit_solution(16545437080233698113)
XLA Ops:
  6.5 0.7 all-gather.3.cloned.1.call-update
  7.3 1.3 reshape.68
  8.7 0.1 reshape.86
  8.9 0.1 reshape.85
  9.0 0.1 copy.33
  9.1 0.2 reshape.70
  9.2 0.3 pad_maximum_fusion.1
  9.6 8.8 %collective-permute-start.1 = (bf16[4,18,432]{2,0,1:T(4,128)(2,1)S(1)}, bf16[4,18,432]{2,0,1:T(4,128)(2,1)S(1)}, u32[]{:S(2)}, u32[]{:S(2)}) collective-permute-start(bf16[4,18,432]{2,0,1:T(4,128)(2,1)S(1)} %dynamic-slice_bitcast_fusion), channel_id=1, source_target_pairs={{0,1},{1,0},{2,3},{3,2},{4,5},{5,4},{6,7},{7,6},{8,9},{9,8},{10,11... | collective-permute-start | bytes 186632 | tf_op jit(solution)/shard_map/ppermute | solution.py:53
  18.4 0.9 collective-permute-done.1
  19.3 0.7 fusion.2
  20.1 0.1 slice.95
  20.1 0.2 fusion.9
  20.4 6.8 %stack.4 = bf16[32,36,432]{2,0,1:T(8,128)(2,1)S(1)} concatenate(bf16[1,36,432]{2,0,1:T(2,128)(2,1)S(1)} %get-tuple-element.20, bf16[1,36,432]{2,0,1:T(2,128)(2,1)S(1)} %get-tuple-element.19, bf16[1,36,432]{2,0,1:T(2,128)(2,1)S(1)} %get-tuple-element.18, bf16[1,36,432]{2,0,1:T(2,128)(2,1)S(1)} %get-tuple-element.17, bf16[1,36,432]{2,0,1:T(2,128)(2,1)S(1)} %get-tuple-element.20, ...), dimensions={0} | concatenate | bytes 1990656 | tf_op jit(solution)/shard_map/stack | solution.py:233
  27.2 0.7 copy.38
  27.9 44.0 %all_to_all.15 = bf16[32,36,432]{2,1,0:T(8,128)(2,1)S(1)} all-to-all(bf16[32,36,432]{2,1,0:T(8,128)(2,1)S(1)} %copy.38), channel_id=1, replica_groups=mesh['x'=4,'yh'=2,'yl'=4,'z'=8,'core'=2] {'yl','z'}, dimensions={0} | all-to-all | bytes 1990656 | tf_op jit(solution)/shard_map/all_to_all | solution.py:235
  71.9 5.7 %all-to-all-start.1 = ((bf16[32,8,1152]{2,1,0:T(8,128)(2,1)}), bf16[32,8,1152]{2,1,0:T(8,128)(2,1)S(1)}, u32[]{:S(2)}, u32[]{:S(2)}) async-start(bf16[32,8,1152]{2,1,0:T(8,128)(2,1)} %bitcast.17), calls=%async_computation.1 | async-start | bytes 1179648 | tf_op jit(solution)/shard_map/all_to_all | solution.py:234
  77.7 0.5 reshape.75.b0
  78.2 0.9 copy.39
  79.1 3.3 %collective-permute-start.2 = (bf16[1152,432]{0,1:T(8,128)(2,1)S(1)}, bf16[1152,432]{0,1:T(8,128)(2,1)}, u32[]{:S(2)}, u32[]{:S(2)}) collective-permute-start(bf16[1152,432]{0,1:T(8,128)(2,1)S(1)} %copy.39), channel_id=1, source_target_pairs={{0,384},{1,129},{2,386},{3,131},{4,388},{5,133},{6,390},{7,135},{8... | collective-permute-start | bytes 2985992 | tf_op jit(solution)/shard_map/ppermute | solution.py:238
  82.4 3.1 %collective-permute-start.3 = (bf16[1152,432]{0,1:T(8,128)(2,1)S(1)}, bf16[1152,432]{0,1:T(8,128)(2,1)}, u32[]{:S(2)}, u32[]{:S(2)}) collective-permute-start(bf16[1152,432]{0,1:T(8,128)(2,1)S(1)} %copy.39), channel_id=1, source_target_pairs={{0,112},{1,17},{2,114},{3,19},{4,116},{5,21},{6,118},{7,23},{8,120... | collective-permute-start | bytes 2985992 | tf_op jit(solution)/shard_map/ppermute | solution.py:238
  85.5 3.1 %collective-permute-start.4 = (bf16[1152,432]{0,1:T(8,128)(2,1)S(1)}, bf16[1152,432]{0,1:T(8,128)(2,1)}, u32[]{:S(2)}, u32[]{:S(2)}) collective-permute-start(bf16[1152,432]{0,1:T(8,128)(2,1)S(1)} %copy.39), channel_id=1, source_target_pairs={{0,14},{1,3},{2,0},{3,5},{4,2},{5,7},{6,4},{7,9},{8,6},{9,11},{10,... | collective-permute-start | bytes 2985992 | tf_op jit(solution)/shard_map/ppermute | solution.py:238
  88.6 7.8 %collective-permute-start = (bf16[256,1152]{1,0:T(8,128)(2,1)}, bf16[256,1152]{1,0:T(8,128)(2,1)}, u32[]{:S(2)}, u32[]{:S(2)}) collective-permute-start(bf16[256,1152]{1,0:T(8,128)(2,1)} %bitcast.1.own.tokens), channel_id=1, source_target_pairs={{0,1},{1,0},{2,3},{3,2},{4,5},{5,4},{6,7},{7,6},{8,9},{9,8},{10,11... | collective-permute-start | bytes 1769480 | tf_op jit(solution)/shard_map/ppermute | solution.py:53
  96.4 0.1 reshape_broadcast_in_dim.3
  96.6 3.2 %collective-permute-start.8 = (bf16[256,1152]{1,0:T(8,128)(2,1)S(1)}, bf16[256,1152]{1,0:T(8,128)(2,1)}, u32[]{:S(2)}, u32[]{:S(2)}) collective-permute-start(bf16[256,1152]{1,0:T(8,128)(2,1)S(1)} %bitcast.53), channel_id=1, source_target_pairs={{0,1},{1,0},{2,3},{3,2},{4,5},{5,4},{6,7},{7,6},{8,9},{9,8},{10,11... | collective-permute-start | bytes 1769480 | tf_op jit(solution)/shard_map/ppermute | solution.py:53
  99.9 0.1 reshape.62
  100.0 0.1 reshape.83
  100.1 0.1 reshape.84
  100.3 2.4 %copy.42.b1 = bf16[1152,432]{1,0:T(8,128)(2,1)} copy(bf16[1152,432]{0,1:T(8,128)(2,1)} %collective-permute-done.2) | data formatting | bytes 1990656 | tf_op jit(solution)/shard_map/ppermute | solution.py:238
  102.7 2.4 %copy.43.b2 = bf16[1152,432]{1,0:T(8,128)(2,1)} copy(bf16[1152,432]{0,1:T(8,128)(2,1)} %collective-permute-done.3) | data formatting | bytes 1990656 | tf_op jit(solution)/shard_map/ppermute | solution.py:238
  105.1 0.6 collective-permute-done.4
  105.8 2.4 %copy.44.b3 = bf16[1152,432]{1,0:T(8,128)(2,1)} copy(bf16[1152,432]{0,1:T(8,128)(2,1)} %collective-permute-done.4) | data formatting | bytes 1990656 | tf_op jit(solution)/shard_map/ppermute | solution.py:238
  108.2 4.9 %shard_map.73 = (bf16[512,144]{1,0:T(8,128)(2,1)S(1)}, bf16[512,288]{1,0:T(8,128)(2,1)S(1)}, bf16[512,1152]{1,0:T(8,128)(2,1)S(1)}) custom-call(s32[5]{0:T(128)S(1)} %pad_add_fusion.order, bf16[256,1152]{1,0:T(8,128)(2,1)} %bitcast.1.own.tokens, bf16[256,1152]{1,0:T(8,128)(2,1)} %collective-permute-done.other, ...), custom_call_target="tpu_custom_call" | custom-call | flops 509607936 | bytes 5177108 | tf_op jit(solution)/shard_map/pallas_call | solution.py:189
  113.1 1.1 copy-done.4
  114.2 4.5 %collective-permute-start.5 = (bf16[512,288]{1,0:T(8,128)(2,1)S(1)}, bf16[512,288]{1,0:T(8,128)(2,1)}, u32[]{:S(2)}, u32[]{:S(2)}) collective-permute-start(bf16[512,288]{1,0:T(8,128)(2,1)S(1)} %get-tuple-element.10), channel_id=1, source_target_pairs={{0,64},{64,128},{128,192},{192,256},{256,320},{320,384},{384,448},... | collective-permute-start | bytes 884744 | tf_op jit(solution)/shard_map/ppermute | solution.py:49
  118.7 6.8 %collective-permute-start.6 = (bf16[512,288]{1,0:T(8,128)(2,1)S(1)}, bf16[512,288]{1,0:T(8,128)(2,1)}, u32[]{:S(2)}, u32[]{:S(2)}) collective-permute-start(bf16[512,288]{1,0:T(8,128)(2,1)S(1)} %get-tuple-element.10), channel_id=1, source_target_pairs={{0,448},{64,0},{128,64},{192,128},{256,192},{320,256},{384,320},{4... | collective-permute-start | bytes 884744 | tf_op jit(solution)/shard_map/ppermute | solution.py:49
  125.5 5.0 %shard_map.76 = bf16[2,256,144]{2,1,0:T(8,128)(2,1)S(1)} custom-call(s32[5]{0:T(128)S(1)} %pad_add_fusion.order, bf16[256,1152]{1,0:T(8,128)(2,1)S(1)} %bitcast.54, bf16[256,1152]{1,0:T(8,128)(2,1)} %collective-permute-done.8.other, f32[1,1152]{1,0:T(1,128)S(1)} %constant_dynamic-slice_fusion.embed, f32[1,1152]{1,0:T(1,128)S(1)} %broadcast_in_dim.13.gain, ...), custom_call_target="tpu_custom_call" | custom-call | flops 509607936 | bytes 5177108 | tf_op jit(solution)/shard_map/pallas_call | solution.py:189
  130.5 0.7 copy.51
  131.3 13.6 %all-to-all-start.2 = ((bf16[64,8,144]{2,1,0:T(8,128)(2,1)}), bf16[64,8,144]{2,1,0:T(8,128)(2,1)}, u32[]{:S(2)}, u32[]{:S(2)}) async-start(bf16[64,8,144]{2,1,0:T(8,128)(2,1)} %bitcast.21), calls=%async_computation.2 | async-start | bytes 524288 | tf_op jit(solution)/shard_map/all_to_all | solution.py:265
  144.8 1.3 copy-done.5
  146.1 6.5 %shard_map.74 = bf16[512,288]{1,0:T(8,128)(2,1)S(1)} custom-call(s32[5]{0:T(128)S(1)} %pad_add_fusion.order, bf16[512,1152]{1,0:T(8,128)(2,1)S(1)} %copy-done.5, f32[4,432]{1,0:T(4,128)S(1)} %fusion.6.gains, bf16[1152,432]{1,0:T(8,128)(2,1)S(1)} %copy-done.2, bf16[1152,432]{1,0:T(8,128)(2,1)S(1)} %copy-done.3, bf16[1152,432]{1,0:T(8,128)(2,1)} %copy.43.b2, ...), custom_call_target="tpu_custom_call" | custom-call | flops 1019215872 | bytes 5167892 | tf_op jit(solution)/shard_map/pallas_call | solution.py:189
  152.7 2.9 %shard_map.75 = bf16[512,144]{1,0:T(8,128)(2,1)S(1)} custom-call(bf16[512,144]{1,0:T(8,128)(2,1)S(1)} %copy-done.7, bf16[512,288]{1,0:T(8,128)(2,1)} %collective-permute-done.5.left, bf16[512,288]{1,0:T(8,128)(2,1)} %collective-permute-done.6.right), custom_call_target="tpu_custom_call" | custom-call | flops 536870912 | bytes 737280 | tf_op jit(solution)/shard_map/pallas_call | solution.py:189
  155.5 0.8 pad_maximum_fusion
  156.4 2.7 %collective-permute-start.7 = (bf16[256,432]{1,0:T(8,128)(2,1)}, bf16[256,432]{1,0:T(8,128)(2,1)S(1)}, u32[]{:S(2)}, u32[]{:S(2)}) collective-permute-start(bf16[256,432]{1,0:T(8,128)(2,1)} %get-tuple-element.11), channel_id=1, source_target_pairs={{0,1},{1,0},{2,3},{3,2},{4,5},{5,4},{6,7},{7,6},{8,9},{9,8},{10,11... | collective-permute-start | bytes 663560 | tf_op jit(solution)/shard_map/ppermute | solution.py:53
  159.0 13.0 %all-to-all-done.2 = bf16[64,8,144]{2,1,0:T(8,128)(2,1)} async-done(((bf16[64,8,144]{2,1,0:T(8,128)(2,1)}), bf16[64,8,144]{2,1,0:T(8,128)(2,1)}, u32[]{:S(2)}, u32[]{:S(2)}) %all-to-all-start.2) | async-done | bytes 147488 | tf_op jit(solution)/shard_map/all_to_all | solution.py:265
  172.0 1.0 copy.58
  173.0 15.7 %all-gather.3.cloned.1.call-done = bf16[64,18,1152]{2,1,0:T(8,128)(2,1)} async-done(((bf16[1,18,1152]{2,1,0:T(8,128)(2,1)}), bf16[64,18,1152]{2,1,0:T(8,128)(2,1)}) %all-gather.3.cloned.1.call-update) | async-done | bytes 2654224 | tf_op jit(solution)/shard_map/all_gather | solution.py:224
  188.7 3.9 %reshape.82.w_out = bf16[1152,1152]{1,0:T(8,128)(2,1)S(1)} reshape(bf16[64,18,1152]{2,1,0:T(8,128)(2,1)} %all-gather.3.cloned.1.call-done) | data formatting | bytes 5308416
  192.6 3.4 %shard_map.77 = bf16[256,1152]{1,0:T(8,128)(2,1)} custom-call(s32[5]{0:T(128)S(1)} %pad_add_fusion.order, bf16[256,1152]{1,0:T(8,128)(2,1)} %bitcast.1.own.tokens, f32[1,1152]{1,0:T(1,128)S(1)} %constant_dynamic-slice_fusion.embed, bf16[256,432]{1,0:T(8,128)(2,1)S(1)} %get-tuple-element.12.own_sc, bf16[256,432]{1,0:T(8,128)(2,1)S(1)} %collective-permute-done.7.other_sc, ...), custom_call_target="tpu_custom_call" | custom-call | flops 679477248 | bytes 3838484 | tf_op jit(solution)/shard_map/pallas_call | solution.py:189
  (47 shorter events, 0.5 us)
Async XLA Ops:
  6.5 93.7 %copy-start = (f32[8,1152]{1,0:T(8,128)S(1)}, f32[8,1152]{1,0:T(8,128)}, u32[]{:S(2)}) copy-start(f32[8,1152]{1,0:T(8,128)} %param.8) | copy-start | bytes 110596
  6.5 182.1 %all-gather.3.cloned.1.call-start = ((), (), s32[]{:S(2)}) async-start(), calls=%async_computation.3 | async-start | bytes 3594240 | tf_op jit(solution)/shard_map/all_gather | solution.py:224
  9.6 9.7 %collective-permute-start.1 = (bf16[4,18,432]{2,0,1:T(4,128)(2,1)S(1)}, bf16[4,18,432]{2,0,1:T(4,128)(2,1)S(1)}, u32[]{:S(2)}, u32[]{:S(2)}) collective-permute-start(bf16[4,18,432]{2,0,1:T(4,128)(2,1)S(1)} %dynamic-slice_bitcast_fusion), channel_id=1, source_target_pairs={{0,1},{1,0},{2,3},{3,2},{4,5},{5,4},{6,7},{7,6},{8,9},{9,8},{10,11... | collective-permute-start | bytes 186632 | tf_op jit(solution)/shard_map/ppermute | solution.py:53
  71.9 24.7 %all-to-all-start.1 = ((bf16[32,8,1152]{2,1,0:T(8,128)(2,1)}), bf16[32,8,1152]{2,1,0:T(8,128)(2,1)S(1)}, u32[]{:S(2)}, u32[]{:S(2)}) async-start(bf16[32,8,1152]{2,1,0:T(8,128)(2,1)} %bitcast.17), calls=%async_computation.1 | async-start | bytes 1179648 | tf_op jit(solution)/shard_map/all_to_all | solution.py:234
  78.2 21.7 %copy-start.1 = (bf16[1152,432]{1,0:T(8,128)(2,1)}, bf16[1152,432]{1,0:T(8,128)(2,1)S(1)}, u32[]{:S(2)}) copy-start(bf16[1152,432]{1,0:T(8,128)(2,1)S(1)} %reshape.75.b0) | copy-start | bytes 2985988
  78.2 18.2 %copy-start.8 = (f32[1152]{0:T(1024)S(1)}, f32[1152]{0:T(1024)}, u32[]{:S(2)}) copy-start(f32[1152]{0:T(1024)} %param.11) | copy-start | bytes 13828
  78.2 18.2 %copy-start.9 = (f32[1152]{0:T(1024)S(1)}, f32[1152]{0:T(1024)}, u32[]{:S(2)}) copy-start(f32[1152]{0:T(1024)} %param.10) | copy-start | bytes 13828
  78.2 21.7 %copy-start.10 = (f32[1152]{0:T(1024)S(1)}, f32[1152]{0:T(1024)}, u32[]{:S(2)}) copy-start(f32[1152]{0:T(1024)} %param.9) | copy-start | bytes 13828
  79.1 21.1 %collective-permute-start.2 = (bf16[1152,432]{0,1:T(8,128)(2,1)S(1)}, bf16[1152,432]{0,1:T(8,128)(2,1)}, u32[]{:S(2)}, u32[]{:S(2)}) collective-permute-start(bf16[1152,432]{0,1:T(8,128)(2,1)S(1)} %copy.39), channel_id=1, source_target_pairs={{0,384},{1,129},{2,386},{3,131},{4,388},{5,133},{6,390},{7,135},{8... | collective-permute-start | bytes 2985992 | tf_op jit(solution)/shard_map/ppermute | solution.py:238
  82.4 20.3 %collective-permute-start.3 = (bf16[1152,432]{0,1:T(8,128)(2,1)S(1)}, bf16[1152,432]{0,1:T(8,128)(2,1)}, u32[]{:S(2)}, u32[]{:S(2)}) collective-permute-start(bf16[1152,432]{0,1:T(8,128)(2,1)S(1)} %copy.39), channel_id=1, source_target_pairs={{0,112},{1,17},{2,114},{3,19},{4,116},{5,21},{6,118},{7,23},{8,120... | collective-permute-start | bytes 2985992 | tf_op jit(solution)/shard_map/ppermute | solution.py:238
  85.5 20.2 %collective-permute-start.4 = (bf16[1152,432]{0,1:T(8,128)(2,1)S(1)}, bf16[1152,432]{0,1:T(8,128)(2,1)}, u32[]{:S(2)}, u32[]{:S(2)}) collective-permute-start(bf16[1152,432]{0,1:T(8,128)(2,1)S(1)} %copy.39), channel_id=1, source_target_pairs={{0,14},{1,3},{2,0},{3,5},{4,2},{5,7},{6,4},{7,9},{8,6},{9,11},{10,... | collective-permute-start | bytes 2985992 | tf_op jit(solution)/shard_map/ppermute | solution.py:238
  88.6 19.6 %collective-permute-start = (bf16[256,1152]{1,0:T(8,128)(2,1)}, bf16[256,1152]{1,0:T(8,128)(2,1)}, u32[]{:S(2)}, u32[]{:S(2)}) collective-permute-start(bf16[256,1152]{1,0:T(8,128)(2,1)} %bitcast.1.own.tokens), channel_id=1, source_target_pairs={{0,1},{1,0},{2,3},{3,2},{4,5},{5,4},{6,7},{7,6},{8,9},{9,8},{10,11... | collective-permute-start | bytes 1769480 | tf_op jit(solution)/shard_map/ppermute | solution.py:53
  96.6 28.9 %collective-permute-start.8 = (bf16[256,1152]{1,0:T(8,128)(2,1)S(1)}, bf16[256,1152]{1,0:T(8,128)(2,1)}, u32[]{:S(2)}, u32[]{:S(2)}) collective-permute-start(bf16[256,1152]{1,0:T(8,128)(2,1)S(1)} %bitcast.53), channel_id=1, source_target_pairs={{0,1},{1,0},{2,3},{3,2},{4,5},{5,4},{6,7},{7,6},{8,9},{9,8},{10,11... | collective-permute-start | bytes 1769480 | tf_op jit(solution)/shard_map/ppermute | solution.py:53
  108.2 17.3 %copy-start.2 = (bf16[1152,432]{1,0:T(8,128)(2,1)S(1)}, bf16[1152,432]{1,0:T(8,128)(2,1)}, u32[]{:S(2)}) copy-start(bf16[1152,432]{1,0:T(8,128)(2,1)} %copy-done.1) | copy-start | bytes 2985988
  108.2 17.3 %copy-start.3 = (bf16[1152,432]{1,0:T(8,128)(2,1)S(1)}, bf16[1152,432]{1,0:T(8,128)(2,1)}, u32[]{:S(2)}) copy-start(bf16[1152,432]{1,0:T(8,128)(2,1)} %copy.42.b1) | copy-start | bytes 2985988
  113.1 1.1 copy-start.4
  114.2 16.3 %copy-start.6 = (bf16[512,144]{1,0:T(8,128)(2,1)}, bf16[512,144]{1,0:T(8,128)(2,1)S(1)}, u32[]{:S(2)}) copy-start(bf16[512,144]{1,0:T(8,128)(2,1)S(1)} %get-tuple-element.9.query) | copy-start | bytes 442372
  114.2 38.4 %collective-permute-start.5 = (bf16[512,288]{1,0:T(8,128)(2,1)S(1)}, bf16[512,288]{1,0:T(8,128)(2,1)}, u32[]{:S(2)}, u32[]{:S(2)}) collective-permute-start(bf16[512,288]{1,0:T(8,128)(2,1)S(1)} %get-tuple-element.10), channel_id=1, source_target_pairs={{0,64},{64,128},{128,192},{192,256},{256,320},{320,384},{384,448},... | collective-permute-start | bytes 884744 | tf_op jit(solution)/shard_map/ppermute | solution.py:49
  118.7 33.9 %collective-permute-start.6 = (bf16[512,288]{1,0:T(8,128)(2,1)S(1)}, bf16[512,288]{1,0:T(8,128)(2,1)}, u32[]{:S(2)}, u32[]{:S(2)}) collective-permute-start(bf16[512,288]{1,0:T(8,128)(2,1)S(1)} %get-tuple-element.10), channel_id=1, source_target_pairs={{0,448},{64,0},{128,64},{192,128},{256,192},{320,256},{384,320},{4... | collective-permute-start | bytes 884744 | tf_op jit(solution)/shard_map/ppermute | solution.py:49
  131.3 40.8 %all-to-all-start.2 = ((bf16[64,8,144]{2,1,0:T(8,128)(2,1)}), bf16[64,8,144]{2,1,0:T(8,128)(2,1)}, u32[]{:S(2)}, u32[]{:S(2)}) async-start(bf16[64,8,144]{2,1,0:T(8,128)(2,1)} %bitcast.21), calls=%async_computation.2 | async-start | bytes 524288 | tf_op jit(solution)/shard_map/all_to_all | solution.py:265
  144.8 1.3 copy-start.5
  146.1 6.5 %copy-start.7 = (bf16[512,144]{1,0:T(8,128)(2,1)S(1)}, bf16[512,144]{1,0:T(8,128)(2,1)}, u32[]{:S(2)}) copy-start(bf16[512,144]{1,0:T(8,128)(2,1)} %copy-done.6) | copy-start | bytes 442372
  156.4 36.2 %collective-permute-start.7 = (bf16[256,432]{1,0:T(8,128)(2,1)}, bf16[256,432]{1,0:T(8,128)(2,1)S(1)}, u32[]{:S(2)}, u32[]{:S(2)}) collective-permute-start(bf16[256,432]{1,0:T(8,128)(2,1)} %get-tuple-element.11), channel_id=1, source_target_pairs={{0,1},{1,0},{2,3},{3,2},{4,5},{5,4},{6,7},{7,6},{8,9},{9,8},{10,11... | collective-permute-start | bytes 663560 | tf_op jit(solution)/shard_map/ppermute | solution.py:53
Sparse Core Ops, SparseCore 0:
  9.5 179.1 all-gather.2

commit v2 on v1

v2 whole, which is shorter than its diff:
```python
import jax
import jax.numpy as jnp
from jax import lax
from jax.experimental import pallas as pl
from jax.experimental.pallas import tpu as pltpu
from jax.sharding import Mesh
from jax.sharding import PartitionSpec as P

HEADS = 16
HD = 72
D = HEADS * HD
PAIR = 2 * HD
TRIPLE = 3 * HD
HALF = 256
ROWS = 2 * HALF
FIRST = TRIPLE
SECOND = PAIR + TRIPLE
CAM = ("x", "yh")
CHIP = ("yl", "z")
SLAB = ("yl", "z", "core")
EVERY = ("x", "yh", "yl", "z", "core")
SCALE = 1.4426950408889634 / HD**0.5
F32 = jnp.float32
BF16 = jnp.bfloat16
VMEM_LIMIT = 50 * 1024 * 1024


def route(move):
    pairs = []
    for x in range(4):
        for y in range(8):
            for z in range(8):
                for core in range(2):
                    a, b, c = move(x, y, z, core)
                    source = ((x * 8 + y) * 8 + z) * 2 + core
                    pairs.append((source, ((a % 4 * 8 + b % 8) * 8 + c % 8) * 2 + core))
    return pairs


def towards(core):
    return 1 if core else -1


ROUTES = (
    route(lambda x, y, z, core: (x + towards(core), y, z)),
    route(lambda x, y, z, core: (x, y + towards(core), z)),
    route(lambda x, y, z, core: (x, y, z + towards(core))),
)

ACROSS = route(lambda x, y, z, core: (x, y + 4, z))
ALONG = route(lambda x, y, z, core: (x + (1 if y < 4 else -1), y, z))


def swap_core(block):
    return lax.ppermute(block, "core", [(0, 1), (1, 0)])


def mm(a, b):
    return jnp.dot(a, b, preferred_element_type=F32)


def mm_t(a, b):
    return lax.dot_general(a, b, (((1,), (1,)), ((), ())), preferred_element_type=F32)


def after(value, *others):
    return lax.optimization_barrier((value,) + others)[0]


def arrange_kernel(order, w_qkv, w_out, out):
    core = order[4]

    def columns(kind, head, count):
        start = kind * D + head * HD
        return w_qkv[:, start : start + count * HD]

    for who in range(2):
        place = (who + core) % 2
        for group in range(4):
            head = (8, 12)[group // 2] + 2 * who
            if group % 2 == 0:
                first = [columns(0, head, 2), columns(1, head, 1)]
            else:
                first = [columns(1, head + 1, 1), columns(2, head, 2)]
            start = (who * 4 + group) * PAIR
            one = 4 * who + group
            second = [w_out[:, start : start + PAIR]] + [columns(kind, one, 1) for kind in range(3)]
            out[place, group] = jnp.concatenate(first + second, 1)


def pack_kernel(order, pair, out):
    x = order[5]
    for i in range(32):
        out[i] = pair[(x + 2 * (i // 8) + 3 * (i % 8)) % 4]


def norm_kernel(own, other, embed, gain, out):
    for i, ref in enumerate((own, other)):
        hidden = ref[...].astype(F32) + embed[...]
        centred = hidden - jnp.mean(hidden, -1, keepdims=True)
        variance = jnp.mean(centred * centred, -1, keepdims=True)
        out[i * HALF : (i + 1) * HALF] = (centred * lax.rsqrt(variance + 1e-06) * gain[...]).astype(BF16)


def start_fetch(order, blocks, group, slot, sem):
    for j, block in enumerate(blocks):
        @pl.when(order[group] == j)
        def _(block=block):
            pltpu.make_async_copy(block, slot, sem).start()


def wait_fetch(blocks, slot, sem):
    pltpu.make_async_copy(blocks[0], slot, sem).wait()


def head_norm(part, gain):
    shaped = part.reshape(part.shape[0] // HD, HD, part.shape[1])
    mean_sq = jnp.mean(shaped * shaped, 1, keepdims=True)
    return (shaped * lax.rsqrt(mean_sq + 1e-06)).reshape(part.shape) * gain


def attend(q_t, sides, mask=None):
    total = None
    for k_t, v_t in sides:
        scores = mm(k_t.T.astype(BF16), q_t.astype(BF16))
        expd = jnp.exp2(scores * SCALE)
        if mask is not None:
            expd = jnp.where(mask, expd, 0.0)
        wide = jnp.concatenate([v_t, jnp.ones((8, v_t.shape[1]), F32)], 0).astype(BF16)
        part = mm(wide, expd.astype(BF16))
        total = part if total is None else total + part
    return total[:HD] / total[HD : HD + 1]


def project_pair(normed, weight, gains):
    projected = jnp.concatenate([mm_t(weight[i], normed[...]) for i in range(2)], 0)
    return head_norm(projected[: 2 * PAIR], gains), projected[2 * PAIR :]


def cross_project_kernel(order, normed, gains, b0, b1, b2, b3, q_t, kv_t, weight, sem):
    blocks = (b0, b1, b2, b3)
    for group in range(2):
        start_fetch(order, blocks, group, weight.at[group], sem.at[group])
    for group in range(2):
        wait_fetch(blocks, weight.at[group], sem.at[group])
    qk, v = project_pair(normed, weight, gains[0])
    q_t[...] = qk[:PAIR].astype(BF16)
    kv_t[...] = jnp.concatenate([qk[PAIR:], v], 0).astype(BF16)


def time_kernel(order, normed, gains, b0, b1, b2, b3, out, weight, sem):
    blocks = (b0, b1, b2, b3)
    for group in range(2):
        start_fetch(order, blocks, 2 + group, weight.at[group], sem.at[group])
    for group in range(2):
        wait_fetch(blocks, weight.at[group], sem.at[group])
    qk, v = project_pair(normed, weight, gains[1])
    row = lax.broadcasted_iota(jnp.int32, (HALF, HALF), 0) % 8
    col = lax.broadcasted_iota(jnp.int32, (HALF, HALF), 1) % 8
    core = order[4]
    for i in range(2):
        part = slice(i * HALF, (i + 1) * HALF)
        heads = []
        for head in range(2):
            at = head * HD
            side = (qk[PAIR + at : PAIR + at + HD, part], v[at : at + HD, part])
            heads.append(attend(qk[at : at + HD, part], [side], row == col))
        place = core if i == 0 else 1 - core
        out[place] = jnp.concatenate(heads, 0).T.astype(BF16)


def space_kernel(order, normed, gains, b0, b1, b2, b3, out, w_out, weight, sem):
    blocks = (b0, b1, b2, b3)
    for group in range(4):
        start_fetch(order, blocks, group, weight.at[group], sem.at[group])
    for group in range(4):
        wait_fetch(blocks, weight.at[group], sem.at[group])
        w_out[group * PAIR : (group + 1) * PAIR] = weight[group, :PAIR]
    heads = []
    for group in range(4):
        projected = mm_t(weight[group, PAIR:], normed[...])
        qk = head_norm(projected[:PAIR], gains[group])
        heads.append(attend(qk[:HD], [(qk[HD:], projected[PAIR:])]))
    out[...] = jnp.concatenate(heads, 0).astype(BF16)


def cross_kernel(q_t, kv_a, kv_b, out):
    query = q_t[...].astype(F32)
    both = [ref[...].astype(F32) for ref in (kv_a, kv_b)]
    heads = []
    for head in range(2):
        at = head * HD
        sides = [(kv[at : at + HD], kv[PAIR + at : PAIR + at + HD]) for kv in both]
        heads.append(attend(query[at : at + HD], sides))
    out[...] = jnp.concatenate(heads, 0).astype(BF16)


def out_kernel(order, tokens, embed, own, arrived, timed, w_own, w_other, out):
    swap = order[4] == 1
    mine, theirs = own[...].astype(F32), arrived[...].astype(F32)
    first = jnp.where(swap, theirs, mine)
    second = jnp.where(swap, mine, theirs)
    split = 2 * PAIR
    mixed_t = jnp.concatenate([first[:split], second[:split], first[split:], second[split:]], 0)
    mixed = jnp.concatenate([mixed_t.T.astype(BF16), timed[0], timed[1]], 1)
    one, two = mm_t(mixed, w_own[...]), mm_t(mixed, w_other[...])
    update = jnp.concatenate([jnp.where(swap, two, one), jnp.where(swap, one, two)], 1)
    out[...] = (tokens[...].astype(F32) + embed[...] + update).astype(BF16)


def call(kernel, out_shapes, args, scratch=(), flops=0, anys=0):
    smem = pl.BlockSpec(memory_space=pltpu.SMEM)
    vmem = pl.BlockSpec(memory_space=pltpu.VMEM)
    hbm = pl.BlockSpec(memory_space=pl.ANY)
    specs = []
    for i, arg in enumerate(args):
        if arg.dtype == jnp.int32:
            specs.append(smem)
        else:
            specs.append(hbm if i >= len(args) - anys else vmem)
    moved = sum(a.size * a.dtype.itemsize for a in args)
    single = not isinstance(out_shapes, tuple)
    return pl.pallas_call(
        kernel,
        out_shape=out_shapes,
        in_specs=specs,
        out_specs=vmem if single else (vmem,) * len(out_shapes),
        scratch_shapes=list(scratch),
        compiler_params=pltpu.CompilerParams(vmem_limit_bytes=VMEM_LIMIT),
        cost_estimate=pl.CostEstimate(flops=flops, bytes_accessed=1, transcendentals=0),
    )(*args)


def shape(*dims):
    return jax.ShapeDtypeStruct(dims, BF16)


def local(frames_in, cam_embed, norm_gain, q_gain, k_gain, w_qkv, w_out):
    tokens = frames_in[0]
    core = lax.axis_index("core")
    x, yl, z = lax.axis_index("x"), lax.axis_index("yl"), lax.axis_index("z")
    colour = (x + 2 * yl + 3 * z) % 4
    groups = jnp.arange(4, dtype=jnp.int32)
    order = jnp.where(core == 0, groups - colour, colour - groups) % 4
    order = jnp.concatenate([order, core[None], x[None]]).astype(jnp.int32)
    embed = lax.dynamic_slice_in_dim(cam_embed, lax.axis_index(CAM), 1, 0)
    gain = norm_gain[None]
    both = jnp.stack([q_gain.reshape(HEADS, HD), k_gain.reshape(HEADS, HD)], 1)

    def gains_of(head, count):
        return lax.dynamic_slice_in_dim(both, head, count, 0)

    pair_gains = jnp.stack([gains_of(8 + 2 * core, 2), gains_of(12 + 2 * core, 2)])
    pair_gains = pair_gains.transpose(0, 2, 1, 3).reshape(2, 2 * PAIR, 1)
    space_gains = gains_of(4 * core, 4).reshape(4, PAIR, 1)

    time_own = lax.all_to_all(tokens.reshape(32, 8, D), CHIP, 0, 0, tiled=True).reshape(HALF, D)
    halves = call(arrange_kernel, shape(2, 4, 18, FIRST + SECOND), (order, w_qkv, w_out))
    received = swap_core(halves[1])
    first = jnp.where(core == 0, halves[0], received)
    second = jnp.where(core == 0, received, halves[0])
    pair = jnp.concatenate([first, second], 1)
    other = swap_core(tokens)
    normed = call(norm_kernel, shape(ROWS, D), (tokens, other, embed, gain), (), 8 * 10**9)

    def gather(part):
        pieces = call(pack_kernel, shape(32, 36, part.shape[2]), (order, part))
        return lax.all_to_all(pieces, CHIP, 0, 0, tiled=True).reshape(D, part.shape[2]).T

    def spread(block):
        return (block,) + tuple(lax.ppermute(block, EVERY, r) for r in ROUTES)

    time_other = swap_core(time_own)
    time_normed = call(norm_kernel, shape(ROWS, D), (time_own, time_other, embed, gain), (), 8 * 10**9)
    block = gather(after(pair[:, :, :FIRST], time_own))
    late = gather(after(pair[:, :, FIRST:], block, normed, time_normed))
    blocks = spread(after(block, normed, time_normed))

    two = [pltpu.VMEM((2, FIRST, D), BF16), pltpu.SemaphoreType.DMA((2,))]
    four = [pltpu.VMEM((4, SECOND, D), BF16), pltpu.SemaphoreType.DMA((4,))]
    q_t, kv_t = call(
        cross_project_kernel,
        (shape(PAIR, ROWS), shape(2 * PAIR, ROWS)),
        (order, normed, pair_gains) + blocks,
        two,
        0,
        4,
    )
    kv_a = lax.ppermute(kv_t, EVERY, ACROSS)
    kv_b = lax.ppermute(kv_a, EVERY, ALONG)
    timed = call(
        time_kernel, shape(2, HALF, PAIR), (order, after(time_normed, kv_t), pair_gains) + blocks, two, 0, 4
    )
    more = spread(after(late, timed, kv_a))
    timed = timed.reshape(2, 32, 8, PAIR).transpose(1, 0, 2, 3).reshape(64, 8, PAIR)
    timed = lax.all_to_all(timed, SLAB, 0, 0, tiled=True)
    timed = timed.reshape(32, 2, 8, PAIR).transpose(1, 0, 2, 3).reshape(2, HALF, PAIR)
    space, w_own = call(
        space_kernel,
        (shape(2 * PAIR, ROWS), shape(4 * PAIR, D)),
        (order, after(normed, kv_b, timed), space_gains) + more,
        four,
        0,
        4,
    )
    w_other = swap_core(w_own)
    cross = call(cross_kernel, shape(PAIR, ROWS), (q_t, kv_a, kv_b), )
    mixed = jnp.concatenate([space, cross], 0)
    arrived = swap_core(mixed[:, HALF:])
    return call(
        out_kernel, shape(HALF, D), (order, tokens, embed, mixed[:, :HALF], arrived, timed, w_own, w_other)
    )[None]


def solution(mesh):
    fine = Mesh(mesh.devices.reshape(4, 2, 4, 8, 2), EVERY)
    placed = (P(CAM, SLAB, None), P(), P(), P(), P(), P(SLAB, None), P(SLAB, None))
    return jax.shard_map(local, mesh=fine, in_specs=placed, out_specs=P(CAM, SLAB, None), check_vma=False)
```

time: 205 us -> 179 us (0.87)
  blocking collectives: 44 us -> 0 us
  waiting for transfers between devices: 30.9 us -> 59.4 us
  starting transfers between devices: 62.5 us -> 82 us
  local copies, waits for them, and re-layouts: 26.8 us -> 10.2 us
  between operations: 13.9 us -> 0.56 us
  Pallas kernels: 22.6 us -> 25.4 us
    all_to_all x1 -> x0, blocking collectives: 44 us -> none  [local(): b0 = lax.all_to_all(pieces, CHIP, 0, 0, tiled=True).reshape(D, GROUP)]
    ppermute x5 -> x8, waiting for transfers between devices: 0.64 us -> 23 us  [the longest x6 20.3 us: spread(): return (block,) + tuple((lax.ppermute(block, EVERY, r) for r in ROUTES))]
    all_gather x1 -> x0, waiting for transfers between devices: 15.7 us -> none  [local(): w_out_all = lax.all_gather(w_out, SLAB, axis=0, tiled=True)]
    all_to_all x0 -> x2, waiting for transfers between devices: none -> 14.1 us  [gather(): lax.all_to_all(pieces, CHIP, 0, 0, tiled=True).reshape(D, part.shape[2])]
    all_to_all x0 -> x2, starting transfers between devices: none -> 12.5 us  [gather(): lax.all_to_all(pieces, CHIP, 0, 0, tiled=True).reshape(D, part.shape[2])]
    all_to_all x1, waiting for transfers between devices: 0.01 us -> 9.43 us  [local(): lax.all_to_all(tokens.reshape(32, 8, D), CHIP, 0, 0, tiled=True)]
    all_to_all x1, starting transfers between devices: 5.73 us -> 14.4 us  [local(): lax.all_to_all(tokens.reshape(32, 8, D), CHIP, 0, 0, tiled=True)]
    ppermute x4 -> x5, starting transfers between devices: 22.4 us -> 14.4 us  [swap_core(): return lax.ppermute(block, 'core', [(0, 1), (1, 0)])]
  transfers between devices with their start and end apart: 12 -> 17, of which waited for: 4 -> 6; matrix products, arithmetic and copies ran while one was open for 13% -> 4% of each run, Pallas kernels for 9% -> 8%
where the time goes in v2:
time: 179 us; the launch traced here: 178 us
  starting transfers between devices  82 us (46%)
  waiting for transfers between devices  59.4 us (33%)
  Pallas kernels  25.4 us (14%)
  local copies, waits for them, and re-layouts  10.2 us (6%)
    pallas_call x10, Pallas kernels, call(): pl.pallas_call(kernel, out_shape=out_shapes, in_specs=specs, out_specs=vm...  25.4 us
    ppermute x6, waiting for transfers between devices, spread(): return (block,) + tuple((lax.ppermute(block, EVERY, r) for r in ROUTES))  20.3 us
    ppermute x6, starting transfers between devices, spread(): return (block,) + tuple((lax.ppermute(block, EVERY, r) for r in ROUTES))  19.8 us
    all_to_all x1, starting transfers between devices, local(): lax.all_to_all(tokens.reshape(32, 8, D), CHIP, 0, 0, tiled=True)  14.4 us
    ppermute x5, starting transfers between devices, swap_core(): return lax.ppermute(block, 'core', [(0, 1), (1, 0)])  14.4 us
    all_to_all x2, waiting for transfers between devices, gather(): lax.all_to_all(pieces, CHIP, 0, 0, tiled=True).reshape(D, part.shape[2])  14.1 us
    all_to_all x1, starting transfers between devices, local(): timed = lax.all_to_all(timed, SLAB, 0, 0, tiled=True)  13.4 us
    all_to_all x2, starting transfers between devices, gather(): lax.all_to_all(pieces, CHIP, 0, 0, tiled=True).reshape(D, part.shape[2])  12.5 us
  transfers between devices with their start and end apart: 17, of which 6 were waited for; matrix products, arithmetic and copies ran while one was open for 4% of the time, Pallas kernels for 8%

profile of v2, /device:TPU:1, one launch (start us, length us, event | category | flops | bytes accessed | tf_op | source)
XLA Modules:
  0.0 178.0 jit_solution(9080795624785915133)
XLA Ops:
  0.0 14.4 %all-to-all-start = ((bf16[32,8,1152]{2,1,0:T(8,128)(2,1)}), bf16[32,8,1152]{2,1,0:T(8,128)(2,1)S(1)}, u32[]{:S(2)}, u32[]{:S(2)}) async-start(bf16[32,8,1152]{2,1,0:T(8,128)(2,1)} %bitcast.41), calls=%async_computation | async-start | bytes 1179648 | tf_op jit(solution)/shard_map/all_to_all | solution.py:257
  14.5 0.1 pad_add_fusion.order
  14.6 0.8 copy-done.9
  15.4 0.8 shard_map.74
  16.2 2.9 %collective-permute-start.1 = (bf16[4,18,576]{2,1,0:T(8,128)(2,1)S(1)}, bf16[4,18,576]{2,1,0:T(8,128)(2,1)S(1)}, u32[]{:S(2)}, u32[]{:S(2)}) collective-permute-start(bf16[4,18,576]{2,1,0:T(8,128)(2,1)S(1)} %slice_bitcast_fusion), channel_id=1, source_target_pairs={{0,1},{1,0},{2,3},{3,2},{4,5},{5,4},{6,7},{7,6},{8,9},{9,8},{10,11... | collective-permute-start | bytes 248840 | tf_op jit(solution)/shard_map/ppermute | solution.py:55
  19.1 1.9 %collective-permute-start = (bf16[256,1152]{1,0:T(8,128)(2,1)S(1)}, bf16[256,1152]{1,0:T(8,128)(2,1)S(1)}, u32[]{:S(2)}, u32[]{:S(2)}) collective-permute-start(bf16[256,1152]{1,0:T(8,128)(2,1)S(1)} %bitcast.42), channel_id=1, source_target_pairs={{0,1},{1,0},{2,3},{3,2},{4,5},{5,4},{6,7},{7,6},{8,9},{9,8},{10,11... | collective-permute-start | bytes 1769480 | tf_op jit(solution)/shard_map/ppermute | solution.py:55
  21.1 0.1 pad_maximum_fusion.1.pair
  21.3 9.4 %all-to-all-done = bf16[32,8,1152]{2,1,0:T(8,128)(2,1)S(1)} async-done(((bf16[32,8,1152]{2,1,0:T(8,128)(2,1)}), bf16[32,8,1152]{2,1,0:T(8,128)(2,1)S(1)}, u32[]{:S(2)}, u32[]{:S(2)}) %all-to-all-start) | async-done | bytes 589856 | tf_op jit(solution)/shard_map/all_to_all | solution.py:257
  30.7 4.6 %collective-permute-start.2 = (bf16[256,1152]{1,0:T(8,128)(2,1)S(1)}, bf16[256,1152]{1,0:T(8,128)(2,1)}, u32[]{:S(2)}, u32[]{:S(2)}) collective-permute-start(bf16[256,1152]{1,0:T(8,128)(2,1)S(1)} %bitcast.47), channel_id=1, source_target_pairs={{0,1},{1,0},{2,3},{3,2},{4,5},{5,4},{6,7},{7,6},{8,9},{9,8},{10,11... | collective-permute-start | bytes 1769480 | tf_op jit(solution)/shard_map/ppermute | solution.py:55
  35.3 1.5 shard_map.75
  36.8 5.5 %all-to-all-start.1 = ((bf16[32,36,216]{2,1,0:T(8,128)(2,1)}), bf16[32,36,216]{2,1,0:T(8,128)(2,1)}, u32[]{:S(2)}, u32[]{:S(2)}) async-start(bf16[32,36,216]{2,1,0:T(8,128)(2,1)} %shard_map.75), calls=%async_computation.1 | async-start | bytes 1310720 | tf_op jit(solution)/shard_map/all_to_all | solution.py:268
  42.3 0.8 shard_map.73.normed
  43.1 2.3 %shard_map.76.normed = bf16[512,1152]{1,0:T(8,128)(2,1)S(1)} custom-call(bf16[256,1152]{1,0:T(8,128)(2,1)S(1)} %bitcast.48, bf16[256,1152]{1,0:T(8,128)(2,1)} %collective-permute-done.2.other, f32[1,1152]{1,0:T(1,128)S(1)} %constant_dynamic-slice_fusion.embed, f32[1,1152]{1,0:T(1,128)S(1)} %broadcast_in_dim.14.gain), custom_call_target="tpu_custom_call" | custom-call | flops 8000000000 | bytes 1 | tf_op jit(solution)/shard_map/pallas_call | solution.py:223
  45.3 1.0 copy-done.4
  46.4 14.1 %all-to-all-done.1 = bf16[32,36,216]{2,1,0:T(8,128)(2,1)} async-done(((bf16[32,36,216]{2,1,0:T(8,128)(2,1)}), bf16[32,36,216]{2,1,0:T(8,128)(2,1)}, u32[]{:S(2)}, u32[]{:S(2)}) %all-to-all-start.1) | async-done | bytes 497696 | tf_op jit(solution)/shard_map/all_to_all | solution.py:268
  60.5 1.4 reshape.29
  61.9 0.3 copy.11
  62.2 1.6 shard_map.79
  63.8 7.0 %all-to-all-start.3 = ((bf16[32,36,360]{2,1,0:T(8,128)(2,1)}), bf16[32,36,360]{2,1,0:T(8,128)(2,1)}, u32[]{:S(2)}, u32[]{:S(2)}) async-start(bf16[32,36,360]{2,1,0:T(8,128)(2,1)} %shard_map.79), calls=%async_computation.3 | async-start | bytes 1966080 | tf_op jit(solution)/shard_map/all_to_all | solution.py:268
  70.8 3.1 %collective-permute-start.5 = (bf16[216,1152]{1,0:T(8,128)(2,1)S(1)}, bf16[216,1152]{1,0:T(8,128)(2,1)S(1)}, u32[]{:S(2)}, u32[]{:S(2)}) collective-permute-start(bf16[216,1152]{1,0:T(8,128)(2,1)S(1)} %bitcast.32), channel_id=1, source_target_pairs={{0,14},{1,3},{2,0},{3,5},{4,2},{5,7},{6,4},{7,9},{8,6},{9,11},{10,... | collective-permute-start | bytes 1493000 | tf_op jit(solution)/shard_map/ppermute | solution.py:271
  73.8 3.1 %collective-permute-start.4 = (bf16[216,1152]{1,0:T(8,128)(2,1)S(1)}, bf16[216,1152]{1,0:T(8,128)(2,1)}, u32[]{:S(2)}, u32[]{:S(2)}) collective-permute-start(bf16[216,1152]{1,0:T(8,128)(2,1)S(1)} %bitcast.33), channel_id=1, source_target_pairs={{0,112},{1,17},{2,114},{3,19},{4,116},{5,21},{6,118},{7,23},{8,120... | collective-permute-start | bytes 1493000 | tf_op jit(solution)/shard_map/ppermute | solution.py:271
  76.9 3.1 %collective-permute-start.3 = (bf16[216,1152]{1,0:T(8,128)(2,1)S(1)}, bf16[216,1152]{1,0:T(8,128)(2,1)}, u32[]{:S(2)}, u32[]{:S(2)}) collective-permute-start(bf16[216,1152]{1,0:T(8,128)(2,1)S(1)} %bitcast.34), channel_id=1, source_target_pairs={{0,384},{1,129},{2,386},{3,131},{4,388},{5,133},{6,390},{7,135},{8... | collective-permute-start | bytes 1493000 | tf_op jit(solution)/shard_map/ppermute | solution.py:271
  80.1 0.1 stack_reshape.6
  80.2 0.1 stack_reshape.7
  80.3 0.1 reshape.36.gains
  80.5 20.3 %collective-permute-done.5.b3 = bf16[216,1152]{1,0:T(8,128)(2,1)S(1)} collective-permute-done((bf16[216,1152]{1,0:T(8,128)(2,1)S(1)}, bf16[216,1152]{1,0:T(8,128)(2,1)S(1)}, u32[]{:S(2)}, u32[]{:S(2)}) %collective-permute-start.5) | collective-permute-done | bytes 497696 | tf_op jit(solution)/shard_map/ppermute | solution.py:271
  100.8 2.1 %shard_map.77 = (bf16[144,512]{1,0:T(8,128)(2,1)S(1)}, bf16[288,512]{1,0:T(8,128)(2,1)S(1)}) custom-call(s32[6]{0:T(128)S(1)} %pad_add_fusion.order, bf16[512,1152]{1,0:T(8,128)(2,1)S(1)} %shard_map.73.normed, f32[2,288,1]{2,1,0:T(8,128)S(1)} %reshape.36.gains, bf16[216,1152]{1,0:T(8,128)(2,1)S(1)} %bitcast.35, bf16[216,1152]{1,0:T(8,128)(2,1)} %collective-permute-done.3.b1, ...), custom_call_target="tpu_custom_call" | custom-call | bytes 1 | tf_op jit(solution)/shard_map/pallas_call | solution.py:223
  103.0 0.7 copy-done.7
  103.6 4.7 %collective-permute-start.6 = (bf16[288,512]{1,0:T(8,128)(2,1)S(1)}, bf16[288,512]{1,0:T(8,128)(2,1)}, u32[]{:S(2)}, u32[]{:S(2)}) collective-permute-start(bf16[288,512]{1,0:T(8,128)(2,1)S(1)} %get-tuple-element.17), channel_id=1, source_target_pairs={{0,64},{1,65},{2,66},{3,67},{4,68},{5,69},{6,70},{7,71},{8,72},{9,... | collective-permute-start | bytes 884744 | tf_op jit(solution)/shard_map/ppermute | solution.py:289
  108.4 3.6 %shard_map.78 = bf16[2,256,144]{2,1,0:T(8,128)(2,1)S(1)} custom-call(s32[6]{0:T(128)S(1)} %pad_add_fusion.order, bf16[512,1152]{1,0:T(8,128)(2,1)S(1)} %copy-done.5, f32[2,288,1]{2,1,0:T(8,128)S(1)} %reshape.36.gains, bf16[216,1152]{1,0:T(8,128)(2,1)S(1)} %bitcast.36, bf16[216,1152]{1,0:T(8,128)(2,1)} %collective-permute-done.3.b1, ...), custom_call_target="tpu_custom_call" | custom-call | bytes 1 | tf_op jit(solution)/shard_map/pallas_call | solution.py:223
  112.0 2.3 %reshape.35 = bf16[1152,360]{1,0:T(8,128)(2,1)} reshape(bf16[32,36,360]{2,1,0:T(8,128)(2,1)} %all-to-all-done.3) | data formatting | bytes 1658880 | tf_op jit(solution)/shard_map/reshape | solution.py:268
  114.3 1.6 copy.16
  115.9 2.7 %collective-permute-done.6.kv_a = bf16[288,512]{1,0:T(8,128)(2,1)} collective-permute-done((bf16[288,512]{1,0:T(8,128)(2,1)S(1)}, bf16[288,512]{1,0:T(8,128)(2,1)}, u32[]{:S(2)}, u32[]{:S(2)}) %collective-permute-start.6) | collective-permute-done | bytes 294944 | tf_op jit(solution)/shard_map/ppermute | solution.py:289
  118.6 2.0 %collective-permute-start.10 = (bf16[360,1152]{1,0:T(8,128)(2,1)S(1)}, bf16[360,1152]{1,0:T(8,128)(2,1)S(1)}, u32[]{:S(2)}, u32[]{:S(2)}) collective-permute-start(bf16[360,1152]{1,0:T(8,128)(2,1)S(1)} %bitcast.37), channel_id=1, source_target_pairs={{0,14},{1,3},{2,0},{3,5},{4,2},{5,7},{6,4},{7,9},{8,6},{9,11},{10,... | collective-permute-start | bytes 2488328 | tf_op jit(solution)/shard_map/ppermute | solution.py:271
  120.6 5.3 %collective-permute-start.9 = (bf16[360,1152]{1,0:T(8,128)(2,1)S(1)}, bf16[360,1152]{1,0:T(8,128)(2,1)S(1)}, u32[]{:S(2)}, u32[]{:S(2)}) collective-permute-start(bf16[360,1152]{1,0:T(8,128)(2,1)S(1)} %bitcast.38), channel_id=1, source_target_pairs={{0,112},{1,17},{2,114},{3,19},{4,116},{5,21},{6,118},{7,23},{8,120... | collective-permute-start | bytes 2488328 | tf_op jit(solution)/shard_map/ppermute | solution.py:271
  125.9 3.2 %collective-permute-start.8 = (bf16[360,1152]{1,0:T(8,128)(2,1)S(1)}, bf16[360,1152]{1,0:T(8,128)(2,1)}, u32[]{:S(2)}, u32[]{:S(2)}) collective-permute-start(bf16[360,1152]{1,0:T(8,128)(2,1)S(1)} %bitcast.39), channel_id=1, source_target_pairs={{0,384},{1,129},{2,386},{3,131},{4,388},{5,133},{6,390},{7,135},{8... | collective-permute-start | bytes 2488328 | tf_op jit(solution)/shard_map/ppermute | solution.py:271
  129.1 2.8 %collective-permute-start.7 = (bf16[288,512]{1,0:T(8,128)(2,1)}, bf16[288,512]{1,0:T(8,128)(2,1)}, u32[]{:S(2)}, u32[]{:S(2)}) collective-permute-start(bf16[288,512]{1,0:T(8,128)(2,1)} %collective-permute-done.6.kv_a), channel_id=1, source_target_pairs={{0,128},{1,129},{2,130},{3,131},{4,132},{5,133},{6,134},{7,135},{8... | collective-permute-start | bytes 884744 | tf_op jit(solution)/shard_map/ppermute | solution.py:290
  131.9 0.7 copy.14
  132.7 13.4 %all-to-all-start.2 = ((bf16[64,8,144]{2,1,0:T(8,128)(2,1)}), bf16[64,8,144]{2,1,0:T(8,128)(2,1)}, u32[]{:S(2)}, u32[]{:S(2)}) async-start(bf16[64,8,144]{2,1,0:T(8,128)(2,1)} %bitcast.49), calls=%async_computation.2 | async-start | bytes 524288 | tf_op jit(solution)/shard_map/all_to_all | solution.py:296
  146.1 0.1 reshape.37.gains
  146.2 11.4 %all-to-all-done.2 = bf16[64,8,144]{2,1,0:T(8,128)(2,1)} async-done(((bf16[64,8,144]{2,1,0:T(8,128)(2,1)}), bf16[64,8,144]{2,1,0:T(8,128)(2,1)}, u32[]{:S(2)}, u32[]{:S(2)}) %all-to-all-start.2) | async-done | bytes 147488 | tf_op jit(solution)/shard_map/all_to_all | solution.py:296
  157.6 1.0 copy.19
  158.6 7.7 %shard_map.80 = (bf16[288,512]{1,0:T(8,128)(2,1)S(1)}, bf16[576,1152]{1,0:T(8,128)(2,1)}) custom-call(s32[6]{0:T(128)S(1)} %pad_add_fusion.order, bf16[512,1152]{1,0:T(8,128)(2,1)} %copy-done.1, f32[4,144,1]{2,1,0:T(8,128)S(1)} %reshape.37.gains, bf16[360,1152]{1,0:T(8,128)(2,1)S(1)} %bitcast.40, bf16[360,1152]{1,0:T(8,128)(2,1)} %collective-permute-done.8.b1, ...), custom_call_target="tpu_custom_call" | custom-call | bytes 1 | tf_op jit(solution)/shard_map/pallas_call | solution.py:223
  166.3 3.1 %collective-permute-start.12 = (bf16[576,1152]{1,0:T(8,128)(2,1)}, bf16[576,1152]{1,0:T(8,128)(2,1)S(1)}, u32[]{:S(2)}, u32[]{:S(2)}) collective-permute-start(bf16[576,1152]{1,0:T(8,128)(2,1)} %get-tuple-element.24.w_own), channel_id=1, source_target_pairs={{0,1},{1,0},{2,3},{3,2},{4,5},{5,4},{6,7},{7,6},{8,9},{9,8},{10,11... | collective-permute-start | bytes 3981320 | tf_op jit(solution)/shard_map/ppermute | solution.py:55
  169.5 2.4 %shard_map.81 = bf16[144,512]{1,0:T(8,128)(2,1)S(1)} custom-call(bf16[144,512]{1,0:T(8,128)(2,1)S(1)} %copy-done.8, bf16[288,512]{1,0:T(8,128)(2,1)} %collective-permute-done.6.kv_a, bf16[288,512]{1,0:T(8,128)(2,1)} %collective-permute-done.7.kv_b), custom_call_target="tpu_custom_call" | custom-call | bytes 1 | tf_op jit(solution)/shard_map/pallas_call | solution.py:223
  171.9 1.9 %collective-permute-start.11 = (bf16[432,256]{1,0:T(8,128)(2,1)S(1)}, bf16[432,256]{1,0:T(8,128)(2,1)S(1)}, u32[]{:S(2)}, u32[]{:S(2)}) collective-permute-start(bf16[432,256]{1,0:T(8,128)(2,1)S(1)} %get-tuple-element.25), channel_id=1, source_target_pairs={{0,1},{1,0},{2,3},{3,2},{4,5},{5,4},{6,7},{7,6},{8,9},{9,8},{10,11... | collective-permute-start | bytes 663560 | tf_op jit(solution)/shard_map/ppermute | solution.py:55
  173.8 1.4 collective-permute-done.11.arrived
  175.3 2.7 %shard_map.82 = bf16[256,1152]{1,0:T(8,128)(2,1)} custom-call(s32[6]{0:T(128)S(1)} %pad_add_fusion.order, bf16[256,1152]{1,0:T(8,128)(2,1)S(1)} %bitcast.44, f32[1,1152]{1,0:T(1,128)S(1)} %constant_dynamic-slice_fusion.embed, bf16[432,256]{1,0:T(8,128)(2,1)S(1)} %get-tuple-element.26.own, bf16[432,256]{1,0:T(8,128)(2,1)S(1)} %collective-permute-done.11.arrived, ...), custom_call_target="tpu_custom_call" | custom-call | bytes 1 | tf_op jit(solution)/shard_map/pallas_call | solution.py:223
  (45 shorter events, 0.2 us)
Async XLA Ops:
  0.0 21.0 %copy-start = (f32[8,1152]{1,0:T(8,128)S(1)}, f32[8,1152]{1,0:T(8,128)}, u32[]{:S(2)}) copy-start(f32[8,1152]{1,0:T(8,128)} %param.8) | copy-start | bytes 110596
  0.0 19.1 %copy-start.2 = (bf16[1,256,1152]{2,1,0:T(8,128)(2,1)S(1)}, bf16[1,256,1152]{2,1,0:T(8,128)(2,1)}, u32[]{:S(2)}) copy-start(bf16[1,256,1152]{2,1,0:T(8,128)(2,1)} %param.7) | copy-start | bytes 1769476
  0.0 14.6 %copy-start.6 = (bf16[18,3456]{1,0:T(8,128)(2,1)S(1)}, bf16[18,3456]{1,0:T(8,128)(2,1)}, u32[]{:S(2)}) copy-start(bf16[18,3456]{1,0:T(8,128)(2,1)} %w_qkv.1) | copy-start | bytes 373252
  0.0 21.0 %copy-start.10 = (f32[1152]{0:T(1024)S(1)}, f32[1152]{0:T(1024)}, u32[]{:S(2)}) copy-start(f32[1152]{0:T(1024)} %param.9) | copy-start | bytes 13828
  0.0 30.7 %all-to-all-start = ((bf16[32,8,1152]{2,1,0:T(8,128)(2,1)}), bf16[32,8,1152]{2,1,0:T(8,128)(2,1)S(1)}, u32[]{:S(2)}, u32[]{:S(2)}) async-start(bf16[32,8,1152]{2,1,0:T(8,128)(2,1)} %bitcast.41), calls=%async_computation | async-start | bytes 1179648 | tf_op jit(solution)/shard_map/all_to_all | solution.py:257
  14.6 0.8 copy-start.9
  16.2 4.9 %collective-permute-start.1 = (bf16[4,18,576]{2,1,0:T(8,128)(2,1)S(1)}, bf16[4,18,576]{2,1,0:T(8,128)(2,1)S(1)}, u32[]{:S(2)}, u32[]{:S(2)}) collective-permute-start(bf16[4,18,576]{2,1,0:T(8,128)(2,1)S(1)} %slice_bitcast_fusion), channel_id=1, source_target_pairs={{0,1},{1,0},{2,3},{3,2},{4,5},{5,4},{6,7},{7,6},{8,9},{9,8},{10,11... | collective-permute-start | bytes 248840 | tf_op jit(solution)/shard_map/ppermute | solution.py:55
  19.1 23.2 %collective-permute-start = (bf16[256,1152]{1,0:T(8,128)(2,1)S(1)}, bf16[256,1152]{1,0:T(8,128)(2,1)S(1)}, u32[]{:S(2)}, u32[]{:S(2)}) collective-permute-start(bf16[256,1152]{1,0:T(8,128)(2,1)S(1)} %bitcast.42), channel_id=1, source_target_pairs={{0,1},{1,0},{2,3},{3,2},{4,5},{5,4},{6,7},{7,6},{8,9},{9,8},{10,11... | collective-permute-start | bytes 1769480 | tf_op jit(solution)/shard_map/ppermute | solution.py:55
  30.7 12.4 %collective-permute-start.2 = (bf16[256,1152]{1,0:T(8,128)(2,1)S(1)}, bf16[256,1152]{1,0:T(8,128)(2,1)}, u32[]{:S(2)}, u32[]{:S(2)}) collective-permute-start(bf16[256,1152]{1,0:T(8,128)(2,1)S(1)} %bitcast.47), channel_id=1, source_target_pairs={{0,1},{1,0},{2,3},{3,2},{4,5},{5,4},{6,7},{7,6},{8,9},{9,8},{10,11... | collective-permute-start | bytes 1769480 | tf_op jit(solution)/shard_map/ppermute | solution.py:55
  36.8 23.7 %all-to-all-start.1 = ((bf16[32,36,216]{2,1,0:T(8,128)(2,1)}), bf16[32,36,216]{2,1,0:T(8,128)(2,1)}, u32[]{:S(2)}, u32[]{:S(2)}) async-start(bf16[32,36,216]{2,1,0:T(8,128)(2,1)} %shard_map.75), calls=%async_computation.1 | async-start | bytes 1310720 | tf_op jit(solution)/shard_map/all_to_all | solution.py:268
  43.1 57.7 %copy-start.1 = (bf16[512,1152]{1,0:T(8,128)(2,1)}, bf16[512,1152]{1,0:T(8,128)(2,1)S(1)}, u32[]{:S(2)}) copy-start(bf16[512,1152]{1,0:T(8,128)(2,1)S(1)} %shard_map.73.normed) | copy-start | bytes 3538948
  45.3 1.0 copy-start.4
  62.1 17.9 %copy-start.11 = (f32[1152]{0:T(1024)S(1)}, f32[1152]{0:T(1024)}, u32[]{:S(2)}) copy-start(f32[1152]{0:T(1024)} %param.10) | copy-start | bytes 13828
  62.2 18.0 %copy-start.12 = (f32[1152]{0:T(1024)S(1)}, f32[1152]{0:T(1024)}, u32[]{:S(2)}) copy-start(f32[1152]{0:T(1024)} %param.11) | copy-start | bytes 13828
  63.8 48.2 %all-to-all-start.3 = ((bf16[32,36,360]{2,1,0:T(8,128)(2,1)}), bf16[32,36,360]{2,1,0:T(8,128)(2,1)}, u32[]{:S(2)}, u32[]{:S(2)}) async-start(bf16[32,36,360]{2,1,0:T(8,128)(2,1)} %shard_map.79), calls=%async_computation.3 | async-start | bytes 1966080 | tf_op jit(solution)/shard_map/all_to_all | solution.py:268
  70.8 30.0 %collective-permute-start.5 = (bf16[216,1152]{1,0:T(8,128)(2,1)S(1)}, bf16[216,1152]{1,0:T(8,128)(2,1)S(1)}, u32[]{:S(2)}, u32[]{:S(2)}) collective-permute-start(bf16[216,1152]{1,0:T(8,128)(2,1)S(1)} %bitcast.32), channel_id=1, source_target_pairs={{0,14},{1,3},{2,0},{3,5},{4,2},{5,7},{6,4},{7,9},{8,6},{9,11},{10,... | collective-permute-start | bytes 1493000 | tf_op jit(solution)/shard_map/ppermute | solution.py:271
  73.8 26.9 %collective-permute-start.4 = (bf16[216,1152]{1,0:T(8,128)(2,1)S(1)}, bf16[216,1152]{1,0:T(8,128)(2,1)}, u32[]{:S(2)}, u32[]{:S(2)}) collective-permute-start(bf16[216,1152]{1,0:T(8,128)(2,1)S(1)} %bitcast.33), channel_id=1, source_target_pairs={{0,112},{1,17},{2,114},{3,19},{4,116},{5,21},{6,118},{7,23},{8,120... | collective-permute-start | bytes 1493000 | tf_op jit(solution)/shard_map/ppermute | solution.py:271
  76.9 23.8 %collective-permute-start.3 = (bf16[216,1152]{1,0:T(8,128)(2,1)S(1)}, bf16[216,1152]{1,0:T(8,128)(2,1)}, u32[]{:S(2)}, u32[]{:S(2)}) collective-permute-start(bf16[216,1152]{1,0:T(8,128)(2,1)S(1)} %bitcast.34), channel_id=1, source_target_pairs={{0,384},{1,129},{2,386},{3,131},{4,388},{5,133},{6,390},{7,135},{8... | collective-permute-start | bytes 1493000 | tf_op jit(solution)/shard_map/ppermute | solution.py:271
  80.5 27.9 %copy-start.5 = (bf16[512,1152]{1,0:T(8,128)(2,1)S(1)}, bf16[512,1152]{1,0:T(8,128)(2,1)}, u32[]{:S(2)}) copy-start(bf16[512,1152]{1,0:T(8,128)(2,1)} %copy-done.4) | copy-start | bytes 3538948
  102.9 0.7 copy-start.7
  103.6 14.9 %collective-permute-start.6 = (bf16[288,512]{1,0:T(8,128)(2,1)S(1)}, bf16[288,512]{1,0:T(8,128)(2,1)}, u32[]{:S(2)}, u32[]{:S(2)}) collective-permute-start(bf16[288,512]{1,0:T(8,128)(2,1)S(1)} %get-tuple-element.17), channel_id=1, source_target_pairs={{0,64},{1,65},{2,66},{3,67},{4,68},{5,69},{6,70},{7,71},{8,72},{9,... | collective-permute-start | bytes 884744 | tf_op jit(solution)/shard_map/ppermute | solution.py:289
  118.6 40.0 %collective-permute-start.10 = (bf16[360,1152]{1,0:T(8,128)(2,1)S(1)}, bf16[360,1152]{1,0:T(8,128)(2,1)S(1)}, u32[]{:S(2)}, u32[]{:S(2)}) collective-permute-start(bf16[360,1152]{1,0:T(8,128)(2,1)S(1)} %bitcast.37), channel_id=1, source_target_pairs={{0,14},{1,3},{2,0},{3,5},{4,2},{5,7},{6,4},{7,9},{8,6},{9,11},{10,... | collective-permute-start | bytes 2488328 | tf_op jit(solution)/shard_map/ppermute | solution.py:271
  120.6 38.0 %collective-permute-start.9 = (bf16[360,1152]{1,0:T(8,128)(2,1)S(1)}, bf16[360,1152]{1,0:T(8,128)(2,1)S(1)}, u32[]{:S(2)}, u32[]{:S(2)}) collective-permute-start(bf16[360,1152]{1,0:T(8,128)(2,1)S(1)} %bitcast.38), channel_id=1, source_target_pairs={{0,112},{1,17},{2,114},{3,19},{4,116},{5,21},{6,118},{7,23},{8,120... | collective-permute-start | bytes 2488328 | tf_op jit(solution)/shard_map/ppermute | solution.py:271
  125.9 32.7 %collective-permute-start.8 = (bf16[360,1152]{1,0:T(8,128)(2,1)S(1)}, bf16[360,1152]{1,0:T(8,128)(2,1)}, u32[]{:S(2)}, u32[]{:S(2)}) collective-permute-start(bf16[360,1152]{1,0:T(8,128)(2,1)S(1)} %bitcast.39), channel_id=1, source_target_pairs={{0,384},{1,129},{2,386},{3,131},{4,388},{5,133},{6,390},{7,135},{8... | collective-permute-start | bytes 2488328 | tf_op jit(solution)/shard_map/ppermute | solution.py:271
  129.1 29.5 %collective-permute-start.7 = (bf16[288,512]{1,0:T(8,128)(2,1)}, bf16[288,512]{1,0:T(8,128)(2,1)}, u32[]{:S(2)}, u32[]{:S(2)}) collective-permute-start(bf16[288,512]{1,0:T(8,128)(2,1)} %collective-permute-done.6.kv_a), channel_id=1, source_target_pairs={{0,128},{1,129},{2,130},{3,131},{4,132},{5,133},{6,134},{7,135},{8... | collective-permute-start | bytes 884744 | tf_op jit(solution)/shard_map/ppermute | solution.py:290
  132.7 25.0 %all-to-all-start.2 = ((bf16[64,8,144]{2,1,0:T(8,128)(2,1)}), bf16[64,8,144]{2,1,0:T(8,128)(2,1)}, u32[]{:S(2)}, u32[]{:S(2)}) async-start(bf16[64,8,144]{2,1,0:T(8,128)(2,1)} %bitcast.49), calls=%async_computation.2 | async-start | bytes 524288 | tf_op jit(solution)/shard_map/all_to_all | solution.py:296
  158.6 10.9 %copy-start.8 = (bf16[144,512]{1,0:T(8,128)(2,1)S(1)}, bf16[144,512]{1,0:T(8,128)(2,1)}, u32[]{:S(2)}) copy-start(bf16[144,512]{1,0:T(8,128)(2,1)} %copy-done.7) | copy-start | bytes 442372
  166.3 8.9 %copy-start.3 = (bf16[576,1152]{1,0:T(8,128)(2,1)S(1)}, bf16[576,1152]{1,0:T(8,128)(2,1)}, u32[]{:S(2)}) copy-start(bf16[576,1152]{1,0:T(8,128)(2,1)} %get-tuple-element.24.w_own) | copy-start | bytes 3981316
  166.3 8.9 %collective-permute-start.12 = (bf16[576,1152]{1,0:T(8,128)(2,1)}, bf16[576,1152]{1,0:T(8,128)(2,1)S(1)}, u32[]{:S(2)}, u32[]{:S(2)}) collective-permute-start(bf16[576,1152]{1,0:T(8,128)(2,1)} %get-tuple-element.24.w_own), channel_id=1, source_target_pairs={{0,1},{1,0},{2,3},{3,2},{4,5},{5,4},{6,7},{7,6},{8,9},{9,8},{10,11... | collective-permute-start | bytes 3981320 | tf_op jit(solution)/shard_map/ppermute | solution.py:55
  171.9 3.4 %collective-permute-start.11 = (bf16[432,256]{1,0:T(8,128)(2,1)S(1)}, bf16[432,256]{1,0:T(8,128)(2,1)S(1)}, u32[]{:S(2)}, u32[]{:S(2)}) collective-permute-start(bf16[432,256]{1,0:T(8,128)(2,1)S(1)} %get-tuple-element.25), channel_id=1, source_target_pairs={{0,1},{1,0},{2,3},{3,2},{4,5},{5,4},{6,7},{7,6},{8,9},{9,8},{10,11... | collective-permute-start | bytes 663560 | tf_op jit(solution)/shard_map/ppermute | solution.py:55

commit v3 on v2

--- a/solution.py
+++ b/solution.py
@@ -67,31 +67,54 @@
     return lax.optimization_barrier((value,) + others)[0]
 
 
-def arrange_kernel(order, w_qkv, w_out, out):
-    core = order[4]
-
+def pack_kernel(order, w_qkv, w_out, tokens, out, pieces):
     def columns(kind, head, count):
         start = kind * D + head * HD
-        return w_qkv[:, start : start + count * HD]
+        return w_qkv[:, start : start + count * HD].astype(F32)
 
     for who in range(2):
-        place = (who + core) % 2
         for group in range(4):
+            start = (who * 4 + group) * PAIR
+            parts = [w_out[:, start : start + PAIR].astype(F32)]
+            parts += [columns(kind, 4 * who + group, 1) for kind in range(3)]
             head = (8, 12)[group // 2] + 2 * who
             if group % 2 == 0:
-                first = [columns(0, head, 2), columns(1, head, 1)]
+                parts += [columns(0, head, 2), columns(1, head, 1)]
             else:
-                first = [columns(1, head + 1, 1), columns(2, head, 2)]
-            start = (who * 4 + group) * PAIR
-            one = 4 * who + group
-            second = [w_out[:, start : start + PAIR]] + [columns(kind, one, 1) for kind in range(3)]
-            out[place, group] = jnp.concatenate(first + second, 1)
-
-
-def pack_kernel(order, pair, out):
+                parts += [columns(1, head + 1, 1), columns(2, head, 2)]
+            wide = jnp.concatenate(parts, 1)
+            place = who * 4 + group
+            for tile in range(4):
+                pieces[place, tile * 18 : tile * 18 + 18] = wide[:, tile * 128 : tile * 128 + 128]
+            pieces[place, 72:81] = jnp.concatenate([wide[:9, 512:], wide[9:, 512:]], 1)
+            pieces[place, 81:84] = jnp.zeros((3, 128), F32)
     x = order[5]
-    for i in range(32):
-        out[i] = pair[(x + 2 * (i // 8) + 3 * (i % 8)) % 4]
+    for dest in range(64):
+        colour = (x + 2 * (dest // 16) + 3 * (dest // 2 % 8)) % 4
+        block = tokens[dest // 2 * 8 : dest // 2 * 8 + 8].astype(F32)
+        block = block[dest % 2 * 4 : dest % 2 * 4 + 4]
+        rows = [block[:, tile * 128 : tile * 128 + 128] for tile in range(9)]
+        out[dest] = jnp.concatenate([pieces[dest % 2 * 4 + colour]] + rows, 0).astype(BF16)
+
+
+def unpack_kernel(got, block, tokens, wide):
+    for source in range(64):
+        rows = got[source].astype(F32)
+        at = source * 18
+        for tile in range(4):
+            wide[tile, at : at + 18] = rows[tile * 18 : tile * 18 + 18]
+        wide[4, at : at + 9, :64] = rows[72:81, :64]
+        wide[4, at + 9 : at + 18, :64] = rows[72:81, 64:]
+        if source % 2 == 1:
+            pair = [got[source - 1].astype(F32), rows]
+            tiles = []
+            for tile in range(9):
+                start = 84 + tile * 4
+                tiles.append(jnp.concatenate([one[start : start + 4] for one in pair], 0))
+            tokens[source * 4 - 4 : source * 4 + 4] = jnp.concatenate(tiles, 1).astype(BF16)
+    for tile in range(4):
+        block[tile * 128 : tile * 128 + 128] = wide[tile].T.astype(BF16)
+    block[512:] = wide[4].T[:64].astype(BF16)
 
 
 def norm_kernel(own, other, embed, gain, out):
@@ -133,31 +156,30 @@
 
 
 def project_pair(normed, weight, gains):
-    projected = jnp.concatenate([mm_t(weight[i], normed[...]) for i in range(2)], 0)
+    projected = jnp.concatenate([mm_t(weight[i, SECOND:], normed[...]) for i in range(2)], 0)
     return head_norm(projected[: 2 * PAIR], gains), projected[2 * PAIR :]
 
 
+def fetch_all(order, blocks, groups, weight, sem):
+    for slot, group in enumerate(groups):
+        start_fetch(order, blocks, group, weight.at[slot], sem.at[slot])
+    for slot in range(len(groups)):
+        wait_fetch(blocks, weight.at[slot], sem.at[slot])
+
+
 def cross_project_kernel(order, normed, gains, b0, b1, b2, b3, q_t, kv_t, weight, sem):
-    blocks = (b0, b1, b2, b3)
-    for group in range(2):
-        start_fetch(order, blocks, group, weight.at[group], sem.at[group])
-    for group in range(2):
-        wait_fetch(blocks, weight.at[group], sem.at[group])
+    fetch_all(order, (b0, b1, b2, b3), (0, 1), weight, sem)
     qk, v = project_pair(normed, weight, gains[0])
     q_t[...] = qk[:PAIR].astype(BF16)
     kv_t[...] = jnp.concatenate([qk[PAIR:], v], 0).astype(BF16)
 
 
 def time_kernel(order, normed, gains, b0, b1, b2, b3, out, weight, sem):
-    blocks = (b0, b1, b2, b3)
-    for group in range(2):
-        start_fetch(order, blocks, 2 + group, weight.at[group], sem.at[group])
-    for group in range(2):
-        wait_fetch(blocks, weight.at[group], sem.at[group])
+    fetch_all(order, (b0, b1, b2, b3), (2, 3), weight, sem)
     qk, v = project_pair(normed, weight, gains[1])
     row = lax.broadcasted_iota(jnp.int32, (HALF, HALF), 0) % 8
     col = lax.broadcasted_iota(jnp.int32, (HALF, HALF), 1) % 8
-    core = order[4]
+    sets = []
     for i in range(2):
         part = slice(i * HALF, (i + 1) * HALF)
         heads = []
@@ -165,20 +187,27 @@
             at = head * HD
             side = (qk[PAIR + at : PAIR + at + HD, part], v[at : at + HD, part])
             heads.append(attend(qk[at : at + HD, part], [side], row == col))
-        place = core if i == 0 else 1 - core
-        out[place] = jnp.concatenate(heads, 0).T.astype(BF16)
-
-
-def space_kernel(order, normed, gains, b0, b1, b2, b3, out, w_out, weight, sem):
-    blocks = (b0, b1, b2, b3)
+        sets.append(jnp.concatenate(heads, 0).T.reshape(64, 4, PAIR))
+    swap = order[4] == 1
+    one = jnp.where(swap, sets[1], sets[0])
+    two = jnp.where(swap, sets[0], sets[1])
+    out[...] = jnp.concatenate([one, two], 1).astype(BF16)
+
+
+def collect_kernel(order, b0, b1, b2, b3, out, sem):
+    blocks = [block.at[pl.ds(0, PAIR)] for block in (b0, b1, b2, b3)]
+    slots = [out.at[pl.ds(group * PAIR, PAIR)] for group in range(4)]
     for group in range(4):
-        start_fetch(order, blocks, group, weight.at[group], sem.at[group])
+        start_fetch(order, blocks, group, slots[group], sem.at[group])
     for group in range(4):
-        wait_fetch(blocks, weight.at[group], sem.at[group])
-        w_out[group * PAIR : (group + 1) * PAIR] = weight[group, :PAIR]
+        wait_fetch(blocks, slots[group], sem.at[group])
+
+
+def space_kernel(order, normed, gains, b0, b1, b2, b3, out, weight, sem):
+    fetch_all(order, (b0, b1, b2, b3), range(4), weight, sem)
     heads = []
     for group in range(4):
-        projected = mm_t(weight[group, PAIR:], normed[...])
+        projected = mm_t(weight[group, PAIR:SECOND], normed[...])
         qk = head_norm(projected[:PAIR], gains[group])
         heads.append(attend(qk[:HD], [(qk[HD:], projected[PAIR:])]))
     out[...] = jnp.concatenate(heads, 0).astype(BF16)
@@ -202,7 +231,9 @@
     second = jnp.where(swap, mine, theirs)
     split = 2 * PAIR
     mixed_t = jnp.concatenate([first[:split], second[:split], first[split:], second[split:]], 0)
-    mixed = jnp.concatenate([mixed_t.T.astype(BF16), timed[0], timed[1]], 1)
+    late = timed[...].astype(F32).reshape(32, 2, 8, PAIR)
+    late = [late[:, who].reshape(HALF, PAIR).astype(BF16) for who in range(2)]
+    mixed = jnp.concatenate([mixed_t.T.astype(BF16)] + late, 1)
     one, two = mm_t(mixed, w_own[...]), mm_t(mixed, w_other[...])
     update = jnp.concatenate([jnp.where(swap, two, one), jnp.where(swap, one, two)], 1)
     out[...] = (tokens[...].astype(F32) + embed[...] + update).astype(BF16)
@@ -254,61 +285,43 @@
     pair_gains = pair_gains.transpose(0, 2, 1, 3).reshape(2, 2 * PAIR, 1)
     space_gains = gains_of(4 * core, 4).reshape(4, PAIR, 1)
 
-    time_own = lax.all_to_all(tokens.reshape(32, 8, D), CHIP, 0, 0, tiled=True).reshape(HALF, D)
-    halves = call(arrange_kernel, shape(2, 4, 18, FIRST + SECOND), (order, w_qkv, w_out))
-    received = swap_core(halves[1])
-    first = jnp.where(core == 0, halves[0], received)
-    second = jnp.where(core == 0, received, halves[0])
-    pair = jnp.concatenate([first, second], 1)
+    pieces = call(
+        pack_kernel, shape(64, 120, 128), (order, w_qkv, w_out, tokens), [pltpu.VMEM((8, 84, 128), F32)]
+    )
+    got = lax.all_to_all(pieces, SLAB, 0, 0, tiled=True)
     other = swap_core(tokens)
     normed = call(norm_kernel, shape(ROWS, D), (tokens, other, embed, gain), (), 8 * 10**9)
-
-    def gather(part):
-        pieces = call(pack_kernel, shape(32, 36, part.shape[2]), (order, part))
-        return lax.all_to_all(pieces, CHIP, 0, 0, tiled=True).reshape(D, part.shape[2]).T
-
-    def spread(block):
-        return (block,) + tuple(lax.ppermute(block, EVERY, r) for r in ROUTES)
-
+    block, time_own = call(
+        unpack_kernel, (shape(SECOND + FIRST, D), shape(HALF, D)), (after(got, normed),), [pltpu.VMEM((5, D, 128), F32)]
+    )
+    blocks = (block,) + tuple(lax.ppermute(block, EVERY, r) for r in ROUTES)
     time_other = swap_core(time_own)
     time_normed = call(norm_kernel, shape(ROWS, D), (time_own, time_other, embed, gain), (), 8 * 10**9)
-    block = gather(after(pair[:, :, :FIRST], time_own))
-    late = gather(after(pair[:, :, FIRST:], block, normed, time_normed))
-    blocks = spread(after(block, normed, time_normed))
-
-    two = [pltpu.VMEM((2, FIRST, D), BF16), pltpu.SemaphoreType.DMA((2,))]
-    four = [pltpu.VMEM((4, SECOND, D), BF16), pltpu.SemaphoreType.DMA((4,))]
+
+    two = [pltpu.VMEM((2, SECOND + FIRST, D), BF16), pltpu.SemaphoreType.DMA((2,))]
+    four = [pltpu.VMEM((4, SECOND + FIRST, D), BF16), pltpu.SemaphoreType.DMA((4,))]
     q_t, kv_t = call(
         cross_project_kernel,
         (shape(PAIR, ROWS), shape(2 * PAIR, ROWS)),
-        (order, normed, pair_gains) + blocks,
+        (order, after(normed, time_normed), pair_gains) + blocks,
         two,
         0,
         4,
     )
     kv_a = lax.ppermute(kv_t, EVERY, ACROSS)
     kv_b = lax.ppermute(kv_a, EVERY, ALONG)
-    timed = call(
-        time_kernel, shape(2, HALF, PAIR), (order, after(time_normed, kv_t), pair_gains) + blocks, two, 0, 4
+    timed = call(time_kernel, shape(64, 8, PAIR), (order, after(time_normed, kv_t), pair_gains) + blocks, two, 0, 4)
+    returned = lax.all_to_all(timed, SLAB, 0, 0, tiled=True)
+    space = call(
+        space_kernel, shape(2 * PAIR, ROWS), (order, after(normed, kv_a, timed), space_gains) + blocks, four, 16 * 10**9, 4
     )
-    more = spread(after(late, timed, kv_a))
-    timed = timed.reshape(2, 32, 8, PAIR).transpose(1, 0, 2, 3).reshape(64, 8, PAIR)
-    timed = lax.all_to_all(timed, SLAB, 0, 0, tiled=True)
-    timed = timed.reshape(32, 2, 8, PAIR).transpose(1, 0, 2, 3).reshape(2, HALF, PAIR)
-    space, w_own = call(
-        space_kernel,
-        (shape(2 * PAIR, ROWS), shape(4 * PAIR, D)),
-        (order, after(normed, kv_b, timed), space_gains) + more,
-        four,
-        0,
-        4,
-    )
+    w_own = call(collect_kernel, shape(4 * PAIR, D), (order,) + blocks, [pltpu.SemaphoreType.DMA((4,))], 0, 4)
     w_other = swap_core(w_own)
     cross = call(cross_kernel, shape(PAIR, ROWS), (q_t, kv_a, kv_b), )
     mixed = jnp.concatenate([space, cross], 0)
     arrived = swap_core(mixed[:, HALF:])
     return call(
-        out_kernel, shape(HALF, D), (order, tokens, embed, mixed[:, :HALF], arrived, timed, w_own, w_other)
+        out_kernel, shape(HALF, D), (order, tokens, embed, mixed[:, :HALF], arrived, returned, w_own, w_other)
     )[None]
 
 

time: 179 us -> 154 us (0.86)
  starting transfers between devices: 82 us -> 53.5 us
  Pallas kernels: 25.4 us -> 28 us
    all_to_all x4 -> x2, starting transfers between devices: 40.3 us -> 24.3 us  [the longest x1 15.5 us: local(): got = lax.all_to_all(pieces, SLAB, 0, 0, tiled=True)]
    ppermute x6 -> x3, starting transfers between devices: 19.8 us -> 10.3 us  [local(): blocks = (block,) + tuple((lax.ppermute(block, EVERY, r) for r in ROUTES))]
    all_to_all x4 -> x2, waiting for transfers between devices: 35 us -> 42.3 us  [the longest x1 42.3 us: local(): got = lax.all_to_all(pieces, SLAB, 0, 0, tiled=True)]
    ppermute x6 -> x3, waiting for transfers between devices: 20.3 us -> 13 us  [local(): blocks = (block,) + tuple((lax.ppermute(block, EVERY, r) for r in ROUTES))]
    reshape x5 -> x0, local copies, waits for them, and re-layouts: 6.22 us -> none  [the longest x4 5.5 us: gather(): lax.all_to_all(pieces, CHIP, 0, 0, tiled=True).reshape(D, part.shape[2])]
    unnamed x26 -> x36, local copies, waits for them, and re-layouts: 2.55 us -> 8.53 us
    ppermute x5 -> x4, starting transfers between devices: 14.4 us -> 9.39 us  [swap_core(): return lax.ppermute(block, 'core', [(0, 1), (1, 0)])]
    ppermute x1, waiting for transfers between devices: 0.01 us -> 3.02 us  [local(): kv_b = lax.ppermute(kv_a, EVERY, ALONG)]
  transfers between devices with their start and end apart: 17 -> 11, of which waited for: 6 -> 7; matrix products, arithmetic and copies ran while one was open for 4% -> 1% of each run, Pallas kernels for 8% -> 12%
where the time goes in v3:
time: 154 us; the launch traced here: 153 us
  waiting for transfers between devices  61 us (40%)
  starting transfers between devices  53.5 us (35%)
  Pallas kernels  28 us (18%)
  local copies, waits for them, and re-layouts  9.74 us (6%)
    all_to_all x1, waiting for transfers between devices, local(): got = lax.all_to_all(pieces, SLAB, 0, 0, tiled=True)  42.3 us
    pallas_call x10, Pallas kernels, call(): pl.pallas_call(kernel, out_shape=out_shapes, in_specs=specs, out_specs=vm...  28 us
    all_to_all x1, starting transfers between devices, local(): got = lax.all_to_all(pieces, SLAB, 0, 0, tiled=True)  15.5 us
    ppermute x3, waiting for transfers between devices, local(): blocks = (block,) + tuple((lax.ppermute(block, EVERY, r) for r in ROUTES))  13 us
    ppermute x3, starting transfers between devices, local(): blocks = (block,) + tuple((lax.ppermute(block, EVERY, r) for r in ROUTES))  10.3 us
    ppermute x4, starting transfers between devices, swap_core(): return lax.ppermute(block, 'core', [(0, 1), (1, 0)])  9.39 us
    all_to_all x1, starting transfers between devices, local(): returned = lax.all_to_all(timed, SLAB, 0, 0, tiled=True)  8.73 us
    unnamed x36, local copies, waits for them, and re-layouts  8.53 us
  transfers between devices with their start and end apart: 11, of which 7 were waited for; matrix products, arithmetic and copies ran while one was open for 1% of the time, Pallas kernels for 12%

profile of v3, /device:TPU:1, one launch (start us, length us, event | category | flops | bytes accessed | tf_op | source)
XLA Modules:
  0.0 152.8 jit_solution(13596606880940471892)
XLA Ops:
  0.0 0.0 copy-start
  0.0 0.1 pad_add_fusion.order
  0.1 1.1 copy-done.4
  1.2 0.9 copy-done.13
  2.1 0.8 copy-done.14
  2.9 1.2 shard_map.74
  4.1 0.0 copy-start.3
  4.1 1.3 copy-done.3
  5.4 15.5 %all-to-all-start = ((bf16[64,120,128]{2,1,0:T(8,128)(2,1)}), bf16[64,120,128]{2,1,0:T(8,128)(2,1)S(1)}, u32[]{:S(2)}, u32[]{:S(2)}) async-start(bf16[64,120,128]{2,1,0:T(8,128)(2,1)} %copy-done.3), calls=%async_computation | async-start | bytes 3932160 | tf_op jit(solution)/shard_map/all_to_all | solution.py:291
  20.9 2.4 %collective-permute-start = (bf16[256,1152]{1,0:T(8,128)(2,1)S(1)}, bf16[256,1152]{1,0:T(8,128)(2,1)S(1)}, u32[]{:S(2)}, u32[]{:S(2)}) collective-permute-start(bf16[256,1152]{1,0:T(8,128)(2,1)S(1)} %bitcast.11), channel_id=1, source_target_pairs={{0,1},{1,0},{2,3},{3,2},{4,5},{5,4},{6,7},{7,6},{8,9},{9,8},{10,11... | collective-permute-start | bytes 1769480 | tf_op jit(solution)/shard_map/ppermute | solution.py:55
  23.3 1.5 %collective-permute-done.other = bf16[256,1152]{1,0:T(8,128)(2,1)S(1)} collective-permute-done((bf16[256,1152]{1,0:T(8,128)(2,1)S(1)}, bf16[256,1152]{1,0:T(8,128)(2,1)S(1)}, u32[]{:S(2)}, u32[]{:S(2)}) %collective-permute-start) | collective-permute-done | bytes 589856 | tf_op jit(solution)/shard_map/ppermute | solution.py:55
  24.9 0.8 shard_map.73.normed
  25.7 1.0 copy-done.9
  26.7 42.3 %all-to-all-done.got = bf16[64,120,128]{2,1,0:T(8,128)(2,1)S(1)} async-done(((bf16[64,120,128]{2,1,0:T(8,128)(2,1)}), bf16[64,120,128]{2,1,0:T(8,128)(2,1)S(1)}, u32[]{:S(2)}, u32[]{:S(2)}) %all-to-all-start) | async-done | bytes 1966112 | tf_op jit(solution)/shard_map/all_to_all | solution.py:291
  69.0 1.0 shard_map.75
  70.0 2.0 %collective-permute-start.1 = (bf16[256,1152]{1,0:T(8,128)(2,1)}, bf16[256,1152]{1,0:T(8,128)(2,1)}, u32[]{:S(2)}, u32[]{:S(2)}) collective-permute-start(bf16[256,1152]{1,0:T(8,128)(2,1)} %get-tuple-element.14.own), channel_id=1, source_target_pairs={{0,1},{1,0},{2,3},{3,2},{4,5},{5,4},{6,7},{7,6},{8,9},{9,8},{10,11... | collective-permute-start | bytes 1769480 | tf_op jit(solution)/shard_map/ppermute | solution.py:55
  72.1 2.2 %collective-permute-start.4 = (bf16[576,1152]{1,0:T(8,128)(2,1)S(1)}, bf16[576,1152]{1,0:T(8,128)(2,1)}, u32[]{:S(2)}, u32[]{:S(2)}) collective-permute-start(bf16[576,1152]{1,0:T(8,128)(2,1)S(1)} %get-tuple-element.16.b0), channel_id=1, source_target_pairs={{0,14},{1,3},{2,0},{3,5},{4,2},{5,7},{6,4},{7,9},{8,6},{9,11},{10,... | collective-permute-start | bytes 3981320 | tf_op jit(solution)/shard_map/ppermute | solution.py:297
  74.3 5.0 %collective-permute-start.3 = (bf16[576,1152]{1,0:T(8,128)(2,1)S(1)}, bf16[576,1152]{1,0:T(8,128)(2,1)}, u32[]{:S(2)}, u32[]{:S(2)}) collective-permute-start(bf16[576,1152]{1,0:T(8,128)(2,1)S(1)} %get-tuple-element.16.b0), channel_id=1, source_target_pairs={{0,112},{1,17},{2,114},{3,19},{4,116},{5,21},{6,118},{7,23},{8,120... | collective-permute-start | bytes 3981320 | tf_op jit(solution)/shard_map/ppermute | solution.py:297
  79.3 3.1 %collective-permute-start.2 = (bf16[576,1152]{1,0:T(8,128)(2,1)S(1)}, bf16[576,1152]{1,0:T(8,128)(2,1)S(1)}, u32[]{:S(2)}, u32[]{:S(2)}) collective-permute-start(bf16[576,1152]{1,0:T(8,128)(2,1)S(1)} %get-tuple-element.16.b0), channel_id=1, source_target_pairs={{0,384},{1,129},{2,386},{3,131},{4,388},{5,133},{6,390},{7,135},{8... | collective-permute-start | bytes 3981320 | tf_op jit(solution)/shard_map/ppermute | solution.py:297
  82.5 0.1 stack_reshape.6
  82.6 0.1 stack_reshape.7
  82.7 0.1 reshape.8.gains
  82.9 0.0 collective-permute-done.1.other
  82.9 2.1 %shard_map.76.normed = bf16[512,1152]{1,0:T(8,128)(2,1)S(1)} custom-call(bf16[256,1152]{1,0:T(8,128)(2,1)} %get-tuple-element.14.own, bf16[256,1152]{1,0:T(8,128)(2,1)} %collective-permute-done.1.other, f32[1,1152]{1,0:T(1,128)S(1)} %constant_dynamic-slice_fusion.embed, f32[1,1152]{1,0:T(1,128)S(1)} %broadcast_in_dim.14.gain), custom_call_target="tpu_custom_call" | custom-call | flops 8000000000 | bytes 1 | tf_op jit(solution)/shard_map/pallas_call | solution.py:254
  85.0 1.0 copy-done.7
  86.0 5.9 %collective-permute-done.4.b3 = bf16[576,1152]{1,0:T(8,128)(2,1)} collective-permute-done((bf16[576,1152]{1,0:T(8,128)(2,1)S(1)}, bf16[576,1152]{1,0:T(8,128)(2,1)}, u32[]{:S(2)}, u32[]{:S(2)}) %collective-permute-start.4) | collective-permute-done | bytes 1327136 | tf_op jit(solution)/shard_map/ppermute | solution.py:297
  91.9 5.7 %collective-permute-done.3.b2 = bf16[576,1152]{1,0:T(8,128)(2,1)} collective-permute-done((bf16[576,1152]{1,0:T(8,128)(2,1)S(1)}, bf16[576,1152]{1,0:T(8,128)(2,1)}, u32[]{:S(2)}, u32[]{:S(2)}) %collective-permute-start.3) | collective-permute-done | bytes 1327136 | tf_op jit(solution)/shard_map/ppermute | solution.py:297
  97.6 1.4 collective-permute-done.2.b1
  99.0 1.1 copy-done.1
  100.1 3.6 %shard_map.77 = (bf16[144,512]{1,0:T(8,128)(2,1)S(1)}, bf16[288,512]{1,0:T(8,128)(2,1)}) custom-call(s32[6]{0:T(128)S(1)} %pad_add_fusion.order, bf16[512,1152]{1,0:T(8,128)(2,1)S(1)} %copy-done.10, f32[2,288,1]{2,1,0:T(8,128)S(1)} %reshape.8.gains, bf16[576,1152]{1,0:T(8,128)(2,1)S(1)} %get-tuple-element.16.b0, bf16[576,1152]{1,0:T(8,128)(2,1)} %copy-done.1, ...), custom_call_target="tpu_custom_call" | custom-call | bytes 1 | tf_op jit(solution)/shard_map/pallas_call | solution.py:254
  103.8 6.8 %collective-permute-start.5 = (bf16[288,512]{1,0:T(8,128)(2,1)}, bf16[288,512]{1,0:T(8,128)(2,1)S(1)}, u32[]{:S(2)}, u32[]{:S(2)}) collective-permute-start(bf16[288,512]{1,0:T(8,128)(2,1)} %get-tuple-element.17), channel_id=1, source_target_pairs={{0,64},{1,65},{2,66},{3,67},{4,68},{5,69},{6,70},{7,71},{8,72},{9,... | collective-permute-start | bytes 884744 | tf_op jit(solution)/shard_map/ppermute | solution.py:311
  110.6 0.9 reshape.9.gains
  111.5 1.3 copy-done.8
  112.8 4.9 %shard_map.78 = bf16[64,8,144]{2,1,0:T(8,128)(2,1)} custom-call(s32[6]{0:T(128)S(1)} %pad_add_fusion.order, bf16[512,1152]{1,0:T(8,128)(2,1)S(1)} %copy-done.8, f32[2,288,1]{2,1,0:T(8,128)S(1)} %reshape.8.gains, bf16[576,1152]{1,0:T(8,128)(2,1)S(1)} %get-tuple-element.16.b0, bf16[576,1152]{1,0:T(8,128)(2,1)} %copy-done.1, ...), custom_call_target="tpu_custom_call" | custom-call | bytes 1 | tf_op jit(solution)/shard_map/pallas_call | solution.py:254
  117.7 8.7 %all-to-all-start.1 = ((bf16[64,8,144]{2,1,0:T(8,128)(2,1)}), bf16[64,8,144]{2,1,0:T(8,128)(2,1)S(1)}, u32[]{:S(2)}, u32[]{:S(2)}) async-start(bf16[64,8,144]{2,1,0:T(8,128)(2,1)} %shard_map.78), calls=%async_computation.1 | async-start | bytes 524288 | tf_op jit(solution)/shard_map/all_to_all | solution.py:314
  126.5 2.9 %shard_map.81.w_own = bf16[576,1152]{1,0:T(8,128)(2,1)} custom-call(s32[6]{0:T(128)S(1)} %pad_add_fusion.order, bf16[576,1152]{1,0:T(8,128)(2,1)S(1)} %get-tuple-element.16.b0, bf16[576,1152]{1,0:T(8,128)(2,1)S(1)} %copy-done.2, bf16[576,1152]{1,0:T(8,128)(2,1)} %collective-permute-done.3.b2, bf16[576,1152]{1,0:T(8,128)(2,1)} %collective-permute-done.4.b3), custom_call_target="tpu_custom_call" | custom-call | bytes 1 | tf_op jit(solution)/shard_map/pallas_call | solution.py:254
  129.4 2.5 %collective-permute-start.8 = (bf16[576,1152]{1,0:T(8,128)(2,1)}, bf16[576,1152]{1,0:T(8,128)(2,1)S(1)}, u32[]{:S(2)}, u32[]{:S(2)}) collective-permute-start(bf16[576,1152]{1,0:T(8,128)(2,1)} %shard_map.81.w_own), channel_id=1, source_target_pairs={{0,1},{1,0},{2,3},{3,2},{4,5},{5,4},{6,7},{7,6},{8,9},{9,8},{10,11... | collective-permute-start | bytes 3981320 | tf_op jit(solution)/shard_map/ppermute | solution.py:55
  131.9 0.0 collective-permute-done.5.kv_a
  131.9 2.7 %collective-permute-start.6 = (bf16[288,512]{1,0:T(8,128)(2,1)S(1)}, bf16[288,512]{1,0:T(8,128)(2,1)S(1)}, u32[]{:S(2)}, u32[]{:S(2)}) collective-permute-start(bf16[288,512]{1,0:T(8,128)(2,1)S(1)} %collective-permute-done.5.kv_a), channel_id=1, source_target_pairs={{0,128},{1,129},{2,130},{3,131},{4,132},{5,133},{6,134},{7,135},{8... | collective-permute-start | bytes 884744 | tf_op jit(solution)/shard_map/ppermute | solution.py:312
  134.6 6.7 %shard_map.79 = bf16[288,512]{1,0:T(8,128)(2,1)S(1)} custom-call(s32[6]{0:T(128)S(1)} %pad_add_fusion.order, bf16[512,1152]{1,0:T(8,128)(2,1)S(1)} %copy-done.11, f32[4,144,1]{2,1,0:T(8,128)S(1)} %copy-done.12, bf16[576,1152]{1,0:T(8,128)(2,1)S(1)} %get-tuple-element.16.b0, bf16[576,1152]{1,0:T(8,128)(2,1)} %copy-done.1, ...), custom_call_target="tpu_custom_call" | custom-call | flops 16000000000 | bytes 1 | tf_op jit(solution)/shard_map/pallas_call | solution.py:254
  141.3 0.0 copy-start.6
  141.3 3.0 %collective-permute-done.6.kv_b = bf16[288,512]{1,0:T(8,128)(2,1)S(1)} collective-permute-done((bf16[288,512]{1,0:T(8,128)(2,1)S(1)}, bf16[288,512]{1,0:T(8,128)(2,1)S(1)}, u32[]{:S(2)}, u32[]{:S(2)}) %collective-permute-start.6) | collective-permute-done | bytes 294944 | tf_op jit(solution)/shard_map/ppermute | solution.py:312
  144.3 1.3 shard_map.80
  145.7 2.5 %collective-permute-start.7 = (bf16[432,256]{1,0:T(8,128)(2,1)S(1)}, bf16[432,256]{1,0:T(8,128)(2,1)S(1)}, u32[]{:S(2)}, u32[]{:S(2)}) collective-permute-start(bf16[432,256]{1,0:T(8,128)(2,1)S(1)} %get-tuple-element.21), channel_id=1, source_target_pairs={{0,1},{1,0},{2,3},{3,2},{4,5},{5,4},{6,7},{7,6},{8,9},{9,8},{10,11... | collective-permute-start | bytes 663560 | tf_op jit(solution)/shard_map/ppermute | solution.py:55
  148.2 0.0 all-to-all-done.1.timed
  148.3 1.1 collective-permute-done.7.arrived
  149.3 0.0 collective-permute-done.8.w_other
  149.3 3.5 %shard_map.82 = bf16[256,1152]{1,0:T(8,128)(2,1)} custom-call(s32[6]{0:T(128)S(1)} %pad_add_fusion.order, bf16[256,1152]{1,0:T(8,128)(2,1)S(1)} %bitcast.13, f32[1,1152]{1,0:T(1,128)S(1)} %constant_dynamic-slice_fusion.embed, bf16[432,256]{1,0:T(8,128)(2,1)S(1)} %get-tuple-element.22.own, bf16[432,256]{1,0:T(8,128)(2,1)S(1)} %collective-permute-done.7.arrived, ...), custom_call_target="tpu_custom_call" | custom-call | bytes 1 | tf_op jit(solution)/shard_map/pallas_call | solution.py:254
  (33 shorter events, 0.1 us)
Async XLA Ops:
  0.0 23.3 %copy-start = (f32[8,1152]{1,0:T(8,128)S(1)}, f32[8,1152]{1,0:T(8,128)}, u32[]{:S(2)}) copy-start(f32[8,1152]{1,0:T(8,128)} %param.8) | copy-start | bytes 110596
  0.1 1.1 copy-start.4
  1.2 0.9 copy-start.13
  2.1 0.8 copy-start.14
  4.1 1.3 copy-start.3
  5.3 15.6 %copy-start.5 = (bf16[1,256,1152]{2,1,0:T(8,128)(2,1)S(1)}, bf16[1,256,1152]{2,1,0:T(8,128)(2,1)}, u32[]{:S(2)}) copy-start(bf16[1,256,1152]{2,1,0:T(8,128)(2,1)} %param.7) | copy-start | bytes 1769476
  5.3 17.9 %copy-start.15 = (f32[1152]{0:T(1024)S(1)}, f32[1152]{0:T(1024)}, u32[]{:S(2)}) copy-start(f32[1152]{0:T(1024)} %param.9) | copy-start | bytes 13828
  5.4 63.7 %all-to-all-start = ((bf16[64,120,128]{2,1,0:T(8,128)(2,1)}), bf16[64,120,128]{2,1,0:T(8,128)(2,1)S(1)}, u32[]{:S(2)}, u32[]{:S(2)}) async-start(bf16[64,120,128]{2,1,0:T(8,128)(2,1)} %copy-done.3), calls=%async_computation | async-start | bytes 3932160 | tf_op jit(solution)/shard_map/all_to_all | solution.py:291
  20.9 4.0 %collective-permute-start = (bf16[256,1152]{1,0:T(8,128)(2,1)S(1)}, bf16[256,1152]{1,0:T(8,128)(2,1)S(1)}, u32[]{:S(2)}, u32[]{:S(2)}) collective-permute-start(bf16[256,1152]{1,0:T(8,128)(2,1)S(1)} %bitcast.11), channel_id=1, source_target_pairs={{0,1},{1,0},{2,3},{3,2},{4,5},{5,4},{6,7},{7,6},{8,9},{9,8},{10,11... | collective-permute-start | bytes 1769480 | tf_op jit(solution)/shard_map/ppermute | solution.py:55
  25.7 1.0 copy-start.9
  26.7 55.7 %copy-start.16 = (f32[1152]{0:T(1024)S(1)}, f32[1152]{0:T(1024)}, u32[]{:S(2)}) copy-start(f32[1152]{0:T(1024)} %param.10) | copy-start | bytes 13828
  26.7 55.8 %copy-start.17 = (f32[1152]{0:T(1024)S(1)}, f32[1152]{0:T(1024)}, u32[]{:S(2)}) copy-start(f32[1152]{0:T(1024)} %param.11) | copy-start | bytes 13828
  70.0 12.8 %collective-permute-start.1 = (bf16[256,1152]{1,0:T(8,128)(2,1)}, bf16[256,1152]{1,0:T(8,128)(2,1)}, u32[]{:S(2)}, u32[]{:S(2)}) collective-permute-start(bf16[256,1152]{1,0:T(8,128)(2,1)} %get-tuple-element.14.own), channel_id=1, source_target_pairs={{0,1},{1,0},{2,3},{3,2},{4,5},{5,4},{6,7},{7,6},{8,9},{9,8},{10,11... | collective-permute-start | bytes 1769480 | tf_op jit(solution)/shard_map/ppermute | solution.py:55
  72.1 19.8 %collective-permute-start.4 = (bf16[576,1152]{1,0:T(8,128)(2,1)S(1)}, bf16[576,1152]{1,0:T(8,128)(2,1)}, u32[]{:S(2)}, u32[]{:S(2)}) collective-permute-start(bf16[576,1152]{1,0:T(8,128)(2,1)S(1)} %get-tuple-element.16.b0), channel_id=1, source_target_pairs={{0,14},{1,3},{2,0},{3,5},{4,2},{5,7},{6,4},{7,9},{8,6},{9,11},{10,... | collective-permute-start | bytes 3981320 | tf_op jit(solution)/shard_map/ppermute | solution.py:297
  74.3 23.3 %collective-permute-start.3 = (bf16[576,1152]{1,0:T(8,128)(2,1)S(1)}, bf16[576,1152]{1,0:T(8,128)(2,1)}, u32[]{:S(2)}, u32[]{:S(2)}) collective-permute-start(bf16[576,1152]{1,0:T(8,128)(2,1)S(1)} %get-tuple-element.16.b0), channel_id=1, source_target_pairs={{0,112},{1,17},{2,114},{3,19},{4,116},{5,21},{6,118},{7,23},{8,120... | collective-permute-start | bytes 3981320 | tf_op jit(solution)/shard_map/ppermute | solution.py:297
  79.3 19.7 %collective-permute-start.2 = (bf16[576,1152]{1,0:T(8,128)(2,1)S(1)}, bf16[576,1152]{1,0:T(8,128)(2,1)S(1)}, u32[]{:S(2)}, u32[]{:S(2)}) collective-permute-start(bf16[576,1152]{1,0:T(8,128)(2,1)S(1)} %get-tuple-element.16.b0), channel_id=1, source_target_pairs={{0,384},{1,129},{2,386},{3,131},{4,388},{5,133},{6,390},{7,135},{8... | collective-permute-start | bytes 3981320 | tf_op jit(solution)/shard_map/ppermute | solution.py:297
  82.9 17.3 %copy-start.10 = (bf16[512,1152]{1,0:T(8,128)(2,1)S(1)}, bf16[512,1152]{1,0:T(8,128)(2,1)}, u32[]{:S(2)}) copy-start(bf16[512,1152]{1,0:T(8,128)(2,1)} %copy-done.9) | copy-start | bytes 3538948
  85.0 1.0 copy-start.7
  99.0 1.1 copy-start.1
  103.8 28.1 %collective-permute-start.5 = (bf16[288,512]{1,0:T(8,128)(2,1)}, bf16[288,512]{1,0:T(8,128)(2,1)S(1)}, u32[]{:S(2)}, u32[]{:S(2)}) collective-permute-start(bf16[288,512]{1,0:T(8,128)(2,1)} %get-tuple-element.17), channel_id=1, source_target_pairs={{0,64},{1,65},{2,66},{3,67},{4,68},{5,69},{6,70},{7,71},{8,72},{9,... | collective-permute-start | bytes 884744 | tf_op jit(solution)/shard_map/ppermute | solution.py:311
  111.5 1.3 copy-start.8
  112.8 13.7 %copy-start.2 = (bf16[576,1152]{1,0:T(8,128)(2,1)S(1)}, bf16[576,1152]{1,0:T(8,128)(2,1)}, u32[]{:S(2)}) copy-start(bf16[576,1152]{1,0:T(8,128)(2,1)} %copy-done.1) | copy-start | bytes 3981316
  117.7 30.5 %all-to-all-start.1 = ((bf16[64,8,144]{2,1,0:T(8,128)(2,1)}), bf16[64,8,144]{2,1,0:T(8,128)(2,1)S(1)}, u32[]{:S(2)}, u32[]{:S(2)}) async-start(bf16[64,8,144]{2,1,0:T(8,128)(2,1)} %shard_map.78), calls=%async_computation.1 | async-start | bytes 524288 | tf_op jit(solution)/shard_map/all_to_all | solution.py:314
  126.5 8.1 %copy-start.11 = (bf16[512,1152]{1,0:T(8,128)(2,1)S(1)}, bf16[512,1152]{1,0:T(8,128)(2,1)}, u32[]{:S(2)}) copy-start(bf16[512,1152]{1,0:T(8,128)(2,1)} %copy-done.9) | copy-start | bytes 3538948
  126.5 8.1 %copy-start.12 = (f32[4,144,1]{2,1,0:T(8,128)S(1)}, f32[4,144,1]{2,1,0:T(8,128)}, u32[]{:S(2)}) copy-start(f32[4,144,1]{2,1,0:T(8,128)} %reshape.9.gains) | copy-start | bytes 6916
  129.4 19.9 %collective-permute-start.8 = (bf16[576,1152]{1,0:T(8,128)(2,1)}, bf16[576,1152]{1,0:T(8,128)(2,1)S(1)}, u32[]{:S(2)}, u32[]{:S(2)}) collective-permute-start(bf16[576,1152]{1,0:T(8,128)(2,1)} %shard_map.81.w_own), channel_id=1, source_target_pairs={{0,1},{1,0},{2,3},{3,2},{4,5},{5,4},{6,7},{7,6},{8,9},{9,8},{10,11... | collective-permute-start | bytes 3981320 | tf_op jit(solution)/shard_map/ppermute | solution.py:55
  131.9 12.5 %collective-permute-start.6 = (bf16[288,512]{1,0:T(8,128)(2,1)S(1)}, bf16[288,512]{1,0:T(8,128)(2,1)S(1)}, u32[]{:S(2)}, u32[]{:S(2)}) collective-permute-start(bf16[288,512]{1,0:T(8,128)(2,1)S(1)} %collective-permute-done.5.kv_a), channel_id=1, source_target_pairs={{0,128},{1,129},{2,130},{3,131},{4,132},{5,133},{6,134},{7,135},{8... | collective-permute-start | bytes 884744 | tf_op jit(solution)/shard_map/ppermute | solution.py:312
  141.3 8.0 %copy-start.6 = (bf16[1,256,1152]{2,1,0:T(8,128)(2,1)S(1)}, bf16[1,256,1152]{2,1,0:T(8,128)(2,1)}, u32[]{:S(2)}) copy-start(bf16[1,256,1152]{2,1,0:T(8,128)(2,1)} %param.7) | copy-start | bytes 1769476
  145.7 3.6 %collective-permute-start.7 = (bf16[432,256]{1,0:T(8,128)(2,1)S(1)}, bf16[432,256]{1,0:T(8,128)(2,1)S(1)}, u32[]{:S(2)}, u32[]{:S(2)}) collective-permute-start(bf16[432,256]{1,0:T(8,128)(2,1)S(1)} %get-tuple-element.21), channel_id=1, source_target_pairs={{0,1},{1,0},{2,3},{3,2},{4,5},{5,4},{6,7},{7,6},{8,9},{9,8},{10,11... | collective-permute-start | bytes 663560 | tf_op jit(solution)/shard_map/ppermute | solution.py:55

commit v4 on v3

--- a/solution.py
+++ b/solution.py
@@ -15,6 +15,7 @@
 ROWS = 2 * HALF
 FIRST = TRIPLE
 SECOND = PAIR + TRIPLE
+PIECE = 96
 CAM = ("x", "yh")
 CHIP = ("yl", "z")
 SLAB = ("yl", "z", "core")
@@ -67,7 +68,16 @@
     return lax.optimization_barrier((value,) + others)[0]
 
 
-def pack_kernel(order, w_qkv, w_out, tokens, out, pieces):
+def pack_kernel(order, w_qkv_hbm, w_out_hbm, out, w_qkv, w_out, wide, pieces, in_sem, out_sem):
+    loads = [
+        pltpu.make_async_copy(w_qkv_hbm, w_qkv, in_sem.at[0]),
+        pltpu.make_async_copy(w_out_hbm, w_out, in_sem.at[1]),
+    ]
+    for load in loads:
+        load.start()
+    for load in loads:
+        load.wait()
+
     def columns(kind, head, count):
         start = kind * D + head * HD
         return w_qkv[:, start : start + count * HD].astype(F32)
@@ -82,22 +92,24 @@
                 parts += [columns(0, head, 2), columns(1, head, 1)]
             else:
                 parts += [columns(1, head + 1, 1), columns(2, head, 2)]
-            wide = jnp.concatenate(parts, 1)
+            whole = jnp.concatenate(parts, 1)
             place = who * 4 + group
             for tile in range(4):
-                pieces[place, tile * 18 : tile * 18 + 18] = wide[:, tile * 128 : tile * 128 + 128]
-            pieces[place, 72:81] = jnp.concatenate([wide[:9, 512:], wide[9:, 512:]], 1)
-            pieces[place, 81:84] = jnp.zeros((3, 128), F32)
+                wide[tile * 18 : tile * 18 + 18] = whole[:, tile * 128 : tile * 128 + 128]
+            wide[72:81] = jnp.concatenate([whole[:9, 512:], whole[9:, 512:]], 1)
+            wide[81:] = jnp.zeros((PIECE - 81, 128), F32)
+            pieces[place] = wide[...].astype(BF16)
     x = order[5]
+    stores = []
     for dest in range(64):
         colour = (x + 2 * (dest // 16) + 3 * (dest // 2 % 8)) % 4
-        block = tokens[dest // 2 * 8 : dest // 2 * 8 + 8].astype(F32)
-        block = block[dest % 2 * 4 : dest % 2 * 4 + 4]
-        rows = [block[:, tile * 128 : tile * 128 + 128] for tile in range(9)]
-        out[dest] = jnp.concatenate([pieces[dest % 2 * 4 + colour]] + rows, 0).astype(BF16)
-
-
-def unpack_kernel(got, block, tokens, wide):
+        stores.append(pltpu.make_async_copy(pieces.at[dest % 2 * 4 + colour], out.at[dest], out_sem))
+        stores[-1].start()
+    for store in stores:
+        store.wait()
+
+
+def unpack_kernel(got, block, wide):
     for source in range(64):
         rows = got[source].astype(F32)
         at = source * 18
@@ -105,13 +117,6 @@
             wide[tile, at : at + 18] = rows[tile * 18 : tile * 18 + 18]
         wide[4, at : at + 9, :64] = rows[72:81, :64]
         wide[4, at + 9 : at + 18, :64] = rows[72:81, 64:]
-        if source % 2 == 1:
-            pair = [got[source - 1].astype(F32), rows]
-            tiles = []
-            for tile in range(9):
-                start = 84 + tile * 4
-                tiles.append(jnp.concatenate([one[start : start + 4] for one in pair], 0))
-            tokens[source * 4 - 4 : source * 4 + 4] = jnp.concatenate(tiles, 1).astype(BF16)
     for tile in range(4):
         block[tile * 128 : tile * 128 + 128] = wide[tile].T.astype(BF16)
     block[512:] = wide[4].T[:64].astype(BF16)
@@ -167,11 +172,20 @@
         wait_fetch(blocks, weight.at[slot], sem.at[slot])
 
 
-def cross_project_kernel(order, normed, gains, b0, b1, b2, b3, q_t, kv_t, weight, sem):
-    fetch_all(order, (b0, b1, b2, b3), (0, 1), weight, sem)
+def cross_project_kernel(order, normed, gains, b0, b1, b2, b3, q_t, kv_t, w_out, weight, sem):
+    blocks = (b0, b1, b2, b3)
+    parts = [block.at[pl.ds(0, PAIR)] for block in blocks]
+    for group in range(2):
+        start_fetch(order, blocks, group, weight.at[group], sem.at[group])
+    for group in range(4):
+        start_fetch(order, parts, group, w_out.at[pl.ds(group * PAIR, PAIR)], sem.at[2 + group])
+    for group in range(2):
+        wait_fetch(blocks, weight.at[group], sem.at[group])
     qk, v = project_pair(normed, weight, gains[0])
     q_t[...] = qk[:PAIR].astype(BF16)
     kv_t[...] = jnp.concatenate([qk[PAIR:], v], 0).astype(BF16)
+    for group in range(4):
+        wait_fetch(parts, w_out.at[pl.ds(group * PAIR, PAIR)], sem.at[2 + group])
 
 
 def time_kernel(order, normed, gains, b0, b1, b2, b3, out, weight, sem):
@@ -187,20 +201,11 @@
             at = head * HD
             side = (qk[PAIR + at : PAIR + at + HD, part], v[at : at + HD, part])
             heads.append(attend(qk[at : at + HD, part], [side], row == col))
-        sets.append(jnp.concatenate(heads, 0).T.reshape(64, 4, PAIR))
+        sets.append(jnp.concatenate(heads, 0).T.reshape(32, 8, PAIR))
     swap = order[4] == 1
     one = jnp.where(swap, sets[1], sets[0])
     two = jnp.where(swap, sets[0], sets[1])
     out[...] = jnp.concatenate([one, two], 1).astype(BF16)
-
-
-def collect_kernel(order, b0, b1, b2, b3, out, sem):
-    blocks = [block.at[pl.ds(0, PAIR)] for block in (b0, b1, b2, b3)]
-    slots = [out.at[pl.ds(group * PAIR, PAIR)] for group in range(4)]
-    for group in range(4):
-        start_fetch(order, blocks, group, slots[group], sem.at[group])
-    for group in range(4):
-        wait_fetch(blocks, slots[group], sem.at[group])
 
 
 def space_kernel(order, normed, gains, b0, b1, b2, b3, out, weight, sem):
@@ -213,33 +218,37 @@
     out[...] = jnp.concatenate(heads, 0).astype(BF16)
 
 
-def cross_kernel(q_t, kv_a, kv_b, out):
+def cross_kernel(order, q_t, kv_a, kv_b, space, timed, keep, give):
     query = q_t[...].astype(F32)
     both = [ref[...].astype(F32) for ref in (kv_a, kv_b)]
-    heads = []
+    heads = [space[...].astype(F32)]
     for head in range(2):
         at = head * HD
         sides = [(kv[at : at + HD], kv[PAIR + at : PAIR + at + HD]) for kv in both]
         heads.append(attend(query[at : at + HD], sides))
-    out[...] = jnp.concatenate(heads, 0).astype(BF16)
-
-
-def out_kernel(order, tokens, embed, own, arrived, timed, w_own, w_other, out):
+    mixed = jnp.concatenate(heads, 0).T
+    late = timed[...].astype(F32)
+    late = [late[:, i * 8 : i * 8 + 8].reshape(HALF, PAIR) for i in range(2)]
+    swap = order[4] == 1
+    keep[...] = jnp.concatenate([mixed[:HALF], jnp.where(swap, late[1], late[0])], 1).astype(BF16)
+    give[...] = jnp.concatenate([mixed[HALF:], jnp.where(swap, late[0], late[1])], 1).astype(BF16)
+
+
+def out_kernel(order, tokens, embed, own, arrived, w_own, w_other, out):
     swap = order[4] == 1
     mine, theirs = own[...].astype(F32), arrived[...].astype(F32)
     first = jnp.where(swap, theirs, mine)
     second = jnp.where(swap, mine, theirs)
-    split = 2 * PAIR
-    mixed_t = jnp.concatenate([first[:split], second[:split], first[split:], second[split:]], 0)
-    late = timed[...].astype(F32).reshape(32, 2, 8, PAIR)
-    late = [late[:, who].reshape(HALF, PAIR).astype(BF16) for who in range(2)]
-    mixed = jnp.concatenate([mixed_t.T.astype(BF16)] + late, 1)
+    parts = []
+    for start, end in ((0, 2 * PAIR), (2 * PAIR, 3 * PAIR), (3 * PAIR, 4 * PAIR)):
+        parts += [first[:, start:end], second[:, start:end]]
+    mixed = jnp.concatenate(parts, 1).astype(BF16)
     one, two = mm_t(mixed, w_own[...]), mm_t(mixed, w_other[...])
     update = jnp.concatenate([jnp.where(swap, two, one), jnp.where(swap, one, two)], 1)
     out[...] = (tokens[...].astype(F32) + embed[...] + update).astype(BF16)
 
 
-def call(kernel, out_shapes, args, scratch=(), flops=0, anys=0):
+def call(kernel, out_shapes, args, scratch=(), flops=0, anys=0, out_any=False):
     smem = pl.BlockSpec(memory_space=pltpu.SMEM)
     vmem = pl.BlockSpec(memory_space=pltpu.VMEM)
     hbm = pl.BlockSpec(memory_space=pl.ANY)
@@ -255,7 +264,7 @@
         kernel,
         out_shape=out_shapes,
         in_specs=specs,
-        out_specs=vmem if single else (vmem,) * len(out_shapes),
+        out_specs=hbm if out_any else vmem if single else (vmem,) * len(out_shapes),
         scratch_shapes=list(scratch),
         compiler_params=pltpu.CompilerParams(vmem_limit_bytes=VMEM_LIMIT),
         cost_estimate=pl.CostEstimate(flops=flops, bytes_accessed=1, transcendentals=0),
@@ -286,42 +295,64 @@
     space_gains = gains_of(4 * core, 4).reshape(4, PAIR, 1)
 
     pieces = call(
-        pack_kernel, shape(64, 120, 128), (order, w_qkv, w_out, tokens), [pltpu.VMEM((8, 84, 128), F32)]
+        pack_kernel,
+        shape(64, PIECE, 128),
+        (order, w_qkv, w_out),
+        [
+            pltpu.VMEM((18, 3 * D), BF16),
+            pltpu.VMEM((18, D), BF16),
+            pltpu.VMEM((PIECE, 128), F32),
+            pltpu.VMEM((8, PIECE, 128), BF16),
+            pltpu.SemaphoreType.DMA((2,)),
+            pltpu.SemaphoreType.DMA,
+        ],
+        0,
+        2,
+        True,
     )
     got = lax.all_to_all(pieces, SLAB, 0, 0, tiled=True)
     other = swap_core(tokens)
     normed = call(norm_kernel, shape(ROWS, D), (tokens, other, embed, gain), (), 8 * 10**9)
-    block, time_own = call(
-        unpack_kernel, (shape(SECOND + FIRST, D), shape(HALF, D)), (after(got, normed),), [pltpu.VMEM((5, D, 128), F32)]
+    block = call(
+        unpack_kernel, shape(SECOND + FIRST, D), (after(got, normed, pair_gains, space_gains),), [pltpu.VMEM((5, D, 128), F32)]
     )
     blocks = (block,) + tuple(lax.ppermute(block, EVERY, r) for r in ROUTES)
+    time_own = lax.all_to_all(after(tokens, block).reshape(32, 8, D), CHIP, 0, 0, tiled=True).reshape(HALF, D)
+
+    two = pltpu.VMEM((2, SECOND + FIRST, D), BF16)
+    four = [pltpu.VMEM((4, SECOND + FIRST, D), BF16), pltpu.SemaphoreType.DMA((4,))]
+    q_t, kv_t, w_own = call(
+        cross_project_kernel,
+        (shape(PAIR, ROWS), shape(2 * PAIR, ROWS), shape(4 * PAIR, D)),
+        (order, normed, pair_gains) + blocks,
+        [two, pltpu.SemaphoreType.DMA((6,))],
+        0,
+        4,
+    )
+    kv_a = lax.ppermute(kv_t, EVERY, ACROSS)
+    kv_b = lax.ppermute(kv_a, EVERY, ALONG)
+    w_other = swap_core(w_own)
+    space = call(
+        space_kernel, shape(2 * PAIR, ROWS), (order, after(normed, kv_t), space_gains) + blocks, four, 16 * 10**9, 4
+    )
+    time_own = after(time_own, kv_t)
     time_other = swap_core(time_own)
     time_normed = call(norm_kernel, shape(ROWS, D), (time_own, time_other, embed, gain), (), 8 * 10**9)
-
-    two = [pltpu.VMEM((2, SECOND + FIRST, D), BF16), pltpu.SemaphoreType.DMA((2,))]
-    four = [pltpu.VMEM((4, SECOND + FIRST, D), BF16), pltpu.SemaphoreType.DMA((4,))]
-    q_t, kv_t = call(
-        cross_project_kernel,
-        (shape(PAIR, ROWS), shape(2 * PAIR, ROWS)),
-        (order, after(normed, time_normed), pair_gains) + blocks,
-        two,
+    timed = call(
+        time_kernel,
+        shape(32, 16, PAIR),
+        (order, after(time_normed, space), pair_gains) + blocks,
+        [two, pltpu.SemaphoreType.DMA((2,))],
         0,
         4,
     )
-    kv_a = lax.ppermute(kv_t, EVERY, ACROSS)
-    kv_b = lax.ppermute(kv_a, EVERY, ALONG)
-    timed = call(time_kernel, shape(64, 8, PAIR), (order, after(time_normed, kv_t), pair_gains) + blocks, two, 0, 4)
-    returned = lax.all_to_all(timed, SLAB, 0, 0, tiled=True)
-    space = call(
-        space_kernel, shape(2 * PAIR, ROWS), (order, after(normed, kv_a, timed), space_gains) + blocks, four, 16 * 10**9, 4
-    )
-    w_own = call(collect_kernel, shape(4 * PAIR, D), (order,) + blocks, [pltpu.SemaphoreType.DMA((4,))], 0, 4)
-    w_other = swap_core(w_own)
-    cross = call(cross_kernel, shape(PAIR, ROWS), (q_t, kv_a, kv_b), )
-    mixed = jnp.concatenate([space, cross], 0)
-    arrived = swap_core(mixed[:, HALF:])
+    returned = lax.all_to_all(timed, CHIP, 0, 0, tiled=True)
+    keep, give = call(
+        cross_kernel, (shape(HALF, 4 * PAIR), shape(HALF, 4 * PAIR)), (order, q_t, kv_a, kv_b, space, returned)
+    )
+    arrived = swap_core(give)
     return call(
-        out_kernel, shape(HALF, D), (order, tokens, embed, mixed[:, :HALF], arrived, returned, w_own, w_other)
+        out_kernel, shape(HALF, D), (order, tokens, embed, keep, arrived, w_own, w_other)
     )[None]
 
 

time: 154 us -> 158 us (1.026)
  starting transfers between devices: 53.5 us -> 66.3 us
  waiting for transfers between devices: 61 us -> 53.4 us
    all_to_all x1 -> x2, waiting for transfers between devices: 0.01 us -> 10.6 us  [the longest x1 10.6 us: local(): returned = lax.all_to_all(timed, CHIP, 0, 0, tiled=True)]
    all_to_all x1, waiting for transfers between devices: 42.3 us -> 32.3 us  [local(): got = lax.all_to_all(pieces, SLAB, 0, 0, tiled=True)]
    all_to_all x1 -> x2, starting transfers between devices: 8.73 us -> 18.4 us  [the longest x1 10.5 us: local(): returned = lax.all_to_all(timed, CHIP, 0, 0, tiled=True)]
    ppermute x3, waiting for transfers between devices: 13 us -> 7.9 us  [local(): blocks = (block,) + tuple((lax.ppermute(block, EVERY, r) for r in ROUTES))]
    ppermute x1, waiting for transfers between devices: 3.02 us -> 0.01 us  [local(): kv_b = lax.ppermute(kv_a, EVERY, ALONG)]
    ppermute x4, starting transfers between devices: 9.39 us -> 11.9 us  [swap_core(): return lax.ppermute(block, 'core', [(0, 1), (1, 0)])]
    pallas_call x10 -> x9, Pallas kernels: 28 us -> 26.8 us  [call(): pl.pallas_call(kernel, out_shape=out_shapes, in_specs=specs, out_specs=hb...]
    unnamed x36 -> x38, local copies, waits for them, and re-layouts: 8.53 us -> 8.77 us
  transfers between devices with their start and end apart: 11 -> 12, of which waited for: 7 -> 7; matrix products, arithmetic and copies ran while one was open for 1% -> 1% of each run, Pallas kernels for 12% -> 13%
where the time goes in v4:
time: 158 us; the launch traced here: 157 us
  starting transfers between devices  66.3 us (42%)
  waiting for transfers between devices  53.4 us (34%)
  Pallas kernels  26.8 us (17%)
  local copies, waits for them, and re-layouts  10.2 us (6%)
    all_to_all x1, waiting for transfers between devices, local(): got = lax.all_to_all(pieces, SLAB, 0, 0, tiled=True)  32.3 us
    pallas_call x9, Pallas kernels, call(): pl.pallas_call(kernel, out_shape=out_shapes, in_specs=specs, out_specs=hb...  26.8 us
    all_to_all x1, starting transfers between devices, local(): got = lax.all_to_all(pieces, SLAB, 0, 0, tiled=True)  15.6 us
    ppermute x4, starting transfers between devices, swap_core(): return lax.ppermute(block, 'core', [(0, 1), (1, 0)])  11.9 us
    all_to_all x1, waiting for transfers between devices, local(): returned = lax.all_to_all(timed, CHIP, 0, 0, tiled=True)  10.6 us
    all_to_all x1, starting transfers between devices, local(): returned = lax.all_to_all(timed, CHIP, 0, 0, tiled=True)  10.5 us
    ppermute x3, starting transfers between devices, local(): blocks = (block,) + tuple((lax.ppermute(block, EVERY, r) for r in ROUTES))  9.7 us
    unnamed x38, local copies, waits for them, and re-layouts  8.77 us
  transfers between devices with their start and end apart: 12, of which 7 were waited for; matrix products, arithmetic and copies ran while one was open for 1% of the time, Pallas kernels for 13%

profile of v4, /device:TPU:1, one launch (start us, length us, event | category | flops | bytes accessed | tf_op | source)
XLA Modules:
  0.0 157.2 jit_solution(17861857084907422843)
XLA Ops:
  0.0 0.1 pad_add_fusion.order
  0.1 0.9 copy-done.12
  1.0 0.8 copy-done.15
  1.8 2.3 %shard_map.74 = bf16[64,96,128]{2,1,0:T(8,128)(2,1)} custom-call(s32[6]{0:T(128)S(1)} %pad_add_fusion.order, bf16[18,3456]{1,0:T(8,128)(2,1)S(1)} %copy-done.12, bf16[18,1152]{1,0:T(8,128)(2,1)S(1)} %copy-done.15), custom_call_target="tpu_custom_call" | custom-call | bytes 1 | tf_op jit(solution)/shard_map/pallas_call | solution.py:263
  4.2 0.0 copy-start.16
  4.2 0.0 copy-start.17
  4.2 0.0 copy-start.18
  4.2 15.6 %all-to-all-start = ((bf16[64,96,128]{2,1,0:T(8,128)(2,1)}), bf16[64,96,128]{2,1,0:T(8,128)(2,1)S(1)}, u32[]{:S(2)}, u32[]{:S(2)}) async-start(bf16[64,96,128]{2,1,0:T(8,128)(2,1)} %shard_map.74), calls=%async_computation | async-start | bytes 3145728 | tf_op jit(solution)/shard_map/all_to_all | solution.py:313
  19.8 2.4 %collective-permute-start = (bf16[256,1152]{1,0:T(8,128)(2,1)}, bf16[256,1152]{1,0:T(8,128)(2,1)S(1)}, u32[]{:S(2)}, u32[]{:S(2)}) collective-permute-start(bf16[256,1152]{1,0:T(8,128)(2,1)} %bitcast.2.own.tokens), channel_id=1, source_target_pairs={{0,1},{1,0},{2,3},{3,2},{4,5},{5,4},{6,7},{7,6},{8,9},{9,8},{10,11... | collective-permute-start | bytes 1769480 | tf_op jit(solution)/shard_map/ppermute | solution.py:56
  22.2 0.1 stack_reshape.6
  22.3 0.1 stack_reshape.7
  22.4 0.1 reshape.13
  22.5 0.1 reshape.12
  22.6 1.3 collective-permute-done.other
  23.9 1.8 %shard_map.73.normed = bf16[512,1152]{1,0:T(8,128)(2,1)S(1)} custom-call(bf16[256,1152]{1,0:T(8,128)(2,1)} %bitcast.2.own.tokens, bf16[256,1152]{1,0:T(8,128)(2,1)S(1)} %collective-permute-done.other, f32[1,1152]{1,0:T(1,128)S(1)} %constant_dynamic-slice_fusion.embed, f32[1,1152]{1,0:T(1,128)S(1)} %broadcast_in_dim.14.gain), custom_call_target="tpu_custom_call" | custom-call | flops 8000000000 | bytes 1 | tf_op jit(solution)/shard_map/pallas_call | solution.py:263
  25.8 1.0 copy-done.6
  26.8 32.3 %all-to-all-done.got = bf16[64,96,128]{2,1,0:T(8,128)(2,1)S(1)} async-done(((bf16[64,96,128]{2,1,0:T(8,128)(2,1)}), bf16[64,96,128]{2,1,0:T(8,128)(2,1)S(1)}, u32[]{:S(2)}, u32[]{:S(2)}) %all-to-all-start) | async-done | bytes 1572896 | tf_op jit(solution)/shard_map/all_to_all | solution.py:313
  59.1 0.6 shard_map.75.b0
  59.8 2.2 %collective-permute-start.3 = (bf16[576,1152]{1,0:T(8,128)(2,1)S(1)}, bf16[576,1152]{1,0:T(8,128)(2,1)}, u32[]{:S(2)}, u32[]{:S(2)}) collective-permute-start(bf16[576,1152]{1,0:T(8,128)(2,1)S(1)} %shard_map.75.b0), channel_id=1, source_target_pairs={{0,14},{1,3},{2,0},{3,5},{4,2},{5,7},{6,4},{7,9},{8,6},{9,11},{10,... | collective-permute-start | bytes 3981320 | tf_op jit(solution)/shard_map/ppermute | solution.py:319
  62.0 4.4 %collective-permute-start.2 = (bf16[576,1152]{1,0:T(8,128)(2,1)S(1)}, bf16[576,1152]{1,0:T(8,128)(2,1)}, u32[]{:S(2)}, u32[]{:S(2)}) collective-permute-start(bf16[576,1152]{1,0:T(8,128)(2,1)S(1)} %shard_map.75.b0), channel_id=1, source_target_pairs={{0,112},{1,17},{2,114},{3,19},{4,116},{5,21},{6,118},{7,23},{8,120... | collective-permute-start | bytes 3981320 | tf_op jit(solution)/shard_map/ppermute | solution.py:319
  66.4 3.1 %collective-permute-start.1 = (bf16[576,1152]{1,0:T(8,128)(2,1)S(1)}, bf16[576,1152]{1,0:T(8,128)(2,1)}, u32[]{:S(2)}, u32[]{:S(2)}) collective-permute-start(bf16[576,1152]{1,0:T(8,128)(2,1)S(1)} %shard_map.75.b0), channel_id=1, source_target_pairs={{0,384},{1,129},{2,386},{3,131},{4,388},{5,133},{6,390},{7,135},{8... | collective-permute-start | bytes 3981320 | tf_op jit(solution)/shard_map/ppermute | solution.py:319
  69.5 7.9 %all-to-all-start.1 = ((bf16[32,8,1152]{2,1,0:T(8,128)(2,1)}), bf16[32,8,1152]{2,1,0:T(8,128)(2,1)S(1)}, u32[]{:S(2)}, u32[]{:S(2)}) async-start(bf16[32,8,1152]{2,1,0:T(8,128)(2,1)} %bitcast.6), calls=%async_computation.1 | async-start | bytes 1179648 | tf_op jit(solution)/shard_map/all_to_all | solution.py:320
  77.4 0.2 copy.14.gains
  77.6 0.9 copy.15.gains
  78.5 1.4 collective-permute-done.3.b3
  79.9 3.3 %collective-permute-done.2.b2 = bf16[576,1152]{1,0:T(8,128)(2,1)} collective-permute-done((bf16[576,1152]{1,0:T(8,128)(2,1)S(1)}, bf16[576,1152]{1,0:T(8,128)(2,1)}, u32[]{:S(2)}, u32[]{:S(2)}) %collective-permute-start.2) | collective-permute-done | bytes 1327136 | tf_op jit(solution)/shard_map/ppermute | solution.py:319
  83.1 3.2 %collective-permute-done.1.b1 = bf16[576,1152]{1,0:T(8,128)(2,1)} collective-permute-done((bf16[576,1152]{1,0:T(8,128)(2,1)S(1)}, bf16[576,1152]{1,0:T(8,128)(2,1)}, u32[]{:S(2)}, u32[]{:S(2)}) %collective-permute-start.1) | collective-permute-done | bytes 1327136 | tf_op jit(solution)/shard_map/ppermute | solution.py:319
  86.4 3.9 %shard_map.76 = (bf16[144,512]{1,0:T(8,128)(2,1)S(1)}, bf16[288,512]{1,0:T(8,128)(2,1)}, bf16[576,1152]{1,0:T(8,128)(2,1)S(1)}) custom-call(s32[6]{0:T(128)S(1)} %pad_add_fusion.order, bf16[512,1152]{1,0:T(8,128)(2,1)S(1)} %copy-done.7, f32[2,288,1]{2,1,0:T(8,128)S(1)} %copy.14.gains, bf16[576,1152]{1,0:T(8,128)(2,1)} %copy-done.1, ...), custom_call_target="tpu_custom_call" | custom-call | bytes 1 | tf_op jit(solution)/shard_map/pallas_call | solution.py:263
  90.4 1.1 copy-done.4
  91.4 0.7 copy-done.13
  92.1 7.7 %collective-permute-start.4 = (bf16[288,512]{1,0:T(8,128)(2,1)}, bf16[288,512]{1,0:T(8,128)(2,1)}, u32[]{:S(2)}, u32[]{:S(2)}) collective-permute-start(bf16[288,512]{1,0:T(8,128)(2,1)} %get-tuple-element.17), channel_id=1, source_target_pairs={{0,64},{1,65},{2,66},{3,67},{4,68},{5,69},{6,70},{7,71},{8,72},{9,... | collective-permute-start | bytes 884744 | tf_op jit(solution)/shard_map/ppermute | solution.py:332
  99.8 3.4 %collective-permute-start.6 = (bf16[256,1152]{1,0:T(8,128)(2,1)S(1)}, bf16[256,1152]{1,0:T(8,128)(2,1)S(1)}, u32[]{:S(2)}, u32[]{:S(2)}) collective-permute-start(bf16[256,1152]{1,0:T(8,128)(2,1)S(1)} %bitcast.12), channel_id=1, source_target_pairs={{0,1},{1,0},{2,3},{3,2},{4,5},{5,4},{6,7},{7,6},{8,9},{9,8},{10,11... | collective-permute-start | bytes 1769480 | tf_op jit(solution)/shard_map/ppermute | solution.py:56
  103.2 1.9 %collective-permute-start.8 = (bf16[576,1152]{1,0:T(8,128)(2,1)}, bf16[576,1152]{1,0:T(8,128)(2,1)S(1)}, u32[]{:S(2)}, u32[]{:S(2)}) collective-permute-start(bf16[576,1152]{1,0:T(8,128)(2,1)} %copy-done.4), channel_id=1, source_target_pairs={{0,1},{1,0},{2,3},{3,2},{4,5},{5,4},{6,7},{7,6},{8,9},{9,8},{10,11... | collective-permute-start | bytes 3981320 | tf_op jit(solution)/shard_map/ppermute | solution.py:56
  105.2 1.3 copy-done.2
  106.5 1.3 copy-done.8
  107.8 1.0 copy-done.9
  108.7 6.7 %shard_map.77.space = bf16[288,512]{1,0:T(8,128)(2,1)S(1)} custom-call(s32[6]{0:T(128)S(1)} %pad_add_fusion.order, bf16[512,1152]{1,0:T(8,128)(2,1)S(1)} %copy-done.8, f32[4,144,1]{2,1,0:T(8,128)S(1)} %copy-done.9, bf16[576,1152]{1,0:T(8,128)(2,1)S(1)} %copy-done.2, bf16[576,1152]{1,0:T(8,128)(2,1)} %collective-permute-done.1.b1, ...), custom_call_target="tpu_custom_call" | custom-call | flops 16000000000 | bytes 1 | tf_op jit(solution)/shard_map/pallas_call | solution.py:263
  115.4 0.7 copy-done.10
  116.1 3.0 %collective-permute-start.5 = (bf16[288,512]{1,0:T(8,128)(2,1)}, bf16[288,512]{1,0:T(8,128)(2,1)}, u32[]{:S(2)}, u32[]{:S(2)}) collective-permute-start(bf16[288,512]{1,0:T(8,128)(2,1)} %collective-permute-done.4.kv_a), channel_id=1, source_target_pairs={{0,128},{1,129},{2,130},{3,131},{4,132},{5,133},{6,134},{7,135},{8... | collective-permute-start | bytes 884744 | tf_op jit(solution)/shard_map/ppermute | solution.py:333
  119.1 0.0 collective-permute-done.6.other
  119.1 0.8 shard_map.78.normed
  119.9 4.9 %shard_map.79 = bf16[32,16,144]{2,1,0:T(8,128)(2,1)} custom-call(s32[6]{0:T(128)S(1)} %pad_add_fusion.order, bf16[512,1152]{1,0:T(8,128)(2,1)S(1)} %shard_map.78.normed, f32[2,288,1]{2,1,0:T(8,128)S(1)} %copy.14.gains, bf16[576,1152]{1,0:T(8,128)(2,1)S(1)} %copy-done.3, bf16[576,1152]{1,0:T(8,128)(2,1)} %collective-permute-done.1.b1, ...), custom_call_target="tpu_custom_call" | custom-call | bytes 1 | tf_op jit(solution)/shard_map/pallas_call | solution.py:263
  124.8 10.5 %all-to-all-start.2 = ((bf16[32,16,144]{2,1,0:T(8,128)(2,1)}), bf16[32,16,144]{2,1,0:T(8,128)(2,1)S(1)}, u32[]{:S(2)}, u32[]{:S(2)}) async-start(bf16[32,16,144]{2,1,0:T(8,128)(2,1)} %shard_map.79), calls=%async_computation.2 | async-start | bytes 524288 | tf_op jit(solution)/shard_map/all_to_all | solution.py:349
  135.3 10.6 %all-to-all-done.2.timed = bf16[32,16,144]{2,1,0:T(8,128)(2,1)S(1)} async-done(((bf16[32,16,144]{2,1,0:T(8,128)(2,1)}), bf16[32,16,144]{2,1,0:T(8,128)(2,1)S(1)}, u32[]{:S(2)}, u32[]{:S(2)}) %all-to-all-start.2) | async-done | bytes 147488 | tf_op jit(solution)/shard_map/all_to_all | solution.py:349
  145.9 2.6 %shard_map.80 = (bf16[256,576]{1,0:T(8,128)(2,1)S(1)}, bf16[256,576]{1,0:T(8,128)(2,1)S(1)}) custom-call(s32[6]{0:T(128)S(1)} %pad_add_fusion.order, bf16[144,512]{1,0:T(8,128)(2,1)S(1)} %copy-done.14, bf16[288,512]{1,0:T(8,128)(2,1)} %collective-permute-done.4.kv_a, bf16[288,512]{1,0:T(8,128)(2,1)} %collective-permute-done.5.kv_b, ...), custom_call_target="tpu_custom_call" | custom-call | bytes 1 | tf_op jit(solution)/shard_map/pallas_call | solution.py:263
  148.5 4.2 %collective-permute-start.7 = (bf16[256,576]{1,0:T(8,128)(2,1)S(1)}, bf16[256,576]{1,0:T(8,128)(2,1)S(1)}, u32[]{:S(2)}, u32[]{:S(2)}) collective-permute-start(bf16[256,576]{1,0:T(8,128)(2,1)S(1)} %get-tuple-element.23), channel_id=1, source_target_pairs={{0,1},{1,0},{2,3},{3,2},{4,5},{5,4},{6,7},{7,6},{8,9},{9,8},{10,11... | collective-permute-start | bytes 884744 | tf_op jit(solution)/shard_map/ppermute | solution.py:56
  152.7 1.2 collective-permute-done.7.arrived
  154.0 3.2 %shard_map.81 = bf16[256,1152]{1,0:T(8,128)(2,1)} custom-call(s32[6]{0:T(128)S(1)} %pad_add_fusion.order, bf16[256,1152]{1,0:T(8,128)(2,1)} %bitcast.2.own.tokens, f32[1,1152]{1,0:T(1,128)S(1)} %constant_dynamic-slice_fusion.embed, bf16[256,576]{1,0:T(8,128)(2,1)S(1)} %get-tuple-element.22.own, bf16[256,576]{1,0:T(8,128)(2,1)S(1)} %collective-permute-done.7.arrived, ...), custom_call_target="tpu_custom_call" | custom-call | bytes 1 | tf_op jit(solution)/shard_map/pallas_call | solution.py:263
  (37 shorter events, 0.1 us)
Async XLA Ops:
  0.0 22.6 %copy-start = (f32[8,1152]{1,0:T(8,128)S(1)}, f32[8,1152]{1,0:T(8,128)}, u32[]{:S(2)}) copy-start(f32[8,1152]{1,0:T(8,128)} %param.8) | copy-start | bytes 110596
  0.1 0.9 copy-start.12
  1.0 0.8 copy-start.15
  4.2 18.0 %copy-start.16 = (f32[1152]{0:T(1024)S(1)}, f32[1152]{0:T(1024)}, u32[]{:S(2)}) copy-start(f32[1152]{0:T(1024)} %param.9) | copy-start | bytes 13828
  4.2 18.0 %copy-start.17 = (f32[1152]{0:T(1024)S(1)}, f32[1152]{0:T(1024)}, u32[]{:S(2)}) copy-start(f32[1152]{0:T(1024)} %param.10) | copy-start | bytes 13828
  4.2 18.1 %copy-start.18 = (f32[1152]{0:T(1024)S(1)}, f32[1152]{0:T(1024)}, u32[]{:S(2)}) copy-start(f32[1152]{0:T(1024)} %param.11) | copy-start | bytes 13828
  4.2 55.0 %all-to-all-start = ((bf16[64,96,128]{2,1,0:T(8,128)(2,1)}), bf16[64,96,128]{2,1,0:T(8,128)(2,1)S(1)}, u32[]{:S(2)}, u32[]{:S(2)}) async-start(bf16[64,96,128]{2,1,0:T(8,128)(2,1)} %shard_map.74), calls=%async_computation | async-start | bytes 3145728 | tf_op jit(solution)/shard_map/all_to_all | solution.py:313
  19.8 4.2 %collective-permute-start = (bf16[256,1152]{1,0:T(8,128)(2,1)}, bf16[256,1152]{1,0:T(8,128)(2,1)S(1)}, u32[]{:S(2)}, u32[]{:S(2)}) collective-permute-start(bf16[256,1152]{1,0:T(8,128)(2,1)} %bitcast.2.own.tokens), channel_id=1, source_target_pairs={{0,1},{1,0},{2,3},{3,2},{4,5},{5,4},{6,7},{7,6},{8,9},{9,8},{10,11... | collective-permute-start | bytes 1769480 | tf_op jit(solution)/shard_map/ppermute | solution.py:56
  25.8 1.0 copy-start.6
  59.7 26.7 %copy-start.1 = (bf16[576,1152]{1,0:T(8,128)(2,1)}, bf16[576,1152]{1,0:T(8,128)(2,1)S(1)}, u32[]{:S(2)}) copy-start(bf16[576,1152]{1,0:T(8,128)(2,1)S(1)} %shard_map.75.b0) | copy-start | bytes 3981316
  59.7 26.6 %copy-start.7 = (bf16[512,1152]{1,0:T(8,128)(2,1)S(1)}, bf16[512,1152]{1,0:T(8,128)(2,1)}, u32[]{:S(2)}) copy-start(bf16[512,1152]{1,0:T(8,128)(2,1)} %copy-done.6) | copy-start | bytes 3538948
  59.8 20.1 %collective-permute-start.3 = (bf16[576,1152]{1,0:T(8,128)(2,1)S(1)}, bf16[576,1152]{1,0:T(8,128)(2,1)}, u32[]{:S(2)}, u32[]{:S(2)}) collective-permute-start(bf16[576,1152]{1,0:T(8,128)(2,1)S(1)} %shard_map.75.b0), channel_id=1, source_target_pairs={{0,14},{1,3},{2,0},{3,5},{4,2},{5,7},{6,4},{7,9},{8,6},{9,11},{10,... | collective-permute-start | bytes 3981320 | tf_op jit(solution)/shard_map/ppermute | solution.py:319
  62.0 21.2 %collective-permute-start.2 = (bf16[576,1152]{1,0:T(8,128)(2,1)S(1)}, bf16[576,1152]{1,0:T(8,128)(2,1)}, u32[]{:S(2)}, u32[]{:S(2)}) collective-permute-start(bf16[576,1152]{1,0:T(8,128)(2,1)S(1)} %shard_map.75.b0), channel_id=1, source_target_pairs={{0,112},{1,17},{2,114},{3,19},{4,116},{5,21},{6,118},{7,23},{8,120... | collective-permute-start | bytes 3981320 | tf_op jit(solution)/shard_map/ppermute | solution.py:319
  66.4 20.0 %collective-permute-start.1 = (bf16[576,1152]{1,0:T(8,128)(2,1)S(1)}, bf16[576,1152]{1,0:T(8,128)(2,1)}, u32[]{:S(2)}, u32[]{:S(2)}) collective-permute-start(bf16[576,1152]{1,0:T(8,128)(2,1)S(1)} %shard_map.75.b0), channel_id=1, source_target_pairs={{0,384},{1,129},{2,386},{3,131},{4,388},{5,133},{6,390},{7,135},{8... | collective-permute-start | bytes 3981320 | tf_op jit(solution)/shard_map/ppermute | solution.py:319
  69.5 30.3 %all-to-all-start.1 = ((bf16[32,8,1152]{2,1,0:T(8,128)(2,1)}), bf16[32,8,1152]{2,1,0:T(8,128)(2,1)S(1)}, u32[]{:S(2)}, u32[]{:S(2)}) async-start(bf16[32,8,1152]{2,1,0:T(8,128)(2,1)} %bitcast.6), calls=%async_computation.1 | async-start | bytes 1179648 | tf_op jit(solution)/shard_map/all_to_all | solution.py:320
  90.3 1.1 copy-start.4
  91.4 0.7 copy-start.13
  92.1 24.0 %collective-permute-start.4 = (bf16[288,512]{1,0:T(8,128)(2,1)}, bf16[288,512]{1,0:T(8,128)(2,1)}, u32[]{:S(2)}, u32[]{:S(2)}) collective-permute-start(bf16[288,512]{1,0:T(8,128)(2,1)} %get-tuple-element.17), channel_id=1, source_target_pairs={{0,64},{1,65},{2,66},{3,67},{4,68},{5,69},{6,70},{7,71},{8,72},{9,... | collective-permute-start | bytes 884744 | tf_op jit(solution)/shard_map/ppermute | solution.py:332
  99.8 19.3 %collective-permute-start.6 = (bf16[256,1152]{1,0:T(8,128)(2,1)S(1)}, bf16[256,1152]{1,0:T(8,128)(2,1)S(1)}, u32[]{:S(2)}, u32[]{:S(2)}) collective-permute-start(bf16[256,1152]{1,0:T(8,128)(2,1)S(1)} %bitcast.12), channel_id=1, source_target_pairs={{0,1},{1,0},{2,3},{3,2},{4,5},{5,4},{6,7},{7,6},{8,9},{9,8},{10,11... | collective-permute-start | bytes 1769480 | tf_op jit(solution)/shard_map/ppermute | solution.py:56
  103.2 50.7 %collective-permute-start.8 = (bf16[576,1152]{1,0:T(8,128)(2,1)}, bf16[576,1152]{1,0:T(8,128)(2,1)S(1)}, u32[]{:S(2)}, u32[]{:S(2)}) collective-permute-start(bf16[576,1152]{1,0:T(8,128)(2,1)} %copy-done.4), channel_id=1, source_target_pairs={{0,1},{1,0},{2,3},{3,2},{4,5},{5,4},{6,7},{7,6},{8,9},{9,8},{10,11... | collective-permute-start | bytes 3981320 | tf_op jit(solution)/shard_map/ppermute | solution.py:56
  105.2 1.3 copy-start.2
  106.5 1.3 copy-start.8
  107.8 1.0 copy-start.9
  115.4 0.7 copy-start.10
  116.1 3.8 %copy-start.3 = (bf16[576,1152]{1,0:T(8,128)(2,1)S(1)}, bf16[576,1152]{1,0:T(8,128)(2,1)}, u32[]{:S(2)}) copy-start(bf16[576,1152]{1,0:T(8,128)(2,1)} %copy-done.1) | copy-start | bytes 3981316
  116.1 19.2 %collective-permute-start.5 = (bf16[288,512]{1,0:T(8,128)(2,1)}, bf16[288,512]{1,0:T(8,128)(2,1)}, u32[]{:S(2)}, u32[]{:S(2)}) collective-permute-start(bf16[288,512]{1,0:T(8,128)(2,1)} %collective-permute-done.4.kv_a), channel_id=1, source_target_pairs={{0,128},{1,129},{2,130},{3,131},{4,132},{5,133},{6,134},{7,135},{8... | collective-permute-start | bytes 884744 | tf_op jit(solution)/shard_map/ppermute | solution.py:333
  119.9 26.0 %copy-start.11 = (bf16[288,512]{1,0:T(8,128)(2,1)S(1)}, bf16[288,512]{1,0:T(8,128)(2,1)}, u32[]{:S(2)}) copy-start(bf16[288,512]{1,0:T(8,128)(2,1)} %copy-done.10) | copy-start | bytes 884740
  119.9 26.0 %copy-start.14 = (bf16[144,512]{1,0:T(8,128)(2,1)S(1)}, bf16[144,512]{1,0:T(8,128)(2,1)}, u32[]{:S(2)}) copy-start(bf16[144,512]{1,0:T(8,128)(2,1)} %copy-done.13) | copy-start | bytes 442372
  124.8 29.2 %copy-start.5 = (bf16[576,1152]{1,0:T(8,128)(2,1)S(1)}, bf16[576,1152]{1,0:T(8,128)(2,1)}, u32[]{:S(2)}) copy-start(bf16[576,1152]{1,0:T(8,128)(2,1)} %copy-done.4) | copy-start | bytes 3981316
  124.8 21.1 %all-to-all-start.2 = ((bf16[32,16,144]{2,1,0:T(8,128)(2,1)}), bf16[32,16,144]{2,1,0:T(8,128)(2,1)S(1)}, u32[]{:S(2)}, u32[]{:S(2)}) async-start(bf16[32,16,144]{2,1,0:T(8,128)(2,1)} %shard_map.79), calls=%async_computation.2 | async-start | bytes 524288 | tf_op jit(solution)/shard_map/all_to_all | solution.py:349
  148.5 5.5 %collective-permute-start.7 = (bf16[256,576]{1,0:T(8,128)(2,1)S(1)}, bf16[256,576]{1,0:T(8,128)(2,1)S(1)}, u32[]{:S(2)}, u32[]{:S(2)}) collective-permute-start(bf16[256,576]{1,0:T(8,128)(2,1)S(1)} %get-tuple-element.23), channel_id=1, source_target_pairs={{0,1},{1,0},{2,3},{3,2},{4,5},{5,4},{6,7},{7,6},{8,9},{9,8},{10,11... | collective-permute-start | bytes 884744 | tf_op jit(solution)/shard_map/ppermute | solution.py:56

commit v5 on v4

--- a/solution.py
+++ b/solution.py
@@ -23,7 +23,7 @@
 SCALE = 1.4426950408889634 / HD**0.5
 F32 = jnp.float32
 BF16 = jnp.bfloat16
-VMEM_LIMIT = 50 * 1024 * 1024
+VMEM_LIMIT = 18 * 1024 * 1024
 
 
 def route(move):
@@ -122,12 +122,22 @@
     block[512:] = wide[4].T[:64].astype(BF16)
 
 
-def norm_kernel(own, other, embed, gain, out):
+def normalise(ref, embed, gain):
+    hidden = ref[...].astype(F32) + embed[...]
+    centred = hidden - jnp.mean(hidden, -1, keepdims=True)
+    variance = jnp.mean(centred * centred, -1, keepdims=True)
+    return (centred * lax.rsqrt(variance + 1e-06) * gain[...]).astype(BF16)
+
+
+def norm_kernel(own, other, embed, gain, out, rows, sem):
+    copies = []
     for i, ref in enumerate((own, other)):
-        hidden = ref[...].astype(F32) + embed[...]
-        centred = hidden - jnp.mean(hidden, -1, keepdims=True)
-        variance = jnp.mean(centred * centred, -1, keepdims=True)
-        out[i * HALF : (i + 1) * HALF] = (centred * lax.rsqrt(variance + 1e-06) * gain[...]).astype(BF16)
+        part = pl.ds(i * HALF, HALF)
+        rows[part] = normalise(ref, embed, gain)
+        copies.append(pltpu.make_async_copy(rows.at[part], out.at[part], sem.at[i]))
+        copies[-1].start()
+    for copy in copies:
+        copy.wait()
 
 
 def start_fetch(order, blocks, group, slot, sem):
@@ -165,32 +175,40 @@
     return head_norm(projected[: 2 * PAIR], gains), projected[2 * PAIR :]
 
 
-def fetch_all(order, blocks, groups, weight, sem):
-    for slot, group in enumerate(groups):
-        start_fetch(order, blocks, group, weight.at[slot], sem.at[slot])
-    for slot in range(len(groups)):
-        wait_fetch(blocks, weight.at[slot], sem.at[slot])
-
-
-def cross_project_kernel(order, normed, gains, b0, b1, b2, b3, q_t, kv_t, w_out, weight, sem):
+def cross_project_kernel(order, gains, normed_hbm, b0, b1, b2, b3, q_out, kv_out, w_out, normed, q_t, kv_t, weight, sem):
     blocks = (b0, b1, b2, b3)
-    parts = [block.at[pl.ds(0, PAIR)] for block in blocks]
+    load = pltpu.make_async_copy(normed_hbm, normed, sem.at[6])
+    load.start()
     for group in range(2):
         start_fetch(order, blocks, group, weight.at[group], sem.at[group])
+    parts = [block.at[pl.ds(0, PAIR)] for block in blocks]
     for group in range(4):
         start_fetch(order, parts, group, w_out.at[pl.ds(group * PAIR, PAIR)], sem.at[2 + group])
+    load.wait()
     for group in range(2):
         wait_fetch(blocks, weight.at[group], sem.at[group])
-    qk, v = project_pair(normed, weight, gains[0])
+    qk, v = project_pair(normed, weight, gains[...].T[:, :1])
+    kv_t[...] = jnp.concatenate([qk[PAIR:], v], 0).astype(BF16)
+    kv_store = pltpu.make_async_copy(kv_t, kv_out, sem.at[7])
+    kv_store.start()
     q_t[...] = qk[:PAIR].astype(BF16)
-    kv_t[...] = jnp.concatenate([qk[PAIR:], v], 0).astype(BF16)
+    q_store = pltpu.make_async_copy(q_t, q_out, sem.at[8])
+    q_store.start()
     for group in range(4):
         wait_fetch(parts, w_out.at[pl.ds(group * PAIR, PAIR)], sem.at[2 + group])
-
-
-def time_kernel(order, normed, gains, b0, b1, b2, b3, out, weight, sem):
-    fetch_all(order, (b0, b1, b2, b3), (2, 3), weight, sem)
-    qk, v = project_pair(normed, weight, gains[1])
+    kv_store.wait()
+    q_store.wait()
+
+
+def time_kernel(order, gains, own, other, embed, gain, b0, b1, b2, b3, out, normed, result, weight, sem):
+    blocks = (b0, b1, b2, b3)
+    for slot in range(2):
+        start_fetch(order, blocks, 2 + slot, weight.at[slot], sem.at[slot])
+    normed[:HALF] = normalise(own, embed, gain)
+    normed[HALF:] = normalise(other, embed, gain)
+    for slot in range(2):
+        wait_fetch(blocks, weight.at[slot], sem.at[slot])
+    qk, v = project_pair(normed, weight, gains[...].T[:, 1:2])
     row = lax.broadcasted_iota(jnp.int32, (HALF, HALF), 0) % 8
     col = lax.broadcasted_iota(jnp.int32, (HALF, HALF), 1) % 8
     sets = []
@@ -205,17 +223,30 @@
     swap = order[4] == 1
     one = jnp.where(swap, sets[1], sets[0])
     two = jnp.where(swap, sets[0], sets[1])
-    out[...] = jnp.concatenate([one, two], 1).astype(BF16)
-
-
-def space_kernel(order, normed, gains, b0, b1, b2, b3, out, weight, sem):
-    fetch_all(order, (b0, b1, b2, b3), range(4), weight, sem)
+    result[...] = jnp.concatenate([one, two], 1).astype(BF16)
+    store = pltpu.make_async_copy(result, out, sem.at[2])
+    store.start()
+    store.wait()
+
+
+def space_kernel(order, gains, normed_hbm, b0, b1, b2, b3, out, normed, result, weight, sem):
+    blocks = (b0, b1, b2, b3)
+    load = pltpu.make_async_copy(normed_hbm, normed, sem.at[4])
+    load.start()
+    for group in range(4):
+        start_fetch(order, blocks, group, weight.at[group], sem.at[group])
+    load.wait()
     heads = []
+    columns = gains[...].T[:PAIR]
     for group in range(4):
+        wait_fetch(blocks, weight.at[group], sem.at[group])
         projected = mm_t(weight[group, PAIR:SECOND], normed[...])
-        qk = head_norm(projected[:PAIR], gains[group])
+        qk = head_norm(projected[:PAIR], columns[:, 2 + group : 3 + group])
         heads.append(attend(qk[:HD], [(qk[HD:], projected[PAIR:])]))
-    out[...] = jnp.concatenate(heads, 0).astype(BF16)
+    result[...] = jnp.concatenate(heads, 0).astype(BF16)
+    store = pltpu.make_async_copy(result, out, sem.at[5])
+    store.start()
+    store.wait()
 
 
 def cross_kernel(order, q_t, kv_a, kv_b, space, timed, keep, give):
@@ -234,7 +265,10 @@
     give[...] = jnp.concatenate([mixed[HALF:], jnp.where(swap, late[0], late[1])], 1).astype(BF16)
 
 
-def out_kernel(order, tokens, embed, own, arrived, w_own, w_other, out):
+def out_kernel(order, tokens, embed, own, arrived, w_own, w_other, out, weight, sem):
+    loads = [pltpu.make_async_copy(ref, weight.at[i], sem.at[i]) for i, ref in enumerate((w_own, w_other))]
+    for load in loads:
+        load.start()
     swap = order[4] == 1
     mine, theirs = own[...].astype(F32), arrived[...].astype(F32)
     first = jnp.where(swap, theirs, mine)
@@ -243,15 +277,17 @@
     for start, end in ((0, 2 * PAIR), (2 * PAIR, 3 * PAIR), (3 * PAIR, 4 * PAIR)):
         parts += [first[:, start:end], second[:, start:end]]
     mixed = jnp.concatenate(parts, 1).astype(BF16)
-    one, two = mm_t(mixed, w_own[...]), mm_t(mixed, w_other[...])
+    for load in loads:
+        load.wait()
+    one, two = mm_t(mixed, weight[0]), mm_t(mixed, weight[1])
     update = jnp.concatenate([jnp.where(swap, two, one), jnp.where(swap, one, two)], 1)
     out[...] = (tokens[...].astype(F32) + embed[...] + update).astype(BF16)
 
 
-def call(kernel, out_shapes, args, scratch=(), flops=0, anys=0, out_any=False):
+def call(kernel, out_shapes, args, scratch=(), flops=0, anys=0, out_any=False, room=VMEM_LIMIT):
     smem = pl.BlockSpec(memory_space=pltpu.SMEM)
     vmem = pl.BlockSpec(memory_space=pltpu.VMEM)
-    hbm = pl.BlockSpec(memory_space=pl.ANY)
+    hbm = pl.BlockSpec(memory_space=pltpu.HBM)
     specs = []
     for i, arg in enumerate(args):
         if arg.dtype == jnp.int32:
@@ -260,19 +296,28 @@
             specs.append(hbm if i >= len(args) - anys else vmem)
     moved = sum(a.size * a.dtype.itemsize for a in args)
     single = not isinstance(out_shapes, tuple)
+    place = hbm if out_any else vmem
     return pl.pallas_call(
         kernel,
         out_shape=out_shapes,
         in_specs=specs,
-        out_specs=hbm if out_any else vmem if single else (vmem,) * len(out_shapes),
+        out_specs=place if single else (place,) * len(out_shapes),
         scratch_shapes=list(scratch),
-        compiler_params=pltpu.CompilerParams(vmem_limit_bytes=VMEM_LIMIT),
+        compiler_params=pltpu.CompilerParams(vmem_limit_bytes=room),
         cost_estimate=pl.CostEstimate(flops=flops, bytes_accessed=1, transcendentals=0),
     )(*args)
 
 
 def shape(*dims):
     return jax.ShapeDtypeStruct(dims, BF16)
+
+
+def far(*dims):
+    return pltpu.HBM(dims, BF16)
+
+
+def stay(array):
+    return pltpu.with_memory_space_constraint(array, pltpu.HBM)
 
 
 def local(frames_in, cam_embed, norm_gain, q_gain, k_gain, w_qkv, w_out):
@@ -291,12 +336,13 @@
         return lax.dynamic_slice_in_dim(both, head, count, 0)
 
     pair_gains = jnp.stack([gains_of(8 + 2 * core, 2), gains_of(12 + 2 * core, 2)])
-    pair_gains = pair_gains.transpose(0, 2, 1, 3).reshape(2, 2 * PAIR, 1)
-    space_gains = gains_of(4 * core, 4).reshape(4, PAIR, 1)
+    pair_gains = pair_gains.transpose(0, 2, 1, 3).reshape(2, 2 * PAIR)
+    space_gains = gains_of(4 * core, 4).reshape(4, PAIR)
+    gains = jnp.concatenate([pair_gains, jnp.pad(space_gains, ((0, 2), (0, PAIR)))], 0)
 
     pieces = call(
         pack_kernel,
-        shape(64, PIECE, 128),
+        far(64, PIECE, 128),
         (order, w_qkv, w_out),
         [
             pltpu.VMEM((18, 3 * D), BF16),
@@ -309,42 +355,64 @@
         0,
         2,
         True,
+        60 * 1024 * 1024,
     )
     got = lax.all_to_all(pieces, SLAB, 0, 0, tiled=True)
     other = swap_core(tokens)
-    normed = call(norm_kernel, shape(ROWS, D), (tokens, other, embed, gain), (), 8 * 10**9)
+    normed = call(
+        norm_kernel,
+        far(ROWS, D),
+        (tokens, other, embed, gain),
+        [pltpu.VMEM((ROWS, D), BF16), pltpu.SemaphoreType.DMA((2,))],
+        8 * 10**9,
+        0,
+        True,
+    )
     block = call(
-        unpack_kernel, shape(SECOND + FIRST, D), (after(got, normed, pair_gains, space_gains),), [pltpu.VMEM((5, D, 128), F32)]
+        unpack_kernel, shape(SECOND + FIRST, D), (after(got, normed, gains),), [pltpu.VMEM((5, D, 128), F32)]
     )
     blocks = (block,) + tuple(lax.ppermute(block, EVERY, r) for r in ROUTES)
     time_own = lax.all_to_all(after(tokens, block).reshape(32, 8, D), CHIP, 0, 0, tiled=True).reshape(HALF, D)
 
-    two = pltpu.VMEM((2, SECOND + FIRST, D), BF16)
-    four = [pltpu.VMEM((4, SECOND + FIRST, D), BF16), pltpu.SemaphoreType.DMA((4,))]
+    frame = pltpu.VMEM((ROWS, D), BF16)
+    two, four = (pltpu.VMEM((n, SECOND + FIRST, D), BF16) for n in (2, 4))
     q_t, kv_t, w_own = call(
         cross_project_kernel,
-        (shape(PAIR, ROWS), shape(2 * PAIR, ROWS), shape(4 * PAIR, D)),
-        (order, normed, pair_gains) + blocks,
-        [two, pltpu.SemaphoreType.DMA((6,))],
+        (far(PAIR, ROWS), far(2 * PAIR, ROWS), far(4 * PAIR, D)),
+        (order, gains, stay(normed)) + blocks,
+        [
+            frame,
+            pltpu.VMEM((PAIR, ROWS), BF16),
+            pltpu.VMEM((2 * PAIR, ROWS), BF16),
+            two,
+            pltpu.SemaphoreType.DMA((9,)),
+        ],
+        0,
+        5,
+        True,
+    )
+    kv_a = lax.ppermute(kv_t, EVERY, ACROSS)
+    w_other = swap_core(w_own)
+    time_own = after(time_own, kv_t)
+    time_other = swap_core(time_own)
+    timed = call(
+        time_kernel,
+        far(32, 16, PAIR),
+        (order, gains, time_own, time_other, embed, gain) + blocks,
+        [frame, pltpu.VMEM((32, 16, PAIR), BF16), two, pltpu.SemaphoreType.DMA((3,))],
         0,
         4,
-    )
-    kv_a = lax.ppermute(kv_t, EVERY, ACROSS)
-    kv_b = lax.ppermute(kv_a, EVERY, ALONG)
-    w_other = swap_core(w_own)
+        True,
+    )
+    kv_b = lax.ppermute(after(kv_a, timed), EVERY, ALONG)
     space = call(
-        space_kernel, shape(2 * PAIR, ROWS), (order, after(normed, kv_t), space_gains) + blocks, four, 16 * 10**9, 4
-    )
-    time_own = after(time_own, kv_t)
-    time_other = swap_core(time_own)
-    time_normed = call(norm_kernel, shape(ROWS, D), (time_own, time_other, embed, gain), (), 8 * 10**9)
-    timed = call(
-        time_kernel,
-        shape(32, 16, PAIR),
-        (order, after(time_normed, space), pair_gains) + blocks,
-        [two, pltpu.SemaphoreType.DMA((2,))],
-        0,
-        4,
+        space_kernel,
+        far(2 * PAIR, ROWS),
+        (order, gains, stay(after(normed, timed))) + blocks,
+        [frame, pltpu.VMEM((2 * PAIR, ROWS), BF16), four, pltpu.SemaphoreType.DMA((6,))],
+        16 * 10**9,
+        5,
+        True,
     )
     returned = lax.all_to_all(timed, CHIP, 0, 0, tiled=True)
     keep, give = call(
@@ -352,7 +420,12 @@
     )
     arrived = swap_core(give)
     return call(
-        out_kernel, shape(HALF, D), (order, tokens, embed, keep, arrived, w_own, w_other)
+        out_kernel,
+        shape(HALF, D),
+        (order, tokens, embed, keep, arrived, w_own, w_other),
+        [pltpu.VMEM((2, 4 * PAIR, D), BF16), pltpu.SemaphoreType.DMA((2,))],
+        0,
+        2,
     )[None]
 
 

time: 158 us -> 163 us (1.032)
  Pallas kernels: 26.8 us -> 47.7 us
  waiting for transfers between devices: 53.4 us -> 44.9 us
  local copies, waits for them, and re-layouts: 10.2 us -> 3.36 us
    pallas_call x9 -> x8, Pallas kernels: 26.8 us -> 47.7 us  [call(): pl.pallas_call(kernel, out_shape=out_shapes, in_specs=specs, out_specs=pl...]
    all_to_all x1, waiting for transfers between devices: 10.6 us -> 0.15 us  [local(): returned = lax.all_to_all(timed, CHIP, 0, 0, tiled=True)]
    unnamed x38 -> x16, local copies, waits for them, and re-layouts: 8.77 us -> 2.99 us
    ppermute x1, starting transfers between devices: 7.7 us -> 4.51 us  [local(): kv_a = lax.ppermute(kv_t, EVERY, ACROSS)]
    ppermute x4, starting transfers between devices: 11.9 us -> 14.1 us  [swap_core(): return lax.ppermute(block, 'core', [(0, 1), (1, 0)])]
  transfers between devices with their start and end apart: 12 -> 12, of which waited for: 7 -> 8; matrix products, arithmetic and copies ran while one was open for 1% -> 0% of each run, Pallas kernels for 13% -> 24%
where the time goes in v5:
time: 163 us; the launch traced here: 162 us
  starting transfers between devices  65.1 us (40%)
  Pallas kernels  47.7 us (29%)
  waiting for transfers between devices  44.9 us (28%)
  local copies, waits for them, and re-layouts  3.36 us (2%)
    pallas_call x8, Pallas kernels, call(): pl.pallas_call(kernel, out_shape=out_shapes, in_specs=specs, out_specs=pl...  47.7 us
    all_to_all x1, waiting for transfers between devices, local(): got = lax.all_to_all(pieces, SLAB, 0, 0, tiled=True)  32.4 us
    all_to_all x1, starting transfers between devices, local(): got = lax.all_to_all(pieces, SLAB, 0, 0, tiled=True)  15.6 us
    ppermute x4, starting transfers between devices, swap_core(): return lax.ppermute(block, 'core', [(0, 1), (1, 0)])  14.1 us
    all_to_all x1, starting transfers between devices, local(): returned = lax.all_to_all(timed, CHIP, 0, 0, tiled=True)  9.77 us
    ppermute x3, starting transfers between devices, local(): blocks = (block,) + tuple((lax.ppermute(block, EVERY, r) for r in ROUTES))  9.43 us
    ppermute x3, waiting for transfers between devices, local(): blocks = (block,) + tuple((lax.ppermute(block, EVERY, r) for r in ROUTES))  8.97 us
    all_to_all x1, starting transfers between devices, local(): lax.all_to_all(after(tokens, block).reshape(32, 8, D), CHIP, 0, 0, tiled=...  7.93 us
  transfers between devices with their start and end apart: 12, of which 8 were waited for; matrix products, arithmetic and copies ran while one was open for 0% of the time, Pallas kernels for 24%

profile of v5, /device:TPU:1, one launch (start us, length us, event | category | flops | bytes accessed | tf_op | source)
XLA Modules:
  0.0 162.1 jit_solution(3376973567061571830)
XLA Ops:
  0.0 0.0 copy-start
  0.0 0.7 pad_add_fusion.order
  0.7 3.1 %shard_map.74 = bf16[64,96,128]{2,1,0:T(8,128)(2,1)} custom-call(s32[6]{0:T(128)} %pad_add_fusion.order, bf16[18,3456]{1,0:T(8,128)(2,1)} %w_qkv_hbm.1, bf16[18,1152]{1,0:T(8,128)(2,1)} %w_out_hbm.1), custom_call_target="tpu_custom_call" | custom-call | bytes 1 | tf_op jit(solution)/shard_map/pallas_call | solution.py:300
  3.8 0.0 copy-start.5
  3.8 0.0 copy-start.6
  3.8 0.0 copy-start.7
  3.8 15.6 %all-to-all-start = ((bf16[64,96,128]{2,1,0:T(8,128)(2,1)}), bf16[64,96,128]{2,1,0:T(8,128)(2,1)S(1)}, u32[]{:S(2)}, u32[]{:S(2)}) async-start(bf16[64,96,128]{2,1,0:T(8,128)(2,1)} %shard_map.74), calls=%async_computation | async-start | bytes 3145728 | tf_op jit(solution)/shard_map/all_to_all | solution.py:360
  19.4 2.4 %collective-permute-start = (bf16[256,1152]{1,0:T(8,128)(2,1)}, bf16[256,1152]{1,0:T(8,128)(2,1)S(1)}, u32[]{:S(2)}, u32[]{:S(2)}) collective-permute-start(bf16[256,1152]{1,0:T(8,128)(2,1)} %bitcast.2.own.tokens), channel_id=1, source_target_pairs={{0,1},{1,0},{2,3},{3,2},{4,5},{5,4},{6,7},{7,6},{8,9},{9,8},{10,11... | collective-permute-start | bytes 1769480 | tf_op jit(solution)/shard_map/ppermute | solution.py:56
  21.7 0.0 copy-done.5
  21.8 0.1 stack_reshape.6
  21.8 0.0 copy-done.6
  21.9 0.1 stack_reshape.7
  22.0 0.0 copy-done.7
  22.0 0.1 reshape.13
  22.1 0.1 reshape.12
  22.2 0.0 copy-done
  22.3 1.3 collective-permute-done.other
  23.6 2.8 %shard_map.73.normed_hbm = bf16[512,1152]{1,0:T(8,128)(2,1)} custom-call(bf16[256,1152]{1,0:T(8,128)(2,1)} %bitcast.2.own.tokens, bf16[256,1152]{1,0:T(8,128)(2,1)S(1)} %collective-permute-done.other, f32[1,1152]{1,0:T(1,128)S(1)} %constant_dynamic-slice_fusion.embed, f32[1,1152]{1,0:T(1,128)S(1)} %broadcast_in_dim.14.gain), custom_call_target="tpu_custom_call" | custom-call | flops 8000000000 | bytes 1 | tf_op jit(solution)/shard_map/pallas_call | solution.py:300
  26.3 32.4 %all-to-all-done.got = bf16[64,96,128]{2,1,0:T(8,128)(2,1)S(1)} async-done(((bf16[64,96,128]{2,1,0:T(8,128)(2,1)}), bf16[64,96,128]{2,1,0:T(8,128)(2,1)S(1)}, u32[]{:S(2)}, u32[]{:S(2)}) %all-to-all-start) | async-done | bytes 1572896 | tf_op jit(solution)/shard_map/all_to_all | solution.py:360
  58.8 0.6 shard_map.75.b0
  59.4 1.9 %collective-permute-start.3 = (bf16[576,1152]{1,0:T(8,128)(2,1)S(1)}, bf16[576,1152]{1,0:T(8,128)(2,1)S(1)}, u32[]{:S(2)}, u32[]{:S(2)}) collective-permute-start(bf16[576,1152]{1,0:T(8,128)(2,1)S(1)} %shard_map.75.b0), channel_id=1, source_target_pairs={{0,14},{1,3},{2,0},{3,5},{4,2},{5,7},{6,4},{7,9},{8,6},{9,11},{10,... | collective-permute-start | bytes 3981320 | tf_op jit(solution)/shard_map/ppermute | solution.py:374
  61.3 4.4 %collective-permute-start.2 = (bf16[576,1152]{1,0:T(8,128)(2,1)S(1)}, bf16[576,1152]{1,0:T(8,128)(2,1)}, u32[]{:S(2)}, u32[]{:S(2)}) collective-permute-start(bf16[576,1152]{1,0:T(8,128)(2,1)S(1)} %shard_map.75.b0), channel_id=1, source_target_pairs={{0,112},{1,17},{2,114},{3,19},{4,116},{5,21},{6,118},{7,23},{8,120... | collective-permute-start | bytes 3981320 | tf_op jit(solution)/shard_map/ppermute | solution.py:374
  65.7 3.1 %collective-permute-start.1 = (bf16[576,1152]{1,0:T(8,128)(2,1)S(1)}, bf16[576,1152]{1,0:T(8,128)(2,1)}, u32[]{:S(2)}, u32[]{:S(2)}) collective-permute-start(bf16[576,1152]{1,0:T(8,128)(2,1)S(1)} %shard_map.75.b0), channel_id=1, source_target_pairs={{0,384},{1,129},{2,386},{3,131},{4,388},{5,133},{6,390},{7,135},{8... | collective-permute-start | bytes 3981320 | tf_op jit(solution)/shard_map/ppermute | solution.py:374
  68.8 7.9 %all-to-all-start.1 = ((bf16[32,8,1152]{2,1,0:T(8,128)(2,1)}), bf16[32,8,1152]{2,1,0:T(8,128)(2,1)S(1)}, u32[]{:S(2)}, u32[]{:S(2)}) async-start(bf16[32,8,1152]{2,1,0:T(8,128)(2,1)} %bitcast.6), calls=%async_computation.1 | async-start | bytes 1179648 | tf_op jit(solution)/shard_map/all_to_all | solution.py:375
  76.7 2.3 %collective-permute-done.3.b3 = bf16[576,1152]{1,0:T(8,128)(2,1)S(1)} collective-permute-done((bf16[576,1152]{1,0:T(8,128)(2,1)S(1)}, bf16[576,1152]{1,0:T(8,128)(2,1)S(1)}, u32[]{:S(2)}, u32[]{:S(2)}) %collective-permute-start.3) | collective-permute-done | bytes 1327136 | tf_op jit(solution)/shard_map/ppermute | solution.py:374
  79.1 3.4 %collective-permute-done.2.b2 = bf16[576,1152]{1,0:T(8,128)(2,1)} collective-permute-done((bf16[576,1152]{1,0:T(8,128)(2,1)S(1)}, bf16[576,1152]{1,0:T(8,128)(2,1)}, u32[]{:S(2)}, u32[]{:S(2)}) %collective-permute-start.2) | collective-permute-done | bytes 1327136 | tf_op jit(solution)/shard_map/ppermute | solution.py:374
  82.5 3.2 %collective-permute-done.1.b1 = bf16[576,1152]{1,0:T(8,128)(2,1)} collective-permute-done((bf16[576,1152]{1,0:T(8,128)(2,1)S(1)}, bf16[576,1152]{1,0:T(8,128)(2,1)}, u32[]{:S(2)}, u32[]{:S(2)}) %collective-permute-start.1) | collective-permute-done | bytes 1327136 | tf_op jit(solution)/shard_map/ppermute | solution.py:374
  85.7 0.7 copy-done.4
  86.4 22.1 %shard_map.76 = (bf16[144,512]{1,0:T(8,128)(2,1)}, bf16[288,512]{1,0:T(8,128)(2,1)}, bf16[576,1152]{1,0:T(8,128)(2,1)}) custom-call(s32[6]{0:T(128)S(1)} %copy-done.4, f32[8,288]{1,0:T(8,128)S(1)} %select_maximum_fusion.gains, bf16[512,1152]{1,0:T(8,128)(2,1)} %shard_map.73.normed_hbm, bf16[576,1152]{1,0:T(8,128)(2,1)S(1)} %shard_map.75.b0, ...), custom_call_target="tpu_custom_call" | custom-call | bytes 1 | tf_op jit(solution)/shard_map/pallas_call | solution.py:300
  108.5 0.0 all-to-all-done.1
  108.5 6.2 %collective-permute-start.5 = (bf16[256,1152]{1,0:T(8,128)(2,1)S(1)}, bf16[256,1152]{1,0:T(8,128)(2,1)S(1)}, u32[]{:S(2)}, u32[]{:S(2)}) collective-permute-start(bf16[256,1152]{1,0:T(8,128)(2,1)S(1)} %bitcast.12), channel_id=1, source_target_pairs={{0,1},{1,0},{2,3},{3,2},{4,5},{5,4},{6,7},{7,6},{8,9},{9,8},{10,11... | collective-permute-start | bytes 1769480 | tf_op jit(solution)/shard_map/ppermute | solution.py:56
  114.7 4.5 %collective-permute-start.4 = (bf16[288,512]{1,0:T(8,128)(2,1)}, bf16[288,512]{1,0:T(8,128)(2,1)}, u32[]{:S(2)}, u32[]{:S(2)}) collective-permute-start(bf16[288,512]{1,0:T(8,128)(2,1)} %get-tuple-element.17), channel_id=1, source_target_pairs={{0,64},{1,65},{2,66},{3,67},{4,68},{5,69},{6,70},{7,71},{8,72},{9,... | collective-permute-start | bytes 884744 | tf_op jit(solution)/shard_map/ppermute | solution.py:394
  119.3 2.2 %collective-permute-start.8 = (bf16[576,1152]{1,0:T(8,128)(2,1)}, bf16[576,1152]{1,0:T(8,128)(2,1)}, u32[]{:S(2)}, u32[]{:S(2)}) collective-permute-start(bf16[576,1152]{1,0:T(8,128)(2,1)} %get-tuple-element.24.w_own), channel_id=1, source_target_pairs={{0,1},{1,0},{2,3},{3,2},{4,5},{5,4},{6,7},{7,6},{8,9},{9,8},{10,11... | collective-permute-start | bytes 3981320 | tf_op jit(solution)/shard_map/ppermute | solution.py:56
  121.5 0.0 collective-permute-done.5.other
  121.5 4.9 %shard_map.77 = bf16[32,16,144]{2,1,0:T(8,128)(2,1)} custom-call(s32[6]{0:T(128)S(1)} %copy-done.4, f32[8,288]{1,0:T(8,128)S(1)} %select_maximum_fusion.gains, bf16[256,1152]{1,0:T(8,128)(2,1)S(1)} %bitcast.13, bf16[256,1152]{1,0:T(8,128)(2,1)S(1)} %collective-permute-done.5.other, f32[1,1152]{1,0:T(1,128)S(1)} %constant_dynamic-slice_fusion.embed, ...), custom_call_target="tpu_custom_call" | custom-call | bytes 1 | tf_op jit(solution)/shard_map/pallas_call | solution.py:300
  126.4 9.8 %all-to-all-start.2 = ((bf16[32,16,144]{2,1,0:T(8,128)(2,1)}), bf16[32,16,144]{2,1,0:T(8,128)(2,1)S(1)}, u32[]{:S(2)}, u32[]{:S(2)}) async-start(bf16[32,16,144]{2,1,0:T(8,128)(2,1)} %shard_map.77), calls=%async_computation.2 | async-start | bytes 524288 | tf_op jit(solution)/shard_map/all_to_all | solution.py:417
  136.2 0.0 collective-permute-done.4.kv_a
  136.2 3.8 %collective-permute-start.6 = (bf16[288,512]{1,0:T(8,128)(2,1)}, bf16[288,512]{1,0:T(8,128)(2,1)S(1)}, u32[]{:S(2)}, u32[]{:S(2)}) collective-permute-start(bf16[288,512]{1,0:T(8,128)(2,1)} %collective-permute-done.4.kv_a), channel_id=1, source_target_pairs={{0,128},{1,129},{2,130},{3,131},{4,132},{5,133},{6,134},{7,135},{8... | collective-permute-start | bytes 884744 | tf_op jit(solution)/shard_map/ppermute | solution.py:407
  140.0 7.0 %shard_map.78.space = bf16[288,512]{1,0:T(8,128)(2,1)} custom-call(s32[6]{0:T(128)S(1)} %copy-done.4, f32[8,288]{1,0:T(8,128)S(1)} %select_maximum_fusion.gains, bf16[512,1152]{1,0:T(8,128)(2,1)} %shard_map.73.normed_hbm, bf16[576,1152]{1,0:T(8,128)(2,1)S(1)} %shard_map.75.b0, bf16[576,1152]{1,0:T(8,128)(2,1)} %collective-permute-done.1.b1, ...), custom_call_target="tpu_custom_call" | custom-call | flops 16000000000 | bytes 1 | tf_op jit(solution)/shard_map/pallas_call | solution.py:300
  147.0 0.2 all-to-all-done.2.timed
  147.1 0.8 collective-permute-done.6.kv_b
  147.9 1.0 copy-done.2
  148.9 2.5 %shard_map.79 = (bf16[256,576]{1,0:T(8,128)(2,1)S(1)}, bf16[256,576]{1,0:T(8,128)(2,1)S(1)}) custom-call(s32[6]{0:T(128)S(1)} %copy-done.4, bf16[144,512]{1,0:T(8,128)(2,1)S(1)} %copy-done.3, bf16[288,512]{1,0:T(8,128)(2,1)} %collective-permute-done.4.kv_a, bf16[288,512]{1,0:T(8,128)(2,1)S(1)} %collective-permute-done.6.kv_b, ...), custom_call_target="tpu_custom_call" | custom-call | bytes 1 | tf_op jit(solution)/shard_map/pallas_call | solution.py:300
  151.4 3.3 %collective-permute-start.7 = (bf16[256,576]{1,0:T(8,128)(2,1)S(1)}, bf16[256,576]{1,0:T(8,128)(2,1)S(1)}, u32[]{:S(2)}, u32[]{:S(2)}) collective-permute-start(bf16[256,576]{1,0:T(8,128)(2,1)S(1)} %get-tuple-element.23), channel_id=1, source_target_pairs={{0,1},{1,0},{2,3},{3,2},{4,5},{5,4},{6,7},{7,6},{8,9},{9,8},{10,11... | collective-permute-start | bytes 884744 | tf_op jit(solution)/shard_map/ppermute | solution.py:56
  154.7 1.2 collective-permute-done.7.arrived
  156.0 0.0 collective-permute-done.8.w_other
  156.0 1.3 copy-done.1
  157.3 4.8 %shard_map.80 = bf16[256,1152]{1,0:T(8,128)(2,1)} custom-call(s32[6]{0:T(128)S(1)} %copy-done.4, bf16[256,1152]{1,0:T(8,128)(2,1)} %bitcast.2.own.tokens, f32[1,1152]{1,0:T(1,128)S(1)} %constant_dynamic-slice_fusion.embed, bf16[256,576]{1,0:T(8,128)(2,1)S(1)} %get-tuple-element.22.own, bf16[256,576]{1,0:T(8,128)(2,1)S(1)} %collective-permute-done.7.arrived, ...), custom_call_target="tpu_custom_call" | custom-call | bytes 1 | tf_op jit(solution)/shard_map/pallas_call | solution.py:300
  (13 shorter events, 0.1 us)
Async XLA Ops:
  0.0 22.2 %copy-start = (f32[8,1152]{1,0:T(8,128)S(1)}, f32[8,1152]{1,0:T(8,128)}, u32[]{:S(2)}) copy-start(f32[8,1152]{1,0:T(8,128)} %param.8) | copy-start | bytes 110596
  3.8 18.0 %copy-start.5 = (f32[1152]{0:T(1024)S(1)}, f32[1152]{0:T(1024)}, u32[]{:S(2)}) copy-start(f32[1152]{0:T(1024)} %param.10) | copy-start | bytes 13828
  3.8 18.1 %copy-start.6 = (f32[1152]{0:T(1024)S(1)}, f32[1152]{0:T(1024)}, u32[]{:S(2)}) copy-start(f32[1152]{0:T(1024)} %param.11) | copy-start | bytes 13828
  3.8 18.2 %copy-start.7 = (f32[1152]{0:T(1024)S(1)}, f32[1152]{0:T(1024)}, u32[]{:S(2)}) copy-start(f32[1152]{0:T(1024)} %param.9) | copy-start | bytes 13828
  3.8 55.0 %all-to-all-start = ((bf16[64,96,128]{2,1,0:T(8,128)(2,1)}), bf16[64,96,128]{2,1,0:T(8,128)(2,1)S(1)}, u32[]{:S(2)}, u32[]{:S(2)}) async-start(bf16[64,96,128]{2,1,0:T(8,128)(2,1)} %shard_map.74), calls=%async_computation | async-start | bytes 3145728 | tf_op jit(solution)/shard_map/all_to_all | solution.py:360
  19.4 4.2 %collective-permute-start = (bf16[256,1152]{1,0:T(8,128)(2,1)}, bf16[256,1152]{1,0:T(8,128)(2,1)S(1)}, u32[]{:S(2)}, u32[]{:S(2)}) collective-permute-start(bf16[256,1152]{1,0:T(8,128)(2,1)} %bitcast.2.own.tokens), channel_id=1, source_target_pairs={{0,1},{1,0},{2,3},{3,2},{4,5},{5,4},{6,7},{7,6},{8,9},{9,8},{10,11... | collective-permute-start | bytes 1769480 | tf_op jit(solution)/shard_map/ppermute | solution.py:56
  59.4 19.7 %collective-permute-start.3 = (bf16[576,1152]{1,0:T(8,128)(2,1)S(1)}, bf16[576,1152]{1,0:T(8,128)(2,1)S(1)}, u32[]{:S(2)}, u32[]{:S(2)}) collective-permute-start(bf16[576,1152]{1,0:T(8,128)(2,1)S(1)} %shard_map.75.b0), channel_id=1, source_target_pairs={{0,14},{1,3},{2,0},{3,5},{4,2},{5,7},{6,4},{7,9},{8,6},{9,11},{10,... | collective-permute-start | bytes 3981320 | tf_op jit(solution)/shard_map/ppermute | solution.py:374
  61.3 21.2 %collective-permute-start.2 = (bf16[576,1152]{1,0:T(8,128)(2,1)S(1)}, bf16[576,1152]{1,0:T(8,128)(2,1)}, u32[]{:S(2)}, u32[]{:S(2)}) collective-permute-start(bf16[576,1152]{1,0:T(8,128)(2,1)S(1)} %shard_map.75.b0), channel_id=1, source_target_pairs={{0,112},{1,17},{2,114},{3,19},{4,116},{5,21},{6,118},{7,23},{8,120... | collective-permute-start | bytes 3981320 | tf_op jit(solution)/shard_map/ppermute | solution.py:374
  65.7 20.0 %collective-permute-start.1 = (bf16[576,1152]{1,0:T(8,128)(2,1)S(1)}, bf16[576,1152]{1,0:T(8,128)(2,1)}, u32[]{:S(2)}, u32[]{:S(2)}) collective-permute-start(bf16[576,1152]{1,0:T(8,128)(2,1)S(1)} %shard_map.75.b0), channel_id=1, source_target_pairs={{0,384},{1,129},{2,386},{3,131},{4,388},{5,133},{6,390},{7,135},{8... | collective-permute-start | bytes 3981320 | tf_op jit(solution)/shard_map/ppermute | solution.py:374
  68.8 39.7 %all-to-all-start.1 = ((bf16[32,8,1152]{2,1,0:T(8,128)(2,1)}), bf16[32,8,1152]{2,1,0:T(8,128)(2,1)S(1)}, u32[]{:S(2)}, u32[]{:S(2)}) async-start(bf16[32,8,1152]{2,1,0:T(8,128)(2,1)} %bitcast.6), calls=%async_computation.1 | async-start | bytes 1179648 | tf_op jit(solution)/shard_map/all_to_all | solution.py:375
  85.7 0.7 copy-start.4
  108.5 13.0 %collective-permute-start.5 = (bf16[256,1152]{1,0:T(8,128)(2,1)S(1)}, bf16[256,1152]{1,0:T(8,128)(2,1)S(1)}, u32[]{:S(2)}, u32[]{:S(2)}) collective-permute-start(bf16[256,1152]{1,0:T(8,128)(2,1)S(1)} %bitcast.12), channel_id=1, source_target_pairs={{0,1},{1,0},{2,3},{3,2},{4,5},{5,4},{6,7},{7,6},{8,9},{9,8},{10,11... | collective-permute-start | bytes 1769480 | tf_op jit(solution)/shard_map/ppermute | solution.py:56
  114.7 21.4 %collective-permute-start.4 = (bf16[288,512]{1,0:T(8,128)(2,1)}, bf16[288,512]{1,0:T(8,128)(2,1)}, u32[]{:S(2)}, u32[]{:S(2)}) collective-permute-start(bf16[288,512]{1,0:T(8,128)(2,1)} %get-tuple-element.17), channel_id=1, source_target_pairs={{0,64},{1,65},{2,66},{3,67},{4,68},{5,69},{6,70},{7,71},{8,72},{9,... | collective-permute-start | bytes 884744 | tf_op jit(solution)/shard_map/ppermute | solution.py:394
  119.3 36.7 %collective-permute-start.8 = (bf16[576,1152]{1,0:T(8,128)(2,1)}, bf16[576,1152]{1,0:T(8,128)(2,1)}, u32[]{:S(2)}, u32[]{:S(2)}) collective-permute-start(bf16[576,1152]{1,0:T(8,128)(2,1)} %get-tuple-element.24.w_own), channel_id=1, source_target_pairs={{0,1},{1,0},{2,3},{3,2},{4,5},{5,4},{6,7},{7,6},{8,9},{9,8},{10,11... | collective-permute-start | bytes 3981320 | tf_op jit(solution)/shard_map/ppermute | solution.py:56
  126.4 20.8 %all-to-all-start.2 = ((bf16[32,16,144]{2,1,0:T(8,128)(2,1)}), bf16[32,16,144]{2,1,0:T(8,128)(2,1)S(1)}, u32[]{:S(2)}, u32[]{:S(2)}) async-start(bf16[32,16,144]{2,1,0:T(8,128)(2,1)} %shard_map.77), calls=%async_computation.2 | async-start | bytes 524288 | tf_op jit(solution)/shard_map/all_to_all | solution.py:417
  136.2 11.8 %copy-start.3 = (bf16[144,512]{1,0:T(8,128)(2,1)S(1)}, bf16[144,512]{1,0:T(8,128)(2,1)}, u32[]{:S(2)}) copy-start(bf16[144,512]{1,0:T(8,128)(2,1)} %get-tuple-element.16.q_t) | copy-start | bytes 442372
  136.2 11.8 %collective-permute-start.6 = (bf16[288,512]{1,0:T(8,128)(2,1)}, bf16[288,512]{1,0:T(8,128)(2,1)S(1)}, u32[]{:S(2)}, u32[]{:S(2)}) collective-permute-start(bf16[288,512]{1,0:T(8,128)(2,1)} %collective-permute-done.4.kv_a), channel_id=1, source_target_pairs={{0,128},{1,129},{2,130},{3,131},{4,132},{5,133},{6,134},{7,135},{8... | collective-permute-start | bytes 884744 | tf_op jit(solution)/shard_map/ppermute | solution.py:407
  147.9 1.0 copy-start.2
  151.4 4.6 %collective-permute-start.7 = (bf16[256,576]{1,0:T(8,128)(2,1)S(1)}, bf16[256,576]{1,0:T(8,128)(2,1)S(1)}, u32[]{:S(2)}, u32[]{:S(2)}) collective-permute-start(bf16[256,576]{1,0:T(8,128)(2,1)S(1)} %get-tuple-element.23), channel_id=1, source_target_pairs={{0,1},{1,0},{2,3},{3,2},{4,5},{5,4},{6,7},{7,6},{8,9},{9,8},{10,11... | collective-permute-start | bytes 884744 | tf_op jit(solution)/shard_map/ppermute | solution.py:56
  156.0 1.3 copy-start.1

commit v6 on v5

v6 whole, which is shorter than its diff:
```python
import jax
import jax.numpy as jnp
from jax import lax
from jax.experimental import pallas as pl
from jax.experimental.pallas import tpu as pltpu
from jax.sharding import Mesh
from jax.sharding import PartitionSpec as P

HEADS = 16
HD = 72
D = HEADS * HD
PAIR = 2 * HD
QUAD = 4 * HD
HALF = 256
ROWS = 2 * HALF
PIECE = 88
REST = (1, 5, 6, 7, 2, 3)
CAM = ("x", "yh")
CHIP = ("yl", "z")
SLAB = ("yl", "z", "core")
EVERY = ("x", "yh", "yl", "z", "core")
SCALE = 1.4426950408889634 / HD**0.5
F32 = jnp.float32
BF16 = jnp.bfloat16
VMEM_LIMIT = 18 * 1024 * 1024


def route(move):
    pairs = []
    for x in range(4):
        for y in range(8):
            for z in range(8):
                for core in range(2):
                    a, b, c = move(x, y, z, core)
                    source = ((x * 8 + y) * 8 + z) * 2 + core
                    pairs.append((source, ((a % 4 * 8 + b % 8) * 8 + c % 8) * 2 + core))
    return pairs


def towards(core):
    return 1 if core else -1


OFFSETS = ((0, 1, 0), (1, 0, 0), (0, 0, 1), (0, 1, 1), (0, 0, -1), (-1, 0, 0), (0, -1, 0))


def bring(offset):
    a, b, c = offset
    return route(lambda x, y, z, core: (x + a * towards(core), y + b * towards(core), z + c * towards(core)))


ROUTES = tuple(bring(offset) for offset in OFFSETS)
ACROSS = route(lambda x, y, z, core: (x, y + 4, z))
ALONG = route(lambda x, y, z, core: (x + (1 if y < 4 else -1), y, z))


def swap_core(block):
    return lax.ppermute(block, "core", [(0, 1), (1, 0)])


def mm(a, b):
    return jnp.dot(a, b, preferred_element_type=F32)


def mm_t(a, b):
    return lax.dot_general(a, b, (((1,), (1,)), ((), ())), preferred_element_type=F32)


def after(value, *others):
    return lax.optimization_barrier((value,) + others)[0]


def pack_kernel(order, tokens, w_qkv_hbm, w_out_hbm, out, w_qkv, w_out, pieces, sem):
    loads = [
        pltpu.make_async_copy(w_qkv_hbm, w_qkv, sem.at[0]),
        pltpu.make_async_copy(w_out_hbm, w_out, sem.at[1]),
    ]
    for load in loads:
        load.start()
    for load in loads:
        load.wait()

    def columns(kind, head):
        start = kind * D + head * HD
        return w_qkv[:, start : start + HD].astype(F32)

    for who in range(2):
        a, b, c = 8 + 2 * who, 12 + 2 * who, 4 * who
        content = (
            ((0, a), (0, a + 1)),
            ((0, b), (0, b + 1)),
            ((2, c + 2), (0, c + 3)),
            ((1, c + 3), (2, c + 3)),
            ((1, a), (1, a + 1), (2, a), (2, a + 1)),
            ((1, b), (1, b + 1), (2, b), (2, b + 1)),
            ((0, c), (1, c), (2, c), (0, c + 1)),
            ((1, c + 1), (2, c + 1), (0, c + 2), (1, c + 2)),
        )
        for colour in range(8):
            parts = [columns(*one) for one in content[colour]]
            if colour < 4:
                start = (who * 4 + colour) * PAIR
                parts = [w_out[:, start : start + PAIR].astype(F32)] + parts
            whole = jnp.concatenate(parts, 1)
            place = who * 8 + colour
            pieces[place, :18] = whole[:, :128]
            pieces[place, 18:36] = whole[:, 128:256]
            tail = jnp.concatenate([whole[:9, 256:], whole[9:, 256:], jnp.zeros((9, 64), F32)], 1)
            pieces[place, 36:45] = tail
            pieces[place, 45:] = jnp.zeros((3, 128), F32)
    base = order[9]
    for dest in range(64):
        colour = (base + dest // 16 + 3 * (dest // 2 % 8)) % 8
        block = tokens[dest // 2 * 8 : dest // 2 * 8 + 8].astype(F32)
        block = block[dest % 2 * 4 : dest % 2 * 4 + 4]
        rows = [block[:, tile * 128 : tile * 128 + 128] for tile in range(9)]
        rows = [pieces[dest % 2 * 8 + colour]] + rows + [jnp.zeros((PIECE - 84, 128), F32)]
        out[dest] = jnp.concatenate(rows, 0).astype(BF16)


def unpack_kernel(got, block_out, tokens_out, block, tokens, wide, sem):
    for source in range(64):
        rows = got[source].astype(F32)
        at = source * 18
        wide[0, at : at + 18] = rows[:18]
        wide[1, at : at + 18] = rows[18:36]
        wide[2, at : at + 9, :32] = rows[36:45, :32]
        wide[2, at + 9 : at + 18, :32] = rows[36:45, 32:64]
        if source % 2 == 1:
            pair = [got[source - 1].astype(F32), rows]
            tiles = []
            for tile in range(9):
                start = 48 + tile * 4
                tiles.append(jnp.concatenate([one[start : start + 4] for one in pair], 0))
            tokens[source * 4 - 4 : source * 4 + 4] = jnp.concatenate(tiles, 1).astype(BF16)
    block[:128] = wide[0].T.astype(BF16)
    block[128:256] = wide[1].T.astype(BF16)
    block[256:] = wide[2].T[:32].astype(BF16)
    stores = [
        pltpu.make_async_copy(block, block_out, sem.at[0]),
        pltpu.make_async_copy(tokens, tokens_out, sem.at[1]),
    ]
    for store in stores:
        store.start()
    for store in stores:
        store.wait()


def normalise(ref, embed, gain):
    hidden = ref[...].astype(F32) + embed[...]
    centred = hidden - jnp.mean(hidden, -1, keepdims=True)
    variance = jnp.mean(centred * centred, -1, keepdims=True)
    return (centred * lax.rsqrt(variance + 1e-06) * gain[...]).astype(BF16)


def norm_kernel(own, other, embed, gain, out, rows, sem):
    copies = []
    for i, ref in enumerate((own, other)):
        part = pl.ds(i * HALF, HALF)
        rows[part] = normalise(ref, embed, gain)
        copies.append(pltpu.make_async_copy(rows.at[part], out.at[part], sem.at[i]))
        copies[-1].start()
    for copy in copies:
        copy.wait()


def start_fetch(order, blocks, group, slot, sem):
    for j, block in enumerate(blocks):
        @pl.when(order[group] == j)
        def _(block=block):
            pltpu.make_async_copy(block, slot, sem).start()


def wait_fetch(blocks, slot, sem):
    pltpu.make_async_copy(blocks[0], slot, sem).wait()


def head_norm(part, gain):
    shaped = part.reshape(part.shape[0] // HD, HD, part.shape[1])
    mean_sq = jnp.mean(shaped * shaped, 1, keepdims=True)
    return (shaped * lax.rsqrt(mean_sq + 1e-06)).reshape(part.shape) * gain


def attend(q_t, sides, mask=None):
    total = None
    for k_t, v_t in sides:
        scores = mm(k_t.T.astype(BF16), q_t.astype(BF16))
        expd = jnp.exp2(scores * SCALE)
        if mask is not None:
            expd = jnp.where(mask, expd, 0.0)
        wide = jnp.concatenate([v_t, jnp.ones((8, v_t.shape[1]), F32)], 0).astype(BF16)
        part = mm(wide, expd.astype(BF16))
        total = part if total is None else total + part
    return total[:HD] / total[HD : HD + 1]


def project_pair(normed, w_q, w_kv, gain):
    q = head_norm(mm_t(w_q, normed[...]), gain[:PAIR])
    kv = mm_t(w_kv, normed[...])
    return q, head_norm(kv[:PAIR], gain[PAIR:]), kv[PAIR:]


def cross_project_kernel(order, gains, normed_hbm, *refs):
    blocks, (q_out, kv_out, w_out, rest, normed, q_t, kv_t, weight, sem) = refs[:8], refs[8:]
    load = pltpu.make_async_copy(normed_hbm, normed, sem.at[8])
    load.start()
    first = (0, 4)
    for colour in first + REST:
        start_fetch(order, blocks, colour, weight.at[colour], sem.at[colour])
    stores = []

    def store(source, target):
        stores.append(pltpu.make_async_copy(source, target, sem.at[9 + len(stores)]))
        stores[-1].start()

    def arrived(colour):
        wait_fetch(blocks, weight.at[colour], sem.at[colour])
        if colour < 4:
            store(weight.at[colour, pl.ds(0, PAIR)], w_out.at[pl.ds(colour * PAIR, PAIR)])

    load.wait()
    for colour in first:
        arrived(colour)
    q, k, v = project_pair(normed, weight[0, PAIR:], weight[4], gains[...].T[:, :1])
    kv_t[...] = jnp.concatenate([k, v], 0).astype(BF16)
    store(kv_t, kv_out)
    q_t[...] = q.astype(BF16)
    store(q_t, q_out)
    for place, colour in enumerate(REST):
        arrived(colour)
        store(weight.at[colour], rest.at[place])
    for copy in stores:
        copy.wait()


def time_kernel(order, gains, own, other, embed, gain, rest, out, normed, result, weight, sem):
    load = pltpu.make_async_copy(rest.at[pl.ds(0, 2)], weight, sem.at[0])
    load.start()
    normed[:HALF] = normalise(own, embed, gain)
    normed[HALF:] = normalise(other, embed, gain)
    load.wait()
    q, k, v = project_pair(normed, weight[0, PAIR:], weight[1], gains[...].T[:, 1:2])
    row = lax.broadcasted_iota(jnp.int32, (HALF, HALF), 0) % 8
    col = lax.broadcasted_iota(jnp.int32, (HALF, HALF), 1) % 8
    sets = []
    for i in range(2):
        part = slice(i * HALF, (i + 1) * HALF)
        heads = []
        for head in range(2):
            at = head * HD
            side = (k[at : at + HD, part], v[at : at + HD, part])
            heads.append(attend(q[at : at + HD, part], [side], row == col))
        sets.append(jnp.concatenate(heads, 0).T.reshape(64, 4, PAIR))
    swap = order[8] == 1
    one = jnp.where(swap, sets[1], sets[0])
    two = jnp.where(swap, sets[0], sets[1])
    result[...] = jnp.concatenate([one, two], 1).reshape(32, 16, PAIR).astype(BF16)
    store = pltpu.make_async_copy(result, out, sem.at[1])
    store.start()
    store.wait()


def space_kernel(order, gains, normed_hbm, rest, out, normed, result, weight, sem):
    loads = [pltpu.make_async_copy(rest.at[2 + slot], weight.at[slot], sem.at[slot]) for slot in range(4)]
    loads.append(pltpu.make_async_copy(normed_hbm, normed, sem.at[4]))
    for load in loads:
        load.start()
    columns = gains[...].T[:PAIR]
    loads[4].wait()
    rows = []
    for slot in range(4):
        loads[slot].wait()
        projected = mm_t(weight[slot, (PAIR if slot > 1 else 0) :], normed[...])
        rows += [projected[at : at + HD] for at in range(0, projected.shape[0], HD)]
    heads = []
    for head in range(4):
        q, k, v = rows[3 * head : 3 * head + 3]
        gain = columns[:, 2 + head : 3 + head]
        q, k = head_norm(q, gain[:HD]), head_norm(k, gain[HD:])
        heads.append(attend(q, [(k, v)]))
    result[...] = jnp.concatenate(heads, 0).astype(BF16)
    store = pltpu.make_async_copy(result, out, sem.at[5])
    store.start()
    store.wait()


def cross_kernel(order, q_t, kv_a, kv_b, timed, space_hbm, keep, give, space, sem):
    load = pltpu.make_async_copy(space_hbm, space, sem)
    load.start()
    query = q_t[...].astype(F32)
    both = [ref[...].astype(F32) for ref in (kv_a, kv_b)]
    heads = []
    for head in range(2):
        at = head * HD
        sides = [(kv[at : at + HD], kv[PAIR + at : PAIR + at + HD]) for kv in both]
        heads.append(attend(query[at : at + HD], sides))
    load.wait()
    mixed = jnp.concatenate([space[...].astype(F32)] + heads, 0).T
    late = timed[...].astype(F32)
    late = [late[:, i * 8 : i * 8 + 8].reshape(HALF, PAIR) for i in range(2)]
    swap = order[8] == 1
    keep[...] = jnp.concatenate([mixed[:HALF], jnp.where(swap, late[1], late[0])], 1).astype(BF16)
    give[...] = jnp.concatenate([mixed[HALF:], jnp.where(swap, late[0], late[1])], 1).astype(BF16)


def out_kernel(order, tokens, embed, own, arrived, w_own, w_other, out):
    swap = order[8] == 1
    mine, theirs = own[...].astype(F32), arrived[...].astype(F32)
    first = jnp.where(swap, theirs, mine)
    second = jnp.where(swap, mine, theirs)
    parts = []
    for start, end in ((0, 2 * PAIR), (2 * PAIR, 3 * PAIR), (3 * PAIR, 4 * PAIR)):
        parts += [first[:, start:end], second[:, start:end]]
    mixed = jnp.concatenate(parts, 1).astype(BF16)
    one, two = mm_t(mixed, w_own[...]), mm_t(mixed, w_other[...])
    update = jnp.concatenate([jnp.where(swap, two, one), jnp.where(swap, one, two)], 1)
    out[...] = (tokens[...].astype(F32) + embed[...] + update).astype(BF16)


def call(kernel, out_shapes, args, scratch=(), flops=0, anys=0, out_any=False, room=VMEM_LIMIT):
    smem = pl.BlockSpec(memory_space=pltpu.SMEM)
    vmem = pl.BlockSpec(memory_space=pltpu.VMEM)
    hbm = pl.BlockSpec(memory_space=pltpu.HBM)
    specs = []
    for i, arg in enumerate(args):
        if arg.dtype == jnp.int32:
            specs.append(smem)
        else:
            specs.append(hbm if i >= len(args) - anys else vmem)
    moved = sum(a.size * a.dtype.itemsize for a in args)
    single = not isinstance(out_shapes, tuple)
    place = hbm if out_any else vmem
    return pl.pallas_call(
        kernel,
        out_shape=out_shapes,
        in_specs=specs,
        out_specs=place if single else (place,) * len(out_shapes),
        scratch_shapes=list(scratch),
        compiler_params=pltpu.CompilerParams(vmem_limit_bytes=room),
        cost_estimate=pl.CostEstimate(flops=flops, bytes_accessed=1, transcendentals=0),
    )(*args)


def shape(*dims):
    return jax.ShapeDtypeStruct(dims, BF16)


def far(*dims):
    return pltpu.HBM(dims, BF16)


def stay(array):
    return pltpu.with_memory_space_constraint(array, pltpu.HBM)


def local(frames_in, cam_embed, norm_gain, q_gain, k_gain, w_qkv, w_out):
    tokens = frames_in[0]
    core = lax.axis_index("core")
    base = 2 * lax.axis_index("x") + 4 * lax.axis_index("yh")
    colour = base + lax.axis_index("yl") + 3 * lax.axis_index("z")
    colours = jnp.arange(8, dtype=jnp.int32)
    order = jnp.where(core == 0, colours + 8 * 8 - colour, colour + 8 - colours) % 8
    order = jnp.concatenate([order, core[None], base[None]]).astype(jnp.int32)
    embed = lax.dynamic_slice_in_dim(cam_embed, lax.axis_index(CAM), 1, 0)
    gain = norm_gain[None]
    both = jnp.stack([q_gain.reshape(HEADS, HD), k_gain.reshape(HEADS, HD)], 1)

    def gains_of(head, count):
        return lax.dynamic_slice_in_dim(both, head, count, 0)

    pair_gains = jnp.stack([gains_of(8 + 2 * core, 2), gains_of(12 + 2 * core, 2)])
    pair_gains = pair_gains.transpose(0, 2, 1, 3).reshape(2, 2 * PAIR)
    space_gains = gains_of(4 * core, 4).reshape(4, PAIR)
    gains = jnp.concatenate([pair_gains, jnp.pad(space_gains, ((0, 2), (0, PAIR)))], 0)

    pieces = call(
        pack_kernel,
        shape(64, PIECE, 128),
        (order, tokens, w_qkv, w_out),
        [
            pltpu.VMEM((18, 3 * D), BF16),
            pltpu.VMEM((18, D), BF16),
            pltpu.VMEM((16, 48, 128), F32),
            pltpu.SemaphoreType.DMA((2,)),
        ],
        0,
        2,
        False,
        58 * 1024 * 1024,
    )
    got = lax.all_to_all(pieces, SLAB, 0, 0, tiled=True)
    other = swap_core(tokens)
    normed = call(
        norm_kernel,
        far(ROWS, D),
        (tokens, other, embed, gain),
        [pltpu.VMEM((ROWS, D), BF16), pltpu.SemaphoreType.DMA((2,))],
        8 * 10**9,
        0,
        True,
    )
    block, time_own = call(
        unpack_kernel,
        (far(QUAD, D), far(HALF, D)),
        (after(got, normed, gains),),
        [
            pltpu.VMEM((QUAD, D), BF16),
            pltpu.VMEM((HALF, D), BF16),
            pltpu.VMEM((3, D, 128), F32),
            pltpu.SemaphoreType.DMA((2,)),
        ],
        0,
        0,
        True,
    )
    blocks = (block,) + tuple(lax.ppermute(block, EVERY, r) for r in ROUTES)
    time_other = swap_core(time_own)

    frame = pltpu.VMEM((ROWS, D), BF16)
    two, four, eight = (pltpu.VMEM((n, QUAD, D), BF16) for n in (2, 4, 8))
    q_t, kv_t, w_own, rest = call(
        cross_project_kernel,
        (far(PAIR, ROWS), far(2 * PAIR, ROWS), far(4 * PAIR, D), far(len(REST), QUAD, D)),
        (order, gains, stay(normed)) + blocks,
        [
            frame,
            pltpu.VMEM((PAIR, ROWS), BF16),
            pltpu.VMEM((2 * PAIR, ROWS), BF16),
            eight,
            pltpu.SemaphoreType.DMA((21,)),
        ],
        0,
        9,
        True,
    )
    rest = stay(rest)
    kv_a = lax.ppermute(kv_t, EVERY, ACROSS)
    w_other = swap_core(w_own)
    timed = call(
        time_kernel,
        far(32, 16, PAIR),
        (order, gains, after(time_own, kv_t), time_other, embed, gain, rest),
        [frame, pltpu.VMEM((32, 16, PAIR), BF16), two, pltpu.SemaphoreType.DMA((2,))],
        0,
        1,
        True,
    )
    kv_b = lax.ppermute(after(kv_a, timed), EVERY, ALONG)
    space = call(
        space_kernel,
        far(2 * PAIR, ROWS),
        (order, gains, stay(after(normed, timed)), rest),
        [frame, pltpu.VMEM((2 * PAIR, ROWS), BF16), four, pltpu.SemaphoreType.DMA((6,))],
        16 * 10**9,
        2,
        True,
    )
    returned = lax.all_to_all(timed, CHIP, 0, 0, tiled=True)
    keep, give = call(
        cross_kernel,
        (shape(HALF, 4 * PAIR), shape(HALF, 4 * PAIR)),
        (order, q_t, kv_a, kv_b, returned, stay(space)),
        [pltpu.VMEM((2 * PAIR, ROWS), BF16), pltpu.SemaphoreType.DMA],
        0,
        1,
    )
    arrived = swap_core(give)
    return call(out_kernel, shape(HALF, D), (order, tokens, embed, keep, arrived, w_own, w_other))[None]


def solution(mesh):
    fine = Mesh(mesh.devices.reshape(4, 2, 4, 8, 2), EVERY)
    placed = (P(CAM, SLAB, None), P(), P(), P(), P(), P(SLAB, None), P(SLAB, None))
    return jax.shard_map(local, mesh=fine, in_specs=placed, out_specs=P(CAM, SLAB, None), check_vma=False)
```

time: 163 us -> 147 us (0.902)
  Pallas kernels: 47.7 us -> 30.9 us
  starting transfers between devices: 65.1 us -> 72.6 us
  waiting for transfers between devices: 44.9 us -> 40 us
  local copies, waits for them, and re-layouts: 3.36 us -> 1.51 us
    pallas_call x8, Pallas kernels: 47.7 us -> 30.9 us  [call(): pl.pallas_call(kernel, out_shape=out_shapes, in_specs=specs, out_specs=pl...]
    ppermute x3 -> x7, starting transfers between devices: 9.43 us -> 23.6 us  [local(): blocks = (block,) + tuple((lax.ppermute(block, EVERY, r) for r in ROUTES))]
    all_to_all x1 -> x0, starting transfers between devices: 7.93 us -> none  [local(): lax.all_to_all(after(tokens, block).reshape(32, 8, D), CHIP, 0, 0, tiled=...]
    ppermute x3 -> x7, waiting for transfers between devices: 8.97 us -> 4.58 us  [local(): blocks = (block,) + tuple((lax.ppermute(block, EVERY, r) for r in ROUTES))]
    ppermute x4, starting transfers between devices: 14.1 us -> 18.3 us  [swap_core(): return lax.ppermute(block, 'core', [(0, 1), (1, 0)])]
    unnamed x16 -> x26, local copies, waits for them, and re-layouts: 2.99 us -> 1.14 us
    ppermute x1, starting transfers between devices: 3.79 us -> 2.09 us  [local(): kv_b = lax.ppermute(after(kv_a, timed), EVERY, ALONG)]
  transfers between devices with their start and end apart: 12 -> 15, of which waited for: 8 -> 6; matrix products, arithmetic and copies ran while one was open for 0% -> 0% of each run, Pallas kernels for 24% -> 16%
where the time goes in v6:
time: 147 us; the launch traced here: 146 us
  starting transfers between devices  72.6 us (49%)
  waiting for transfers between devices  40 us (27%)
  Pallas kernels  30.9 us (21%)
  local copies, waits for them, and re-layouts  1.51 us (1%)
    all_to_all x1, waiting for transfers between devices, local(): got = lax.all_to_all(pieces, SLAB, 0, 0, tiled=True)  30.9 us
    pallas_call x8, Pallas kernels, call(): pl.pallas_call(kernel, out_shape=out_shapes, in_specs=specs, out_specs=pl...  30.9 us
    ppermute x7, starting transfers between devices, local(): blocks = (block,) + tuple((lax.ppermute(block, EVERY, r) for r in ROUTES))  23.6 us
    ppermute x4, starting transfers between devices, swap_core(): return lax.ppermute(block, 'core', [(0, 1), (1, 0)])  18.3 us
    all_to_all x1, starting transfers between devices, local(): got = lax.all_to_all(pieces, SLAB, 0, 0, tiled=True)  15.6 us
    all_to_all x1, starting transfers between devices, local(): returned = lax.all_to_all(timed, CHIP, 0, 0, tiled=True)  8.44 us
    ppermute x7, waiting for transfers between devices, local(): blocks = (block,) + tuple((lax.ppermute(block, EVERY, r) for r in ROUTES))  4.58 us
    ppermute x1, starting transfers between devices, local(): kv_a = lax.ppermute(kv_t, EVERY, ACROSS)  4.57 us
  transfers between devices with their start and end apart: 15, of which 6 were waited for; matrix products, arithmetic and copies ran while one was open for 0% of the time, Pallas kernels for 16%

profile of v6, /device:TPU:1, one launch (start us, length us, event | category | flops | bytes accessed | tf_op | source)
XLA Modules:
  0.0 146.1 jit_solution(4938457149085457383)
XLA Ops:
  0.0 0.6 pad_add_fusion.order
  0.6 3.8 %shard_map.74 = bf16[64,88,128]{2,1,0:T(8,128)(2,1)} custom-call(s32[10]{0:T(128)} %pad_add_fusion.order, bf16[256,1152]{1,0:T(8,128)(2,1)} %bitcast.10, bf16[18,3456]{1,0:T(8,128)(2,1)} %w_qkv_hbm.1, bf16[18,1152]{1,0:T(8,128)(2,1)} %w_out_hbm.1), custom_call_target="tpu_custom_call" | custom-call | bytes 1 | tf_op jit(solution)/shard_map/pallas_call | solution.py:333
  4.4 0.0 copy-start.1
  4.4 0.0 copy-start.10
  4.4 0.0 copy-start.11
  4.5 0.0 copy-start.12
  4.5 15.6 %all-to-all-start = ((bf16[64,88,128]{2,1,0:T(8,128)(2,1)}), bf16[64,88,128]{2,1,0:T(8,128)(2,1)S(1)}, u32[]{:S(2)}, u32[]{:S(2)}) async-start(bf16[64,88,128]{2,1,0:T(8,128)(2,1)} %shard_map.74), calls=%async_computation | async-start | bytes 2883584 | tf_op jit(solution)/shard_map/all_to_all | solution.py:391
  20.0 2.4 %collective-permute-start = (bf16[256,1152]{1,0:T(8,128)(2,1)S(1)}, bf16[256,1152]{1,0:T(8,128)(2,1)S(1)}, u32[]{:S(2)}, u32[]{:S(2)}) collective-permute-start(bf16[256,1152]{1,0:T(8,128)(2,1)S(1)} %bitcast.11), channel_id=1, source_target_pairs={{0,1},{1,0},{2,3},{3,2},{4,5},{5,4},{6,7},{7,6},{8,9},{9,8},{10,11... | collective-permute-start | bytes 1769480 | tf_op jit(solution)/shard_map/ppermute | solution.py:58
  22.4 0.1 stack_reshape.6
  22.5 0.1 stack_reshape.7
  22.7 0.1 reshape.6
  22.8 0.1 reshape.7
  22.9 1.1 collective-permute-done.other
  24.0 1.7 %shard_map.73.normed_hbm = bf16[512,1152]{1,0:T(8,128)(2,1)} custom-call(bf16[256,1152]{1,0:T(8,128)(2,1)S(1)} %bitcast.12, bf16[256,1152]{1,0:T(8,128)(2,1)S(1)} %collective-permute-done.other, f32[1,1152]{1,0:T(1,128)S(1)} %constant_dynamic-slice_fusion.embed, f32[1,1152]{1,0:T(1,128)S(1)} %broadcast_in_dim.14.gain), custom_call_target="tpu_custom_call" | custom-call | flops 8000000000 | bytes 1 | tf_op jit(solution)/shard_map/pallas_call | solution.py:333
  25.7 30.9 %all-to-all-done.got = bf16[64,88,128]{2,1,0:T(8,128)(2,1)S(1)} async-done(((bf16[64,88,128]{2,1,0:T(8,128)(2,1)}), bf16[64,88,128]{2,1,0:T(8,128)(2,1)S(1)}, u32[]{:S(2)}, u32[]{:S(2)}) %all-to-all-start) | async-done | bytes 1441824 | tf_op jit(solution)/shard_map/all_to_all | solution.py:391
  56.7 1.6 %shard_map.75 = (bf16[288,1152]{1,0:T(8,128)(2,1)}, bf16[256,1152]{1,0:T(8,128)(2,1)}) custom-call(bf16[64,88,128]{2,1,0:T(8,128)(2,1)S(1)} %all-to-all-done.got), custom_call_target="tpu_custom_call" | custom-call | bytes 1 | tf_op jit(solution)/shard_map/pallas_call | solution.py:333
  58.2 3.2 %collective-permute-start.1 = (bf16[288,1152]{1,0:T(8,128)(2,1)}, bf16[288,1152]{1,0:T(8,128)(2,1)S(1)}, u32[]{:S(2)}, u32[]{:S(2)}) collective-permute-start(bf16[288,1152]{1,0:T(8,128)(2,1)} %get-tuple-element.18.refs_0_), channel_id=1, source_target_pairs={{0,112},{1,17},{2,114},{3,19},{4,116},{5,21},{6,118},{7,23},{8,120... | collective-permute-start | bytes 1990664 | tf_op jit(solution)/shard_map/ppermute | solution.py:416
  61.4 3.1 %collective-permute-start.2 = (bf16[288,1152]{1,0:T(8,128)(2,1)}, bf16[288,1152]{1,0:T(8,128)(2,1)S(1)}, u32[]{:S(2)}, u32[]{:S(2)}) collective-permute-start(bf16[288,1152]{1,0:T(8,128)(2,1)} %get-tuple-element.18.refs_0_), channel_id=1, source_target_pairs={{0,384},{1,129},{2,386},{3,131},{4,388},{5,133},{6,390},{7,135},{8... | collective-permute-start | bytes 1990664 | tf_op jit(solution)/shard_map/ppermute | solution.py:416
  64.6 3.1 %collective-permute-start.3 = (bf16[288,1152]{1,0:T(8,128)(2,1)}, bf16[288,1152]{1,0:T(8,128)(2,1)S(1)}, u32[]{:S(2)}, u32[]{:S(2)}) collective-permute-start(bf16[288,1152]{1,0:T(8,128)(2,1)} %get-tuple-element.18.refs_0_), channel_id=1, source_target_pairs={{0,14},{1,3},{2,0},{3,5},{4,2},{5,7},{6,4},{7,9},{8,6},{9,11},{10,... | collective-permute-start | bytes 1990664 | tf_op jit(solution)/shard_map/ppermute | solution.py:416
  67.7 3.7 %collective-permute-start.4 = (bf16[288,1152]{1,0:T(8,128)(2,1)}, bf16[288,1152]{1,0:T(8,128)(2,1)S(1)}, u32[]{:S(2)}, u32[]{:S(2)}) collective-permute-start(bf16[288,1152]{1,0:T(8,128)(2,1)} %get-tuple-element.18.refs_0_), channel_id=1, source_target_pairs={{0,126},{1,19},{2,112},{3,21},{4,114},{5,23},{6,116},{7,25},{8,118... | collective-permute-start | bytes 1990664 | tf_op jit(solution)/shard_map/ppermute | solution.py:416
  71.4 4.2 %collective-permute-start.5 = (bf16[288,1152]{1,0:T(8,128)(2,1)}, bf16[288,1152]{1,0:T(8,128)(2,1)S(1)}, u32[]{:S(2)}, u32[]{:S(2)}) collective-permute-start(bf16[288,1152]{1,0:T(8,128)(2,1)} %get-tuple-element.18.refs_0_), channel_id=1, source_target_pairs={{0,2},{1,15},{2,4},{3,1},{4,6},{5,3},{6,8},{7,5},{8,10},{9,7},{10,... | collective-permute-start | bytes 1990664 | tf_op jit(solution)/shard_map/ppermute | solution.py:416
  75.6 0.0 collective-permute-done.1.refs_1_
  75.7 3.4 %collective-permute-start.6 = (bf16[288,1152]{1,0:T(8,128)(2,1)}, bf16[288,1152]{1,0:T(8,128)(2,1)S(1)}, u32[]{:S(2)}, u32[]{:S(2)}) collective-permute-start(bf16[288,1152]{1,0:T(8,128)(2,1)} %get-tuple-element.18.refs_0_), channel_id=1, source_target_pairs={{0,128},{1,385},{2,130},{3,387},{4,132},{5,389},{6,134},{7,391},{8... | collective-permute-start | bytes 1990664 | tf_op jit(solution)/shard_map/ppermute | solution.py:416
  79.0 0.0 collective-permute-done.2.refs_2_
  79.0 2.9 %collective-permute-start.7 = (bf16[288,1152]{1,0:T(8,128)(2,1)}, bf16[288,1152]{1,0:T(8,128)(2,1)S(1)}, u32[]{:S(2)}, u32[]{:S(2)}) collective-permute-start(bf16[288,1152]{1,0:T(8,128)(2,1)} %get-tuple-element.18.refs_0_), channel_id=1, source_target_pairs={{0,16},{1,113},{2,18},{3,115},{4,20},{5,117},{6,22},{7,119},{8,24}... | collective-permute-start | bytes 1990664 | tf_op jit(solution)/shard_map/ppermute | solution.py:416
  81.9 4.6 %collective-permute-done.3.refs_3_ = bf16[288,1152]{1,0:T(8,128)(2,1)S(1)} collective-permute-done((bf16[288,1152]{1,0:T(8,128)(2,1)}, bf16[288,1152]{1,0:T(8,128)(2,1)S(1)}, u32[]{:S(2)}, u32[]{:S(2)}) %collective-permute-start.3) | collective-permute-done | bytes 663584 | tf_op jit(solution)/shard_map/ppermute | solution.py:416
  86.5 9.3 %collective-permute-start.9 = (bf16[256,1152]{1,0:T(8,128)(2,1)}, bf16[256,1152]{1,0:T(8,128)(2,1)S(1)}, u32[]{:S(2)}, u32[]{:S(2)}) collective-permute-start(bf16[256,1152]{1,0:T(8,128)(2,1)} %get-tuple-element.22.own), channel_id=1, source_target_pairs={{0,1},{1,0},{2,3},{3,2},{4,5},{5,4},{6,7},{7,6},{8,9},{9,8},{10,11... | collective-permute-start | bytes 1769480 | tf_op jit(solution)/shard_map/ppermute | solution.py:58
  95.8 0.0 collective-permute-done.4.refs_4_
  95.8 0.0 collective-permute-done.5.refs_5_
  95.8 0.0 collective-permute-done.6.refs_6_
  95.8 0.0 collective-permute-done.7.refs_7_
  95.8 1.1 copy-done.3
  96.9 6.3 %shard_map.76 = (bf16[144,512]{1,0:T(8,128)(2,1)}, bf16[288,512]{1,0:T(8,128)(2,1)}, bf16[576,1152]{1,0:T(8,128)(2,1)}, bf16[6,288,1152]{2,1,0:T(8,128)(2,1)}) custom-call(s32[10]{0:T(128)S(1)} %copy-done.8, f32[8,288]{1,0:T(8,128)S(1)} %select_maximum_fusion.gains, bf16[512,1152]{1,0:T(8,128)(2,1)} %shard_map.73.normed_hbm, ...), custom_call_target="tpu_custom_call" | custom-call | bytes 1 | tf_op jit(solution)/shard_map/pallas_call | solution.py:333
  103.2 4.6 %collective-permute-start.8 = (bf16[288,512]{1,0:T(8,128)(2,1)}, bf16[288,512]{1,0:T(8,128)(2,1)}, u32[]{:S(2)}, u32[]{:S(2)}) collective-permute-start(bf16[288,512]{1,0:T(8,128)(2,1)} %get-tuple-element.20), channel_id=1, source_target_pairs={{0,64},{1,65},{2,66},{3,67},{4,68},{5,69},{6,70},{7,71},{8,72},{9,... | collective-permute-start | bytes 884744 | tf_op jit(solution)/shard_map/ppermute | solution.py:437
  107.8 0.0 collective-permute-done.9.other
  107.8 4.9 %shard_map.77 = bf16[32,16,144]{2,1,0:T(8,128)(2,1)} custom-call(s32[10]{0:T(128)S(1)} %copy-done.8, f32[8,288]{1,0:T(8,128)S(1)} %select_maximum_fusion.gains, bf16[256,1152]{1,0:T(8,128)(2,1)S(1)} %copy-done.4, bf16[256,1152]{1,0:T(8,128)(2,1)S(1)} %collective-permute-done.9.other, f32[1,1152]{1,0:T(1,128)S(1)} %constant_dynamic-slice_fusion.embed, ...), custom_call_target="tpu_custom_call" | custom-call | bytes 1 | tf_op jit(solution)/shard_map/pallas_call | solution.py:333
  112.8 8.4 %all-to-all-start.1 = ((bf16[32,16,144]{2,1,0:T(8,128)(2,1)}), bf16[32,16,144]{2,1,0:T(8,128)(2,1)}, u32[]{:S(2)}, u32[]{:S(2)}) async-start(bf16[32,16,144]{2,1,0:T(8,128)(2,1)} %shard_map.77), calls=%async_computation.1 | async-start | bytes 524288 | tf_op jit(solution)/shard_map/all_to_all | solution.py:458
  121.2 2.6 %collective-permute-start.12 = (bf16[576,1152]{1,0:T(8,128)(2,1)S(1)}, bf16[576,1152]{1,0:T(8,128)(2,1)S(1)}, u32[]{:S(2)}, u32[]{:S(2)}) collective-permute-start(bf16[576,1152]{1,0:T(8,128)(2,1)S(1)} %copy-done.2), channel_id=1, source_target_pairs={{0,1},{1,0},{2,3},{3,2},{4,5},{5,4},{6,7},{7,6},{8,9},{9,8},{10,11... | collective-permute-start | bytes 3981320 | tf_op jit(solution)/shard_map/ppermute | solution.py:58
  123.9 0.5 collective-permute-done.8.kv_a
  124.3 2.1 %collective-permute-start.10 = (bf16[288,512]{1,0:T(8,128)(2,1)}, bf16[288,512]{1,0:T(8,128)(2,1)}, u32[]{:S(2)}, u32[]{:S(2)}) collective-permute-start(bf16[288,512]{1,0:T(8,128)(2,1)} %collective-permute-done.8.kv_a), channel_id=1, source_target_pairs={{0,128},{1,129},{2,130},{3,131},{4,132},{5,133},{6,134},{7,135},{8... | collective-permute-start | bytes 884744 | tf_op jit(solution)/shard_map/ppermute | solution.py:448
  126.4 6.9 %shard_map.78.space_hbm = bf16[288,512]{1,0:T(8,128)(2,1)} custom-call(s32[10]{0:T(128)S(1)} %copy-done.9, f32[8,288]{1,0:T(8,128)S(1)} %select_maximum_fusion.gains, bf16[512,1152]{1,0:T(8,128)(2,1)} %shard_map.73.normed_hbm, bf16[6,288,1152]{2,1,0:T(8,128)(2,1)} %get-tuple-element.23.rest), custom_call_target="tpu_custom_call" | custom-call | flops 16000000000 | bytes 1 | tf_op jit(solution)/shard_map/pallas_call | solution.py:333
  133.4 0.0 all-to-all-done.1.timed
  133.4 1.6 %collective-permute-done.10.kv_b = bf16[288,512]{1,0:T(8,128)(2,1)} collective-permute-done((bf16[288,512]{1,0:T(8,128)(2,1)}, bf16[288,512]{1,0:T(8,128)(2,1)}, u32[]{:S(2)}, u32[]{:S(2)}) %collective-permute-start.10) | collective-permute-done | bytes 294944 | tf_op jit(solution)/shard_map/ppermute | solution.py:448
  135.0 3.0 %shard_map.79 = (bf16[256,576]{1,0:T(8,128)(2,1)S(1)}, bf16[256,576]{1,0:T(8,128)(2,1)S(1)}) custom-call(s32[10]{0:T(128)S(1)} %copy-done.9, bf16[144,512]{1,0:T(8,128)(2,1)S(1)} %copy-done.5, bf16[288,512]{1,0:T(8,128)(2,1)} %collective-permute-done.8.kv_a, bf16[288,512]{1,0:T(8,128)(2,1)} %collective-permute-done.10.kv_b, ...), custom_call_target="tpu_custom_call" | custom-call | bytes 1 | tf_op jit(solution)/shard_map/pallas_call | solution.py:333
  138.1 4.0 %collective-permute-start.11 = (bf16[256,576]{1,0:T(8,128)(2,1)S(1)}, bf16[256,576]{1,0:T(8,128)(2,1)S(1)}, u32[]{:S(2)}, u32[]{:S(2)}) collective-permute-start(bf16[256,576]{1,0:T(8,128)(2,1)S(1)} %get-tuple-element.27), channel_id=1, source_target_pairs={{0,1},{1,0},{2,3},{3,2},{4,5},{5,4},{6,7},{7,6},{8,9},{9,8},{10,11... | collective-permute-start | bytes 884744 | tf_op jit(solution)/shard_map/ppermute | solution.py:58
  142.1 1.2 collective-permute-done.11.arrived
  143.3 0.0 collective-permute-done.12.w_other
  143.4 2.7 %shard_map.80 = bf16[256,1152]{1,0:T(8,128)(2,1)} custom-call(s32[10]{0:T(128)S(1)} %copy-done.9, bf16[256,1152]{1,0:T(8,128)(2,1)S(1)} %bitcast.13, f32[1,1152]{1,0:T(1,128)S(1)} %copy-done.7, bf16[256,576]{1,0:T(8,128)(2,1)S(1)} %get-tuple-element.26.own, bf16[256,576]{1,0:T(8,128)(2,1)S(1)} %collective-permute-done.11.arrived, ...), custom_call_target="tpu_custom_call" | custom-call | bytes 1 | tf_op jit(solution)/shard_map/pallas_call | solution.py:333
  (29 shorter events, 0.1 us)
Async XLA Ops:
  0.0 22.9 %copy-start = (f32[8,1152]{1,0:T(8,128)S(1)}, f32[8,1152]{1,0:T(8,128)}, u32[]{:S(2)}) copy-start(f32[8,1152]{1,0:T(8,128)} %param.8) | copy-start | bytes 110596
  4.4 15.6 %copy-start.1 = (bf16[1,256,1152]{2,1,0:T(8,128)(2,1)S(1)}, bf16[1,256,1152]{2,1,0:T(8,128)(2,1)}, u32[]{:S(2)}) copy-start(bf16[1,256,1152]{2,1,0:T(8,128)(2,1)} %param.7) | copy-start | bytes 1769476
  4.4 18.0 %copy-start.10 = (f32[1152]{0:T(1024)S(1)}, f32[1152]{0:T(1024)}, u32[]{:S(2)}) copy-start(f32[1152]{0:T(1024)} %param.10) | copy-start | bytes 13828
  4.4 18.1 %copy-start.11 = (f32[1152]{0:T(1024)S(1)}, f32[1152]{0:T(1024)}, u32[]{:S(2)}) copy-start(f32[1152]{0:T(1024)} %param.11) | copy-start | bytes 13828
  4.5 18.4 %copy-start.12 = (f32[1152]{0:T(1024)S(1)}, f32[1152]{0:T(1024)}, u32[]{:S(2)}) copy-start(f32[1152]{0:T(1024)} %param.9) | copy-start | bytes 13828
  4.5 52.2 %all-to-all-start = ((bf16[64,88,128]{2,1,0:T(8,128)(2,1)}), bf16[64,88,128]{2,1,0:T(8,128)(2,1)S(1)}, u32[]{:S(2)}, u32[]{:S(2)}) async-start(bf16[64,88,128]{2,1,0:T(8,128)(2,1)} %shard_map.74), calls=%async_computation | async-start | bytes 2883584 | tf_op jit(solution)/shard_map/all_to_all | solution.py:391
  20.0 4.0 %collective-permute-start = (bf16[256,1152]{1,0:T(8,128)(2,1)S(1)}, bf16[256,1152]{1,0:T(8,128)(2,1)S(1)}, u32[]{:S(2)}, u32[]{:S(2)}) collective-permute-start(bf16[256,1152]{1,0:T(8,128)(2,1)S(1)} %bitcast.11), channel_id=1, source_target_pairs={{0,1},{1,0},{2,3},{3,2},{4,5},{5,4},{6,7},{7,6},{8,9},{9,8},{10,11... | collective-permute-start | bytes 1769480 | tf_op jit(solution)/shard_map/ppermute | solution.py:58
  22.9 84.9 %copy-start.6 = (f32[1,1152]{1,0:T(1,128)}, f32[1,1152]{1,0:T(1,128)S(1)}, u32[]{:S(2)}) copy-start(f32[1,1152]{1,0:T(1,128)S(1)} %constant_dynamic-slice_fusion.embed) | copy-start | bytes 13828
  25.7 70.1 %copy-start.8 = (s32[10]{0:T(128)S(1)}, s32[10]{0:T(128)}, u32[]{:S(2)}) copy-start(s32[10]{0:T(128)} %pad_add_fusion.order) | copy-start | bytes 124
  58.2 17.4 %collective-permute-start.1 = (bf16[288,1152]{1,0:T(8,128)(2,1)}, bf16[288,1152]{1,0:T(8,128)(2,1)S(1)}, u32[]{:S(2)}, u32[]{:S(2)}) collective-permute-start(bf16[288,1152]{1,0:T(8,128)(2,1)} %get-tuple-element.18.refs_0_), channel_id=1, source_target_pairs={{0,112},{1,17},{2,114},{3,19},{4,116},{5,21},{6,118},{7,23},{8,120... | collective-permute-start | bytes 1990664 | tf_op jit(solution)/shard_map/ppermute | solution.py:416
  61.4 17.6 %collective-permute-start.2 = (bf16[288,1152]{1,0:T(8,128)(2,1)}, bf16[288,1152]{1,0:T(8,128)(2,1)S(1)}, u32[]{:S(2)}, u32[]{:S(2)}) collective-permute-start(bf16[288,1152]{1,0:T(8,128)(2,1)} %get-tuple-element.18.refs_0_), channel_id=1, source_target_pairs={{0,384},{1,129},{2,386},{3,131},{4,388},{5,133},{6,390},{7,135},{8... | collective-permute-start | bytes 1990664 | tf_op jit(solution)/shard_map/ppermute | solution.py:416
  64.6 21.9 %collective-permute-start.3 = (bf16[288,1152]{1,0:T(8,128)(2,1)}, bf16[288,1152]{1,0:T(8,128)(2,1)S(1)}, u32[]{:S(2)}, u32[]{:S(2)}) collective-permute-start(bf16[288,1152]{1,0:T(8,128)(2,1)} %get-tuple-element.18.refs_0_), channel_id=1, source_target_pairs={{0,14},{1,3},{2,0},{3,5},{4,2},{5,7},{6,4},{7,9},{8,6},{9,11},{10,... | collective-permute-start | bytes 1990664 | tf_op jit(solution)/shard_map/ppermute | solution.py:416
  67.7 28.1 %collective-permute-start.4 = (bf16[288,1152]{1,0:T(8,128)(2,1)}, bf16[288,1152]{1,0:T(8,128)(2,1)S(1)}, u32[]{:S(2)}, u32[]{:S(2)}) collective-permute-start(bf16[288,1152]{1,0:T(8,128)(2,1)} %get-tuple-element.18.refs_0_), channel_id=1, source_target_pairs={{0,126},{1,19},{2,112},{3,21},{4,114},{5,23},{6,116},{7,25},{8,118... | collective-permute-start | bytes 1990664 | tf_op jit(solution)/shard_map/ppermute | solution.py:416
  71.4 24.4 %collective-permute-start.5 = (bf16[288,1152]{1,0:T(8,128)(2,1)}, bf16[288,1152]{1,0:T(8,128)(2,1)S(1)}, u32[]{:S(2)}, u32[]{:S(2)}) collective-permute-start(bf16[288,1152]{1,0:T(8,128)(2,1)} %get-tuple-element.18.refs_0_), channel_id=1, source_target_pairs={{0,2},{1,15},{2,4},{3,1},{4,6},{5,3},{6,8},{7,5},{8,10},{9,7},{10,... | collective-permute-start | bytes 1990664 | tf_op jit(solution)/shard_map/ppermute | solution.py:416
  75.7 20.2 %collective-permute-start.6 = (bf16[288,1152]{1,0:T(8,128)(2,1)}, bf16[288,1152]{1,0:T(8,128)(2,1)S(1)}, u32[]{:S(2)}, u32[]{:S(2)}) collective-permute-start(bf16[288,1152]{1,0:T(8,128)(2,1)} %get-tuple-element.18.refs_0_), channel_id=1, source_target_pairs={{0,128},{1,385},{2,130},{3,387},{4,132},{5,389},{6,134},{7,391},{8... | collective-permute-start | bytes 1990664 | tf_op jit(solution)/shard_map/ppermute | solution.py:416
  79.0 16.8 %collective-permute-start.7 = (bf16[288,1152]{1,0:T(8,128)(2,1)}, bf16[288,1152]{1,0:T(8,128)(2,1)S(1)}, u32[]{:S(2)}, u32[]{:S(2)}) collective-permute-start(bf16[288,1152]{1,0:T(8,128)(2,1)} %get-tuple-element.18.refs_0_), channel_id=1, source_target_pairs={{0,16},{1,113},{2,18},{3,115},{4,20},{5,117},{6,22},{7,119},{8,24}... | collective-permute-start | bytes 1990664 | tf_op jit(solution)/shard_map/ppermute | solution.py:416
  86.5 21.3 %collective-permute-start.9 = (bf16[256,1152]{1,0:T(8,128)(2,1)}, bf16[256,1152]{1,0:T(8,128)(2,1)S(1)}, u32[]{:S(2)}, u32[]{:S(2)}) collective-permute-start(bf16[256,1152]{1,0:T(8,128)(2,1)} %get-tuple-element.22.own), channel_id=1, source_target_pairs={{0,1},{1,0},{2,3},{3,2},{4,5},{5,4},{6,7},{7,6},{8,9},{9,8},{10,11... | collective-permute-start | bytes 1769480 | tf_op jit(solution)/shard_map/ppermute | solution.py:58
  95.8 1.1 copy-start.3
  96.9 10.9 %copy-start.4 = (bf16[256,1152]{1,0:T(8,128)(2,1)S(1)}, bf16[256,1152]{1,0:T(8,128)(2,1)}, u32[]{:S(2)}) copy-start(bf16[256,1152]{1,0:T(8,128)(2,1)} %get-tuple-element.22.own) | copy-start | bytes 1769476
  103.2 21.1 %collective-permute-start.8 = (bf16[288,512]{1,0:T(8,128)(2,1)}, bf16[288,512]{1,0:T(8,128)(2,1)}, u32[]{:S(2)}, u32[]{:S(2)}) collective-permute-start(bf16[288,512]{1,0:T(8,128)(2,1)} %get-tuple-element.20), channel_id=1, source_target_pairs={{0,64},{1,65},{2,66},{3,67},{4,68},{5,69},{6,70},{7,71},{8,72},{9,... | collective-permute-start | bytes 884744 | tf_op jit(solution)/shard_map/ppermute | solution.py:437
  107.8 13.4 %copy-start.2 = (bf16[576,1152]{1,0:T(8,128)(2,1)S(1)}, bf16[576,1152]{1,0:T(8,128)(2,1)}, u32[]{:S(2)}) copy-start(bf16[576,1152]{1,0:T(8,128)(2,1)} %get-tuple-element.28.w_own) | copy-start | bytes 3981316
  107.8 18.6 %copy-start.9 = (s32[10]{0:T(128)S(1)}, s32[10]{0:T(128)}, u32[]{:S(2)}) copy-start(s32[10]{0:T(128)} %pad_add_fusion.order) | copy-start | bytes 124
  112.8 20.6 %all-to-all-start.1 = ((bf16[32,16,144]{2,1,0:T(8,128)(2,1)}), bf16[32,16,144]{2,1,0:T(8,128)(2,1)}, u32[]{:S(2)}, u32[]{:S(2)}) async-start(bf16[32,16,144]{2,1,0:T(8,128)(2,1)} %shard_map.77), calls=%async_computation.1 | async-start | bytes 524288 | tf_op jit(solution)/shard_map/all_to_all | solution.py:458
  121.2 13.8 %copy-start.5 = (bf16[144,512]{1,0:T(8,128)(2,1)S(1)}, bf16[144,512]{1,0:T(8,128)(2,1)}, u32[]{:S(2)}) copy-start(bf16[144,512]{1,0:T(8,128)(2,1)} %get-tuple-element.19.q_t) | copy-start | bytes 442372
  121.2 22.1 %copy-start.7 = (f32[1,1152]{1,0:T(1,128)S(1)}, f32[1,1152]{1,0:T(1,128)}, u32[]{:S(2)}) copy-start(f32[1,1152]{1,0:T(1,128)} %copy-done.6) | copy-start | bytes 13828
  121.2 22.1 %collective-permute-start.12 = (bf16[576,1152]{1,0:T(8,128)(2,1)S(1)}, bf16[576,1152]{1,0:T(8,128)(2,1)S(1)}, u32[]{:S(2)}, u32[]{:S(2)}) collective-permute-start(bf16[576,1152]{1,0:T(8,128)(2,1)S(1)} %copy-done.2), channel_id=1, source_target_pairs={{0,1},{1,0},{2,3},{3,2},{4,5},{5,4},{6,7},{7,6},{8,9},{9,8},{10,11... | collective-permute-start | bytes 3981320 | tf_op jit(solution)/shard_map/ppermute | solution.py:58
  124.3 10.7 %collective-permute-start.10 = (bf16[288,512]{1,0:T(8,128)(2,1)}, bf16[288,512]{1,0:T(8,128)(2,1)}, u32[]{:S(2)}, u32[]{:S(2)}) collective-permute-start(bf16[288,512]{1,0:T(8,128)(2,1)} %collective-permute-done.8.kv_a), channel_id=1, source_target_pairs={{0,128},{1,129},{2,130},{3,131},{4,132},{5,133},{6,134},{7,135},{8... | collective-permute-start | bytes 884744 | tf_op jit(solution)/shard_map/ppermute | solution.py:448
  138.1 5.3 %collective-permute-start.11 = (bf16[256,576]{1,0:T(8,128)(2,1)S(1)}, bf16[256,576]{1,0:T(8,128)(2,1)S(1)}, u32[]{:S(2)}, u32[]{:S(2)}) collective-permute-start(bf16[256,576]{1,0:T(8,128)(2,1)S(1)} %get-tuple-element.27), channel_id=1, source_target_pairs={{0,1},{1,0},{2,3},{3,2},{4,5},{5,4},{6,7},{7,6},{8,9},{9,8},{10,11... | collective-permute-start | bytes 884744 | tf_op jit(solution)/shard_map/ppermute | solution.py:58

commit v7 on v6

v7 whole, which is shorter than its diff:
```python
import jax
import jax.numpy as jnp
from jax import lax
from jax.experimental import pallas as pl
from jax.experimental.pallas import tpu as pltpu
from jax.sharding import Mesh
from jax.sharding import PartitionSpec as P

HEADS = 16
HD = 72
D = HEADS * HD
PAIR = 2 * HD
QUAD = 4 * HD
HALF = 256
ROWS = 2 * HALF
PIECE = 88
LATE = (6, 7, 2, 3)
CAM = ("x", "yh")
CHIP = ("yl", "z")
SLAB = ("yl", "z", "core")
EVERY = ("x", "yh", "yl", "z", "core")
SCALE = 1.4426950408889634 / HD**0.5
F32 = jnp.float32
BF16 = jnp.bfloat16
VMEM_LIMIT = 18 * 1024 * 1024


def route(move):
    pairs = []
    for x in range(4):
        for y in range(8):
            for z in range(8):
                for core in range(2):
                    a, b, c = move(x, y, z, core)
                    source = ((x * 8 + y) * 8 + z) * 2 + core
                    pairs.append((source, ((a % 4 * 8 + b % 8) * 8 + c % 8) * 2 + core))
    return pairs


def towards(core):
    return 1 if core else -1


OFFSETS = ((0, 0, 1), (0, 1, 0), (1, 0, 0), (0, 0, -1), (0, -1, 0), (0, 1, 1), (-1, 0, 0))
TURNS = (0,) + tuple((2 * a + b + 3 * c) % 8 for a, b, c in OFFSETS)


def bring(offset):
    a, b, c = offset
    return route(lambda x, y, z, core: (x + a * towards(core), y + b * towards(core), z + c * towards(core)))


ROUTES = tuple(bring(offset) for offset in OFFSETS)
ACROSS = route(lambda x, y, z, core: (x, y + 4, z))
ALONG = route(lambda x, y, z, core: (x + (1 if y < 4 else -1), y, z))


def swap_core(block):
    return lax.ppermute(block, "core", [(0, 1), (1, 0)])


def mm(a, b):
    return jnp.dot(a, b, preferred_element_type=F32)


def mm_t(a, b):
    return lax.dot_general(a, b, (((1,), (1,)), ((), ())), preferred_element_type=F32)


def position():
    return [lax.axis_index(axis) for axis in EVERY]


def after(value, *others):
    return lax.optimization_barrier((value,) + others)[0]


def pack_kernel(tokens, w_qkv_hbm, w_out_hbm, out, w_qkv, w_out, pieces, sem):
    loads = [
        pltpu.make_async_copy(w_qkv_hbm, w_qkv, sem.at[0]),
        pltpu.make_async_copy(w_out_hbm, w_out, sem.at[1]),
    ]
    for load in loads:
        load.start()
    for load in loads:
        load.wait()

    def columns(kind, head):
        start = kind * D + head * HD
        return w_qkv[:, start : start + HD].astype(F32)

    for who in range(2):
        a, b, c = 8 + 2 * who, 12 + 2 * who, 4 * who
        content = (
            ((0, a), (0, a + 1)),
            ((0, b), (0, b + 1)),
            ((2, c + 2), (0, c + 3)),
            ((1, c + 3), (2, c + 3)),
            ((1, a), (1, a + 1), (2, a), (2, a + 1)),
            ((1, b), (1, b + 1), (2, b), (2, b + 1)),
            ((0, c), (1, c), (2, c), (0, c + 1)),
            ((1, c + 1), (2, c + 1), (0, c + 2), (1, c + 2)),
        )
        for colour in range(8):
            parts = [columns(*one) for one in content[colour]]
            if colour < 4:
                start = (who * 4 + colour) * PAIR
                parts = [w_out[:, start : start + PAIR].astype(F32)] + parts
            whole = jnp.concatenate(parts, 1)
            place = who * 8 + colour
            pieces[place, :18] = whole[:, :128]
            pieces[place, 18:36] = whole[:, 128:256]
            tail = jnp.concatenate([whole[:9, 256:], whole[9:, 256:], jnp.zeros((9, 64), F32)], 1)
            pieces[place, 36:45] = tail
            pieces[place, 45:] = jnp.zeros((3, 128), F32)
    x, yh = position()[:2]
    base = 2 * x + 4 * yh
    for dest in range(64):
        colour = (base + dest // 16 + 3 * (dest // 2 % 8)) % 8
        block = tokens[dest // 2 * 8 : dest // 2 * 8 + 8].astype(F32)
        block = block[dest % 2 * 4 : dest % 2 * 4 + 4]
        rows = [block[:, tile * 128 : tile * 128 + 128] for tile in range(9)]
        rows = [pieces[dest % 2 * 8 + colour]] + rows + [jnp.zeros((PIECE - 84, 128), F32)]
        out[dest] = jnp.concatenate(rows, 0).astype(BF16)


def unpack_kernel(got, block, block_out, tokens_out, tokens, wide, sem):
    for source in range(64):
        rows = got[source].astype(F32)
        at = source * 18
        wide[0, at : at + 18] = rows[:18]
        wide[1, at : at + 18] = rows[18:36]
        wide[2, at : at + 9, :32] = rows[36:45, :32]
        wide[2, at + 9 : at + 18, :32] = rows[36:45, 32:64]
        if source % 2 == 1:
            pair = [got[source - 1].astype(F32), rows]
            tiles = []
            for tile in range(9):
                start = 48 + tile * 4
                tiles.append(jnp.concatenate([one[start : start + 4] for one in pair], 0))
            tokens[source * 4 - 4 : source * 4 + 4] = jnp.concatenate(tiles, 1).astype(BF16)
    block[:128] = wide[0].T.astype(BF16)
    block[128:256] = wide[1].T.astype(BF16)
    block[256:] = wide[2].T[:32].astype(BF16)
    stores = [
        pltpu.make_async_copy(block, block_out, sem.at[0]),
        pltpu.make_async_copy(tokens, tokens_out, sem.at[1]),
    ]
    for store in stores:
        store.start()
    for store in stores:
        store.wait()


def own_embed(cam_embed):
    return cam_embed[pl.ds(lax.axis_index("x") * 2 + lax.axis_index("yh"), 1)]


def normalise(ref, embed, gain):
    hidden = ref[...].astype(F32) + embed
    centred = hidden - jnp.mean(hidden, -1, keepdims=True)
    variance = jnp.mean(centred * centred, -1, keepdims=True)
    return (centred * lax.rsqrt(variance + 1e-06) * gain[...]).astype(BF16)


def norm_kernel(own, other, cam_embed, gain, out):
    for i, ref in enumerate((own, other)):
        out[i * HALF : (i + 1) * HALF] = normalise(ref, own_embed(cam_embed), gain)


def start_fetch(blocks, colour, slot, sem):
    x, yh, yl, z, core = position()
    ahead = colour - (2 * x + 4 * yh + yl + 3 * z) + 64
    turn = lax.rem(jnp.where(core == 0, ahead, 128 - ahead), 8)
    for block, own in zip(blocks, TURNS):
        @pl.when(turn == own)
        def _(block=block):
            pltpu.make_async_copy(block, slot, sem).start()


def wait_fetch(blocks, slot, sem):
    pltpu.make_async_copy(blocks[0], slot, sem).wait()


def head_norm(part, gain):
    shaped = part.reshape(part.shape[0] // HD, HD, part.shape[1])
    mean_sq = jnp.mean(shaped * shaped, 1, keepdims=True)
    return (shaped * lax.rsqrt(mean_sq + 1e-06)).reshape(part.shape) * gain


def attend(q_t, sides, mask=None):
    total = None
    for k_t, v_t in sides:
        scores = mm(k_t.T.astype(BF16), q_t.astype(BF16))
        expd = jnp.exp2(scores * SCALE)
        if mask is not None:
            expd = jnp.where(mask, expd, 0.0)
        wide = jnp.concatenate([v_t, jnp.ones((8, v_t.shape[1]), F32)], 0).astype(BF16)
        part = mm(wide, expd.astype(BF16))
        total = part if total is None else total + part
    return total[:HD] / total[HD : HD + 1]


def project_pair(normed, w_q, w_kv, gain):
    q = head_norm(mm_t(w_q, normed[...]), gain[:PAIR])
    kv = mm_t(w_kv, normed[...])
    return q, head_norm(kv[:PAIR], gain[PAIR:]), kv[PAIR:]


def cross_project_kernel(gains, normed, *refs):
    blocks, (q_out, kv_t, w_out, early, late, q_t, weight, sem) = refs[:8], refs[8:]
    slots = {0: weight.at[0], 4: weight.at[1], 1: early.at[0], 5: early.at[1]}
    slots.update({colour: late.at[place] for place, colour in enumerate(LATE)})
    for colour, slot in slots.items():
        start_fetch(blocks, colour, slot, sem.at[colour])
    parts = [block.at[pl.ds(0, PAIR)] for block in blocks]
    thirds = [w_out.at[pl.ds(colour * PAIR, PAIR)] for colour in range(4)]
    for colour in range(4):
        start_fetch(parts, colour, thirds[colour], sem.at[8 + colour])
    for colour in (0, 4):
        wait_fetch(blocks, slots[colour], sem.at[colour])
    q, k, v = project_pair(normed, weight[0, PAIR:], weight[1], gains[...].T[:, :1])
    kv_t[...] = jnp.concatenate([k, v], 0).astype(BF16)
    q_t[...] = q.astype(BF16)
    store = pltpu.make_async_copy(q_t, q_out, sem.at[12])
    store.start()
    for colour in (1, 5) + LATE:
        wait_fetch(blocks, slots[colour], sem.at[colour])
    for colour in range(4):
        wait_fetch(parts, thirds[colour], sem.at[8 + colour])
    store.wait()


def time_kernel(gains, normed, weight, out):
    q, k, v = project_pair(normed, weight[0, PAIR:], weight[1], gains[...].T[:, 1:2])
    row = lax.broadcasted_iota(jnp.int32, (HALF, HALF), 0) % 8
    col = lax.broadcasted_iota(jnp.int32, (HALF, HALF), 1) % 8
    sets = []
    for i in range(2):
        part = slice(i * HALF, (i + 1) * HALF)
        heads = []
        for head in range(2):
            at = head * HD
            side = (k[at : at + HD, part], v[at : at + HD, part])
            heads.append(attend(q[at : at + HD, part], [side], row == col))
        sets.append(jnp.concatenate(heads, 0).T.reshape(64, 4, PAIR))
    swap = lax.axis_index("core") == 1
    one = jnp.where(swap, sets[1], sets[0])
    two = jnp.where(swap, sets[0], sets[1])
    out[...] = jnp.concatenate([one, two], 1).reshape(32, 16, PAIR).astype(BF16)


def space_kernel(gains, normed_hbm, weight_hbm, out, normed, result, weight, sem):
    loads = [pltpu.make_async_copy(weight_hbm.at[slot], weight.at[slot], sem.at[slot]) for slot in range(4)]
    loads.insert(0, pltpu.make_async_copy(normed_hbm, normed, sem.at[4]))
    for load in loads:
        load.start()
    columns = gains[...].T[:PAIR]
    loads[0].wait()
    rows = []
    for slot in range(4):
        loads[1 + slot].wait()
        projected = mm_t(weight[slot, (PAIR if slot > 1 else 0) :], normed[...])
        rows += [projected[at : at + HD] for at in range(0, projected.shape[0], HD)]
    heads = []
    for head in range(4):
        q, k, v = rows[3 * head : 3 * head + 3]
        gain = columns[:, 2 + head : 3 + head]
        q, k = head_norm(q, gain[:HD]), head_norm(k, gain[HD:])
        heads.append(attend(q, [(k, v)]))
    result[...] = jnp.concatenate(heads, 0).astype(BF16)
    store = pltpu.make_async_copy(result, out, sem.at[5])
    store.start()
    store.wait()


def cross_kernel(kv_a, kv_b, timed, space_hbm, q_hbm, keep, give, space, q_t, sem):
    loads = [pltpu.make_async_copy(q_hbm, q_t, sem.at[0]), pltpu.make_async_copy(space_hbm, space, sem.at[1])]
    for load in loads:
        load.start()
    both = [ref[...].astype(F32) for ref in (kv_a, kv_b)]
    loads[0].wait()
    query = q_t[...].astype(F32)
    heads = []
    for head in range(2):
        at = head * HD
        sides = [(kv[at : at + HD], kv[PAIR + at : PAIR + at + HD]) for kv in both]
        heads.append(attend(query[at : at + HD], sides))
    loads[1].wait()
    mixed = jnp.concatenate([space[...].astype(F32)] + heads, 0).T
    late = timed[...].astype(F32)
    late = [late[:, i * 8 : i * 8 + 8].reshape(HALF, PAIR) for i in range(2)]
    swap = lax.axis_index("core") == 1
    keep[...] = jnp.concatenate([mixed[:HALF], jnp.where(swap, late[1], late[0])], 1).astype(BF16)
    give[...] = jnp.concatenate([mixed[HALF:], jnp.where(swap, late[0], late[1])], 1).astype(BF16)


def out_kernel(tokens, own, arrived, w_own, w_other, embed_hbm, out, cam_embed, sem):
    load = pltpu.make_async_copy(embed_hbm, cam_embed, sem)
    load.start()
    swap = lax.axis_index("core") == 1
    mine, theirs = own[...].astype(F32), arrived[...].astype(F32)
    first = jnp.where(swap, theirs, mine)
    second = jnp.where(swap, mine, theirs)
    parts = []
    for start, end in ((0, 2 * PAIR), (2 * PAIR, 3 * PAIR), (3 * PAIR, 4 * PAIR)):
        parts += [first[:, start:end], second[:, start:end]]
    mixed = jnp.concatenate(parts, 1).astype(BF16)
    one, two = mm_t(mixed, w_own[...]), mm_t(mixed, w_other[...])
    update = jnp.concatenate([jnp.where(swap, two, one), jnp.where(swap, one, two)], 1)
    load.wait()
    out[...] = (tokens[...].astype(F32) + own_embed(cam_embed) + update).astype(BF16)


def call(kernel, out_shapes, args, scratch=(), flops=0, anys=0, room=VMEM_LIMIT):
    vmem = pl.BlockSpec(memory_space=pltpu.VMEM)
    hbm = pl.BlockSpec(memory_space=pltpu.HBM)
    specs = []
    for i in range(len(args)):
        specs.append(hbm if i >= len(args) - anys else vmem)

    def place(out):
        return hbm if getattr(out, "memory_space", None) == pltpu.HBM else vmem

    single = not isinstance(out_shapes, tuple)
    return pl.pallas_call(
        kernel,
        out_shape=out_shapes,
        in_specs=specs,
        out_specs=place(out_shapes) if single else tuple(place(out) for out in out_shapes),
        scratch_shapes=list(scratch),
        compiler_params=pltpu.CompilerParams(vmem_limit_bytes=room),
        cost_estimate=pl.CostEstimate(flops=flops, bytes_accessed=1, transcendentals=0),
    )(*args)


def shape(*dims):
    return jax.ShapeDtypeStruct(dims, BF16)


def far(*dims):
    return pltpu.HBM(dims, BF16)


def near(*dims):
    return pltpu.VMEM(dims, BF16)


def keep_near(array):
    return pltpu.with_memory_space_constraint(array, pltpu.VMEM)


def stay(array):
    return pltpu.with_memory_space_constraint(array, pltpu.HBM)


def local(frames_in, cam_embed, norm_gain, q_gain, k_gain, w_qkv, w_out):
    tokens = frames_in[0]
    core = lax.axis_index("core")
    gain = norm_gain[None]
    both = jnp.stack([q_gain.reshape(HEADS, HD), k_gain.reshape(HEADS, HD)], 1)

    def gains_of(head, count):
        return lax.dynamic_slice_in_dim(both, head, count, 0)

    pair_gains = jnp.stack([gains_of(8 + 2 * core, 2), gains_of(12 + 2 * core, 2)])
    pair_gains = pair_gains.transpose(0, 2, 1, 3).reshape(2, 2 * PAIR)
    space_gains = gains_of(4 * core, 4).reshape(4, PAIR)
    gains = jnp.concatenate([pair_gains, jnp.pad(space_gains, ((0, 2), (0, PAIR)))], 0)

    pieces = call(
        pack_kernel,
        shape(64, PIECE, 128),
        (tokens, w_qkv, w_out),
        [
            pltpu.VMEM((18, 3 * D), BF16),
            pltpu.VMEM((18, D), BF16),
            pltpu.VMEM((16, 48, 128), F32),
            pltpu.SemaphoreType.DMA((2,)),
        ],
        0,
        2,
        58 * 1024 * 1024,
    )
    got = lax.all_to_all(pieces, SLAB, 0, 0, tiled=True)
    other = swap_core(tokens)
    normed = keep_near(call(norm_kernel, near(ROWS, D), (tokens, other, cam_embed, gain), (), 8 * 10**9))
    own_block, block, time_own = call(
        unpack_kernel,
        (near(QUAD, D), far(QUAD, D), far(HALF, D)),
        (after(got, normed, gains),),
        [
            pltpu.VMEM((HALF, D), BF16),
            pltpu.VMEM((3, D, 128), F32),
            pltpu.SemaphoreType.DMA((2,)),
        ],
    )
    blocks = (keep_near(own_block),) + tuple(lax.ppermute(block, EVERY, r) for r in ROUTES)
    time_other = swap_core(time_own)
    time_normed = keep_near(call(norm_kernel, near(ROWS, D), (time_own, time_other, cam_embed, gain), (), 8 * 10**9))
    q_t, kv_t, w_own, early, late = call(
        cross_project_kernel,
        (far(PAIR, ROWS), shape(2 * PAIR, ROWS), near(4 * PAIR, D), near(2, QUAD, D), far(4, QUAD, D)),
        (gains, after(normed, time_normed)) + blocks,
        [pltpu.VMEM((PAIR, ROWS), BF16), pltpu.VMEM((2, QUAD, D), BF16), pltpu.SemaphoreType.DMA((13,))],
        0,
        8,
    )
    kv_a = lax.ppermute(kv_t, EVERY, ACROSS)
    w_other = swap_core(w_own)
    timed = call(time_kernel, shape(32, 16, PAIR), (gains, after(time_normed, kv_t), keep_near(early)))
    kv_b = lax.ppermute(after(kv_a, timed), EVERY, ALONG)
    space = call(
        space_kernel,
        far(2 * PAIR, ROWS),
        (gains, stay(after(normed, timed)), stay(late)),
        [
            pltpu.VMEM((ROWS, D), BF16),
            pltpu.VMEM((2 * PAIR, ROWS), BF16),
            pltpu.VMEM((4, QUAD, D), BF16),
            pltpu.SemaphoreType.DMA((6,)),
        ],
        16 * 10**9,
        2,
    )
    returned = lax.all_to_all(timed, CHIP, 0, 0, tiled=True)
    keep, give = call(
        cross_kernel,
        (shape(HALF, 4 * PAIR), shape(HALF, 4 * PAIR)),
        (kv_a, kv_b, returned, stay(space), stay(q_t)),
        [pltpu.VMEM((2 * PAIR, ROWS), BF16), pltpu.VMEM((PAIR, ROWS), BF16), pltpu.SemaphoreType.DMA((2,))],
        0,
        2,
    )
    arrived = swap_core(give)
    return call(
        out_kernel,
        shape(HALF, D),
        (tokens, keep, arrived, w_own, w_other, stay(cam_embed)),
        [pltpu.VMEM((8, D), F32), pltpu.SemaphoreType.DMA],
        0,
        1,
    )[None]


def solution(mesh):
    fine = Mesh(mesh.devices.reshape(4, 2, 4, 8, 2), EVERY)
    placed = (P(CAM, SLAB, None), P(), P(), P(), P(), P(SLAB, None), P(SLAB, None))
    return jax.shard_map(local, mesh=fine, in_specs=placed, out_specs=P(CAM, SLAB, None), check_vma=False)
```

time: 147 us -> 143 us (0.973)
  starting transfers between devices: 72.6 us -> 66.5 us
  waiting for transfers between devices: 40 us -> 45.8 us
  Pallas kernels: 30.9 us -> 25.9 us
  local copies, waits for them, and re-layouts: 1.51 us -> 3.33 us
    pallas_call x8 -> x9, Pallas kernels: 30.9 us -> 25.9 us  [call(): pl.pallas_call(kernel, out_shape=out_shapes, in_specs=specs, out_specs=pl...]
    ppermute x4, starting transfers between devices: 18.3 us -> 14.6 us  [swap_core(): return lax.ppermute(block, 'core', [(0, 1), (1, 0)])]
    ppermute x7, waiting for transfers between devices: 4.58 us -> 7.87 us  [local(): lax.ppermute(block, EVERY, r)]
    ppermute x1, waiting for transfers between devices: 0.47 us -> 3.15 us  [local(): kv_a = lax.ppermute(kv_t, EVERY, ACROSS)]
    all_to_all x1, starting transfers between devices: 8.44 us -> 6.42 us  [local(): returned = lax.all_to_all(timed, CHIP, 0, 0, tiled=True)]
    unnamed x26 -> x18, local copies, waits for them, and re-layouts: 1.14 us -> 2.97 us
  transfers between devices with their start and end apart: 15 -> 15, of which waited for: 6 -> 8; matrix products, arithmetic and copies ran while one was open for 0% -> 0% of each run, Pallas kernels for 16% -> 10%
where the time goes in v7:
time: 143 us; the launch traced here: 142 us
  starting transfers between devices  66.5 us (47%)
  waiting for transfers between devices  45.8 us (32%)
  Pallas kernels  25.9 us (18%)
  local copies, waits for them, and re-layouts  3.33 us (2%)
    all_to_all x1, waiting for transfers between devices, local(): got = lax.all_to_all(pieces, SLAB, 0, 0, tiled=True)  30 us
    pallas_call x9, Pallas kernels, call(): pl.pallas_call(kernel, out_shape=out_shapes, in_specs=specs, out_specs=pl...  25.9 us
    ppermute x7, starting transfers between devices, local(): lax.ppermute(block, EVERY, r)  22.2 us
    all_to_all x1, starting transfers between devices, local(): got = lax.all_to_all(pieces, SLAB, 0, 0, tiled=True)  15.6 us
    ppermute x4, starting transfers between devices, swap_core(): return lax.ppermute(block, 'core', [(0, 1), (1, 0)])  14.6 us
    ppermute x7, waiting for transfers between devices, local(): lax.ppermute(block, EVERY, r)  7.87 us
    all_to_all x1, starting transfers between devices, local(): returned = lax.all_to_all(timed, CHIP, 0, 0, tiled=True)  6.42 us
    ppermute x1, starting transfers between devices, local(): kv_a = lax.ppermute(kv_t, EVERY, ACROSS)  5.04 us
  transfers between devices with their start and end apart: 15, of which 8 were waited for; matrix products, arithmetic and copies ran while one was open for 0% of the time, Pallas kernels for 10%

profile of v7, /device:TPU:1, one launch (start us, length us, event | category | flops | bytes accessed | tf_op | source)
XLA Modules:
  0.0 142.0 jit_solution(11326192304313108263)
XLA Ops:
  0.0 3.8 %shard_map.74 = bf16[64,88,128]{2,1,0:T(8,128)(2,1)} custom-call(bf16[256,1152]{1,0:T(8,128)(2,1)} %bitcast.8, bf16[18,3456]{1,0:T(8,128)(2,1)} %w_qkv_hbm.1, bf16[18,1152]{1,0:T(8,128)(2,1)} %w_out_hbm.1), custom_call_target="tpu_custom_call" | custom-call | bytes 1 | tf_op jit(solution)/shard_map/pallas_call | solution.py:326
  3.8 0.0 copy-start
  3.8 0.0 copy-start.6
  3.8 0.0 copy-start.7
  3.8 0.0 copy-start.8
  3.8 0.0 copy-start.2
  3.8 15.6 %all-to-all-start = ((bf16[64,88,128]{2,1,0:T(8,128)(2,1)}), bf16[64,88,128]{2,1,0:T(8,128)(2,1)S(1)}, u32[]{:S(2)}, u32[]{:S(2)}) async-start(bf16[64,88,128]{2,1,0:T(8,128)(2,1)} %shard_map.74), calls=%async_computation | async-start | bytes 2883584 | tf_op jit(solution)/shard_map/all_to_all | solution.py:385
  19.4 2.4 %collective-permute-start = (bf16[256,1152]{1,0:T(8,128)(2,1)S(1)}, bf16[256,1152]{1,0:T(8,128)(2,1)S(1)}, u32[]{:S(2)}, u32[]{:S(2)}) collective-permute-start(bf16[256,1152]{1,0:T(8,128)(2,1)S(1)} %bitcast.9), channel_id=1, source_target_pairs={{0,1},{1,0},{2,3},{3,2},{4,5},{5,4},{6,7},{7,6},{8,9},{9,8},{10,11... | collective-permute-start | bytes 1769480 | tf_op jit(solution)/shard_map/ppermute | solution.py:59
  21.8 0.1 stack_reshape.6
  21.9 0.1 stack_reshape.7
  22.1 0.1 reshape.7
  22.2 0.1 reshape.6
  22.3 1.1 collective-permute-done.other
  23.4 0.8 copy-done.3
  24.2 1.1 copy-done.4
  25.3 0.8 shard_map.73.normed.normed_hbm
  26.1 30.0 %all-to-all-done.got = bf16[64,88,128]{2,1,0:T(8,128)(2,1)S(1)} async-done(((bf16[64,88,128]{2,1,0:T(8,128)(2,1)}), bf16[64,88,128]{2,1,0:T(8,128)(2,1)S(1)}, u32[]{:S(2)}, u32[]{:S(2)}) %all-to-all-start) | async-done | bytes 1441824 | tf_op jit(solution)/shard_map/all_to_all | solution.py:385
  56.1 1.6 %shard_map.75 = (bf16[288,1152]{1,0:T(8,128)(2,1)S(1)}, bf16[288,1152]{1,0:T(8,128)(2,1)}, bf16[256,1152]{1,0:T(8,128)(2,1)}) custom-call(bf16[64,88,128]{2,1,0:T(8,128)(2,1)S(1)} %all-to-all-done.got), custom_call_target="tpu_custom_call" | custom-call | bytes 1 | tf_op jit(solution)/shard_map/pallas_call | solution.py:326
  57.6 4.4 %collective-permute-start.8 = (bf16[288,1152]{1,0:T(8,128)(2,1)}, bf16[288,1152]{1,0:T(8,128)(2,1)S(1)}, u32[]{:S(2)}, u32[]{:S(2)}) collective-permute-start(bf16[288,1152]{1,0:T(8,128)(2,1)} %get-tuple-element.24), channel_id=1, source_target_pairs={{0,128},{1,385},{2,130},{3,387},{4,132},{5,389},{6,134},{7,391},{8... | collective-permute-start | bytes 1990664 | tf_op jit(solution)/shard_map/ppermute | solution.py:398
  62.0 4.1 %collective-permute-start.7 = (bf16[288,1152]{1,0:T(8,128)(2,1)}, bf16[288,1152]{1,0:T(8,128)(2,1)S(1)}, u32[]{:S(2)}, u32[]{:S(2)}) collective-permute-start(bf16[288,1152]{1,0:T(8,128)(2,1)} %get-tuple-element.24), channel_id=1, source_target_pairs={{0,126},{1,19},{2,112},{3,21},{4,114},{5,23},{6,116},{7,25},{8,118... | collective-permute-start | bytes 1990664 | tf_op jit(solution)/shard_map/ppermute | solution.py:398
  66.2 4.7 %collective-permute-start.1 = (bf16[256,1152]{1,0:T(8,128)(2,1)}, bf16[256,1152]{1,0:T(8,128)(2,1)S(1)}, u32[]{:S(2)}, u32[]{:S(2)}) collective-permute-start(bf16[256,1152]{1,0:T(8,128)(2,1)} %get-tuple-element.21.own), channel_id=1, source_target_pairs={{0,1},{1,0},{2,3},{3,2},{4,5},{5,4},{6,7},{7,6},{8,9},{9,8},{10,11... | collective-permute-start | bytes 1769480 | tf_op jit(solution)/shard_map/ppermute | solution.py:59
  70.8 1.9 %collective-permute-start.6 = (bf16[288,1152]{1,0:T(8,128)(2,1)}, bf16[288,1152]{1,0:T(8,128)(2,1)S(1)}, u32[]{:S(2)}, u32[]{:S(2)}) collective-permute-start(bf16[288,1152]{1,0:T(8,128)(2,1)} %get-tuple-element.24), channel_id=1, source_target_pairs={{0,16},{1,113},{2,18},{3,115},{4,20},{5,117},{6,22},{7,119},{8,24}... | collective-permute-start | bytes 1990664 | tf_op jit(solution)/shard_map/ppermute | solution.py:398
  72.8 2.2 %collective-permute-start.5 = (bf16[288,1152]{1,0:T(8,128)(2,1)}, bf16[288,1152]{1,0:T(8,128)(2,1)S(1)}, u32[]{:S(2)}, u32[]{:S(2)}) collective-permute-start(bf16[288,1152]{1,0:T(8,128)(2,1)} %get-tuple-element.24), channel_id=1, source_target_pairs={{0,2},{1,15},{2,4},{3,1},{4,6},{5,3},{6,8},{7,5},{8,10},{9,7},{10,... | collective-permute-start | bytes 1990664 | tf_op jit(solution)/shard_map/ppermute | solution.py:398
  74.9 0.0 collective-permute-done.1.other
  75.0 3.1 %collective-permute-start.4 = (bf16[288,1152]{1,0:T(8,128)(2,1)}, bf16[288,1152]{1,0:T(8,128)(2,1)S(1)}, u32[]{:S(2)}, u32[]{:S(2)}) collective-permute-start(bf16[288,1152]{1,0:T(8,128)(2,1)} %get-tuple-element.24), channel_id=1, source_target_pairs={{0,384},{1,129},{2,386},{3,131},{4,388},{5,133},{6,390},{7,135},{8... | collective-permute-start | bytes 1990664 | tf_op jit(solution)/shard_map/ppermute | solution.py:398
  78.1 3.4 %collective-permute-start.3 = (bf16[288,1152]{1,0:T(8,128)(2,1)}, bf16[288,1152]{1,0:T(8,128)(2,1)S(1)}, u32[]{:S(2)}, u32[]{:S(2)}) collective-permute-start(bf16[288,1152]{1,0:T(8,128)(2,1)} %get-tuple-element.24), channel_id=1, source_target_pairs={{0,112},{1,17},{2,114},{3,19},{4,116},{5,21},{6,118},{7,23},{8,120... | collective-permute-start | bytes 1990664 | tf_op jit(solution)/shard_map/ppermute | solution.py:398
  81.5 3.1 %collective-permute-start.2 = (bf16[288,1152]{1,0:T(8,128)(2,1)}, bf16[288,1152]{1,0:T(8,128)(2,1)S(1)}, u32[]{:S(2)}, u32[]{:S(2)}) collective-permute-start(bf16[288,1152]{1,0:T(8,128)(2,1)} %get-tuple-element.24), channel_id=1, source_target_pairs={{0,14},{1,3},{2,0},{3,5},{4,2},{5,7},{6,4},{7,9},{8,6},{9,11},{10,... | collective-permute-start | bytes 1990664 | tf_op jit(solution)/shard_map/ppermute | solution.py:398
  84.6 0.0 copy-start.5
  84.6 1.1 copy-done.5
  85.6 0.8 shard_map.76.normed
  86.4 0.0 collective-permute-done.6.refs_5_
  86.4 0.0 collective-permute-done.5.refs_4_
  86.4 1.3 collective-permute-done.4.refs_3_
  87.8 3.4 %collective-permute-done.3.refs_2_ = bf16[288,1152]{1,0:T(8,128)(2,1)S(1)} collective-permute-done((bf16[288,1152]{1,0:T(8,128)(2,1)}, bf16[288,1152]{1,0:T(8,128)(2,1)S(1)}, u32[]{:S(2)}, u32[]{:S(2)}) %collective-permute-start.3) | collective-permute-done | bytes 663584 | tf_op jit(solution)/shard_map/ppermute | solution.py:398
  91.2 3.1 %collective-permute-done.2.refs_1_ = bf16[288,1152]{1,0:T(8,128)(2,1)S(1)} collective-permute-done((bf16[288,1152]{1,0:T(8,128)(2,1)}, bf16[288,1152]{1,0:T(8,128)(2,1)S(1)}, u32[]{:S(2)}, u32[]{:S(2)}) %collective-permute-start.2) | collective-permute-done | bytes 663584 | tf_op jit(solution)/shard_map/ppermute | solution.py:398
  94.3 3.9 %shard_map.77 = (bf16[144,512]{1,0:T(8,128)(2,1)}, bf16[288,512]{1,0:T(8,128)(2,1)}, bf16[576,1152]{1,0:T(8,128)(2,1)S(1)}, bf16[2,288,1152]{2,1,0:T(8,128)(2,1)S(1)}, bf16[4,288,1152]{2,1,0:T(8,128)(2,1)}) custom-call(f32[8,288]{1,0:T(8,128)S(1)} %select_maximum_fusion.gains, bf16[512,1152]{1,0:T(8,128)(2,1)S(1)} %shard_map.73.normed.normed_hbm, ...), custom_call_target="tpu_custom_call" | custom-call | bytes 1 | tf_op jit(solution)/shard_map/pallas_call | solution.py:326
  98.2 5.0 %collective-permute-start.9 = (bf16[288,512]{1,0:T(8,128)(2,1)}, bf16[288,512]{1,0:T(8,128)(2,1)}, u32[]{:S(2)}, u32[]{:S(2)}) collective-permute-start(bf16[288,512]{1,0:T(8,128)(2,1)} %get-tuple-element.25), channel_id=1, source_target_pairs={{0,64},{1,65},{2,66},{3,67},{4,68},{5,69},{6,70},{7,71},{8,72},{9,... | collective-permute-start | bytes 884744 | tf_op jit(solution)/shard_map/ppermute | solution.py:409
  103.3 2.8 %shard_map.78 = bf16[32,16,144]{2,1,0:T(8,128)(2,1)} custom-call(f32[8,288]{1,0:T(8,128)S(1)} %select_maximum_fusion.gains, bf16[512,1152]{1,0:T(8,128)(2,1)S(1)} %shard_map.76.normed, bf16[2,288,1152]{2,1,0:T(8,128)(2,1)S(1)} %get-tuple-element.27.weight), custom_call_target="tpu_custom_call" | custom-call | bytes 1 | tf_op jit(solution)/shard_map/pallas_call | solution.py:326
  106.1 6.4 %all-to-all-start.1 = ((bf16[32,16,144]{2,1,0:T(8,128)(2,1)}), bf16[32,16,144]{2,1,0:T(8,128)(2,1)}, u32[]{:S(2)}, u32[]{:S(2)}) async-start(bf16[32,16,144]{2,1,0:T(8,128)(2,1)} %shard_map.78), calls=%async_computation.1 | async-start | bytes 524288 | tf_op jit(solution)/shard_map/all_to_all | solution.py:426
  112.5 3.7 %collective-permute-start.12 = (bf16[576,1152]{1,0:T(8,128)(2,1)S(1)}, bf16[576,1152]{1,0:T(8,128)(2,1)S(1)}, u32[]{:S(2)}, u32[]{:S(2)}) collective-permute-start(bf16[576,1152]{1,0:T(8,128)(2,1)S(1)} %get-tuple-element.34.w_own), channel_id=1, source_target_pairs={{0,1},{1,0},{2,3},{3,2},{4,5},{5,4},{6,7},{7,6},{8,9},{9,8},{10,11... | collective-permute-start | bytes 3981320 | tf_op jit(solution)/shard_map/ppermute | solution.py:59
  116.3 3.1 %collective-permute-done.9.kv_a = bf16[288,512]{1,0:T(8,128)(2,1)} collective-permute-done((bf16[288,512]{1,0:T(8,128)(2,1)}, bf16[288,512]{1,0:T(8,128)(2,1)}, u32[]{:S(2)}, u32[]{:S(2)}) %collective-permute-start.9) | collective-permute-done | bytes 294944 | tf_op jit(solution)/shard_map/ppermute | solution.py:409
  119.4 2.6 %collective-permute-start.10 = (bf16[288,512]{1,0:T(8,128)(2,1)}, bf16[288,512]{1,0:T(8,128)(2,1)}, u32[]{:S(2)}, u32[]{:S(2)}) collective-permute-start(bf16[288,512]{1,0:T(8,128)(2,1)} %collective-permute-done.9.kv_a), channel_id=1, source_target_pairs={{0,128},{1,129},{2,130},{3,131},{4,132},{5,133},{6,134},{7,135},{8... | collective-permute-start | bytes 884744 | tf_op jit(solution)/shard_map/ppermute | solution.py:412
  122.1 5.8 %shard_map.79.space_hbm = bf16[288,512]{1,0:T(8,128)(2,1)} custom-call(f32[8,288]{1,0:T(8,128)S(1)} %select_maximum_fusion.gains, bf16[512,1152]{1,0:T(8,128)(2,1)} %copy-done.1, bf16[4,288,1152]{2,1,0:T(8,128)(2,1)} %get-tuple-element.30.weight_hbm), custom_call_target="tpu_custom_call" | custom-call | flops 16000000000 | bytes 1 | tf_op jit(solution)/shard_map/pallas_call | solution.py:326
  127.9 2.4 %collective-permute-done.10.kv_b = bf16[288,512]{1,0:T(8,128)(2,1)} collective-permute-done((bf16[288,512]{1,0:T(8,128)(2,1)}, bf16[288,512]{1,0:T(8,128)(2,1)}, u32[]{:S(2)}, u32[]{:S(2)}) %collective-permute-start.10) | collective-permute-done | bytes 294944 | tf_op jit(solution)/shard_map/ppermute | solution.py:412
  130.3 3.7 %shard_map.80 = (bf16[256,576]{1,0:T(8,128)(2,1)S(1)}, bf16[256,576]{1,0:T(8,128)(2,1)S(1)}) custom-call(bf16[288,512]{1,0:T(8,128)(2,1)} %collective-permute-done.9.kv_a, bf16[288,512]{1,0:T(8,128)(2,1)} %collective-permute-done.10.kv_b, bf16[32,16,144]{2,1,0:T(8,128)(2,1)} %all-to-all-done.1.timed, bf16[288,512]{1,0:T(8,128)(2,1)} %shard_map.79.space_hbm, ...), custom_call_target="tpu_custom_call" | custom-call | bytes 1 | tf_op jit(solution)/shard_map/pallas_call | solution.py:326
  134.0 3.9 %collective-permute-start.11 = (bf16[256,576]{1,0:T(8,128)(2,1)S(1)}, bf16[256,576]{1,0:T(8,128)(2,1)S(1)}, u32[]{:S(2)}, u32[]{:S(2)}) collective-permute-start(bf16[256,576]{1,0:T(8,128)(2,1)S(1)} %get-tuple-element.33), channel_id=1, source_target_pairs={{0,1},{1,0},{2,3},{3,2},{4,5},{5,4},{6,7},{7,6},{8,9},{9,8},{10,11... | collective-permute-start | bytes 884744 | tf_op jit(solution)/shard_map/ppermute | solution.py:59
  137.9 1.2 collective-permute-done.11.arrived
  139.1 2.8 %shard_map.81 = bf16[256,1152]{1,0:T(8,128)(2,1)} custom-call(bf16[256,1152]{1,0:T(8,128)(2,1)S(1)} %bitcast.11, bf16[256,576]{1,0:T(8,128)(2,1)S(1)} %get-tuple-element.32.own, bf16[256,576]{1,0:T(8,128)(2,1)S(1)} %collective-permute-done.11.arrived, bf16[576,1152]{1,0:T(8,128)(2,1)S(1)} %get-tuple-element.34.w_own, ...), custom_call_target="tpu_custom_call" | custom-call | bytes 1 | tf_op jit(solution)/shard_map/pallas_call | solution.py:326
  (19 shorter events, 0.1 us)
Async XLA Ops:
  3.8 15.6 %copy-start = (bf16[1,256,1152]{2,1,0:T(8,128)(2,1)S(1)}, bf16[1,256,1152]{2,1,0:T(8,128)(2,1)}, u32[]{:S(2)}) copy-start(bf16[1,256,1152]{2,1,0:T(8,128)(2,1)} %param.7) | copy-start | bytes 1769476
  3.8 18.0 %copy-start.6 = (f32[1152]{0:T(1024)S(1)}, f32[1152]{0:T(1024)}, u32[]{:S(2)}) copy-start(f32[1152]{0:T(1024)} %param.9) | copy-start | bytes 13828
  3.8 18.0 %copy-start.7 = (f32[1152]{0:T(1024)S(1)}, f32[1152]{0:T(1024)}, u32[]{:S(2)}) copy-start(f32[1152]{0:T(1024)} %param.10) | copy-start | bytes 13828
  3.8 18.1 %copy-start.8 = (f32[1152]{0:T(1024)S(1)}, f32[1152]{0:T(1024)}, u32[]{:S(2)}) copy-start(f32[1152]{0:T(1024)} %param.11) | copy-start | bytes 13828
  3.8 20.4 %copy-start.2 = (f32[8,1152]{1,0:T(8,128)S(1)}, f32[8,1152]{1,0:T(8,128)}, u32[]{:S(2)}) copy-start(f32[8,1152]{1,0:T(8,128)} %embed_hbm.1) | copy-start | bytes 110596
  3.8 52.2 %all-to-all-start = ((bf16[64,88,128]{2,1,0:T(8,128)(2,1)}), bf16[64,88,128]{2,1,0:T(8,128)(2,1)S(1)}, u32[]{:S(2)}, u32[]{:S(2)}) async-start(bf16[64,88,128]{2,1,0:T(8,128)(2,1)} %shard_map.74), calls=%async_computation | async-start | bytes 2883584 | tf_op jit(solution)/shard_map/all_to_all | solution.py:385
  19.4 4.0 %collective-permute-start = (bf16[256,1152]{1,0:T(8,128)(2,1)S(1)}, bf16[256,1152]{1,0:T(8,128)(2,1)S(1)}, u32[]{:S(2)}, u32[]{:S(2)}) collective-permute-start(bf16[256,1152]{1,0:T(8,128)(2,1)S(1)} %bitcast.9), channel_id=1, source_target_pairs={{0,1},{1,0},{2,3},{3,2},{4,5},{5,4},{6,7},{7,6},{8,9},{9,8},{10,11... | collective-permute-start | bytes 1769480 | tf_op jit(solution)/shard_map/ppermute | solution.py:59
  23.4 0.8 copy-start.3
  24.2 1.1 copy-start.4
  26.1 68.3 %copy-start.1 = (bf16[512,1152]{1,0:T(8,128)(2,1)}, bf16[512,1152]{1,0:T(8,128)(2,1)S(1)}, u32[]{:S(2)}) copy-start(bf16[512,1152]{1,0:T(8,128)(2,1)S(1)} %shard_map.73.normed.normed_hbm) | copy-start | bytes 3538948
  57.6 20.5 %collective-permute-start.8 = (bf16[288,1152]{1,0:T(8,128)(2,1)}, bf16[288,1152]{1,0:T(8,128)(2,1)S(1)}, u32[]{:S(2)}, u32[]{:S(2)}) collective-permute-start(bf16[288,1152]{1,0:T(8,128)(2,1)} %get-tuple-element.24), channel_id=1, source_target_pairs={{0,128},{1,385},{2,130},{3,387},{4,132},{5,389},{6,134},{7,391},{8... | collective-permute-start | bytes 1990664 | tf_op jit(solution)/shard_map/ppermute | solution.py:398
  62.0 19.4 %collective-permute-start.7 = (bf16[288,1152]{1,0:T(8,128)(2,1)}, bf16[288,1152]{1,0:T(8,128)(2,1)S(1)}, u32[]{:S(2)}, u32[]{:S(2)}) collective-permute-start(bf16[288,1152]{1,0:T(8,128)(2,1)} %get-tuple-element.24), channel_id=1, source_target_pairs={{0,126},{1,19},{2,112},{3,21},{4,114},{5,23},{6,116},{7,25},{8,118... | collective-permute-start | bytes 1990664 | tf_op jit(solution)/shard_map/ppermute | solution.py:398
  66.2 8.8 %collective-permute-start.1 = (bf16[256,1152]{1,0:T(8,128)(2,1)}, bf16[256,1152]{1,0:T(8,128)(2,1)S(1)}, u32[]{:S(2)}, u32[]{:S(2)}) collective-permute-start(bf16[256,1152]{1,0:T(8,128)(2,1)} %get-tuple-element.21.own), channel_id=1, source_target_pairs={{0,1},{1,0},{2,3},{3,2},{4,5},{5,4},{6,7},{7,6},{8,9},{9,8},{10,11... | collective-permute-start | bytes 1769480 | tf_op jit(solution)/shard_map/ppermute | solution.py:59
  70.8 15.6 %collective-permute-start.6 = (bf16[288,1152]{1,0:T(8,128)(2,1)}, bf16[288,1152]{1,0:T(8,128)(2,1)S(1)}, u32[]{:S(2)}, u32[]{:S(2)}) collective-permute-start(bf16[288,1152]{1,0:T(8,128)(2,1)} %get-tuple-element.24), channel_id=1, source_target_pairs={{0,16},{1,113},{2,18},{3,115},{4,20},{5,117},{6,22},{7,119},{8,24}... | collective-permute-start | bytes 1990664 | tf_op jit(solution)/shard_map/ppermute | solution.py:398
  72.8 13.7 %collective-permute-start.5 = (bf16[288,1152]{1,0:T(8,128)(2,1)}, bf16[288,1152]{1,0:T(8,128)(2,1)S(1)}, u32[]{:S(2)}, u32[]{:S(2)}) collective-permute-start(bf16[288,1152]{1,0:T(8,128)(2,1)} %get-tuple-element.24), channel_id=1, source_target_pairs={{0,2},{1,15},{2,4},{3,1},{4,6},{5,3},{6,8},{7,5},{8,10},{9,7},{10,... | collective-permute-start | bytes 1990664 | tf_op jit(solution)/shard_map/ppermute | solution.py:398
  75.0 12.8 %collective-permute-start.4 = (bf16[288,1152]{1,0:T(8,128)(2,1)}, bf16[288,1152]{1,0:T(8,128)(2,1)S(1)}, u32[]{:S(2)}, u32[]{:S(2)}) collective-permute-start(bf16[288,1152]{1,0:T(8,128)(2,1)} %get-tuple-element.24), channel_id=1, source_target_pairs={{0,384},{1,129},{2,386},{3,131},{4,388},{5,133},{6,390},{7,135},{8... | collective-permute-start | bytes 1990664 | tf_op jit(solution)/shard_map/ppermute | solution.py:398
  78.1 13.2 %collective-permute-start.3 = (bf16[288,1152]{1,0:T(8,128)(2,1)}, bf16[288,1152]{1,0:T(8,128)(2,1)S(1)}, u32[]{:S(2)}, u32[]{:S(2)}) collective-permute-start(bf16[288,1152]{1,0:T(8,128)(2,1)} %get-tuple-element.24), channel_id=1, source_target_pairs={{0,112},{1,17},{2,114},{3,19},{4,116},{5,21},{6,118},{7,23},{8,120... | collective-permute-start | bytes 1990664 | tf_op jit(solution)/shard_map/ppermute | solution.py:398
  81.5 12.8 %collective-permute-start.2 = (bf16[288,1152]{1,0:T(8,128)(2,1)}, bf16[288,1152]{1,0:T(8,128)(2,1)S(1)}, u32[]{:S(2)}, u32[]{:S(2)}) collective-permute-start(bf16[288,1152]{1,0:T(8,128)(2,1)} %get-tuple-element.24), channel_id=1, source_target_pairs={{0,14},{1,3},{2,0},{3,5},{4,2},{5,7},{6,4},{7,9},{8,6},{9,11},{10,... | collective-permute-start | bytes 1990664 | tf_op jit(solution)/shard_map/ppermute | solution.py:398
  84.6 1.1 copy-start.5
  98.2 21.2 %collective-permute-start.9 = (bf16[288,512]{1,0:T(8,128)(2,1)}, bf16[288,512]{1,0:T(8,128)(2,1)}, u32[]{:S(2)}, u32[]{:S(2)}) collective-permute-start(bf16[288,512]{1,0:T(8,128)(2,1)} %get-tuple-element.25), channel_id=1, source_target_pairs={{0,64},{1,65},{2,66},{3,67},{4,68},{5,69},{6,70},{7,71},{8,72},{9,... | collective-permute-start | bytes 884744 | tf_op jit(solution)/shard_map/ppermute | solution.py:409
  106.1 21.7 %all-to-all-start.1 = ((bf16[32,16,144]{2,1,0:T(8,128)(2,1)}), bf16[32,16,144]{2,1,0:T(8,128)(2,1)}, u32[]{:S(2)}, u32[]{:S(2)}) async-start(bf16[32,16,144]{2,1,0:T(8,128)(2,1)} %shard_map.78), calls=%async_computation.1 | async-start | bytes 524288 | tf_op jit(solution)/shard_map/all_to_all | solution.py:426
  112.5 26.6 %collective-permute-start.12 = (bf16[576,1152]{1,0:T(8,128)(2,1)S(1)}, bf16[576,1152]{1,0:T(8,128)(2,1)S(1)}, u32[]{:S(2)}, u32[]{:S(2)}) collective-permute-start(bf16[576,1152]{1,0:T(8,128)(2,1)S(1)} %get-tuple-element.34.w_own), channel_id=1, source_target_pairs={{0,1},{1,0},{2,3},{3,2},{4,5},{5,4},{6,7},{7,6},{8,9},{9,8},{10,11... | collective-permute-start | bytes 3981320 | tf_op jit(solution)/shard_map/ppermute | solution.py:59
  119.4 10.9 %collective-permute-start.10 = (bf16[288,512]{1,0:T(8,128)(2,1)}, bf16[288,512]{1,0:T(8,128)(2,1)}, u32[]{:S(2)}, u32[]{:S(2)}) collective-permute-start(bf16[288,512]{1,0:T(8,128)(2,1)} %collective-permute-done.9.kv_a), channel_id=1, source_target_pairs={{0,128},{1,129},{2,130},{3,131},{4,132},{5,133},{6,134},{7,135},{8... | collective-permute-start | bytes 884744 | tf_op jit(solution)/shard_map/ppermute | solution.py:412
  134.0 5.1 %collective-permute-start.11 = (bf16[256,576]{1,0:T(8,128)(2,1)S(1)}, bf16[256,576]{1,0:T(8,128)(2,1)S(1)}, u32[]{:S(2)}, u32[]{:S(2)}) collective-permute-start(bf16[256,576]{1,0:T(8,128)(2,1)S(1)} %get-tuple-element.33), channel_id=1, source_target_pairs={{0,1},{1,0},{2,3},{3,2},{4,5},{5,4},{6,7},{7,6},{8,9},{9,8},{10,11... | collective-permute-start | bytes 884744 | tf_op jit(solution)/shard_map/ppermute | solution.py:59

commit v8 on v7

--- a/solution.py
+++ b/solution.py
@@ -13,7 +13,7 @@
 QUAD = 4 * HD
 HALF = 256
 ROWS = 2 * HALF
-PIECE = 88
+PIECE = 80
 LATE = (6, 7, 2, 3)
 CAM = ("x", "yh")
 CHIP = ("yl", "z")
@@ -41,7 +41,7 @@
     return 1 if core else -1
 
 
-OFFSETS = ((0, 0, 1), (0, 1, 0), (1, 0, 0), (0, 0, -1), (0, -1, 0), (0, 1, 1), (-1, 0, 0))
+OFFSETS = ((-1, 0, 0), (0, 1, 1), (0, -1, 0), (0, 0, -1), (1, 0, 0), (0, 1, 0), (0, 0, 1))
 TURNS = (0,) + tuple((2 * a + b + 3 * c) % 8 for a, b, c in OFFSETS)
 
 
@@ -110,9 +110,9 @@
             place = who * 8 + colour
             pieces[place, :18] = whole[:, :128]
             pieces[place, 18:36] = whole[:, 128:256]
-            tail = jnp.concatenate([whole[:9, 256:], whole[9:, 256:], jnp.zeros((9, 64), F32)], 1)
-            pieces[place, 36:45] = tail
-            pieces[place, 45:] = jnp.zeros((3, 128), F32)
+            tail = whole[:, 256:]
+            pieces[place, 36:41] = jnp.concatenate([tail[:5], tail[5:10], tail[9:14], tail[13:18]], 1)
+            pieces[place, 41:] = jnp.zeros((3, 128), F32)
     x, yh = position()[:2]
     base = 2 * x + 4 * yh
     for dest in range(64):
@@ -120,7 +120,7 @@
         block = tokens[dest // 2 * 8 : dest // 2 * 8 + 8].astype(F32)
         block = block[dest % 2 * 4 : dest % 2 * 4 + 4]
         rows = [block[:, tile * 128 : tile * 128 + 128] for tile in range(9)]
-        rows = [pieces[dest % 2 * 8 + colour]] + rows + [jnp.zeros((PIECE - 84, 128), F32)]
+        rows = [pieces[dest % 2 * 8 + colour]] + rows
         out[dest] = jnp.concatenate(rows, 0).astype(BF16)
 
 
@@ -130,13 +130,15 @@
         at = source * 18
         wide[0, at : at + 18] = rows[:18]
         wide[1, at : at + 18] = rows[18:36]
-        wide[2, at : at + 9, :32] = rows[36:45, :32]
-        wide[2, at + 9 : at + 18, :32] = rows[36:45, 32:64]
+        wide[2, at : at + 5, :32] = rows[36:41, :32]
+        wide[2, at + 5 : at + 10, :32] = rows[36:41, 32:64]
+        wide[2, at + 10 : at + 14, :32] = rows[37:41, 64:96]
+        wide[2, at + 14 : at + 18, :32] = rows[37:41, 96:]
         if source % 2 == 1:
             pair = [got[source - 1].astype(F32), rows]
             tiles = []
             for tile in range(9):
-                start = 48 + tile * 4
+                start = 44 + tile * 4
                 tiles.append(jnp.concatenate([one[start : start + 4] for one in pair], 0))
             tokens[source * 4 - 4 : source * 4 + 4] = jnp.concatenate(tiles, 1).astype(BF16)
     block[:128] = wide[0].T.astype(BF16)
@@ -375,7 +377,7 @@
         [
             pltpu.VMEM((18, 3 * D), BF16),
             pltpu.VMEM((18, D), BF16),
-            pltpu.VMEM((16, 48, 128), F32),
+            pltpu.VMEM((16, 44, 128), F32),
             pltpu.SemaphoreType.DMA((2,)),
         ],
         0,

time: 143 us -> 142 us (level)
  waiting for transfers between devices: 45.8 us -> 51.3 us
  starting transfers between devices: 66.5 us -> 62.2 us
    ppermute x7, waiting for transfers between devices: 7.87 us -> 12.9 us  [local(): lax.ppermute(block, EVERY, r)]
    all_to_all x1, waiting for transfers between devices: 30 us -> 28.1 us  [local(): got = lax.all_to_all(pieces, SLAB, 0, 0, tiled=True)]
    all_to_all x1, starting transfers between devices: 6.42 us -> 4.65 us  [local(): returned = lax.all_to_all(timed, CHIP, 0, 0, tiled=True)]
    ppermute x1, waiting for transfers between devices: 3.15 us -> 4.74 us  [local(): kv_a = lax.ppermute(kv_t, EVERY, ACROSS)]
    unnamed x18 -> x16, local copies, waits for them, and re-layouts: 2.97 us -> 2.11 us
  transfers between devices with their start and end apart: 15 -> 15, of which waited for: 8 -> 7; matrix products, arithmetic and copies ran while one was open for 0% -> 0% of each run, Pallas kernels for 10% -> 9%
where the time goes in v8:
time: 142 us
  starting transfers between devices  62.2 us (44%)
  waiting for transfers between devices  51.3 us (36%)
  Pallas kernels  25 us (18%)
  local copies, waits for them, and re-layouts  2.46 us (2%)
    all_to_all x1, waiting for transfers between devices, local(): got = lax.all_to_all(pieces, SLAB, 0, 0, tiled=True)  28.1 us
    pallas_call x9, Pallas kernels, call(): pl.pallas_call(kernel, out_shape=out_shapes, in_specs=specs, out_specs=pl...  25 us
    ppermute x7, starting transfers between devices, local(): lax.ppermute(block, EVERY, r)  21.2 us
    all_to_all x1, starting transfers between devices, local(): got = lax.all_to_all(pieces, SLAB, 0, 0, tiled=True)  15.6 us
    ppermute x4, starting transfers between devices, swap_core(): return lax.ppermute(block, 'core', [(0, 1), (1, 0)])  13.4 us
    ppermute x7, waiting for transfers between devices, local(): lax.ppermute(block, EVERY, r)  12.9 us
    ppermute x1, starting transfers between devices, local(): kv_a = lax.ppermute(kv_t, EVERY, ACROSS)  5.37 us
    ppermute x1, waiting for transfers between devices, local(): kv_a = lax.ppermute(kv_t, EVERY, ACROSS)  4.74 us
  transfers between devices with their start and end apart: 15, of which 7 were waited for; matrix products, arithmetic and copies ran while one was open for 0% of the time, Pallas kernels for 9%

profile of v8, /device:TPU:1, one launch (start us, length us, event | category | flops | bytes accessed | tf_op | source)
XLA Modules:
  0.0 141.6 jit_solution(3599749587222081477)
XLA Ops:
  0.0 3.8 %shard_map.74 = bf16[64,80,128]{2,1,0:T(8,128)(2,1)} custom-call(bf16[256,1152]{1,0:T(8,128)(2,1)} %bitcast.8, bf16[18,3456]{1,0:T(8,128)(2,1)} %w_qkv_hbm.1, bf16[18,1152]{1,0:T(8,128)(2,1)} %w_out_hbm.1), custom_call_target="tpu_custom_call" | custom-call | bytes 1 | tf_op jit(solution)/shard_map/pallas_call | solution.py:328
  3.8 0.0 copy-start
  3.9 0.0 copy-start.5
  3.9 0.0 copy-start.6
  3.9 0.0 copy-start.7
  3.9 0.0 copy-start.3
  3.9 15.6 %all-to-all-start = ((bf16[64,80,128]{2,1,0:T(8,128)(2,1)}), bf16[64,80,128]{2,1,0:T(8,128)(2,1)S(1)}, u32[]{:S(2)}, u32[]{:S(2)}) async-start(bf16[64,80,128]{2,1,0:T(8,128)(2,1)} %shard_map.74), calls=%async_computation | async-start | bytes 2621440 | tf_op jit(solution)/shard_map/all_to_all | solution.py:387
  19.5 2.4 %collective-permute-start = (bf16[256,1152]{1,0:T(8,128)(2,1)S(1)}, bf16[256,1152]{1,0:T(8,128)(2,1)S(1)}, u32[]{:S(2)}, u32[]{:S(2)}) collective-permute-start(bf16[256,1152]{1,0:T(8,128)(2,1)S(1)} %bitcast.9), channel_id=1, source_target_pairs={{0,1},{1,0},{2,3},{3,2},{4,5},{5,4},{6,7},{7,6},{8,9},{9,8},{10,11... | collective-permute-start | bytes 1769480 | tf_op jit(solution)/shard_map/ppermute | solution.py:59
  21.9 0.1 stack_reshape.6
  22.0 0.1 stack_reshape.7
  22.1 0.1 reshape.7
  22.2 0.1 reshape.6
  22.3 1.1 collective-permute-done.other
  23.5 0.8 shard_map.73.normed.normed_hbm
  24.3 1.0 copy-done.1
  25.3 28.1 %all-to-all-done.got = bf16[64,80,128]{2,1,0:T(8,128)(2,1)S(1)} async-done(((bf16[64,80,128]{2,1,0:T(8,128)(2,1)}), bf16[64,80,128]{2,1,0:T(8,128)(2,1)S(1)}, u32[]{:S(2)}, u32[]{:S(2)}) %all-to-all-start) | async-done | bytes 1310752 | tf_op jit(solution)/shard_map/all_to_all | solution.py:387
  53.4 1.6 %shard_map.75 = (bf16[288,1152]{1,0:T(8,128)(2,1)S(1)}, bf16[288,1152]{1,0:T(8,128)(2,1)}, bf16[256,1152]{1,0:T(8,128)(2,1)}) custom-call(bf16[64,80,128]{2,1,0:T(8,128)(2,1)S(1)} %all-to-all-done.got), custom_call_target="tpu_custom_call" | custom-call | bytes 1 | tf_op jit(solution)/shard_map/pallas_call | solution.py:328
  55.0 1.9 %collective-permute-start.8 = (bf16[288,1152]{1,0:T(8,128)(2,1)}, bf16[288,1152]{1,0:T(8,128)(2,1)S(1)}, u32[]{:S(2)}, u32[]{:S(2)}) collective-permute-start(bf16[288,1152]{1,0:T(8,128)(2,1)} %get-tuple-element.24), channel_id=1, source_target_pairs={{0,14},{1,3},{2,0},{3,5},{4,2},{5,7},{6,4},{7,9},{8,6},{9,11},{10,... | collective-permute-start | bytes 1990664 | tf_op jit(solution)/shard_map/ppermute | solution.py:400
  56.9 4.4 %collective-permute-start.7 = (bf16[288,1152]{1,0:T(8,128)(2,1)}, bf16[288,1152]{1,0:T(8,128)(2,1)S(1)}, u32[]{:S(2)}, u32[]{:S(2)}) collective-permute-start(bf16[288,1152]{1,0:T(8,128)(2,1)} %get-tuple-element.24), channel_id=1, source_target_pairs={{0,112},{1,17},{2,114},{3,19},{4,116},{5,21},{6,118},{7,23},{8,120... | collective-permute-start | bytes 1990664 | tf_op jit(solution)/shard_map/ppermute | solution.py:400
  61.3 4.5 %collective-permute-start.1 = (bf16[256,1152]{1,0:T(8,128)(2,1)}, bf16[256,1152]{1,0:T(8,128)(2,1)S(1)}, u32[]{:S(2)}, u32[]{:S(2)}) collective-permute-start(bf16[256,1152]{1,0:T(8,128)(2,1)} %get-tuple-element.21.own), channel_id=1, source_target_pairs={{0,1},{1,0},{2,3},{3,2},{4,5},{5,4},{6,7},{7,6},{8,9},{9,8},{10,11... | collective-permute-start | bytes 1769480 | tf_op jit(solution)/shard_map/ppermute | solution.py:59
  65.8 3.1 %collective-permute-start.6 = (bf16[288,1152]{1,0:T(8,128)(2,1)}, bf16[288,1152]{1,0:T(8,128)(2,1)S(1)}, u32[]{:S(2)}, u32[]{:S(2)}) collective-permute-start(bf16[288,1152]{1,0:T(8,128)(2,1)} %get-tuple-element.24), channel_id=1, source_target_pairs={{0,384},{1,129},{2,386},{3,131},{4,388},{5,133},{6,390},{7,135},{8... | collective-permute-start | bytes 1990664 | tf_op jit(solution)/shard_map/ppermute | solution.py:400
  68.9 2.0 %collective-permute-start.5 = (bf16[288,1152]{1,0:T(8,128)(2,1)}, bf16[288,1152]{1,0:T(8,128)(2,1)S(1)}, u32[]{:S(2)}, u32[]{:S(2)}) collective-permute-start(bf16[288,1152]{1,0:T(8,128)(2,1)} %get-tuple-element.24), channel_id=1, source_target_pairs={{0,2},{1,15},{2,4},{3,1},{4,6},{5,3},{6,8},{7,5},{8,10},{9,7},{10,... | collective-permute-start | bytes 1990664 | tf_op jit(solution)/shard_map/ppermute | solution.py:400
  71.0 2.7 %collective-permute-start.4 = (bf16[288,1152]{1,0:T(8,128)(2,1)}, bf16[288,1152]{1,0:T(8,128)(2,1)S(1)}, u32[]{:S(2)}, u32[]{:S(2)}) collective-permute-start(bf16[288,1152]{1,0:T(8,128)(2,1)} %get-tuple-element.24), channel_id=1, source_target_pairs={{0,16},{1,113},{2,18},{3,115},{4,20},{5,117},{6,22},{7,119},{8,24}... | collective-permute-start | bytes 1990664 | tf_op jit(solution)/shard_map/ppermute | solution.py:400
  73.7 0.0 collective-permute-done.8.refs_7_
  73.7 3.6 %collective-permute-start.3 = (bf16[288,1152]{1,0:T(8,128)(2,1)}, bf16[288,1152]{1,0:T(8,128)(2,1)S(1)}, u32[]{:S(2)}, u32[]{:S(2)}) collective-permute-start(bf16[288,1152]{1,0:T(8,128)(2,1)} %get-tuple-element.24), channel_id=1, source_target_pairs={{0,126},{1,19},{2,112},{3,21},{4,114},{5,23},{6,116},{7,25},{8,118... | collective-permute-start | bytes 1990664 | tf_op jit(solution)/shard_map/ppermute | solution.py:400
  77.4 0.0 collective-permute-done.7.refs_6_
  77.4 3.4 %collective-permute-start.2 = (bf16[288,1152]{1,0:T(8,128)(2,1)}, bf16[288,1152]{1,0:T(8,128)(2,1)S(1)}, u32[]{:S(2)}, u32[]{:S(2)}) collective-permute-start(bf16[288,1152]{1,0:T(8,128)(2,1)} %get-tuple-element.24), channel_id=1, source_target_pairs={{0,128},{1,385},{2,130},{3,387},{4,132},{5,389},{6,134},{7,391},{8... | collective-permute-start | bytes 1990664 | tf_op jit(solution)/shard_map/ppermute | solution.py:400
  80.7 0.0 copy-start.4
  80.8 1.1 copy-done.4
  81.8 0.8 shard_map.76.normed
  82.6 0.0 collective-permute-done.6.refs_5_
  82.6 0.9 collective-permute-done.4.refs_3_
  83.5 12.0 %collective-permute-done.3.refs_2_ = bf16[288,1152]{1,0:T(8,128)(2,1)S(1)} collective-permute-done((bf16[288,1152]{1,0:T(8,128)(2,1)}, bf16[288,1152]{1,0:T(8,128)(2,1)S(1)}, u32[]{:S(2)}, u32[]{:S(2)}) %collective-permute-start.3) | collective-permute-done | bytes 663584 | tf_op jit(solution)/shard_map/ppermute | solution.py:400
  95.5 0.0 collective-permute-done.2.refs_1_
  95.5 3.2 %shard_map.77 = (bf16[144,512]{1,0:T(8,128)(2,1)}, bf16[288,512]{1,0:T(8,128)(2,1)S(1)}, bf16[576,1152]{1,0:T(8,128)(2,1)S(1)}, bf16[2,288,1152]{2,1,0:T(8,128)(2,1)S(1)}, bf16[4,288,1152]{2,1,0:T(8,128)(2,1)}) custom-call(f32[8,288]{1,0:T(8,128)S(1)} %select_maximum_fusion.gains, bf16[512,1152]{1,0:T(8,128)(2,1)S(1)} %copy-done.2, ...), custom_call_target="tpu_custom_call" | custom-call | bytes 1 | tf_op jit(solution)/shard_map/pallas_call | solution.py:328
  98.7 5.4 %collective-permute-start.9 = (bf16[288,512]{1,0:T(8,128)(2,1)S(1)}, bf16[288,512]{1,0:T(8,128)(2,1)S(1)}, u32[]{:S(2)}, u32[]{:S(2)}) collective-permute-start(bf16[288,512]{1,0:T(8,128)(2,1)S(1)} %get-tuple-element.25), channel_id=1, source_target_pairs={{0,64},{1,65},{2,66},{3,67},{4,68},{5,69},{6,70},{7,71},{8,72},{9,... | collective-permute-start | bytes 884744 | tf_op jit(solution)/shard_map/ppermute | solution.py:411
  104.1 2.8 %shard_map.78 = bf16[32,16,144]{2,1,0:T(8,128)(2,1)} custom-call(f32[8,288]{1,0:T(8,128)S(1)} %select_maximum_fusion.gains, bf16[512,1152]{1,0:T(8,128)(2,1)S(1)} %shard_map.76.normed, bf16[2,288,1152]{2,1,0:T(8,128)(2,1)S(1)} %get-tuple-element.27.weight), custom_call_target="tpu_custom_call" | custom-call | bytes 1 | tf_op jit(solution)/shard_map/pallas_call | solution.py:328
  106.9 4.7 %all-to-all-start.1 = ((bf16[32,16,144]{2,1,0:T(8,128)(2,1)}), bf16[32,16,144]{2,1,0:T(8,128)(2,1)S(1)}, u32[]{:S(2)}, u32[]{:S(2)}) async-start(bf16[32,16,144]{2,1,0:T(8,128)(2,1)} %shard_map.78), calls=%async_computation.1 | async-start | bytes 524288 | tf_op jit(solution)/shard_map/all_to_all | solution.py:428
  111.6 3.1 %collective-permute-start.12 = (bf16[576,1152]{1,0:T(8,128)(2,1)S(1)}, bf16[576,1152]{1,0:T(8,128)(2,1)}, u32[]{:S(2)}, u32[]{:S(2)}) collective-permute-start(bf16[576,1152]{1,0:T(8,128)(2,1)S(1)} %get-tuple-element.34.w_own), channel_id=1, source_target_pairs={{0,1},{1,0},{2,3},{3,2},{4,5},{5,4},{6,7},{7,6},{8,9},{9,8},{10,11... | collective-permute-start | bytes 3981320 | tf_op jit(solution)/shard_map/ppermute | solution.py:59
  114.7 4.7 %collective-permute-done.9.kv_a = bf16[288,512]{1,0:T(8,128)(2,1)S(1)} collective-permute-done((bf16[288,512]{1,0:T(8,128)(2,1)S(1)}, bf16[288,512]{1,0:T(8,128)(2,1)S(1)}, u32[]{:S(2)}, u32[]{:S(2)}) %collective-permute-start.9) | collective-permute-done | bytes 294944 | tf_op jit(solution)/shard_map/ppermute | solution.py:411
  119.5 2.1 %collective-permute-start.10 = (bf16[288,512]{1,0:T(8,128)(2,1)S(1)}, bf16[288,512]{1,0:T(8,128)(2,1)S(1)}, u32[]{:S(2)}, u32[]{:S(2)}) collective-permute-start(bf16[288,512]{1,0:T(8,128)(2,1)S(1)} %collective-permute-done.9.kv_a), channel_id=1, source_target_pairs={{0,128},{1,129},{2,130},{3,131},{4,132},{5,133},{6,134},{7,135},{8... | collective-permute-start | bytes 884744 | tf_op jit(solution)/shard_map/ppermute | solution.py:414
  121.6 5.8 %shard_map.79.space_hbm = bf16[288,512]{1,0:T(8,128)(2,1)} custom-call(f32[8,288]{1,0:T(8,128)S(1)} %select_maximum_fusion.gains, bf16[512,1152]{1,0:T(8,128)(2,1)} %copy-done.1, bf16[4,288,1152]{2,1,0:T(8,128)(2,1)} %get-tuple-element.30.weight_hbm), custom_call_target="tpu_custom_call" | custom-call | flops 16000000000 | bytes 1 | tf_op jit(solution)/shard_map/pallas_call | solution.py:328
  127.4 0.0 all-to-all-done.1.timed
  127.4 3.1 %collective-permute-done.10.kv_b = bf16[288,512]{1,0:T(8,128)(2,1)S(1)} collective-permute-done((bf16[288,512]{1,0:T(8,128)(2,1)S(1)}, bf16[288,512]{1,0:T(8,128)(2,1)S(1)}, u32[]{:S(2)}, u32[]{:S(2)}) %collective-permute-start.10) | collective-permute-done | bytes 294944 | tf_op jit(solution)/shard_map/ppermute | solution.py:414
  130.5 2.6 %shard_map.80 = (bf16[256,576]{1,0:T(8,128)(2,1)S(1)}, bf16[256,576]{1,0:T(8,128)(2,1)S(1)}) custom-call(bf16[288,512]{1,0:T(8,128)(2,1)S(1)} %collective-permute-done.9.kv_a, bf16[288,512]{1,0:T(8,128)(2,1)S(1)} %collective-permute-done.10.kv_b, bf16[32,16,144]{2,1,0:T(8,128)(2,1)S(1)} %all-to-all-done.1.timed, bf16[288,512]{1,0:T(8,128)(2,1)} %shard_map.79.space_hbm, ...), custom_call_target="tpu_custom_call" | custom-call | bytes 1 | tf_op jit(solution)/shard_map/pallas_call | solution.py:328
  133.0 3.4 %collective-permute-start.11 = (bf16[256,576]{1,0:T(8,128)(2,1)S(1)}, bf16[256,576]{1,0:T(8,128)(2,1)S(1)}, u32[]{:S(2)}, u32[]{:S(2)}) collective-permute-start(bf16[256,576]{1,0:T(8,128)(2,1)S(1)} %get-tuple-element.33), channel_id=1, source_target_pairs={{0,1},{1,0},{2,3},{3,2},{4,5},{5,4},{6,7},{7,6},{8,9},{9,8},{10,11... | collective-permute-start | bytes 884744 | tf_op jit(solution)/shard_map/ppermute | solution.py:59
  136.5 1.2 collective-permute-done.11.arrived
  137.7 3.7 %shard_map.81 = bf16[256,1152]{1,0:T(8,128)(2,1)} custom-call(bf16[256,1152]{1,0:T(8,128)(2,1)S(1)} %bitcast.11, bf16[256,576]{1,0:T(8,128)(2,1)S(1)} %get-tuple-element.32.own, bf16[256,576]{1,0:T(8,128)(2,1)S(1)} %collective-permute-done.11.arrived, bf16[576,1152]{1,0:T(8,128)(2,1)S(1)} %get-tuple-element.34.w_own, ...), custom_call_target="tpu_custom_call" | custom-call | bytes 1 | tf_op jit(solution)/shard_map/pallas_call | solution.py:328
  (17 shorter events, 0.1 us)
Async XLA Ops:
  3.8 15.6 %copy-start = (bf16[1,256,1152]{2,1,0:T(8,128)(2,1)S(1)}, bf16[1,256,1152]{2,1,0:T(8,128)(2,1)}, u32[]{:S(2)}) copy-start(bf16[1,256,1152]{2,1,0:T(8,128)(2,1)} %param.7) | copy-start | bytes 1769476
  3.9 18.0 %copy-start.5 = (f32[1152]{0:T(1024)S(1)}, f32[1152]{0:T(1024)}, u32[]{:S(2)}) copy-start(f32[1152]{0:T(1024)} %param.9) | copy-start | bytes 13828
  3.9 18.0 %copy-start.6 = (f32[1152]{0:T(1024)S(1)}, f32[1152]{0:T(1024)}, u32[]{:S(2)}) copy-start(f32[1152]{0:T(1024)} %param.10) | copy-start | bytes 13828
  3.9 18.1 %copy-start.7 = (f32[1152]{0:T(1024)S(1)}, f32[1152]{0:T(1024)}, u32[]{:S(2)}) copy-start(f32[1152]{0:T(1024)} %param.11) | copy-start | bytes 13828
  3.9 19.6 %copy-start.3 = (f32[8,1152]{1,0:T(8,128)S(1)}, f32[8,1152]{1,0:T(8,128)}, u32[]{:S(2)}) copy-start(f32[8,1152]{1,0:T(8,128)} %embed_hbm.1) | copy-start | bytes 110596
  3.9 49.5 %all-to-all-start = ((bf16[64,80,128]{2,1,0:T(8,128)(2,1)}), bf16[64,80,128]{2,1,0:T(8,128)(2,1)S(1)}, u32[]{:S(2)}, u32[]{:S(2)}) async-start(bf16[64,80,128]{2,1,0:T(8,128)(2,1)} %shard_map.74), calls=%async_computation | async-start | bytes 2621440 | tf_op jit(solution)/shard_map/all_to_all | solution.py:387
  19.5 4.0 %collective-permute-start = (bf16[256,1152]{1,0:T(8,128)(2,1)S(1)}, bf16[256,1152]{1,0:T(8,128)(2,1)S(1)}, u32[]{:S(2)}, u32[]{:S(2)}) collective-permute-start(bf16[256,1152]{1,0:T(8,128)(2,1)S(1)} %bitcast.9), channel_id=1, source_target_pairs={{0,1},{1,0},{2,3},{3,2},{4,5},{5,4},{6,7},{7,6},{8,9},{9,8},{10,11... | collective-permute-start | bytes 1769480 | tf_op jit(solution)/shard_map/ppermute | solution.py:59
  24.2 1.0 copy-start.1
  55.0 18.7 %collective-permute-start.8 = (bf16[288,1152]{1,0:T(8,128)(2,1)}, bf16[288,1152]{1,0:T(8,128)(2,1)S(1)}, u32[]{:S(2)}, u32[]{:S(2)}) collective-permute-start(bf16[288,1152]{1,0:T(8,128)(2,1)} %get-tuple-element.24), channel_id=1, source_target_pairs={{0,14},{1,3},{2,0},{3,5},{4,2},{5,7},{6,4},{7,9},{8,6},{9,11},{10,... | collective-permute-start | bytes 1990664 | tf_op jit(solution)/shard_map/ppermute | solution.py:400
  56.9 20.4 %collective-permute-start.7 = (bf16[288,1152]{1,0:T(8,128)(2,1)}, bf16[288,1152]{1,0:T(8,128)(2,1)S(1)}, u32[]{:S(2)}, u32[]{:S(2)}) collective-permute-start(bf16[288,1152]{1,0:T(8,128)(2,1)} %get-tuple-element.24), channel_id=1, source_target_pairs={{0,112},{1,17},{2,114},{3,19},{4,116},{5,21},{6,118},{7,23},{8,120... | collective-permute-start | bytes 1990664 | tf_op jit(solution)/shard_map/ppermute | solution.py:400
  61.3 34.2 %copy-start.2 = (bf16[512,1152]{1,0:T(8,128)(2,1)S(1)}, bf16[512,1152]{1,0:T(8,128)(2,1)}, u32[]{:S(2)}) copy-start(bf16[512,1152]{1,0:T(8,128)(2,1)} %copy-done.1) | copy-start | bytes 3538948
  61.3 9.7 %collective-permute-start.1 = (bf16[256,1152]{1,0:T(8,128)(2,1)}, bf16[256,1152]{1,0:T(8,128)(2,1)S(1)}, u32[]{:S(2)}, u32[]{:S(2)}) collective-permute-start(bf16[256,1152]{1,0:T(8,128)(2,1)} %get-tuple-element.21.own), channel_id=1, source_target_pairs={{0,1},{1,0},{2,3},{3,2},{4,5},{5,4},{6,7},{7,6},{8,9},{9,8},{10,11... | collective-permute-start | bytes 1769480 | tf_op jit(solution)/shard_map/ppermute | solution.py:59
  65.8 16.8 %collective-permute-start.6 = (bf16[288,1152]{1,0:T(8,128)(2,1)}, bf16[288,1152]{1,0:T(8,128)(2,1)S(1)}, u32[]{:S(2)}, u32[]{:S(2)}) collective-permute-start(bf16[288,1152]{1,0:T(8,128)(2,1)} %get-tuple-element.24), channel_id=1, source_target_pairs={{0,384},{1,129},{2,386},{3,131},{4,388},{5,133},{6,390},{7,135},{8... | collective-permute-start | bytes 1990664 | tf_op jit(solution)/shard_map/ppermute | solution.py:400
  68.9 13.7 %collective-permute-start.5 = (bf16[288,1152]{1,0:T(8,128)(2,1)}, bf16[288,1152]{1,0:T(8,128)(2,1)S(1)}, u32[]{:S(2)}, u32[]{:S(2)}) collective-permute-start(bf16[288,1152]{1,0:T(8,128)(2,1)} %get-tuple-element.24), channel_id=1, source_target_pairs={{0,2},{1,15},{2,4},{3,1},{4,6},{5,3},{6,8},{7,5},{8,10},{9,7},{10,... | collective-permute-start | bytes 1990664 | tf_op jit(solution)/shard_map/ppermute | solution.py:400
  71.0 12.5 %collective-permute-start.4 = (bf16[288,1152]{1,0:T(8,128)(2,1)}, bf16[288,1152]{1,0:T(8,128)(2,1)S(1)}, u32[]{:S(2)}, u32[]{:S(2)}) collective-permute-start(bf16[288,1152]{1,0:T(8,128)(2,1)} %get-tuple-element.24), channel_id=1, source_target_pairs={{0,16},{1,113},{2,18},{3,115},{4,20},{5,117},{6,22},{7,119},{8,24}... | collective-permute-start | bytes 1990664 | tf_op jit(solution)/shard_map/ppermute | solution.py:400
  73.7 21.8 %collective-permute-start.3 = (bf16[288,1152]{1,0:T(8,128)(2,1)}, bf16[288,1152]{1,0:T(8,128)(2,1)S(1)}, u32[]{:S(2)}, u32[]{:S(2)}) collective-permute-start(bf16[288,1152]{1,0:T(8,128)(2,1)} %get-tuple-element.24), channel_id=1, source_target_pairs={{0,126},{1,19},{2,112},{3,21},{4,114},{5,23},{6,116},{7,25},{8,118... | collective-permute-start | bytes 1990664 | tf_op jit(solution)/shard_map/ppermute | solution.py:400
  77.4 18.1 %collective-permute-start.2 = (bf16[288,1152]{1,0:T(8,128)(2,1)}, bf16[288,1152]{1,0:T(8,128)(2,1)S(1)}, u32[]{:S(2)}, u32[]{:S(2)}) collective-permute-start(bf16[288,1152]{1,0:T(8,128)(2,1)} %get-tuple-element.24), channel_id=1, source_target_pairs={{0,128},{1,385},{2,130},{3,387},{4,132},{5,389},{6,134},{7,391},{8... | collective-permute-start | bytes 1990664 | tf_op jit(solution)/shard_map/ppermute | solution.py:400
  80.7 1.1 copy-start.4
  98.7 20.8 %collective-permute-start.9 = (bf16[288,512]{1,0:T(8,128)(2,1)S(1)}, bf16[288,512]{1,0:T(8,128)(2,1)S(1)}, u32[]{:S(2)}, u32[]{:S(2)}) collective-permute-start(bf16[288,512]{1,0:T(8,128)(2,1)S(1)} %get-tuple-element.25), channel_id=1, source_target_pairs={{0,64},{1,65},{2,66},{3,67},{4,68},{5,69},{6,70},{7,71},{8,72},{9,... | collective-permute-start | bytes 884744 | tf_op jit(solution)/shard_map/ppermute | solution.py:411
  106.9 20.4 %all-to-all-start.1 = ((bf16[32,16,144]{2,1,0:T(8,128)(2,1)}), bf16[32,16,144]{2,1,0:T(8,128)(2,1)S(1)}, u32[]{:S(2)}, u32[]{:S(2)}) async-start(bf16[32,16,144]{2,1,0:T(8,128)(2,1)} %shard_map.78), calls=%async_computation.1 | async-start | bytes 524288 | tf_op jit(solution)/shard_map/all_to_all | solution.py:428
  111.6 26.1 %collective-permute-start.12 = (bf16[576,1152]{1,0:T(8,128)(2,1)S(1)}, bf16[576,1152]{1,0:T(8,128)(2,1)}, u32[]{:S(2)}, u32[]{:S(2)}) collective-permute-start(bf16[576,1152]{1,0:T(8,128)(2,1)S(1)} %get-tuple-element.34.w_own), channel_id=1, source_target_pairs={{0,1},{1,0},{2,3},{3,2},{4,5},{5,4},{6,7},{7,6},{8,9},{9,8},{10,11... | collective-permute-start | bytes 3981320 | tf_op jit(solution)/shard_map/ppermute | solution.py:59
  119.5 11.0 %collective-permute-start.10 = (bf16[288,512]{1,0:T(8,128)(2,1)S(1)}, bf16[288,512]{1,0:T(8,128)(2,1)S(1)}, u32[]{:S(2)}, u32[]{:S(2)}) collective-permute-start(bf16[288,512]{1,0:T(8,128)(2,1)S(1)} %collective-permute-done.9.kv_a), channel_id=1, source_target_pairs={{0,128},{1,129},{2,130},{3,131},{4,132},{5,133},{6,134},{7,135},{8... | collective-permute-start | bytes 884744 | tf_op jit(solution)/shard_map/ppermute | solution.py:414
  133.0 4.7 %collective-permute-start.11 = (bf16[256,576]{1,0:T(8,128)(2,1)S(1)}, bf16[256,576]{1,0:T(8,128)(2,1)S(1)}, u32[]{:S(2)}, u32[]{:S(2)}) collective-permute-start(bf16[256,576]{1,0:T(8,128)(2,1)S(1)} %get-tuple-element.33), channel_id=1, source_target_pairs={{0,1},{1,0},{2,3},{3,2},{4,5},{5,4},{6,7},{7,6},{8,9},{9,8},{10,11... | collective-permute-start | bytes 884744 | tf_op jit(solution)/shard_map/ppermute | solution.py:59

commit v9 on v8

--- a/solution.py
+++ b/solution.py
@@ -41,8 +41,7 @@
     return 1 if core else -1
 
 
-OFFSETS = ((-1, 0, 0), (0, 1, 1), (0, -1, 0), (0, 0, -1), (1, 0, 0), (0, 1, 0), (0, 0, 1))
-TURNS = (0,) + tuple((2 * a + b + 3 * c) % 8 for a, b, c in OFFSETS)
+TURNS = (0, 2, 1, 6, 3, 7, 4, 5)
 
 
 def bring(offset):
@@ -50,7 +49,9 @@
     return route(lambda x, y, z, core: (x + a * towards(core), y + b * towards(core), z + c * towards(core)))
 
 
-ROUTES = tuple(bring(offset) for offset in OFFSETS)
+X_NEXT, X_LAST = bring((1, 0, 0)), bring((-1, 0, 0))
+Y_NEXT, Y_LAST = bring((0, 1, 0)), bring((0, -1, 0))
+Z_NEXT, Z_LAST = bring((0, 0, 1)), bring((0, 0, -1))
 ACROSS = route(lambda x, y, z, core: (x, y + 4, z))
 ALONG = route(lambda x, y, z, core: (x + (1 if y < 4 else -1), y, z))
 
@@ -397,13 +398,19 @@
             pltpu.SemaphoreType.DMA((2,)),
         ],
     )
-    blocks = (keep_near(own_block),) + tuple(lax.ppermute(block, EVERY, r) for r in ROUTES)
+    blocks = [keep_near(own_block)]
+    for way in (X_NEXT, Y_NEXT, X_LAST, Z_NEXT, Y_LAST, None, Z_LAST):
+        if way is None:
+            blocks.append(lax.ppermute(blocks[1], EVERY, X_NEXT))
+        else:
+            blocks.append(lax.ppermute(block, EVERY, way))
+    blocks = tuple(blocks)
     time_other = swap_core(time_own)
     time_normed = keep_near(call(norm_kernel, near(ROWS, D), (time_own, time_other, cam_embed, gain), (), 8 * 10**9))
     q_t, kv_t, w_own, early, late = call(
         cross_project_kernel,
         (far(PAIR, ROWS), shape(2 * PAIR, ROWS), near(4 * PAIR, D), near(2, QUAD, D), far(4, QUAD, D)),
-        (gains, after(normed, time_normed)) + blocks,
+        (gains, normed) + blocks,
         [pltpu.VMEM((PAIR, ROWS), BF16), pltpu.VMEM((2, QUAD, D), BF16), pltpu.SemaphoreType.DMA((13,))],
         0,
         8,

time: 142 us -> 135 us (0.951)
  waiting for transfers between devices: 51.3 us -> 39.2 us
  starting transfers between devices: 62.2 us -> 67.4 us
    ppermute x7, waiting for transfers between devices: 12.9 us -> 5.82 us  [the longest x6 4.61 us: local(): blocks.append(lax.ppermute(block, EVERY, way))]
    ppermute x1, waiting for transfers between devices: 4.74 us -> 0.22 us  [local(): kv_a = lax.ppermute(kv_t, EVERY, ACROSS)]
    ppermute x4, starting transfers between devices: 13.4 us -> 16.7 us  [swap_core(): return lax.ppermute(block, 'core', [(0, 1), (1, 0)])]
    ppermute x1, starting transfers between devices: 5.37 us -> 6.99 us  [local(): kv_a = lax.ppermute(kv_t, EVERY, ACROSS)]
  transfers between devices with their start and end apart: 15 -> 15, of which waited for: 7 -> 7; matrix products, arithmetic and copies ran while one was open for 0% -> 0% of each run, Pallas kernels for 9% -> 12%
where the time goes in v9:
time: 135 us; the launch traced here: 134 us
  starting transfers between devices  67.4 us (50%)
  waiting for transfers between devices  39.2 us (29%)
  Pallas kernels  25.8 us (19%)
  local copies, waits for them, and re-layouts  1.41 us (1%)
    all_to_all x1, waiting for transfers between devices, local(): got = lax.all_to_all(pieces, SLAB, 0, 0, tiled=True)  28.1 us
    pallas_call x9, Pallas kernels, call(): pl.pallas_call(kernel, out_shape=out_shapes, in_specs=specs, out_specs=pl...  25.8 us
    ppermute x6, starting transfers between devices, local(): blocks.append(lax.ppermute(block, EVERY, way))  19.5 us
    ppermute x4, starting transfers between devices, swap_core(): return lax.ppermute(block, 'core', [(0, 1), (1, 0)])  16.7 us
    all_to_all x1, starting transfers between devices, local(): got = lax.all_to_all(pieces, SLAB, 0, 0, tiled=True)  15.6 us
    ppermute x1, starting transfers between devices, local(): kv_a = lax.ppermute(kv_t, EVERY, ACROSS)  6.99 us
    all_to_all x1, starting transfers between devices, local(): returned = lax.all_to_all(timed, CHIP, 0, 0, tiled=True)  4.65 us
    ppermute x6, waiting for transfers between devices, local(): blocks.append(lax.ppermute(block, EVERY, way))  4.61 us
  transfers between devices with their start and end apart: 15, of which 7 were waited for; matrix products, arithmetic and copies ran while one was open for 0% of the time, Pallas kernels for 12%

profile of v9, /device:TPU:1, one launch (start us, length us, event | category | flops | bytes accessed | tf_op | source)
XLA Modules:
  0.0 134.3 jit_solution(9842854919001535526)
XLA Ops:
  0.0 3.8 %shard_map.74 = bf16[64,80,128]{2,1,0:T(8,128)(2,1)} custom-call(bf16[256,1152]{1,0:T(8,128)(2,1)} %bitcast.8, bf16[18,3456]{1,0:T(8,128)(2,1)} %w_qkv_hbm.1, bf16[18,1152]{1,0:T(8,128)(2,1)} %w_out_hbm.1), custom_call_target="tpu_custom_call" | custom-call | bytes 1 | tf_op jit(solution)/shard_map/pallas_call | solution.py:329
  3.8 0.0 copy-start
  3.9 0.0 copy-start.5
  3.9 0.0 copy-start.6
  3.9 0.0 copy-start.7
  3.9 0.0 copy-start.3
  3.9 15.6 %all-to-all-start = ((bf16[64,80,128]{2,1,0:T(8,128)(2,1)}), bf16[64,80,128]{2,1,0:T(8,128)(2,1)S(1)}, u32[]{:S(2)}, u32[]{:S(2)}) async-start(bf16[64,80,128]{2,1,0:T(8,128)(2,1)} %shard_map.74), calls=%async_computation | async-start | bytes 2621440 | tf_op jit(solution)/shard_map/all_to_all | solution.py:388
  19.5 2.4 %collective-permute-start = (bf16[256,1152]{1,0:T(8,128)(2,1)S(1)}, bf16[256,1152]{1,0:T(8,128)(2,1)S(1)}, u32[]{:S(2)}, u32[]{:S(2)}) collective-permute-start(bf16[256,1152]{1,0:T(8,128)(2,1)S(1)} %bitcast.9), channel_id=1, source_target_pairs={{0,1},{1,0},{2,3},{3,2},{4,5},{5,4},{6,7},{7,6},{8,9},{9,8},{10,11... | collective-permute-start | bytes 1769480 | tf_op jit(solution)/shard_map/ppermute | solution.py:60
  21.9 0.1 stack_reshape.6
  22.0 0.1 stack_reshape.7
  22.1 0.1 reshape.6
  22.2 0.1 reshape.7
  22.3 1.1 collective-permute-done.other
  23.5 0.8 shard_map.73.normed.normed_hbm
  24.3 1.0 copy-done.1
  25.3 28.1 %all-to-all-done.got = bf16[64,80,128]{2,1,0:T(8,128)(2,1)S(1)} async-done(((bf16[64,80,128]{2,1,0:T(8,128)(2,1)}), bf16[64,80,128]{2,1,0:T(8,128)(2,1)S(1)}, u32[]{:S(2)}, u32[]{:S(2)}) %all-to-all-start) | async-done | bytes 1310752 | tf_op jit(solution)/shard_map/all_to_all | solution.py:388
  53.4 1.6 %shard_map.75 = (bf16[288,1152]{1,0:T(8,128)(2,1)S(1)}, bf16[288,1152]{1,0:T(8,128)(2,1)}, bf16[256,1152]{1,0:T(8,128)(2,1)}) custom-call(bf16[64,80,128]{2,1,0:T(8,128)(2,1)S(1)} %all-to-all-done.got), custom_call_target="tpu_custom_call" | custom-call | bytes 1 | tf_op jit(solution)/shard_map/pallas_call | solution.py:329
  55.0 3.1 %collective-permute-start.1 = (bf16[288,1152]{1,0:T(8,128)(2,1)}, bf16[288,1152]{1,0:T(8,128)(2,1)S(1)}, u32[]{:S(2)}, u32[]{:S(2)}) collective-permute-start(bf16[288,1152]{1,0:T(8,128)(2,1)} %get-tuple-element.21), channel_id=1, source_target_pairs={{0,384},{1,129},{2,386},{3,131},{4,388},{5,133},{6,390},{7,135},{8... | collective-permute-start | bytes 1990664 | tf_op jit(solution)/shard_map/ppermute | solution.py:406
  58.1 3.1 %collective-permute-start.2 = (bf16[288,1152]{1,0:T(8,128)(2,1)}, bf16[288,1152]{1,0:T(8,128)(2,1)S(1)}, u32[]{:S(2)}, u32[]{:S(2)}) collective-permute-start(bf16[288,1152]{1,0:T(8,128)(2,1)} %get-tuple-element.21), channel_id=1, source_target_pairs={{0,112},{1,17},{2,114},{3,19},{4,116},{5,21},{6,118},{7,23},{8,120... | collective-permute-start | bytes 1990664 | tf_op jit(solution)/shard_map/ppermute | solution.py:406
  61.3 3.4 %collective-permute-start.3 = (bf16[288,1152]{1,0:T(8,128)(2,1)}, bf16[288,1152]{1,0:T(8,128)(2,1)S(1)}, u32[]{:S(2)}, u32[]{:S(2)}) collective-permute-start(bf16[288,1152]{1,0:T(8,128)(2,1)} %get-tuple-element.21), channel_id=1, source_target_pairs={{0,128},{1,385},{2,130},{3,387},{4,132},{5,389},{6,134},{7,391},{8... | collective-permute-start | bytes 1990664 | tf_op jit(solution)/shard_map/ppermute | solution.py:406
  64.6 3.2 %collective-permute-start.4 = (bf16[288,1152]{1,0:T(8,128)(2,1)}, bf16[288,1152]{1,0:T(8,128)(2,1)S(1)}, u32[]{:S(2)}, u32[]{:S(2)}) collective-permute-start(bf16[288,1152]{1,0:T(8,128)(2,1)} %get-tuple-element.21), channel_id=1, source_target_pairs={{0,14},{1,3},{2,0},{3,5},{4,2},{5,7},{6,4},{7,9},{8,6},{9,11},{10,... | collective-permute-start | bytes 1990664 | tf_op jit(solution)/shard_map/ppermute | solution.py:406
  67.8 3.3 %collective-permute-start.5 = (bf16[288,1152]{1,0:T(8,128)(2,1)}, bf16[288,1152]{1,0:T(8,128)(2,1)S(1)}, u32[]{:S(2)}, u32[]{:S(2)}) collective-permute-start(bf16[288,1152]{1,0:T(8,128)(2,1)} %get-tuple-element.21), channel_id=1, source_target_pairs={{0,16},{1,113},{2,18},{3,115},{4,20},{5,117},{6,22},{7,119},{8,24}... | collective-permute-start | bytes 1990664 | tf_op jit(solution)/shard_map/ppermute | solution.py:406
  71.1 0.0 collective-permute-done.1.refs_1_
  71.1 3.4 %collective-permute-start.7 = (bf16[288,1152]{1,0:T(8,128)(2,1)}, bf16[288,1152]{1,0:T(8,128)(2,1)S(1)}, u32[]{:S(2)}, u32[]{:S(2)}) collective-permute-start(bf16[288,1152]{1,0:T(8,128)(2,1)} %get-tuple-element.21), channel_id=1, source_target_pairs={{0,2},{1,15},{2,4},{3,1},{4,6},{5,3},{6,8},{7,5},{8,10},{9,7},{10,... | collective-permute-start | bytes 1990664 | tf_op jit(solution)/shard_map/ppermute | solution.py:406
  74.5 0.0 collective-permute-done.2.refs_2_
  74.6 1.9 %collective-permute-start.6 = (bf16[288,1152]{1,0:T(8,128)(2,1)S(1)}, bf16[288,1152]{1,0:T(8,128)(2,1)S(1)}, u32[]{:S(2)}, u32[]{:S(2)}) collective-permute-start(bf16[288,1152]{1,0:T(8,128)(2,1)S(1)} %collective-permute-done.1.refs_1_), channel_id=1, source_target_pairs={{0,384},{1,129},{2,386},{3,131},{4,388},{5,133},{6,390},{7,135},{8... | collective-permute-start | bytes 1990664 | tf_op jit(solution)/shard_map/ppermute | solution.py:404
  76.5 0.0 collective-permute-done.3.refs_3_
  76.5 4.9 %collective-permute-start.9 = (bf16[256,1152]{1,0:T(8,128)(2,1)}, bf16[256,1152]{1,0:T(8,128)(2,1)S(1)}, u32[]{:S(2)}, u32[]{:S(2)}) collective-permute-start(bf16[256,1152]{1,0:T(8,128)(2,1)} %get-tuple-element.23.own), channel_id=1, source_target_pairs={{0,1},{1,0},{2,3},{3,2},{4,5},{5,4},{6,7},{7,6},{8,9},{9,8},{10,11... | collective-permute-start | bytes 1769480 | tf_op jit(solution)/shard_map/ppermute | solution.py:60
  81.3 0.0 collective-permute-done.4.refs_4_
  81.4 0.0 collective-permute-done.5.refs_5_
  81.4 4.6 %collective-permute-done.7.refs_7_ = bf16[288,1152]{1,0:T(8,128)(2,1)S(1)} collective-permute-done((bf16[288,1152]{1,0:T(8,128)(2,1)}, bf16[288,1152]{1,0:T(8,128)(2,1)S(1)}, u32[]{:S(2)}, u32[]{:S(2)}) %collective-permute-start.7) | collective-permute-done | bytes 663584 | tf_op jit(solution)/shard_map/ppermute | solution.py:406
  86.0 1.2 collective-permute-done.6.refs_6_
  87.2 3.9 %shard_map.76 = (bf16[144,512]{1,0:T(8,128)(2,1)}, bf16[288,512]{1,0:T(8,128)(2,1)}, bf16[576,1152]{1,0:T(8,128)(2,1)S(1)}, bf16[2,288,1152]{2,1,0:T(8,128)(2,1)S(1)}, bf16[4,288,1152]{2,1,0:T(8,128)(2,1)}) custom-call(f32[8,288]{1,0:T(8,128)S(1)} %select_maximum_fusion.gains, bf16[512,1152]{1,0:T(8,128)(2,1)S(1)} %copy-done.2, ...), custom_call_target="tpu_custom_call" | custom-call | bytes 1 | tf_op jit(solution)/shard_map/pallas_call | solution.py:329
  91.1 7.0 %collective-permute-start.8 = (bf16[288,512]{1,0:T(8,128)(2,1)}, bf16[288,512]{1,0:T(8,128)(2,1)S(1)}, u32[]{:S(2)}, u32[]{:S(2)}) collective-permute-start(bf16[288,512]{1,0:T(8,128)(2,1)} %get-tuple-element.22), channel_id=1, source_target_pairs={{0,64},{1,65},{2,66},{3,67},{4,68},{5,69},{6,70},{7,71},{8,72},{9,... | collective-permute-start | bytes 884744 | tf_op jit(solution)/shard_map/ppermute | solution.py:418
  98.1 0.0 collective-permute-done.9.other
  98.1 0.8 shard_map.77.normed
  98.9 2.8 %shard_map.78 = bf16[32,16,144]{2,1,0:T(8,128)(2,1)} custom-call(f32[8,288]{1,0:T(8,128)S(1)} %select_maximum_fusion.gains, bf16[512,1152]{1,0:T(8,128)(2,1)S(1)} %shard_map.77.normed, bf16[2,288,1152]{2,1,0:T(8,128)(2,1)S(1)} %get-tuple-element.25.weight), custom_call_target="tpu_custom_call" | custom-call | bytes 1 | tf_op jit(solution)/shard_map/pallas_call | solution.py:329
  101.7 4.6 %all-to-all-start.1 = ((bf16[32,16,144]{2,1,0:T(8,128)(2,1)}), bf16[32,16,144]{2,1,0:T(8,128)(2,1)S(1)}, u32[]{:S(2)}, u32[]{:S(2)}) async-start(bf16[32,16,144]{2,1,0:T(8,128)(2,1)} %shard_map.78), calls=%async_computation.1 | async-start | bytes 524288 | tf_op jit(solution)/shard_map/all_to_all | solution.py:435
  106.4 5.1 %collective-permute-start.12 = (bf16[576,1152]{1,0:T(8,128)(2,1)S(1)}, bf16[576,1152]{1,0:T(8,128)(2,1)}, u32[]{:S(2)}, u32[]{:S(2)}) collective-permute-start(bf16[576,1152]{1,0:T(8,128)(2,1)S(1)} %get-tuple-element.32.w_own), channel_id=1, source_target_pairs={{0,1},{1,0},{2,3},{3,2},{4,5},{5,4},{6,7},{7,6},{8,9},{9,8},{10,11... | collective-permute-start | bytes 3981320 | tf_op jit(solution)/shard_map/ppermute | solution.py:60
  111.5 0.2 collective-permute-done.8.kv_a
  111.7 2.1 %collective-permute-start.10 = (bf16[288,512]{1,0:T(8,128)(2,1)S(1)}, bf16[288,512]{1,0:T(8,128)(2,1)S(1)}, u32[]{:S(2)}, u32[]{:S(2)}) collective-permute-start(bf16[288,512]{1,0:T(8,128)(2,1)S(1)} %collective-permute-done.8.kv_a), channel_id=1, source_target_pairs={{0,128},{1,129},{2,130},{3,131},{4,132},{5,133},{6,134},{7,135},{8... | collective-permute-start | bytes 884744 | tf_op jit(solution)/shard_map/ppermute | solution.py:421
  113.8 5.8 %shard_map.79.space_hbm = bf16[288,512]{1,0:T(8,128)(2,1)} custom-call(f32[8,288]{1,0:T(8,128)S(1)} %select_maximum_fusion.gains, bf16[512,1152]{1,0:T(8,128)(2,1)} %copy-done.1, bf16[4,288,1152]{2,1,0:T(8,128)(2,1)} %get-tuple-element.28.weight_hbm), custom_call_target="tpu_custom_call" | custom-call | flops 16000000000 | bytes 1 | tf_op jit(solution)/shard_map/pallas_call | solution.py:329
  119.6 0.0 all-to-all-done.1.timed
  119.6 2.6 %collective-permute-done.10.kv_b = bf16[288,512]{1,0:T(8,128)(2,1)S(1)} collective-permute-done((bf16[288,512]{1,0:T(8,128)(2,1)S(1)}, bf16[288,512]{1,0:T(8,128)(2,1)S(1)}, u32[]{:S(2)}, u32[]{:S(2)}) %collective-permute-start.10) | collective-permute-done | bytes 294944 | tf_op jit(solution)/shard_map/ppermute | solution.py:421
  122.2 2.6 %shard_map.80 = (bf16[256,576]{1,0:T(8,128)(2,1)S(1)}, bf16[256,576]{1,0:T(8,128)(2,1)S(1)}) custom-call(bf16[288,512]{1,0:T(8,128)(2,1)S(1)} %collective-permute-done.8.kv_a, bf16[288,512]{1,0:T(8,128)(2,1)S(1)} %collective-permute-done.10.kv_b, bf16[32,16,144]{2,1,0:T(8,128)(2,1)S(1)} %all-to-all-done.1.timed, bf16[288,512]{1,0:T(8,128)(2,1)} %shard_map.79.space_hbm, ...), custom_call_target="tpu_custom_call" | custom-call | bytes 1 | tf_op jit(solution)/shard_map/pallas_call | solution.py:329
  124.8 4.4 %collective-permute-start.11 = (bf16[256,576]{1,0:T(8,128)(2,1)S(1)}, bf16[256,576]{1,0:T(8,128)(2,1)S(1)}, u32[]{:S(2)}, u32[]{:S(2)}) collective-permute-start(bf16[256,576]{1,0:T(8,128)(2,1)S(1)} %get-tuple-element.31), channel_id=1, source_target_pairs={{0,1},{1,0},{2,3},{3,2},{4,5},{5,4},{6,7},{7,6},{8,9},{9,8},{10,11... | collective-permute-start | bytes 884744 | tf_op jit(solution)/shard_map/ppermute | solution.py:60
  129.2 1.2 collective-permute-done.11.arrived
  130.5 3.7 %shard_map.81 = bf16[256,1152]{1,0:T(8,128)(2,1)} custom-call(bf16[256,1152]{1,0:T(8,128)(2,1)S(1)} %bitcast.11, bf16[256,576]{1,0:T(8,128)(2,1)S(1)} %get-tuple-element.30.own, bf16[256,576]{1,0:T(8,128)(2,1)S(1)} %collective-permute-done.11.arrived, bf16[576,1152]{1,0:T(8,128)(2,1)S(1)} %get-tuple-element.32.w_own, ...), custom_call_target="tpu_custom_call" | custom-call | bytes 1 | tf_op jit(solution)/shard_map/pallas_call | solution.py:329
  (17 shorter events, 0.1 us)
Async XLA Ops:
  3.8 15.6 %copy-start = (bf16[1,256,1152]{2,1,0:T(8,128)(2,1)S(1)}, bf16[1,256,1152]{2,1,0:T(8,128)(2,1)}, u32[]{:S(2)}) copy-start(bf16[1,256,1152]{2,1,0:T(8,128)(2,1)} %param.7) | copy-start | bytes 1769476
  3.9 18.0 %copy-start.5 = (f32[1152]{0:T(1024)S(1)}, f32[1152]{0:T(1024)}, u32[]{:S(2)}) copy-start(f32[1152]{0:T(1024)} %param.10) | copy-start | bytes 13828
  3.9 18.1 %copy-start.6 = (f32[1152]{0:T(1024)S(1)}, f32[1152]{0:T(1024)}, u32[]{:S(2)}) copy-start(f32[1152]{0:T(1024)} %param.11) | copy-start | bytes 13828
  3.9 18.4 %copy-start.7 = (f32[1152]{0:T(1024)S(1)}, f32[1152]{0:T(1024)}, u32[]{:S(2)}) copy-start(f32[1152]{0:T(1024)} %param.9) | copy-start | bytes 13828
  3.9 19.6 %copy-start.3 = (f32[8,1152]{1,0:T(8,128)S(1)}, f32[8,1152]{1,0:T(8,128)}, u32[]{:S(2)}) copy-start(f32[8,1152]{1,0:T(8,128)} %embed_hbm.1) | copy-start | bytes 110596
  3.9 49.5 %all-to-all-start = ((bf16[64,80,128]{2,1,0:T(8,128)(2,1)}), bf16[64,80,128]{2,1,0:T(8,128)(2,1)S(1)}, u32[]{:S(2)}, u32[]{:S(2)}) async-start(bf16[64,80,128]{2,1,0:T(8,128)(2,1)} %shard_map.74), calls=%async_computation | async-start | bytes 2621440 | tf_op jit(solution)/shard_map/all_to_all | solution.py:388
  19.5 4.0 %collective-permute-start = (bf16[256,1152]{1,0:T(8,128)(2,1)S(1)}, bf16[256,1152]{1,0:T(8,128)(2,1)S(1)}, u32[]{:S(2)}, u32[]{:S(2)}) collective-permute-start(bf16[256,1152]{1,0:T(8,128)(2,1)S(1)} %bitcast.9), channel_id=1, source_target_pairs={{0,1},{1,0},{2,3},{3,2},{4,5},{5,4},{6,7},{7,6},{8,9},{9,8},{10,11... | collective-permute-start | bytes 1769480 | tf_op jit(solution)/shard_map/ppermute | solution.py:60
  24.2 1.0 copy-start.1
  53.4 33.8 %copy-start.2 = (bf16[512,1152]{1,0:T(8,128)(2,1)S(1)}, bf16[512,1152]{1,0:T(8,128)(2,1)}, u32[]{:S(2)}) copy-start(bf16[512,1152]{1,0:T(8,128)(2,1)} %copy-done.1) | copy-start | bytes 3538948
  55.0 16.1 %collective-permute-start.1 = (bf16[288,1152]{1,0:T(8,128)(2,1)}, bf16[288,1152]{1,0:T(8,128)(2,1)S(1)}, u32[]{:S(2)}, u32[]{:S(2)}) collective-permute-start(bf16[288,1152]{1,0:T(8,128)(2,1)} %get-tuple-element.21), channel_id=1, source_target_pairs={{0,384},{1,129},{2,386},{3,131},{4,388},{5,133},{6,390},{7,135},{8... | collective-permute-start | bytes 1990664 | tf_op jit(solution)/shard_map/ppermute | solution.py:406
  58.1 16.4 %collective-permute-start.2 = (bf16[288,1152]{1,0:T(8,128)(2,1)}, bf16[288,1152]{1,0:T(8,128)(2,1)S(1)}, u32[]{:S(2)}, u32[]{:S(2)}) collective-permute-start(bf16[288,1152]{1,0:T(8,128)(2,1)} %get-tuple-element.21), channel_id=1, source_target_pairs={{0,112},{1,17},{2,114},{3,19},{4,116},{5,21},{6,118},{7,23},{8,120... | collective-permute-start | bytes 1990664 | tf_op jit(solution)/shard_map/ppermute | solution.py:406
  61.3 15.2 %collective-permute-start.3 = (bf16[288,1152]{1,0:T(8,128)(2,1)}, bf16[288,1152]{1,0:T(8,128)(2,1)S(1)}, u32[]{:S(2)}, u32[]{:S(2)}) collective-permute-start(bf16[288,1152]{1,0:T(8,128)(2,1)} %get-tuple-element.21), channel_id=1, source_target_pairs={{0,128},{1,385},{2,130},{3,387},{4,132},{5,389},{6,134},{7,391},{8... | collective-permute-start | bytes 1990664 | tf_op jit(solution)/shard_map/ppermute | solution.py:406
  64.6 16.7 %collective-permute-start.4 = (bf16[288,1152]{1,0:T(8,128)(2,1)}, bf16[288,1152]{1,0:T(8,128)(2,1)S(1)}, u32[]{:S(2)}, u32[]{:S(2)}) collective-permute-start(bf16[288,1152]{1,0:T(8,128)(2,1)} %get-tuple-element.21), channel_id=1, source_target_pairs={{0,14},{1,3},{2,0},{3,5},{4,2},{5,7},{6,4},{7,9},{8,6},{9,11},{10,... | collective-permute-start | bytes 1990664 | tf_op jit(solution)/shard_map/ppermute | solution.py:406
  67.8 13.5 %collective-permute-start.5 = (bf16[288,1152]{1,0:T(8,128)(2,1)}, bf16[288,1152]{1,0:T(8,128)(2,1)S(1)}, u32[]{:S(2)}, u32[]{:S(2)}) collective-permute-start(bf16[288,1152]{1,0:T(8,128)(2,1)} %get-tuple-element.21), channel_id=1, source_target_pairs={{0,16},{1,113},{2,18},{3,115},{4,20},{5,117},{6,22},{7,119},{8,24}... | collective-permute-start | bytes 1990664 | tf_op jit(solution)/shard_map/ppermute | solution.py:406
  71.1 14.8 %collective-permute-start.7 = (bf16[288,1152]{1,0:T(8,128)(2,1)}, bf16[288,1152]{1,0:T(8,128)(2,1)S(1)}, u32[]{:S(2)}, u32[]{:S(2)}) collective-permute-start(bf16[288,1152]{1,0:T(8,128)(2,1)} %get-tuple-element.21), channel_id=1, source_target_pairs={{0,2},{1,15},{2,4},{3,1},{4,6},{5,3},{6,8},{7,5},{8,10},{9,7},{10,... | collective-permute-start | bytes 1990664 | tf_op jit(solution)/shard_map/ppermute | solution.py:406
  74.6 12.6 %collective-permute-start.6 = (bf16[288,1152]{1,0:T(8,128)(2,1)S(1)}, bf16[288,1152]{1,0:T(8,128)(2,1)S(1)}, u32[]{:S(2)}, u32[]{:S(2)}) collective-permute-start(bf16[288,1152]{1,0:T(8,128)(2,1)S(1)} %collective-permute-done.1.refs_1_), channel_id=1, source_target_pairs={{0,384},{1,129},{2,386},{3,131},{4,388},{5,133},{6,390},{7,135},{8... | collective-permute-start | bytes 1990664 | tf_op jit(solution)/shard_map/ppermute | solution.py:404
  76.5 21.6 %collective-permute-start.9 = (bf16[256,1152]{1,0:T(8,128)(2,1)}, bf16[256,1152]{1,0:T(8,128)(2,1)S(1)}, u32[]{:S(2)}, u32[]{:S(2)}) collective-permute-start(bf16[256,1152]{1,0:T(8,128)(2,1)} %get-tuple-element.23.own), channel_id=1, source_target_pairs={{0,1},{1,0},{2,3},{3,2},{4,5},{5,4},{6,7},{7,6},{8,9},{9,8},{10,11... | collective-permute-start | bytes 1769480 | tf_op jit(solution)/shard_map/ppermute | solution.py:60
  87.2 10.9 %copy-start.4 = (bf16[256,1152]{1,0:T(8,128)(2,1)S(1)}, bf16[256,1152]{1,0:T(8,128)(2,1)}, u32[]{:S(2)}) copy-start(bf16[256,1152]{1,0:T(8,128)(2,1)} %get-tuple-element.23.own) | copy-start | bytes 1769476
  91.1 20.6 %collective-permute-start.8 = (bf16[288,512]{1,0:T(8,128)(2,1)}, bf16[288,512]{1,0:T(8,128)(2,1)S(1)}, u32[]{:S(2)}, u32[]{:S(2)}) collective-permute-start(bf16[288,512]{1,0:T(8,128)(2,1)} %get-tuple-element.22), channel_id=1, source_target_pairs={{0,64},{1,65},{2,66},{3,67},{4,68},{5,69},{6,70},{7,71},{8,72},{9,... | collective-permute-start | bytes 884744 | tf_op jit(solution)/shard_map/ppermute | solution.py:418
  101.7 17.8 %all-to-all-start.1 = ((bf16[32,16,144]{2,1,0:T(8,128)(2,1)}), bf16[32,16,144]{2,1,0:T(8,128)(2,1)S(1)}, u32[]{:S(2)}, u32[]{:S(2)}) async-start(bf16[32,16,144]{2,1,0:T(8,128)(2,1)} %shard_map.78), calls=%async_computation.1 | async-start | bytes 524288 | tf_op jit(solution)/shard_map/all_to_all | solution.py:435
  106.4 24.1 %collective-permute-start.12 = (bf16[576,1152]{1,0:T(8,128)(2,1)S(1)}, bf16[576,1152]{1,0:T(8,128)(2,1)}, u32[]{:S(2)}, u32[]{:S(2)}) collective-permute-start(bf16[576,1152]{1,0:T(8,128)(2,1)S(1)} %get-tuple-element.32.w_own), channel_id=1, source_target_pairs={{0,1},{1,0},{2,3},{3,2},{4,5},{5,4},{6,7},{7,6},{8,9},{9,8},{10,11... | collective-permute-start | bytes 3981320 | tf_op jit(solution)/shard_map/ppermute | solution.py:60
  111.7 10.5 %collective-permute-start.10 = (bf16[288,512]{1,0:T(8,128)(2,1)S(1)}, bf16[288,512]{1,0:T(8,128)(2,1)S(1)}, u32[]{:S(2)}, u32[]{:S(2)}) collective-permute-start(bf16[288,512]{1,0:T(8,128)(2,1)S(1)} %collective-permute-done.8.kv_a), channel_id=1, source_target_pairs={{0,128},{1,129},{2,130},{3,131},{4,132},{5,133},{6,134},{7,135},{8... | collective-permute-start | bytes 884744 | tf_op jit(solution)/shard_map/ppermute | solution.py:421
  124.8 5.7 %collective-permute-start.11 = (bf16[256,576]{1,0:T(8,128)(2,1)S(1)}, bf16[256,576]{1,0:T(8,128)(2,1)S(1)}, u32[]{:S(2)}, u32[]{:S(2)}) collective-permute-start(bf16[256,576]{1,0:T(8,128)(2,1)S(1)} %get-tuple-element.31), channel_id=1, source_target_pairs={{0,1},{1,0},{2,3},{3,2},{4,5},{5,4},{6,7},{7,6},{8,9},{9,8},{10,11... | collective-permute-start | bytes 884744 | tf_op jit(solution)/shard_map/ppermute | solution.py:60

commit v10 on v9

--- a/solution.py
+++ b/solution.py
@@ -76,14 +76,15 @@
     return lax.optimization_barrier((value,) + others)[0]
 
 
-def pack_kernel(tokens, w_qkv_hbm, w_out_hbm, out, w_qkv, w_out, pieces, sem):
+def pack_kernel(w_qkv_hbm, w_out_hbm, tokens_hbm, out, w_qkv, w_out, tokens, pieces, staged, sem):
     loads = [
         pltpu.make_async_copy(w_qkv_hbm, w_qkv, sem.at[0]),
         pltpu.make_async_copy(w_out_hbm, w_out, sem.at[1]),
+        pltpu.make_async_copy(tokens_hbm, tokens, sem.at[2]),
     ]
     for load in loads:
         load.start()
-    for load in loads:
+    for load in loads[:2]:
         load.wait()
 
     def columns(kind, head):
@@ -116,13 +117,19 @@
             pieces[place, 41:] = jnp.zeros((3, 128), F32)
     x, yh = position()[:2]
     base = 2 * x + 4 * yh
+    loads[2].wait()
+    stores = []
     for dest in range(64):
         colour = (base + dest // 16 + 3 * (dest // 2 % 8)) % 8
         block = tokens[dest // 2 * 8 : dest // 2 * 8 + 8].astype(F32)
         block = block[dest % 2 * 4 : dest % 2 * 4 + 4]
         rows = [block[:, tile * 128 : tile * 128 + 128] for tile in range(9)]
         rows = [pieces[dest % 2 * 8 + colour]] + rows
-        out[dest] = jnp.concatenate(rows, 0).astype(BF16)
+        staged[dest] = jnp.concatenate(rows, 0).astype(BF16)
+        stores.append(pltpu.make_async_copy(staged.at[dest], out.at[dest], sem.at[3]))
+        stores[-1].start()
+    for store in stores:
+        store.wait()
 
 
 def unpack_kernel(got, block, block_out, tokens_out, tokens, wide, sem):
@@ -234,7 +241,9 @@
     store.wait()
 
 
-def time_kernel(gains, normed, weight, out):
+def time_kernel(gains, normed, weight, late, out, late_out, sem):
+    store = pltpu.make_async_copy(late, late_out, sem)
+    store.start()
     q, k, v = project_pair(normed, weight[0, PAIR:], weight[1], gains[...].T[:, 1:2])
     row = lax.broadcasted_iota(jnp.int32, (HALF, HALF), 0) % 8
     col = lax.broadcasted_iota(jnp.int32, (HALF, HALF), 1) % 8
@@ -251,6 +260,7 @@
     one = jnp.where(swap, sets[1], sets[0])
     two = jnp.where(swap, sets[0], sets[1])
     out[...] = jnp.concatenate([one, two], 1).reshape(32, 16, PAIR).astype(BF16)
+    store.wait()
 
 
 def space_kernel(gains, normed_hbm, weight_hbm, out, normed, result, weight, sem):
@@ -373,16 +383,18 @@
 
     pieces = call(
         pack_kernel,
-        shape(64, PIECE, 128),
-        (tokens, w_qkv, w_out),
+        far(64, PIECE, 128),
+        (w_qkv, w_out, tokens),
         [
             pltpu.VMEM((18, 3 * D), BF16),
             pltpu.VMEM((18, D), BF16),
+            pltpu.VMEM((HALF, D), BF16),
             pltpu.VMEM((16, 44, 128), F32),
-            pltpu.SemaphoreType.DMA((2,)),
+            pltpu.VMEM((64, PIECE, 128), BF16),
+            pltpu.SemaphoreType.DMA((4,)),
         ],
         0,
-        2,
+        3,
         58 * 1024 * 1024,
     )
     got = lax.all_to_all(pieces, SLAB, 0, 0, tiled=True)
@@ -409,15 +421,20 @@
     time_normed = keep_near(call(norm_kernel, near(ROWS, D), (time_own, time_other, cam_embed, gain), (), 8 * 10**9))
     q_t, kv_t, w_own, early, late = call(
         cross_project_kernel,
-        (far(PAIR, ROWS), shape(2 * PAIR, ROWS), near(4 * PAIR, D), near(2, QUAD, D), far(4, QUAD, D)),
+        (far(PAIR, ROWS), shape(2 * PAIR, ROWS), near(4 * PAIR, D), near(2, QUAD, D), near(4, QUAD, D)),
         (gains, normed) + blocks,
         [pltpu.VMEM((PAIR, ROWS), BF16), pltpu.VMEM((2, QUAD, D), BF16), pltpu.SemaphoreType.DMA((13,))],
         0,
         8,
     )
     kv_a = lax.ppermute(kv_t, EVERY, ACROSS)
-    w_other = swap_core(w_own)
-    timed = call(time_kernel, shape(32, 16, PAIR), (gains, after(time_normed, kv_t), keep_near(early)))
+    w_other = keep_near(swap_core(w_own))
+    timed, late = call(
+        time_kernel,
+        (shape(32, 16, PAIR), far(4, QUAD, D)),
+        (gains, after(time_normed, kv_t), keep_near(early), keep_near(late)),
+        [pltpu.SemaphoreType.DMA],
+    )
     kv_b = lax.ppermute(after(kv_a, timed), EVERY, ALONG)
     space = call(
         space_kernel,

time: 135 us -> 135 us (level)
  transfers between devices with their start and end apart: 15 -> 15, of which waited for: 7 -> 7; matrix products, arithmetic and copies ran while one was open for 0% -> 0% of each run, Pallas kernels for 12% -> 13%
where the time goes in v10:
time: 135 us; the launch traced here: 134 us
  starting transfers between devices  67.3 us (50%)
  waiting for transfers between devices  39.2 us (29%)
  Pallas kernels  25.6 us (19%)
  local copies, waits for them, and re-layouts  1.43 us (1%)
    all_to_all x1, waiting for transfers between devices, local(): got = lax.all_to_all(pieces, SLAB, 0, 0, tiled=True)  28.1 us
    pallas_call x9, Pallas kernels, call(): pl.pallas_call(kernel, out_shape=out_shapes, in_specs=specs, out_specs=pl...  25.6 us
    ppermute x6, starting transfers between devices, local(): blocks.append(lax.ppermute(block, EVERY, way))  19.5 us
    ppermute x4, starting transfers between devices, swap_core(): return lax.ppermute(block, 'core', [(0, 1), (1, 0)])  16.6 us
    all_to_all x1, starting transfers between devices, local(): got = lax.all_to_all(pieces, SLAB, 0, 0, tiled=True)  15.6 us
    ppermute x1, starting transfers between devices, local(): kv_a = lax.ppermute(kv_t, EVERY, ACROSS)  6.99 us
    all_to_all x1, starting transfers between devices, local(): returned = lax.all_to_all(timed, CHIP, 0, 0, tiled=True)  4.66 us
    ppermute x6, waiting for transfers between devices, local(): blocks.append(lax.ppermute(block, EVERY, way))  4.61 us
  transfers between devices with their start and end apart: 15, of which 7 were waited for; matrix products, arithmetic and copies ran while one was open for 0% of the time, Pallas kernels for 13%

profile of v10, /device:TPU:1, one launch (start us, length us, event | category | flops | bytes accessed | tf_op | source)
XLA Modules:
  0.0 134.2 jit_solution(1061999592758619203)
XLA Ops:
  0.0 2.7 %shard_map.74 = bf16[64,80,128]{2,1,0:T(8,128)(2,1)} custom-call(bf16[18,3456]{1,0:T(8,128)(2,1)} %w_qkv_hbm.1, bf16[18,1152]{1,0:T(8,128)(2,1)} %w_out_hbm.1, bf16[256,1152]{1,0:T(8,128)(2,1)} %bitcast.8), custom_call_target="tpu_custom_call" | custom-call | bytes 1 | tf_op jit(solution)/shard_map/pallas_call | solution.py:339
  2.7 0.0 copy-start
  2.7 0.0 copy-start.5
  2.7 0.0 copy-start.6
  2.7 0.0 copy-start.7
  2.7 0.0 copy-start.3
  2.7 15.6 %all-to-all-start = ((bf16[64,80,128]{2,1,0:T(8,128)(2,1)}), bf16[64,80,128]{2,1,0:T(8,128)(2,1)S(1)}, u32[]{:S(2)}, u32[]{:S(2)}) async-start(bf16[64,80,128]{2,1,0:T(8,128)(2,1)} %shard_map.74), calls=%async_computation | async-start | bytes 2621440 | tf_op jit(solution)/shard_map/all_to_all | solution.py:400
  18.3 2.4 %collective-permute-start = (bf16[256,1152]{1,0:T(8,128)(2,1)S(1)}, bf16[256,1152]{1,0:T(8,128)(2,1)S(1)}, u32[]{:S(2)}, u32[]{:S(2)}) collective-permute-start(bf16[256,1152]{1,0:T(8,128)(2,1)S(1)} %bitcast.9), channel_id=1, source_target_pairs={{0,1},{1,0},{2,3},{3,2},{4,5},{5,4},{6,7},{7,6},{8,9},{9,8},{10,11... | collective-permute-start | bytes 1769480 | tf_op jit(solution)/shard_map/ppermute | solution.py:60
  20.7 0.1 stack_reshape.6
  20.8 0.1 stack_reshape.7
  21.0 0.1 reshape.6
  21.0 0.1 reshape.7
  21.2 1.1 collective-permute-done.other
  22.3 0.8 shard_map.73.normed.normed_hbm
  23.1 1.0 copy-done.1
  24.1 28.1 %all-to-all-done.got = bf16[64,80,128]{2,1,0:T(8,128)(2,1)S(1)} async-done(((bf16[64,80,128]{2,1,0:T(8,128)(2,1)}), bf16[64,80,128]{2,1,0:T(8,128)(2,1)S(1)}, u32[]{:S(2)}, u32[]{:S(2)}) %all-to-all-start) | async-done | bytes 1310752 | tf_op jit(solution)/shard_map/all_to_all | solution.py:400
  52.2 1.6 %shard_map.75 = (bf16[288,1152]{1,0:T(8,128)(2,1)S(1)}, bf16[288,1152]{1,0:T(8,128)(2,1)}, bf16[256,1152]{1,0:T(8,128)(2,1)}) custom-call(bf16[64,80,128]{2,1,0:T(8,128)(2,1)S(1)} %all-to-all-done.got), custom_call_target="tpu_custom_call" | custom-call | bytes 1 | tf_op jit(solution)/shard_map/pallas_call | solution.py:339
  53.8 3.1 %collective-permute-start.1 = (bf16[288,1152]{1,0:T(8,128)(2,1)}, bf16[288,1152]{1,0:T(8,128)(2,1)S(1)}, u32[]{:S(2)}, u32[]{:S(2)}) collective-permute-start(bf16[288,1152]{1,0:T(8,128)(2,1)} %get-tuple-element.23), channel_id=1, source_target_pairs={{0,384},{1,129},{2,386},{3,131},{4,388},{5,133},{6,390},{7,135},{8... | collective-permute-start | bytes 1990664 | tf_op jit(solution)/shard_map/ppermute | solution.py:418
  57.0 3.1 %collective-permute-start.2 = (bf16[288,1152]{1,0:T(8,128)(2,1)}, bf16[288,1152]{1,0:T(8,128)(2,1)S(1)}, u32[]{:S(2)}, u32[]{:S(2)}) collective-permute-start(bf16[288,1152]{1,0:T(8,128)(2,1)} %get-tuple-element.23), channel_id=1, source_target_pairs={{0,112},{1,17},{2,114},{3,19},{4,116},{5,21},{6,118},{7,23},{8,120... | collective-permute-start | bytes 1990664 | tf_op jit(solution)/shard_map/ppermute | solution.py:418
  60.1 3.4 %collective-permute-start.3 = (bf16[288,1152]{1,0:T(8,128)(2,1)}, bf16[288,1152]{1,0:T(8,128)(2,1)S(1)}, u32[]{:S(2)}, u32[]{:S(2)}) collective-permute-start(bf16[288,1152]{1,0:T(8,128)(2,1)} %get-tuple-element.23), channel_id=1, source_target_pairs={{0,128},{1,385},{2,130},{3,387},{4,132},{5,389},{6,134},{7,391},{8... | collective-permute-start | bytes 1990664 | tf_op jit(solution)/shard_map/ppermute | solution.py:418
  63.5 3.2 %collective-permute-start.4 = (bf16[288,1152]{1,0:T(8,128)(2,1)}, bf16[288,1152]{1,0:T(8,128)(2,1)S(1)}, u32[]{:S(2)}, u32[]{:S(2)}) collective-permute-start(bf16[288,1152]{1,0:T(8,128)(2,1)} %get-tuple-element.23), channel_id=1, source_target_pairs={{0,14},{1,3},{2,0},{3,5},{4,2},{5,7},{6,4},{7,9},{8,6},{9,11},{10,... | collective-permute-start | bytes 1990664 | tf_op jit(solution)/shard_map/ppermute | solution.py:418
  66.7 3.3 %collective-permute-start.5 = (bf16[288,1152]{1,0:T(8,128)(2,1)}, bf16[288,1152]{1,0:T(8,128)(2,1)S(1)}, u32[]{:S(2)}, u32[]{:S(2)}) collective-permute-start(bf16[288,1152]{1,0:T(8,128)(2,1)} %get-tuple-element.23), channel_id=1, source_target_pairs={{0,16},{1,113},{2,18},{3,115},{4,20},{5,117},{6,22},{7,119},{8,24}... | collective-permute-start | bytes 1990664 | tf_op jit(solution)/shard_map/ppermute | solution.py:418
  70.0 0.0 collective-permute-done.1.refs_1_
  70.0 3.4 %collective-permute-start.7 = (bf16[288,1152]{1,0:T(8,128)(2,1)}, bf16[288,1152]{1,0:T(8,128)(2,1)S(1)}, u32[]{:S(2)}, u32[]{:S(2)}) collective-permute-start(bf16[288,1152]{1,0:T(8,128)(2,1)} %get-tuple-element.23), channel_id=1, source_target_pairs={{0,2},{1,15},{2,4},{3,1},{4,6},{5,3},{6,8},{7,5},{8,10},{9,7},{10,... | collective-permute-start | bytes 1990664 | tf_op jit(solution)/shard_map/ppermute | solution.py:418
  73.4 0.0 collective-permute-done.2.refs_2_
  73.4 1.9 %collective-permute-start.6 = (bf16[288,1152]{1,0:T(8,128)(2,1)S(1)}, bf16[288,1152]{1,0:T(8,128)(2,1)S(1)}, u32[]{:S(2)}, u32[]{:S(2)}) collective-permute-start(bf16[288,1152]{1,0:T(8,128)(2,1)S(1)} %collective-permute-done.1.refs_1_), channel_id=1, source_target_pairs={{0,384},{1,129},{2,386},{3,131},{4,388},{5,133},{6,390},{7,135},{8... | collective-permute-start | bytes 1990664 | tf_op jit(solution)/shard_map/ppermute | solution.py:416
  75.3 0.0 collective-permute-done.3.refs_3_
  75.3 4.9 %collective-permute-start.9 = (bf16[256,1152]{1,0:T(8,128)(2,1)}, bf16[256,1152]{1,0:T(8,128)(2,1)S(1)}, u32[]{:S(2)}, u32[]{:S(2)}) collective-permute-start(bf16[256,1152]{1,0:T(8,128)(2,1)} %get-tuple-element.25.own), channel_id=1, source_target_pairs={{0,1},{1,0},{2,3},{3,2},{4,5},{5,4},{6,7},{7,6},{8,9},{9,8},{10,11... | collective-permute-start | bytes 1769480 | tf_op jit(solution)/shard_map/ppermute | solution.py:60
  80.2 0.0 collective-permute-done.4.refs_4_
  80.2 0.0 collective-permute-done.5.refs_5_
  80.2 4.6 %collective-permute-done.7.refs_7_ = bf16[288,1152]{1,0:T(8,128)(2,1)S(1)} collective-permute-done((bf16[288,1152]{1,0:T(8,128)(2,1)}, bf16[288,1152]{1,0:T(8,128)(2,1)S(1)}, u32[]{:S(2)}, u32[]{:S(2)}) %collective-permute-start.7) | collective-permute-done | bytes 663584 | tf_op jit(solution)/shard_map/ppermute | solution.py:418
  84.8 1.2 collective-permute-done.6.refs_6_
  86.0 4.9 %shard_map.76 = (bf16[144,512]{1,0:T(8,128)(2,1)}, bf16[288,512]{1,0:T(8,128)(2,1)}, bf16[576,1152]{1,0:T(8,128)(2,1)S(1)}, bf16[2,288,1152]{2,1,0:T(8,128)(2,1)S(1)}, bf16[4,288,1152]{2,1,0:T(8,128)(2,1)S(1)}) custom-call(f32[8,288]{1,0:T(8,128)S(1)} %select_maximum_fusion.gains, bf16[512,1152]{1,0:T(8,128)(2,1)S(1)} %copy-done.2, ...), custom_call_target="tpu_custom_call" | custom-call | bytes 1 | tf_op jit(solution)/shard_map/pallas_call | solution.py:339
  90.9 7.0 %collective-permute-start.8 = (bf16[288,512]{1,0:T(8,128)(2,1)}, bf16[288,512]{1,0:T(8,128)(2,1)S(1)}, u32[]{:S(2)}, u32[]{:S(2)}) collective-permute-start(bf16[288,512]{1,0:T(8,128)(2,1)} %get-tuple-element.24), channel_id=1, source_target_pairs={{0,64},{1,65},{2,66},{3,67},{4,68},{5,69},{6,70},{7,71},{8,72},{9,... | collective-permute-start | bytes 884744 | tf_op jit(solution)/shard_map/ppermute | solution.py:430
  97.9 0.0 collective-permute-done.9.other
  97.9 0.8 shard_map.77.normed
  98.7 2.8 %shard_map.78 = (bf16[32,16,144]{2,1,0:T(8,128)(2,1)}, bf16[4,288,1152]{2,1,0:T(8,128)(2,1)}) custom-call(f32[8,288]{1,0:T(8,128)S(1)} %select_maximum_fusion.gains, bf16[512,1152]{1,0:T(8,128)(2,1)S(1)} %shard_map.77.normed, bf16[2,288,1152]{2,1,0:T(8,128)(2,1)S(1)} %get-tuple-element.27.weight, bf16[4,288,1152]{2,1,0:T(8,128)(2,1)S(1)} %get-tuple-element.28.late), custom_call_target="tpu_custom_call" | custom-call | bytes 1 | tf_op jit(solution)/shard_map/pallas_call | solution.py:339
  101.6 4.7 %all-to-all-start.1 = ((bf16[32,16,144]{2,1,0:T(8,128)(2,1)}), bf16[32,16,144]{2,1,0:T(8,128)(2,1)S(1)}, u32[]{:S(2)}, u32[]{:S(2)}) async-start(bf16[32,16,144]{2,1,0:T(8,128)(2,1)} %get-tuple-element.29), calls=%async_computation.1 | async-start | bytes 524288 | tf_op jit(solution)/shard_map/all_to_all | solution.py:452
  106.3 5.1 %collective-permute-start.12 = (bf16[576,1152]{1,0:T(8,128)(2,1)S(1)}, bf16[576,1152]{1,0:T(8,128)(2,1)}, u32[]{:S(2)}, u32[]{:S(2)}) collective-permute-start(bf16[576,1152]{1,0:T(8,128)(2,1)S(1)} %get-tuple-element.36.w_own), channel_id=1, source_target_pairs={{0,1},{1,0},{2,3},{3,2},{4,5},{5,4},{6,7},{7,6},{8,9},{9,8},{10,11... | collective-permute-start | bytes 3981320 | tf_op jit(solution)/shard_map/ppermute | solution.py:60
  111.3 0.2 collective-permute-done.8.kv_a
  111.5 2.1 %collective-permute-start.10 = (bf16[288,512]{1,0:T(8,128)(2,1)S(1)}, bf16[288,512]{1,0:T(8,128)(2,1)S(1)}, u32[]{:S(2)}, u32[]{:S(2)}) collective-permute-start(bf16[288,512]{1,0:T(8,128)(2,1)S(1)} %collective-permute-done.8.kv_a), channel_id=1, source_target_pairs={{0,128},{1,129},{2,130},{3,131},{4,132},{5,133},{6,134},{7,135},{8... | collective-permute-start | bytes 884744 | tf_op jit(solution)/shard_map/ppermute | solution.py:438
  113.6 5.8 %shard_map.79.space_hbm = bf16[288,512]{1,0:T(8,128)(2,1)} custom-call(f32[8,288]{1,0:T(8,128)S(1)} %select_maximum_fusion.gains, bf16[512,1152]{1,0:T(8,128)(2,1)} %copy-done.1, bf16[4,288,1152]{2,1,0:T(8,128)(2,1)} %get-tuple-element.32.weight_hbm), custom_call_target="tpu_custom_call" | custom-call | flops 16000000000 | bytes 1 | tf_op jit(solution)/shard_map/pallas_call | solution.py:339
  119.4 0.0 all-to-all-done.1.timed
  119.4 2.7 %collective-permute-done.10.kv_b = bf16[288,512]{1,0:T(8,128)(2,1)S(1)} collective-permute-done((bf16[288,512]{1,0:T(8,128)(2,1)S(1)}, bf16[288,512]{1,0:T(8,128)(2,1)S(1)}, u32[]{:S(2)}, u32[]{:S(2)}) %collective-permute-start.10) | collective-permute-done | bytes 294944 | tf_op jit(solution)/shard_map/ppermute | solution.py:438
  122.1 2.6 %shard_map.80 = (bf16[256,576]{1,0:T(8,128)(2,1)S(1)}, bf16[256,576]{1,0:T(8,128)(2,1)S(1)}) custom-call(bf16[288,512]{1,0:T(8,128)(2,1)S(1)} %collective-permute-done.8.kv_a, bf16[288,512]{1,0:T(8,128)(2,1)S(1)} %collective-permute-done.10.kv_b, bf16[32,16,144]{2,1,0:T(8,128)(2,1)S(1)} %all-to-all-done.1.timed, bf16[288,512]{1,0:T(8,128)(2,1)} %shard_map.79.space_hbm, ...), custom_call_target="tpu_custom_call" | custom-call | bytes 1 | tf_op jit(solution)/shard_map/pallas_call | solution.py:339
  124.7 4.4 %collective-permute-start.11 = (bf16[256,576]{1,0:T(8,128)(2,1)S(1)}, bf16[256,576]{1,0:T(8,128)(2,1)S(1)}, u32[]{:S(2)}, u32[]{:S(2)}) collective-permute-start(bf16[256,576]{1,0:T(8,128)(2,1)S(1)} %get-tuple-element.35), channel_id=1, source_target_pairs={{0,1},{1,0},{2,3},{3,2},{4,5},{5,4},{6,7},{7,6},{8,9},{9,8},{10,11... | collective-permute-start | bytes 884744 | tf_op jit(solution)/shard_map/ppermute | solution.py:60
  129.1 1.2 collective-permute-done.11.arrived
  130.3 3.7 %shard_map.81 = bf16[256,1152]{1,0:T(8,128)(2,1)} custom-call(bf16[256,1152]{1,0:T(8,128)(2,1)S(1)} %bitcast.11, bf16[256,576]{1,0:T(8,128)(2,1)S(1)} %get-tuple-element.34.own, bf16[256,576]{1,0:T(8,128)(2,1)S(1)} %collective-permute-done.11.arrived, bf16[576,1152]{1,0:T(8,128)(2,1)S(1)} %get-tuple-element.36.w_own, ...), custom_call_target="tpu_custom_call" | custom-call | bytes 1 | tf_op jit(solution)/shard_map/pallas_call | solution.py:339
  (17 shorter events, 0.1 us)
Async XLA Ops:
  2.7 15.6 %copy-start = (bf16[1,256,1152]{2,1,0:T(8,128)(2,1)S(1)}, bf16[1,256,1152]{2,1,0:T(8,128)(2,1)}, u32[]{:S(2)}) copy-start(bf16[1,256,1152]{2,1,0:T(8,128)(2,1)} %param.7) | copy-start | bytes 1769476
  2.7 18.0 %copy-start.5 = (f32[1152]{0:T(1024)S(1)}, f32[1152]{0:T(1024)}, u32[]{:S(2)}) copy-start(f32[1152]{0:T(1024)} %param.10) | copy-start | bytes 13828
  2.7 18.1 %copy-start.6 = (f32[1152]{0:T(1024)S(1)}, f32[1152]{0:T(1024)}, u32[]{:S(2)}) copy-start(f32[1152]{0:T(1024)} %param.11) | copy-start | bytes 13828
  2.7 18.4 %copy-start.7 = (f32[1152]{0:T(1024)S(1)}, f32[1152]{0:T(1024)}, u32[]{:S(2)}) copy-start(f32[1152]{0:T(1024)} %param.9) | copy-start | bytes 13828
  2.7 19.6 %copy-start.3 = (f32[8,1152]{1,0:T(8,128)S(1)}, f32[8,1152]{1,0:T(8,128)}, u32[]{:S(2)}) copy-start(f32[8,1152]{1,0:T(8,128)} %embed_hbm.1) | copy-start | bytes 110596
  2.7 49.5 %all-to-all-start = ((bf16[64,80,128]{2,1,0:T(8,128)(2,1)}), bf16[64,80,128]{2,1,0:T(8,128)(2,1)S(1)}, u32[]{:S(2)}, u32[]{:S(2)}) async-start(bf16[64,80,128]{2,1,0:T(8,128)(2,1)} %shard_map.74), calls=%async_computation | async-start | bytes 2621440 | tf_op jit(solution)/shard_map/all_to_all | solution.py:400
  18.3 4.0 %collective-permute-start = (bf16[256,1152]{1,0:T(8,128)(2,1)S(1)}, bf16[256,1152]{1,0:T(8,128)(2,1)S(1)}, u32[]{:S(2)}, u32[]{:S(2)}) collective-permute-start(bf16[256,1152]{1,0:T(8,128)(2,1)S(1)} %bitcast.9), channel_id=1, source_target_pairs={{0,1},{1,0},{2,3},{3,2},{4,5},{5,4},{6,7},{7,6},{8,9},{9,8},{10,11... | collective-permute-start | bytes 1769480 | tf_op jit(solution)/shard_map/ppermute | solution.py:60
  23.1 1.1 copy-start.1
  52.2 33.8 %copy-start.2 = (bf16[512,1152]{1,0:T(8,128)(2,1)S(1)}, bf16[512,1152]{1,0:T(8,128)(2,1)}, u32[]{:S(2)}) copy-start(bf16[512,1152]{1,0:T(8,128)(2,1)} %copy-done.1) | copy-start | bytes 3538948
  53.8 16.1 %collective-permute-start.1 = (bf16[288,1152]{1,0:T(8,128)(2,1)}, bf16[288,1152]{1,0:T(8,128)(2,1)S(1)}, u32[]{:S(2)}, u32[]{:S(2)}) collective-permute-start(bf16[288,1152]{1,0:T(8,128)(2,1)} %get-tuple-element.23), channel_id=1, source_target_pairs={{0,384},{1,129},{2,386},{3,131},{4,388},{5,133},{6,390},{7,135},{8... | collective-permute-start | bytes 1990664 | tf_op jit(solution)/shard_map/ppermute | solution.py:418
  57.0 16.4 %collective-permute-start.2 = (bf16[288,1152]{1,0:T(8,128)(2,1)}, bf16[288,1152]{1,0:T(8,128)(2,1)S(1)}, u32[]{:S(2)}, u32[]{:S(2)}) collective-permute-start(bf16[288,1152]{1,0:T(8,128)(2,1)} %get-tuple-element.23), channel_id=1, source_target_pairs={{0,112},{1,17},{2,114},{3,19},{4,116},{5,21},{6,118},{7,23},{8,120... | collective-permute-start | bytes 1990664 | tf_op jit(solution)/shard_map/ppermute | solution.py:418
  60.1 15.2 %collective-permute-start.3 = (bf16[288,1152]{1,0:T(8,128)(2,1)}, bf16[288,1152]{1,0:T(8,128)(2,1)S(1)}, u32[]{:S(2)}, u32[]{:S(2)}) collective-permute-start(bf16[288,1152]{1,0:T(8,128)(2,1)} %get-tuple-element.23), channel_id=1, source_target_pairs={{0,128},{1,385},{2,130},{3,387},{4,132},{5,389},{6,134},{7,391},{8... | collective-permute-start | bytes 1990664 | tf_op jit(solution)/shard_map/ppermute | solution.py:418
  63.5 16.7 %collective-permute-start.4 = (bf16[288,1152]{1,0:T(8,128)(2,1)}, bf16[288,1152]{1,0:T(8,128)(2,1)S(1)}, u32[]{:S(2)}, u32[]{:S(2)}) collective-permute-start(bf16[288,1152]{1,0:T(8,128)(2,1)} %get-tuple-element.23), channel_id=1, source_target_pairs={{0,14},{1,3},{2,0},{3,5},{4,2},{5,7},{6,4},{7,9},{8,6},{9,11},{10,... | collective-permute-start | bytes 1990664 | tf_op jit(solution)/shard_map/ppermute | solution.py:418
  66.7 13.5 %collective-permute-start.5 = (bf16[288,1152]{1,0:T(8,128)(2,1)}, bf16[288,1152]{1,0:T(8,128)(2,1)S(1)}, u32[]{:S(2)}, u32[]{:S(2)}) collective-permute-start(bf16[288,1152]{1,0:T(8,128)(2,1)} %get-tuple-element.23), channel_id=1, source_target_pairs={{0,16},{1,113},{2,18},{3,115},{4,20},{5,117},{6,22},{7,119},{8,24}... | collective-permute-start | bytes 1990664 | tf_op jit(solution)/shard_map/ppermute | solution.py:418
  70.0 14.8 %collective-permute-start.7 = (bf16[288,1152]{1,0:T(8,128)(2,1)}, bf16[288,1152]{1,0:T(8,128)(2,1)S(1)}, u32[]{:S(2)}, u32[]{:S(2)}) collective-permute-start(bf16[288,1152]{1,0:T(8,128)(2,1)} %get-tuple-element.23), channel_id=1, source_target_pairs={{0,2},{1,15},{2,4},{3,1},{4,6},{5,3},{6,8},{7,5},{8,10},{9,7},{10,... | collective-permute-start | bytes 1990664 | tf_op jit(solution)/shard_map/ppermute | solution.py:418
  73.4 12.6 %collective-permute-start.6 = (bf16[288,1152]{1,0:T(8,128)(2,1)S(1)}, bf16[288,1152]{1,0:T(8,128)(2,1)S(1)}, u32[]{:S(2)}, u32[]{:S(2)}) collective-permute-start(bf16[288,1152]{1,0:T(8,128)(2,1)S(1)} %collective-permute-done.1.refs_1_), channel_id=1, source_target_pairs={{0,384},{1,129},{2,386},{3,131},{4,388},{5,133},{6,390},{7,135},{8... | collective-permute-start | bytes 1990664 | tf_op jit(solution)/shard_map/ppermute | solution.py:416
  75.3 22.6 %collective-permute-start.9 = (bf16[256,1152]{1,0:T(8,128)(2,1)}, bf16[256,1152]{1,0:T(8,128)(2,1)S(1)}, u32[]{:S(2)}, u32[]{:S(2)}) collective-permute-start(bf16[256,1152]{1,0:T(8,128)(2,1)} %get-tuple-element.25.own), channel_id=1, source_target_pairs={{0,1},{1,0},{2,3},{3,2},{4,5},{5,4},{6,7},{7,6},{8,9},{9,8},{10,11... | collective-permute-start | bytes 1769480 | tf_op jit(solution)/shard_map/ppermute | solution.py:60
  86.0 11.9 %copy-start.4 = (bf16[256,1152]{1,0:T(8,128)(2,1)S(1)}, bf16[256,1152]{1,0:T(8,128)(2,1)}, u32[]{:S(2)}) copy-start(bf16[256,1152]{1,0:T(8,128)(2,1)} %get-tuple-element.25.own) | copy-start | bytes 1769476
  90.9 20.6 %collective-permute-start.8 = (bf16[288,512]{1,0:T(8,128)(2,1)}, bf16[288,512]{1,0:T(8,128)(2,1)S(1)}, u32[]{:S(2)}, u32[]{:S(2)}) collective-permute-start(bf16[288,512]{1,0:T(8,128)(2,1)} %get-tuple-element.24), channel_id=1, source_target_pairs={{0,64},{1,65},{2,66},{3,67},{4,68},{5,69},{6,70},{7,71},{8,72},{9,... | collective-permute-start | bytes 884744 | tf_op jit(solution)/shard_map/ppermute | solution.py:430
  101.6 17.8 %all-to-all-start.1 = ((bf16[32,16,144]{2,1,0:T(8,128)(2,1)}), bf16[32,16,144]{2,1,0:T(8,128)(2,1)S(1)}, u32[]{:S(2)}, u32[]{:S(2)}) async-start(bf16[32,16,144]{2,1,0:T(8,128)(2,1)} %get-tuple-element.29), calls=%async_computation.1 | async-start | bytes 524288 | tf_op jit(solution)/shard_map/all_to_all | solution.py:452
  106.3 24.1 %collective-permute-start.12 = (bf16[576,1152]{1,0:T(8,128)(2,1)S(1)}, bf16[576,1152]{1,0:T(8,128)(2,1)}, u32[]{:S(2)}, u32[]{:S(2)}) collective-permute-start(bf16[576,1152]{1,0:T(8,128)(2,1)S(1)} %get-tuple-element.36.w_own), channel_id=1, source_target_pairs={{0,1},{1,0},{2,3},{3,2},{4,5},{5,4},{6,7},{7,6},{8,9},{9,8},{10,11... | collective-permute-start | bytes 3981320 | tf_op jit(solution)/shard_map/ppermute | solution.py:60
  111.5 10.6 %collective-permute-start.10 = (bf16[288,512]{1,0:T(8,128)(2,1)S(1)}, bf16[288,512]{1,0:T(8,128)(2,1)S(1)}, u32[]{:S(2)}, u32[]{:S(2)}) collective-permute-start(bf16[288,512]{1,0:T(8,128)(2,1)S(1)} %collective-permute-done.8.kv_a), channel_id=1, source_target_pairs={{0,128},{1,129},{2,130},{3,131},{4,132},{5,133},{6,134},{7,135},{8... | collective-permute-start | bytes 884744 | tf_op jit(solution)/shard_map/ppermute | solution.py:438
  124.7 5.6 %collective-permute-start.11 = (bf16[256,576]{1,0:T(8,128)(2,1)S(1)}, bf16[256,576]{1,0:T(8,128)(2,1)S(1)}, u32[]{:S(2)}, u32[]{:S(2)}) collective-permute-start(bf16[256,576]{1,0:T(8,128)(2,1)S(1)} %get-tuple-element.35), channel_id=1, source_target_pairs={{0,1},{1,0},{2,3},{3,2},{4,5},{5,4},{6,7},{7,6},{8,9},{9,8},{10,11... | collective-permute-start | bytes 884744 | tf_op jit(solution)/shard_map/ppermute | solution.py:60

commit v11 on v10

--- a/solution.py
+++ b/solution.py
@@ -132,7 +132,7 @@
         store.wait()
 
 
-def unpack_kernel(got, block, block_out, tokens_out, tokens, wide, sem):
+def unpack_kernel(got, own_out, block_out, tokens_out, block, tokens, wide, sem):
     for source in range(64):
         rows = got[source].astype(F32)
         at = source * 18
@@ -155,6 +155,7 @@
     stores = [
         pltpu.make_async_copy(block, block_out, sem.at[0]),
         pltpu.make_async_copy(tokens, tokens_out, sem.at[1]),
+        pltpu.make_async_copy(block, own_out, sem.at[2]),
     ]
     for store in stores:
         store.start()
@@ -287,7 +288,9 @@
     store.wait()
 
 
-def cross_kernel(kv_a, kv_b, timed, space_hbm, q_hbm, keep, give, space, q_t, sem):
+def cross_kernel(kv_a, kv_b, timed, space_hbm, q_hbm, w_hbm, keep, give, w_out, space, q_t, sem):
+    w_load = pltpu.make_async_copy(w_hbm, w_out, sem.at[2])
+    w_load.start()
     loads = [pltpu.make_async_copy(q_hbm, q_t, sem.at[0]), pltpu.make_async_copy(space_hbm, space, sem.at[1])]
     for load in loads:
         load.start()
@@ -306,6 +309,7 @@
     swap = lax.axis_index("core") == 1
     keep[...] = jnp.concatenate([mixed[:HALF], jnp.where(swap, late[1], late[0])], 1).astype(BF16)
     give[...] = jnp.concatenate([mixed[HALF:], jnp.where(swap, late[0], late[1])], 1).astype(BF16)
+    w_load.wait()
 
 
 def out_kernel(tokens, own, arrived, w_own, w_other, embed_hbm, out, cam_embed, sem):
@@ -333,7 +337,7 @@
         specs.append(hbm if i >= len(args) - anys else vmem)
 
     def place(out):
-        return hbm if getattr(out, "memory_space", None) == pltpu.HBM else vmem
+        return pl.BlockSpec(memory_space=pl.ANY) if hasattr(out, "memory_space") else vmem
 
     single = not isinstance(out_shapes, tuple)
     return pl.pallas_call(
@@ -399,15 +403,16 @@
     )
     got = lax.all_to_all(pieces, SLAB, 0, 0, tiled=True)
     other = swap_core(tokens)
-    normed = keep_near(call(norm_kernel, near(ROWS, D), (tokens, other, cam_embed, gain), (), 8 * 10**9))
+    normed = keep_near(call(norm_kernel, shape(ROWS, D), (tokens, other, cam_embed, gain), (), 8 * 10**9))
     own_block, block, time_own = call(
         unpack_kernel,
         (near(QUAD, D), far(QUAD, D), far(HALF, D)),
         (after(got, normed, gains),),
         [
+            pltpu.VMEM((QUAD, D), BF16),
             pltpu.VMEM((HALF, D), BF16),
             pltpu.VMEM((3, D, 128), F32),
-            pltpu.SemaphoreType.DMA((2,)),
+            pltpu.SemaphoreType.DMA((3,)),
         ],
     )
     blocks = [keep_near(own_block)]
@@ -418,7 +423,7 @@
             blocks.append(lax.ppermute(block, EVERY, way))
     blocks = tuple(blocks)
     time_other = swap_core(time_own)
-    time_normed = keep_near(call(norm_kernel, near(ROWS, D), (time_own, time_other, cam_embed, gain), (), 8 * 10**9))
+    time_normed = keep_near(call(norm_kernel, shape(ROWS, D), (time_own, time_other, cam_embed, gain), (), 8 * 10**9))
     q_t, kv_t, w_own, early, late = call(
         cross_project_kernel,
         (far(PAIR, ROWS), shape(2 * PAIR, ROWS), near(4 * PAIR, D), near(2, QUAD, D), near(4, QUAD, D)),
@@ -428,12 +433,14 @@
         8,
     )
     kv_a = lax.ppermute(kv_t, EVERY, ACROSS)
-    w_other = keep_near(swap_core(w_own))
+    w_other = swap_core(w_own)
     timed, late = call(
         time_kernel,
         (shape(32, 16, PAIR), far(4, QUAD, D)),
         (gains, after(time_normed, kv_t), keep_near(early), keep_near(late)),
         [pltpu.SemaphoreType.DMA],
+        0,
+        1,
     )
     kv_b = lax.ppermute(after(kv_a, timed), EVERY, ALONG)
     space = call(
@@ -450,19 +457,19 @@
         2,
     )
     returned = lax.all_to_all(timed, CHIP, 0, 0, tiled=True)
-    keep, give = call(
+    keep, give, w_other = call(
         cross_kernel,
-        (shape(HALF, 4 * PAIR), shape(HALF, 4 * PAIR)),
-        (kv_a, kv_b, returned, stay(space), stay(q_t)),
-        [pltpu.VMEM((2 * PAIR, ROWS), BF16), pltpu.VMEM((PAIR, ROWS), BF16), pltpu.SemaphoreType.DMA((2,))],
+        (shape(HALF, 4 * PAIR), shape(HALF, 4 * PAIR), near(4 * PAIR, D)),
+        (kv_a, kv_b, returned, stay(space), stay(q_t), w_other),
+        [pltpu.VMEM((2 * PAIR, ROWS), BF16), pltpu.VMEM((PAIR, ROWS), BF16), pltpu.SemaphoreType.DMA((3,))],
         0,
-        2,
+        3,
     )
     arrived = swap_core(give)
     return call(
         out_kernel,
         shape(HALF, D),
-        (tokens, keep, arrived, w_own, w_other, stay(cam_embed)),
+        (tokens, keep, arrived, w_own, keep_near(w_other), stay(cam_embed)),
         [pltpu.VMEM((8, D), F32), pltpu.SemaphoreType.DMA],
         0,
         1,

time: 135 us -> 134 us (level)
  transfers between devices with their start and end apart: 15 -> 15, of which waited for: 7 -> 7; matrix products, arithmetic and copies ran while one was open for 0% -> 0% of each run, Pallas kernels for 13% -> 11%
where the time goes in v11:
time: 134 us
  starting transfers between devices  67.3 us (50%)
  waiting for transfers between devices  39.2 us (29%)
  Pallas kernels  25.1 us (19%)
  local copies, waits for them, and re-layouts  1.43 us (1%)
    all_to_all x1, waiting for transfers between devices, local(): got = lax.all_to_all(pieces, SLAB, 0, 0, tiled=True)  28.1 us
    pallas_call x9, Pallas kernels, call(): pl.pallas_call(kernel, out_shape=out_shapes, in_specs=specs, out_specs=pl...  25.1 us
    ppermute x6, starting transfers between devices, local(): blocks.append(lax.ppermute(block, EVERY, way))  19.5 us
    ppermute x4, starting transfers between devices, swap_core(): return lax.ppermute(block, 'core', [(0, 1), (1, 0)])  16.7 us
    all_to_all x1, starting transfers between devices, local(): got = lax.all_to_all(pieces, SLAB, 0, 0, tiled=True)  15.6 us
    ppermute x1, starting transfers between devices, local(): kv_a = lax.ppermute(kv_t, EVERY, ACROSS)  6.99 us
    all_to_all x1, starting transfers between devices, local(): returned = lax.all_to_all(timed, CHIP, 0, 0, tiled=True)  4.65 us
    ppermute x6, waiting for transfers between devices, local(): blocks.append(lax.ppermute(block, EVERY, way))  4.61 us
  transfers between devices with their start and end apart: 15, of which 7 were waited for; matrix products, arithmetic and copies ran while one was open for 0% of the time, Pallas kernels for 11%

profile of v11, /device:TPU:1, one launch (start us, length us, event | category | flops | bytes accessed | tf_op | source)
XLA Modules:
  0.0 133.7 jit_solution(8538356446956252789)
XLA Ops:
  0.0 2.7 %shard_map.74 = bf16[64,80,128]{2,1,0:T(8,128)(2,1)} custom-call(bf16[18,3456]{1,0:T(8,128)(2,1)} %w_qkv_hbm.1, bf16[18,1152]{1,0:T(8,128)(2,1)} %w_out_hbm.1, bf16[256,1152]{1,0:T(8,128)(2,1)} %bitcast.8), custom_call_target="tpu_custom_call" | custom-call | bytes 1 | tf_op jit(solution)/shard_map/pallas_call | solution.py:343
  2.7 0.0 copy-start
  2.7 0.0 copy-start.5
  2.7 0.0 copy-start.6
  2.7 0.0 copy-start.7
  2.7 0.0 copy-start.3
  2.7 15.6 %all-to-all-start = ((bf16[64,80,128]{2,1,0:T(8,128)(2,1)}), bf16[64,80,128]{2,1,0:T(8,128)(2,1)S(1)}, u32[]{:S(2)}, u32[]{:S(2)}) async-start(bf16[64,80,128]{2,1,0:T(8,128)(2,1)} %shard_map.74), calls=%async_computation | async-start | bytes 2621440 | tf_op jit(solution)/shard_map/all_to_all | solution.py:404
  18.3 2.4 %collective-permute-start = (bf16[256,1152]{1,0:T(8,128)(2,1)S(1)}, bf16[256,1152]{1,0:T(8,128)(2,1)S(1)}, u32[]{:S(2)}, u32[]{:S(2)}) collective-permute-start(bf16[256,1152]{1,0:T(8,128)(2,1)S(1)} %bitcast.9), channel_id=1, source_target_pairs={{0,1},{1,0},{2,3},{3,2},{4,5},{5,4},{6,7},{7,6},{8,9},{9,8},{10,11... | collective-permute-start | bytes 1769480 | tf_op jit(solution)/shard_map/ppermute | solution.py:60
  20.7 0.1 stack_reshape.6
  20.8 0.1 stack_reshape.7
  21.0 0.1 reshape.6
  21.0 0.1 reshape.7
  21.2 1.1 collective-permute-done.other
  22.3 0.8 shard_map.73.normed.normed_hbm
  23.1 1.0 copy-done.1
  24.1 28.1 %all-to-all-done.got = bf16[64,80,128]{2,1,0:T(8,128)(2,1)S(1)} async-done(((bf16[64,80,128]{2,1,0:T(8,128)(2,1)}), bf16[64,80,128]{2,1,0:T(8,128)(2,1)S(1)}, u32[]{:S(2)}, u32[]{:S(2)}) %all-to-all-start) | async-done | bytes 1310752 | tf_op jit(solution)/shard_map/all_to_all | solution.py:404
  52.2 1.6 %shard_map.75 = (bf16[288,1152]{1,0:T(8,128)(2,1)S(1)}, bf16[288,1152]{1,0:T(8,128)(2,1)}, bf16[256,1152]{1,0:T(8,128)(2,1)}) custom-call(bf16[64,80,128]{2,1,0:T(8,128)(2,1)S(1)} %all-to-all-done.got), custom_call_target="tpu_custom_call" | custom-call | bytes 1 | tf_op jit(solution)/shard_map/pallas_call | solution.py:343
  53.9 3.1 %collective-permute-start.1 = (bf16[288,1152]{1,0:T(8,128)(2,1)}, bf16[288,1152]{1,0:T(8,128)(2,1)S(1)}, u32[]{:S(2)}, u32[]{:S(2)}) collective-permute-start(bf16[288,1152]{1,0:T(8,128)(2,1)} %get-tuple-element.24), channel_id=1, source_target_pairs={{0,384},{1,129},{2,386},{3,131},{4,388},{5,133},{6,390},{7,135},{8... | collective-permute-start | bytes 1990664 | tf_op jit(solution)/shard_map/ppermute | solution.py:423
  57.0 3.1 %collective-permute-start.2 = (bf16[288,1152]{1,0:T(8,128)(2,1)}, bf16[288,1152]{1,0:T(8,128)(2,1)S(1)}, u32[]{:S(2)}, u32[]{:S(2)}) collective-permute-start(bf16[288,1152]{1,0:T(8,128)(2,1)} %get-tuple-element.24), channel_id=1, source_target_pairs={{0,112},{1,17},{2,114},{3,19},{4,116},{5,21},{6,118},{7,23},{8,120... | collective-permute-start | bytes 1990664 | tf_op jit(solution)/shard_map/ppermute | solution.py:423
  60.1 3.4 %collective-permute-start.3 = (bf16[288,1152]{1,0:T(8,128)(2,1)}, bf16[288,1152]{1,0:T(8,128)(2,1)S(1)}, u32[]{:S(2)}, u32[]{:S(2)}) collective-permute-start(bf16[288,1152]{1,0:T(8,128)(2,1)} %get-tuple-element.24), channel_id=1, source_target_pairs={{0,128},{1,385},{2,130},{3,387},{4,132},{5,389},{6,134},{7,391},{8... | collective-permute-start | bytes 1990664 | tf_op jit(solution)/shard_map/ppermute | solution.py:423
  63.5 3.2 %collective-permute-start.4 = (bf16[288,1152]{1,0:T(8,128)(2,1)}, bf16[288,1152]{1,0:T(8,128)(2,1)S(1)}, u32[]{:S(2)}, u32[]{:S(2)}) collective-permute-start(bf16[288,1152]{1,0:T(8,128)(2,1)} %get-tuple-element.24), channel_id=1, source_target_pairs={{0,14},{1,3},{2,0},{3,5},{4,2},{5,7},{6,4},{7,9},{8,6},{9,11},{10,... | collective-permute-start | bytes 1990664 | tf_op jit(solution)/shard_map/ppermute | solution.py:423
  66.7 3.3 %collective-permute-start.5 = (bf16[288,1152]{1,0:T(8,128)(2,1)}, bf16[288,1152]{1,0:T(8,128)(2,1)S(1)}, u32[]{:S(2)}, u32[]{:S(2)}) collective-permute-start(bf16[288,1152]{1,0:T(8,128)(2,1)} %get-tuple-element.24), channel_id=1, source_target_pairs={{0,16},{1,113},{2,18},{3,115},{4,20},{5,117},{6,22},{7,119},{8,24}... | collective-permute-start | bytes 1990664 | tf_op jit(solution)/shard_map/ppermute | solution.py:423
  70.0 0.0 collective-permute-done.1.refs_1_
  70.0 3.4 %collective-permute-start.7 = (bf16[288,1152]{1,0:T(8,128)(2,1)}, bf16[288,1152]{1,0:T(8,128)(2,1)S(1)}, u32[]{:S(2)}, u32[]{:S(2)}) collective-permute-start(bf16[288,1152]{1,0:T(8,128)(2,1)} %get-tuple-element.24), channel_id=1, source_target_pairs={{0,2},{1,15},{2,4},{3,1},{4,6},{5,3},{6,8},{7,5},{8,10},{9,7},{10,... | collective-permute-start | bytes 1990664 | tf_op jit(solution)/shard_map/ppermute | solution.py:423
  73.4 0.0 collective-permute-done.2.refs_2_
  73.4 1.9 %collective-permute-start.6 = (bf16[288,1152]{1,0:T(8,128)(2,1)S(1)}, bf16[288,1152]{1,0:T(8,128)(2,1)S(1)}, u32[]{:S(2)}, u32[]{:S(2)}) collective-permute-start(bf16[288,1152]{1,0:T(8,128)(2,1)S(1)} %collective-permute-done.1.refs_1_), channel_id=1, source_target_pairs={{0,384},{1,129},{2,386},{3,131},{4,388},{5,133},{6,390},{7,135},{8... | collective-permute-start | bytes 1990664 | tf_op jit(solution)/shard_map/ppermute | solution.py:421
  75.3 0.0 collective-permute-done.3.refs_3_
  75.3 4.9 %collective-permute-start.9 = (bf16[256,1152]{1,0:T(8,128)(2,1)}, bf16[256,1152]{1,0:T(8,128)(2,1)S(1)}, u32[]{:S(2)}, u32[]{:S(2)}) collective-permute-start(bf16[256,1152]{1,0:T(8,128)(2,1)} %get-tuple-element.26.own), channel_id=1, source_target_pairs={{0,1},{1,0},{2,3},{3,2},{4,5},{5,4},{6,7},{7,6},{8,9},{9,8},{10,11... | collective-permute-start | bytes 1769480 | tf_op jit(solution)/shard_map/ppermute | solution.py:60
  80.2 0.0 collective-permute-done.5.refs_5_
  80.2 4.6 %collective-permute-done.7.refs_7_ = bf16[288,1152]{1,0:T(8,128)(2,1)S(1)} collective-permute-done((bf16[288,1152]{1,0:T(8,128)(2,1)}, bf16[288,1152]{1,0:T(8,128)(2,1)S(1)}, u32[]{:S(2)}, u32[]{:S(2)}) %collective-permute-start.7) | collective-permute-done | bytes 663584 | tf_op jit(solution)/shard_map/ppermute | solution.py:423
  84.8 1.2 collective-permute-done.6.refs_6_
  86.0 4.9 %shard_map.76 = (bf16[144,512]{1,0:T(8,128)(2,1)}, bf16[288,512]{1,0:T(8,128)(2,1)}, bf16[576,1152]{1,0:T(8,128)(2,1)S(1)}, bf16[2,288,1152]{2,1,0:T(8,128)(2,1)S(1)}, bf16[4,288,1152]{2,1,0:T(8,128)(2,1)S(1)}) custom-call(f32[8,288]{1,0:T(8,128)S(1)} %select_maximum_fusion.gains, bf16[512,1152]{1,0:T(8,128)(2,1)S(1)} %copy-done.2, ...), custom_call_target="tpu_custom_call" | custom-call | bytes 1 | tf_op jit(solution)/shard_map/pallas_call | solution.py:343
  90.9 7.0 %collective-permute-start.8 = (bf16[288,512]{1,0:T(8,128)(2,1)}, bf16[288,512]{1,0:T(8,128)(2,1)S(1)}, u32[]{:S(2)}, u32[]{:S(2)}) collective-permute-start(bf16[288,512]{1,0:T(8,128)(2,1)} %get-tuple-element.25), channel_id=1, source_target_pairs={{0,64},{1,65},{2,66},{3,67},{4,68},{5,69},{6,70},{7,71},{8,72},{9,... | collective-permute-start | bytes 884744 | tf_op jit(solution)/shard_map/ppermute | solution.py:435
  97.9 0.0 collective-permute-done.9.other
  98.0 0.8 shard_map.77.normed
  98.7 2.9 %shard_map.78 = (bf16[32,16,144]{2,1,0:T(8,128)(2,1)}, bf16[4,288,1152]{2,1,0:T(8,128)(2,1)}) custom-call(f32[8,288]{1,0:T(8,128)S(1)} %select_maximum_fusion.gains, bf16[512,1152]{1,0:T(8,128)(2,1)S(1)} %shard_map.77.normed, bf16[2,288,1152]{2,1,0:T(8,128)(2,1)S(1)} %get-tuple-element.28.weight, bf16[4,288,1152]{2,1,0:T(8,128)(2,1)S(1)} %get-tuple-element.29.late), custom_call_target="tpu_custom_call" | custom-call | bytes 1 | tf_op jit(solution)/shard_map/pallas_call | solution.py:343
  101.6 4.6 %all-to-all-start.1 = ((bf16[32,16,144]{2,1,0:T(8,128)(2,1)}), bf16[32,16,144]{2,1,0:T(8,128)(2,1)S(1)}, u32[]{:S(2)}, u32[]{:S(2)}) async-start(bf16[32,16,144]{2,1,0:T(8,128)(2,1)} %get-tuple-element.30), calls=%async_computation.1 | async-start | bytes 524288 | tf_op jit(solution)/shard_map/all_to_all | solution.py:459
  106.3 5.1 %collective-permute-start.11 = (bf16[576,1152]{1,0:T(8,128)(2,1)S(1)}, bf16[576,1152]{1,0:T(8,128)(2,1)}, u32[]{:S(2)}, u32[]{:S(2)}) collective-permute-start(bf16[576,1152]{1,0:T(8,128)(2,1)S(1)} %get-tuple-element.35.w_own), channel_id=1, source_target_pairs={{0,1},{1,0},{2,3},{3,2},{4,5},{5,4},{6,7},{7,6},{8,9},{9,8},{10,11... | collective-permute-start | bytes 3981320 | tf_op jit(solution)/shard_map/ppermute | solution.py:60
  111.3 0.2 collective-permute-done.8.kv_a
  111.5 2.1 %collective-permute-start.10 = (bf16[288,512]{1,0:T(8,128)(2,1)S(1)}, bf16[288,512]{1,0:T(8,128)(2,1)S(1)}, u32[]{:S(2)}, u32[]{:S(2)}) collective-permute-start(bf16[288,512]{1,0:T(8,128)(2,1)S(1)} %collective-permute-done.8.kv_a), channel_id=1, source_target_pairs={{0,128},{1,129},{2,130},{3,131},{4,132},{5,133},{6,134},{7,135},{8... | collective-permute-start | bytes 884744 | tf_op jit(solution)/shard_map/ppermute | solution.py:445
  113.6 5.8 %shard_map.79.space_hbm = bf16[288,512]{1,0:T(8,128)(2,1)} custom-call(f32[8,288]{1,0:T(8,128)S(1)} %select_maximum_fusion.gains, bf16[512,1152]{1,0:T(8,128)(2,1)} %copy-done.1, bf16[4,288,1152]{2,1,0:T(8,128)(2,1)} %get-tuple-element.33.weight_hbm), custom_call_target="tpu_custom_call" | custom-call | flops 16000000000 | bytes 1 | tf_op jit(solution)/shard_map/pallas_call | solution.py:343
  119.4 0.0 all-to-all-done.1.timed
  119.4 2.8 %collective-permute-done.10.kv_b = bf16[288,512]{1,0:T(8,128)(2,1)S(1)} collective-permute-done((bf16[288,512]{1,0:T(8,128)(2,1)S(1)}, bf16[288,512]{1,0:T(8,128)(2,1)S(1)}, u32[]{:S(2)}, u32[]{:S(2)}) %collective-permute-start.10) | collective-permute-done | bytes 294944 | tf_op jit(solution)/shard_map/ppermute | solution.py:445
  122.2 0.0 collective-permute-done.11.w_hbm
  122.2 3.0 %shard_map.80 = (bf16[256,576]{1,0:T(8,128)(2,1)S(1)}, bf16[256,576]{1,0:T(8,128)(2,1)S(1)}, bf16[576,1152]{1,0:T(8,128)(2,1)S(1)}) custom-call(bf16[288,512]{1,0:T(8,128)(2,1)S(1)} %collective-permute-done.8.kv_a, bf16[288,512]{1,0:T(8,128)(2,1)S(1)} %collective-permute-done.10.kv_b, bf16[32,16,144]{2,1,0:T(8,128)(2,1)S(1)} %all-to-all-done.1.timed, ...), custom_call_target="tpu_custom_call" | custom-call | bytes 1 | tf_op jit(solution)/shard_map/pallas_call | solution.py:343
  125.1 4.4 %collective-permute-start.12 = (bf16[256,576]{1,0:T(8,128)(2,1)S(1)}, bf16[256,576]{1,0:T(8,128)(2,1)S(1)}, u32[]{:S(2)}, u32[]{:S(2)}) collective-permute-start(bf16[256,576]{1,0:T(8,128)(2,1)S(1)} %get-tuple-element.37), channel_id=1, source_target_pairs={{0,1},{1,0},{2,3},{3,2},{4,5},{5,4},{6,7},{7,6},{8,9},{9,8},{10,11... | collective-permute-start | bytes 884744 | tf_op jit(solution)/shard_map/ppermute | solution.py:60
  129.5 1.2 collective-permute-done.12.arrived
  130.8 2.8 %shard_map.81 = bf16[256,1152]{1,0:T(8,128)(2,1)} custom-call(bf16[256,1152]{1,0:T(8,128)(2,1)S(1)} %bitcast.11, bf16[256,576]{1,0:T(8,128)(2,1)S(1)} %get-tuple-element.36.own, bf16[256,576]{1,0:T(8,128)(2,1)S(1)} %collective-permute-done.12.arrived, bf16[576,1152]{1,0:T(8,128)(2,1)S(1)} %get-tuple-element.35.w_own, ...), custom_call_target="tpu_custom_call" | custom-call | bytes 1 | tf_op jit(solution)/shard_map/pallas_call | solution.py:343
  (17 shorter events, 0.1 us)
Async XLA Ops:
  2.7 15.6 %copy-start = (bf16[1,256,1152]{2,1,0:T(8,128)(2,1)S(1)}, bf16[1,256,1152]{2,1,0:T(8,128)(2,1)}, u32[]{:S(2)}) copy-start(bf16[1,256,1152]{2,1,0:T(8,128)(2,1)} %param.7) | copy-start | bytes 1769476
  2.7 18.0 %copy-start.5 = (f32[1152]{0:T(1024)S(1)}, f32[1152]{0:T(1024)}, u32[]{:S(2)}) copy-start(f32[1152]{0:T(1024)} %param.10) | copy-start | bytes 13828
  2.7 18.1 %copy-start.6 = (f32[1152]{0:T(1024)S(1)}, f32[1152]{0:T(1024)}, u32[]{:S(2)}) copy-start(f32[1152]{0:T(1024)} %param.11) | copy-start | bytes 13828
  2.7 18.4 %copy-start.7 = (f32[1152]{0:T(1024)S(1)}, f32[1152]{0:T(1024)}, u32[]{:S(2)}) copy-start(f32[1152]{0:T(1024)} %param.9) | copy-start | bytes 13828
  2.7 19.6 %copy-start.3 = (f32[8,1152]{1,0:T(8,128)S(1)}, f32[8,1152]{1,0:T(8,128)}, u32[]{:S(2)}) copy-start(f32[8,1152]{1,0:T(8,128)} %embed_hbm.1) | copy-start | bytes 110596
  2.7 49.5 %all-to-all-start = ((bf16[64,80,128]{2,1,0:T(8,128)(2,1)}), bf16[64,80,128]{2,1,0:T(8,128)(2,1)S(1)}, u32[]{:S(2)}, u32[]{:S(2)}) async-start(bf16[64,80,128]{2,1,0:T(8,128)(2,1)} %shard_map.74), calls=%async_computation | async-start | bytes 2621440 | tf_op jit(solution)/shard_map/all_to_all | solution.py:404
  18.3 4.0 %collective-permute-start = (bf16[256,1152]{1,0:T(8,128)(2,1)S(1)}, bf16[256,1152]{1,0:T(8,128)(2,1)S(1)}, u32[]{:S(2)}, u32[]{:S(2)}) collective-permute-start(bf16[256,1152]{1,0:T(8,128)(2,1)S(1)} %bitcast.9), channel_id=1, source_target_pairs={{0,1},{1,0},{2,3},{3,2},{4,5},{5,4},{6,7},{7,6},{8,9},{9,8},{10,11... | collective-permute-start | bytes 1769480 | tf_op jit(solution)/shard_map/ppermute | solution.py:60
  23.1 1.1 copy-start.1
  52.2 33.8 %copy-start.2 = (bf16[512,1152]{1,0:T(8,128)(2,1)S(1)}, bf16[512,1152]{1,0:T(8,128)(2,1)}, u32[]{:S(2)}) copy-start(bf16[512,1152]{1,0:T(8,128)(2,1)} %copy-done.1) | copy-start | bytes 3538948
  53.9 16.1 %collective-permute-start.1 = (bf16[288,1152]{1,0:T(8,128)(2,1)}, bf16[288,1152]{1,0:T(8,128)(2,1)S(1)}, u32[]{:S(2)}, u32[]{:S(2)}) collective-permute-start(bf16[288,1152]{1,0:T(8,128)(2,1)} %get-tuple-element.24), channel_id=1, source_target_pairs={{0,384},{1,129},{2,386},{3,131},{4,388},{5,133},{6,390},{7,135},{8... | collective-permute-start | bytes 1990664 | tf_op jit(solution)/shard_map/ppermute | solution.py:423
  57.0 16.4 %collective-permute-start.2 = (bf16[288,1152]{1,0:T(8,128)(2,1)}, bf16[288,1152]{1,0:T(8,128)(2,1)S(1)}, u32[]{:S(2)}, u32[]{:S(2)}) collective-permute-start(bf16[288,1152]{1,0:T(8,128)(2,1)} %get-tuple-element.24), channel_id=1, source_target_pairs={{0,112},{1,17},{2,114},{3,19},{4,116},{5,21},{6,118},{7,23},{8,120... | collective-permute-start | bytes 1990664 | tf_op jit(solution)/shard_map/ppermute | solution.py:423
  60.1 15.2 %collective-permute-start.3 = (bf16[288,1152]{1,0:T(8,128)(2,1)}, bf16[288,1152]{1,0:T(8,128)(2,1)S(1)}, u32[]{:S(2)}, u32[]{:S(2)}) collective-permute-start(bf16[288,1152]{1,0:T(8,128)(2,1)} %get-tuple-element.24), channel_id=1, source_target_pairs={{0,128},{1,385},{2,130},{3,387},{4,132},{5,389},{6,134},{7,391},{8... | collective-permute-start | bytes 1990664 | tf_op jit(solution)/shard_map/ppermute | solution.py:423
  63.5 16.7 %collective-permute-start.4 = (bf16[288,1152]{1,0:T(8,128)(2,1)}, bf16[288,1152]{1,0:T(8,128)(2,1)S(1)}, u32[]{:S(2)}, u32[]{:S(2)}) collective-permute-start(bf16[288,1152]{1,0:T(8,128)(2,1)} %get-tuple-element.24), channel_id=1, source_target_pairs={{0,14},{1,3},{2,0},{3,5},{4,2},{5,7},{6,4},{7,9},{8,6},{9,11},{10,... | collective-permute-start | bytes 1990664 | tf_op jit(solution)/shard_map/ppermute | solution.py:423
  66.7 13.5 %collective-permute-start.5 = (bf16[288,1152]{1,0:T(8,128)(2,1)}, bf16[288,1152]{1,0:T(8,128)(2,1)S(1)}, u32[]{:S(2)}, u32[]{:S(2)}) collective-permute-start(bf16[288,1152]{1,0:T(8,128)(2,1)} %get-tuple-element.24), channel_id=1, source_target_pairs={{0,16},{1,113},{2,18},{3,115},{4,20},{5,117},{6,22},{7,119},{8,24}... | collective-permute-start | bytes 1990664 | tf_op jit(solution)/shard_map/ppermute | solution.py:423
  70.0 14.8 %collective-permute-start.7 = (bf16[288,1152]{1,0:T(8,128)(2,1)}, bf16[288,1152]{1,0:T(8,128)(2,1)S(1)}, u32[]{:S(2)}, u32[]{:S(2)}) collective-permute-start(bf16[288,1152]{1,0:T(8,128)(2,1)} %get-tuple-element.24), channel_id=1, source_target_pairs={{0,2},{1,15},{2,4},{3,1},{4,6},{5,3},{6,8},{7,5},{8,10},{9,7},{10,... | collective-permute-start | bytes 1990664 | tf_op jit(solution)/shard_map/ppermute | solution.py:423
  73.4 12.6 %collective-permute-start.6 = (bf16[288,1152]{1,0:T(8,128)(2,1)S(1)}, bf16[288,1152]{1,0:T(8,128)(2,1)S(1)}, u32[]{:S(2)}, u32[]{:S(2)}) collective-permute-start(bf16[288,1152]{1,0:T(8,128)(2,1)S(1)} %collective-permute-done.1.refs_1_), channel_id=1, source_target_pairs={{0,384},{1,129},{2,386},{3,131},{4,388},{5,133},{6,390},{7,135},{8... | collective-permute-start | bytes 1990664 | tf_op jit(solution)/shard_map/ppermute | solution.py:421
  75.3 22.6 %collective-permute-start.9 = (bf16[256,1152]{1,0:T(8,128)(2,1)}, bf16[256,1152]{1,0:T(8,128)(2,1)S(1)}, u32[]{:S(2)}, u32[]{:S(2)}) collective-permute-start(bf16[256,1152]{1,0:T(8,128)(2,1)} %get-tuple-element.26.own), channel_id=1, source_target_pairs={{0,1},{1,0},{2,3},{3,2},{4,5},{5,4},{6,7},{7,6},{8,9},{9,8},{10,11... | collective-permute-start | bytes 1769480 | tf_op jit(solution)/shard_map/ppermute | solution.py:60
  86.0 11.9 %copy-start.4 = (bf16[256,1152]{1,0:T(8,128)(2,1)S(1)}, bf16[256,1152]{1,0:T(8,128)(2,1)}, u32[]{:S(2)}) copy-start(bf16[256,1152]{1,0:T(8,128)(2,1)} %get-tuple-element.26.own) | copy-start | bytes 1769476
  90.9 20.6 %collective-permute-start.8 = (bf16[288,512]{1,0:T(8,128)(2,1)}, bf16[288,512]{1,0:T(8,128)(2,1)S(1)}, u32[]{:S(2)}, u32[]{:S(2)}) collective-permute-start(bf16[288,512]{1,0:T(8,128)(2,1)} %get-tuple-element.25), channel_id=1, source_target_pairs={{0,64},{1,65},{2,66},{3,67},{4,68},{5,69},{6,70},{7,71},{8,72},{9,... | collective-permute-start | bytes 884744 | tf_op jit(solution)/shard_map/ppermute | solution.py:435
  101.6 17.8 %all-to-all-start.1 = ((bf16[32,16,144]{2,1,0:T(8,128)(2,1)}), bf16[32,16,144]{2,1,0:T(8,128)(2,1)S(1)}, u32[]{:S(2)}, u32[]{:S(2)}) async-start(bf16[32,16,144]{2,1,0:T(8,128)(2,1)} %get-tuple-element.30), calls=%async_computation.1 | async-start | bytes 524288 | tf_op jit(solution)/shard_map/all_to_all | solution.py:459
  106.3 15.9 %collective-permute-start.11 = (bf16[576,1152]{1,0:T(8,128)(2,1)S(1)}, bf16[576,1152]{1,0:T(8,128)(2,1)}, u32[]{:S(2)}, u32[]{:S(2)}) collective-permute-start(bf16[576,1152]{1,0:T(8,128)(2,1)S(1)} %get-tuple-element.35.w_own), channel_id=1, source_target_pairs={{0,1},{1,0},{2,3},{3,2},{4,5},{5,4},{6,7},{7,6},{8,9},{9,8},{10,11... | collective-permute-start | bytes 3981320 | tf_op jit(solution)/shard_map/ppermute | solution.py:60
  111.5 10.6 %collective-permute-start.10 = (bf16[288,512]{1,0:T(8,128)(2,1)S(1)}, bf16[288,512]{1,0:T(8,128)(2,1)S(1)}, u32[]{:S(2)}, u32[]{:S(2)}) collective-permute-start(bf16[288,512]{1,0:T(8,128)(2,1)S(1)} %collective-permute-done.8.kv_a), channel_id=1, source_target_pairs={{0,128},{1,129},{2,130},{3,131},{4,132},{5,133},{6,134},{7,135},{8... | collective-permute-start | bytes 884744 | tf_op jit(solution)/shard_map/ppermute | solution.py:445
  125.1 5.6 %collective-permute-start.12 = (bf16[256,576]{1,0:T(8,128)(2,1)S(1)}, bf16[256,576]{1,0:T(8,128)(2,1)S(1)}, u32[]{:S(2)}, u32[]{:S(2)}) collective-permute-start(bf16[256,576]{1,0:T(8,128)(2,1)S(1)} %get-tuple-element.37), channel_id=1, source_target_pairs={{0,1},{1,0},{2,3},{3,2},{4,5},{5,4},{6,7},{7,6},{8,9},{9,8},{10,11... | collective-permute-start | bytes 884744 | tf_op jit(solution)/shard_map/ppermute | solution.py:60

commit v12 on v10

--- a/solution.py
+++ b/solution.py
@@ -132,7 +132,7 @@
         store.wait()
 
 
-def unpack_kernel(got, block, block_out, tokens_out, tokens, wide, sem):
+def unpack_kernel(got, own_out, block_out, tokens_out, block, tokens, wide, sem):
     for source in range(64):
         rows = got[source].astype(F32)
         at = source * 18
@@ -155,6 +155,7 @@
     stores = [
         pltpu.make_async_copy(block, block_out, sem.at[0]),
         pltpu.make_async_copy(tokens, tokens_out, sem.at[1]),
+        pltpu.make_async_copy(block, own_out, sem.at[2]),
     ]
     for store in stores:
         store.start()
@@ -241,9 +242,7 @@
     store.wait()
 
 
-def time_kernel(gains, normed, weight, late, out, late_out, sem):
-    store = pltpu.make_async_copy(late, late_out, sem)
-    store.start()
+def time_kernel(gains, normed, weight, out):
     q, k, v = project_pair(normed, weight[0, PAIR:], weight[1], gains[...].T[:, 1:2])
     row = lax.broadcasted_iota(jnp.int32, (HALF, HALF), 0) % 8
     col = lax.broadcasted_iota(jnp.int32, (HALF, HALF), 1) % 8
@@ -260,7 +259,6 @@
     one = jnp.where(swap, sets[1], sets[0])
     two = jnp.where(swap, sets[0], sets[1])
     out[...] = jnp.concatenate([one, two], 1).reshape(32, 16, PAIR).astype(BF16)
-    store.wait()
 
 
 def space_kernel(gains, normed_hbm, weight_hbm, out, normed, result, weight, sem):
@@ -308,9 +306,13 @@
     give[...] = jnp.concatenate([mixed[HALF:], jnp.where(swap, late[0], late[1])], 1).astype(BF16)
 
 
-def out_kernel(tokens, own, arrived, w_own, w_other, embed_hbm, out, cam_embed, sem):
-    load = pltpu.make_async_copy(embed_hbm, cam_embed, sem)
-    load.start()
+def out_kernel(tokens, own, arrived, w_own, w_hbm, embed_hbm, out, w_other, cam_embed, sem):
+    loads = [
+        pltpu.make_async_copy(w_hbm, w_other, sem.at[0]),
+        pltpu.make_async_copy(embed_hbm, cam_embed, sem.at[1]),
+    ]
+    for load in loads:
+        load.start()
     swap = lax.axis_index("core") == 1
     mine, theirs = own[...].astype(F32), arrived[...].astype(F32)
     first = jnp.where(swap, theirs, mine)
@@ -319,9 +321,11 @@
     for start, end in ((0, 2 * PAIR), (2 * PAIR, 3 * PAIR), (3 * PAIR, 4 * PAIR)):
         parts += [first[:, start:end], second[:, start:end]]
     mixed = jnp.concatenate(parts, 1).astype(BF16)
-    one, two = mm_t(mixed, w_own[...]), mm_t(mixed, w_other[...])
+    one = mm_t(mixed, w_own[...])
+    for load in loads:
+        load.wait()
+    two = mm_t(mixed, w_other[...])
     update = jnp.concatenate([jnp.where(swap, two, one), jnp.where(swap, one, two)], 1)
-    load.wait()
     out[...] = (tokens[...].astype(F32) + own_embed(cam_embed) + update).astype(BF16)
 
 
@@ -333,7 +337,7 @@
         specs.append(hbm if i >= len(args) - anys else vmem)
 
     def place(out):
-        return hbm if getattr(out, "memory_space", None) == pltpu.HBM else vmem
+        return pl.BlockSpec(memory_space=pl.ANY) if hasattr(out, "memory_space") else vmem
 
     single = not isinstance(out_shapes, tuple)
     return pl.pallas_call(
@@ -399,15 +403,16 @@
     )
     got = lax.all_to_all(pieces, SLAB, 0, 0, tiled=True)
     other = swap_core(tokens)
-    normed = keep_near(call(norm_kernel, near(ROWS, D), (tokens, other, cam_embed, gain), (), 8 * 10**9))
+    normed = keep_near(call(norm_kernel, shape(ROWS, D), (tokens, other, cam_embed, gain), (), 8 * 10**9))
     own_block, block, time_own = call(
         unpack_kernel,
         (near(QUAD, D), far(QUAD, D), far(HALF, D)),
         (after(got, normed, gains),),
         [
+            pltpu.VMEM((QUAD, D), BF16),
             pltpu.VMEM((HALF, D), BF16),
             pltpu.VMEM((3, D, 128), F32),
-            pltpu.SemaphoreType.DMA((2,)),
+            pltpu.SemaphoreType.DMA((3,)),
         ],
     )
     blocks = [keep_near(own_block)]
@@ -418,23 +423,17 @@
             blocks.append(lax.ppermute(block, EVERY, way))
     blocks = tuple(blocks)
     time_other = swap_core(time_own)
-    time_normed = keep_near(call(norm_kernel, near(ROWS, D), (time_own, time_other, cam_embed, gain), (), 8 * 10**9))
+    time_normed = keep_near(call(norm_kernel, shape(ROWS, D), (time_own, time_other, cam_embed, gain), (), 8 * 10**9))
     q_t, kv_t, w_own, early, late = call(
         cross_project_kernel,
-        (far(PAIR, ROWS), shape(2 * PAIR, ROWS), near(4 * PAIR, D), near(2, QUAD, D), near(4, QUAD, D)),
+        (far(PAIR, ROWS), shape(2 * PAIR, ROWS), near(4 * PAIR, D), near(2, QUAD, D), far(4, QUAD, D)),
         (gains, normed) + blocks,
         [pltpu.VMEM((PAIR, ROWS), BF16), pltpu.VMEM((2, QUAD, D), BF16), pltpu.SemaphoreType.DMA((13,))],
         0,
         8,
     )
     kv_a = lax.ppermute(kv_t, EVERY, ACROSS)
-    w_other = keep_near(swap_core(w_own))
-    timed, late = call(
-        time_kernel,
-        (shape(32, 16, PAIR), far(4, QUAD, D)),
-        (gains, after(time_normed, kv_t), keep_near(early), keep_near(late)),
-        [pltpu.SemaphoreType.DMA],
-    )
+    timed = call(time_kernel, shape(32, 16, PAIR), (gains, after(time_normed, kv_t), keep_near(early)))
     kv_b = lax.ppermute(after(kv_a, timed), EVERY, ALONG)
     space = call(
         space_kernel,
@@ -450,6 +449,7 @@
         2,
     )
     returned = lax.all_to_all(timed, CHIP, 0, 0, tiled=True)
+    w_other = swap_core(w_own)
     keep, give = call(
         cross_kernel,
         (shape(HALF, 4 * PAIR), shape(HALF, 4 * PAIR)),
@@ -463,9 +463,9 @@
         out_kernel,
         shape(HALF, D),
         (tokens, keep, arrived, w_own, w_other, stay(cam_embed)),
-        [pltpu.VMEM((8, D), F32), pltpu.SemaphoreType.DMA],
+        [pltpu.VMEM((4 * PAIR, D), BF16), pltpu.VMEM((8, D), F32), pltpu.SemaphoreType.DMA((2,))],
         0,
-        1,
+        2,
     )[None]
 
 

time: 135 us -> 134 us (level)
  no operation moved by 1% of the time
where the time goes in v12:
time: 134 us; the launch traced here: 133 us
  starting transfers between devices  67.4 us (50%)
  waiting for transfers between devices  39.2 us (29%)
  Pallas kernels  24.6 us (18%)
  local copies, waits for them, and re-layouts  1.41 us (1%)
    all_to_all x1, waiting for transfers between devices, local(): got = lax.all_to_all(pieces, SLAB, 0, 0, tiled=True)  28.1 us
    pallas_call x9, Pallas kernels, call(): pl.pallas_call(kernel, out_shape=out_shapes, in_specs=specs, out_specs=pl...  24.6 us
    ppermute x6, starting transfers between devices, local(): blocks.append(lax.ppermute(block, EVERY, way))  19.5 us
    ppermute x4, starting transfers between devices, swap_core(): return lax.ppermute(block, 'core', [(0, 1), (1, 0)])  16.7 us
    all_to_all x1, starting transfers between devices, local(): got = lax.all_to_all(pieces, SLAB, 0, 0, tiled=True)  15.6 us
    ppermute x1, starting transfers between devices, local(): kv_a = lax.ppermute(kv_t, EVERY, ACROSS)  6.99 us
    all_to_all x1, starting transfers between devices, local(): returned = lax.all_to_all(timed, CHIP, 0, 0, tiled=True)  4.65 us
    ppermute x6, waiting for transfers between devices, local(): blocks.append(lax.ppermute(block, EVERY, way))  4.61 us
  transfers between devices with their start and end apart: 15, of which 7 were waited for; matrix products, arithmetic and copies ran while one was open for 0% of the time, Pallas kernels for 13%

profile of v12, /device:TPU:1, one launch (start us, length us, event | category | flops | bytes accessed | tf_op | source)
XLA Modules:
  0.0 133.1 jit_solution(1326226533528118830)
XLA Ops:
  0.0 2.7 %shard_map.74 = bf16[64,80,128]{2,1,0:T(8,128)(2,1)} custom-call(bf16[18,3456]{1,0:T(8,128)(2,1)} %w_qkv_hbm.1, bf16[18,1152]{1,0:T(8,128)(2,1)} %w_out_hbm.1, bf16[256,1152]{1,0:T(8,128)(2,1)} %bitcast.8), custom_call_target="tpu_custom_call" | custom-call | bytes 1 | tf_op jit(solution)/shard_map/pallas_call | solution.py:343
  2.7 0.0 copy-start
  2.7 0.0 copy-start.5
  2.7 0.0 copy-start.6
  2.7 0.0 copy-start.7
  2.7 0.0 copy-start.3
  2.7 15.6 %all-to-all-start = ((bf16[64,80,128]{2,1,0:T(8,128)(2,1)}), bf16[64,80,128]{2,1,0:T(8,128)(2,1)S(1)}, u32[]{:S(2)}, u32[]{:S(2)}) async-start(bf16[64,80,128]{2,1,0:T(8,128)(2,1)} %shard_map.74), calls=%async_computation | async-start | bytes 2621440 | tf_op jit(solution)/shard_map/all_to_all | solution.py:404
  18.3 2.4 %collective-permute-start = (bf16[256,1152]{1,0:T(8,128)(2,1)S(1)}, bf16[256,1152]{1,0:T(8,128)(2,1)S(1)}, u32[]{:S(2)}, u32[]{:S(2)}) collective-permute-start(bf16[256,1152]{1,0:T(8,128)(2,1)S(1)} %bitcast.9), channel_id=1, source_target_pairs={{0,1},{1,0},{2,3},{3,2},{4,5},{5,4},{6,7},{7,6},{8,9},{9,8},{10,11... | collective-permute-start | bytes 1769480 | tf_op jit(solution)/shard_map/ppermute | solution.py:60
  20.7 0.1 stack_reshape.6
  20.8 0.1 stack_reshape.7
  21.0 0.1 reshape.6
  21.1 0.1 reshape.7
  21.2 1.1 collective-permute-done.other
  22.3 0.8 shard_map.73.normed.normed_hbm
  23.1 1.0 copy-done.1
  24.1 28.1 %all-to-all-done.got = bf16[64,80,128]{2,1,0:T(8,128)(2,1)S(1)} async-done(((bf16[64,80,128]{2,1,0:T(8,128)(2,1)}), bf16[64,80,128]{2,1,0:T(8,128)(2,1)S(1)}, u32[]{:S(2)}, u32[]{:S(2)}) %all-to-all-start) | async-done | bytes 1310752 | tf_op jit(solution)/shard_map/all_to_all | solution.py:404
  52.2 1.6 %shard_map.75 = (bf16[288,1152]{1,0:T(8,128)(2,1)S(1)}, bf16[288,1152]{1,0:T(8,128)(2,1)}, bf16[256,1152]{1,0:T(8,128)(2,1)}) custom-call(bf16[64,80,128]{2,1,0:T(8,128)(2,1)S(1)} %all-to-all-done.got), custom_call_target="tpu_custom_call" | custom-call | bytes 1 | tf_op jit(solution)/shard_map/pallas_call | solution.py:343
  53.9 3.1 %collective-permute-start.1 = (bf16[288,1152]{1,0:T(8,128)(2,1)}, bf16[288,1152]{1,0:T(8,128)(2,1)S(1)}, u32[]{:S(2)}, u32[]{:S(2)}) collective-permute-start(bf16[288,1152]{1,0:T(8,128)(2,1)} %get-tuple-element.21), channel_id=1, source_target_pairs={{0,384},{1,129},{2,386},{3,131},{4,388},{5,133},{6,390},{7,135},{8... | collective-permute-start | bytes 1990664 | tf_op jit(solution)/shard_map/ppermute | solution.py:423
  57.0 3.1 %collective-permute-start.2 = (bf16[288,1152]{1,0:T(8,128)(2,1)}, bf16[288,1152]{1,0:T(8,128)(2,1)S(1)}, u32[]{:S(2)}, u32[]{:S(2)}) collective-permute-start(bf16[288,1152]{1,0:T(8,128)(2,1)} %get-tuple-element.21), channel_id=1, source_target_pairs={{0,112},{1,17},{2,114},{3,19},{4,116},{5,21},{6,118},{7,23},{8,120... | collective-permute-start | bytes 1990664 | tf_op jit(solution)/shard_map/ppermute | solution.py:423
  60.1 3.4 %collective-permute-start.3 = (bf16[288,1152]{1,0:T(8,128)(2,1)}, bf16[288,1152]{1,0:T(8,128)(2,1)S(1)}, u32[]{:S(2)}, u32[]{:S(2)}) collective-permute-start(bf16[288,1152]{1,0:T(8,128)(2,1)} %get-tuple-element.21), channel_id=1, source_target_pairs={{0,128},{1,385},{2,130},{3,387},{4,132},{5,389},{6,134},{7,391},{8... | collective-permute-start | bytes 1990664 | tf_op jit(solution)/shard_map/ppermute | solution.py:423
  63.5 3.2 %collective-permute-start.4 = (bf16[288,1152]{1,0:T(8,128)(2,1)}, bf16[288,1152]{1,0:T(8,128)(2,1)S(1)}, u32[]{:S(2)}, u32[]{:S(2)}) collective-permute-start(bf16[288,1152]{1,0:T(8,128)(2,1)} %get-tuple-element.21), channel_id=1, source_target_pairs={{0,14},{1,3},{2,0},{3,5},{4,2},{5,7},{6,4},{7,9},{8,6},{9,11},{10,... | collective-permute-start | bytes 1990664 | tf_op jit(solution)/shard_map/ppermute | solution.py:423
  66.7 3.3 %collective-permute-start.5 = (bf16[288,1152]{1,0:T(8,128)(2,1)}, bf16[288,1152]{1,0:T(8,128)(2,1)S(1)}, u32[]{:S(2)}, u32[]{:S(2)}) collective-permute-start(bf16[288,1152]{1,0:T(8,128)(2,1)} %get-tuple-element.21), channel_id=1, source_target_pairs={{0,16},{1,113},{2,18},{3,115},{4,20},{5,117},{6,22},{7,119},{8,24}... | collective-permute-start | bytes 1990664 | tf_op jit(solution)/shard_map/ppermute | solution.py:423
  70.0 0.0 collective-permute-done.1.refs_1_
  70.0 3.4 %collective-permute-start.7 = (bf16[288,1152]{1,0:T(8,128)(2,1)}, bf16[288,1152]{1,0:T(8,128)(2,1)S(1)}, u32[]{:S(2)}, u32[]{:S(2)}) collective-permute-start(bf16[288,1152]{1,0:T(8,128)(2,1)} %get-tuple-element.21), channel_id=1, source_target_pairs={{0,2},{1,15},{2,4},{3,1},{4,6},{5,3},{6,8},{7,5},{8,10},{9,7},{10,... | collective-permute-start | bytes 1990664 | tf_op jit(solution)/shard_map/ppermute | solution.py:423
  73.4 0.0 collective-permute-done.2.refs_2_
  73.4 1.9 %collective-permute-start.6 = (bf16[288,1152]{1,0:T(8,128)(2,1)S(1)}, bf16[288,1152]{1,0:T(8,128)(2,1)S(1)}, u32[]{:S(2)}, u32[]{:S(2)}) collective-permute-start(bf16[288,1152]{1,0:T(8,128)(2,1)S(1)} %collective-permute-done.1.refs_1_), channel_id=1, source_target_pairs={{0,384},{1,129},{2,386},{3,131},{4,388},{5,133},{6,390},{7,135},{8... | collective-permute-start | bytes 1990664 | tf_op jit(solution)/shard_map/ppermute | solution.py:421
  75.3 0.0 collective-permute-done.3.refs_3_
  75.3 4.9 %collective-permute-start.9 = (bf16[256,1152]{1,0:T(8,128)(2,1)}, bf16[256,1152]{1,0:T(8,128)(2,1)S(1)}, u32[]{:S(2)}, u32[]{:S(2)}) collective-permute-start(bf16[256,1152]{1,0:T(8,128)(2,1)} %get-tuple-element.23.own), channel_id=1, source_target_pairs={{0,1},{1,0},{2,3},{3,2},{4,5},{5,4},{6,7},{7,6},{8,9},{9,8},{10,11... | collective-permute-start | bytes 1769480 | tf_op jit(solution)/shard_map/ppermute | solution.py:60
  80.2 0.0 collective-permute-done.4.refs_4_
  80.2 0.0 collective-permute-done.5.refs_5_
  80.2 4.6 %collective-permute-done.7.refs_7_ = bf16[288,1152]{1,0:T(8,128)(2,1)S(1)} collective-permute-done((bf16[288,1152]{1,0:T(8,128)(2,1)}, bf16[288,1152]{1,0:T(8,128)(2,1)S(1)}, u32[]{:S(2)}, u32[]{:S(2)}) %collective-permute-start.7) | collective-permute-done | bytes 663584 | tf_op jit(solution)/shard_map/ppermute | solution.py:423
  84.8 1.2 collective-permute-done.6.refs_6_
  86.0 3.9 %shard_map.76 = (bf16[144,512]{1,0:T(8,128)(2,1)}, bf16[288,512]{1,0:T(8,128)(2,1)}, bf16[576,1152]{1,0:T(8,128)(2,1)S(1)}, bf16[2,288,1152]{2,1,0:T(8,128)(2,1)S(1)}, bf16[4,288,1152]{2,1,0:T(8,128)(2,1)}) custom-call(f32[8,288]{1,0:T(8,128)S(1)} %select_maximum_fusion.gains, bf16[512,1152]{1,0:T(8,128)(2,1)S(1)} %copy-done.2, ...), custom_call_target="tpu_custom_call" | custom-call | bytes 1 | tf_op jit(solution)/shard_map/pallas_call | solution.py:343
  90.0 7.0 %collective-permute-start.8 = (bf16[288,512]{1,0:T(8,128)(2,1)}, bf16[288,512]{1,0:T(8,128)(2,1)S(1)}, u32[]{:S(2)}, u32[]{:S(2)}) collective-permute-start(bf16[288,512]{1,0:T(8,128)(2,1)} %get-tuple-element.22), channel_id=1, source_target_pairs={{0,64},{1,65},{2,66},{3,67},{4,68},{5,69},{6,70},{7,71},{8,72},{9,... | collective-permute-start | bytes 884744 | tf_op jit(solution)/shard_map/ppermute | solution.py:435
  97.0 0.0 collective-permute-done.9.other
  97.0 0.8 shard_map.77.normed
  97.8 2.8 %shard_map.78 = bf16[32,16,144]{2,1,0:T(8,128)(2,1)} custom-call(f32[8,288]{1,0:T(8,128)S(1)} %select_maximum_fusion.gains, bf16[512,1152]{1,0:T(8,128)(2,1)S(1)} %shard_map.77.normed, bf16[2,288,1152]{2,1,0:T(8,128)(2,1)S(1)} %get-tuple-element.25.weight), custom_call_target="tpu_custom_call" | custom-call | bytes 1 | tf_op jit(solution)/shard_map/pallas_call | solution.py:343
  100.6 4.7 %all-to-all-start.1 = ((bf16[32,16,144]{2,1,0:T(8,128)(2,1)}), bf16[32,16,144]{2,1,0:T(8,128)(2,1)S(1)}, u32[]{:S(2)}, u32[]{:S(2)}) async-start(bf16[32,16,144]{2,1,0:T(8,128)(2,1)} %shard_map.78), calls=%async_computation.1 | async-start | bytes 524288 | tf_op jit(solution)/shard_map/all_to_all | solution.py:451
  105.2 5.1 %collective-permute-start.12 = (bf16[576,1152]{1,0:T(8,128)(2,1)S(1)}, bf16[576,1152]{1,0:T(8,128)(2,1)}, u32[]{:S(2)}, u32[]{:S(2)}) collective-permute-start(bf16[576,1152]{1,0:T(8,128)(2,1)S(1)} %get-tuple-element.32.w_own), channel_id=1, source_target_pairs={{0,1},{1,0},{2,3},{3,2},{4,5},{5,4},{6,7},{7,6},{8,9},{9,8},{10,11... | collective-permute-start | bytes 3981320 | tf_op jit(solution)/shard_map/ppermute | solution.py:60
  110.3 0.2 collective-permute-done.8.kv_a
  110.6 2.1 %collective-permute-start.10 = (bf16[288,512]{1,0:T(8,128)(2,1)S(1)}, bf16[288,512]{1,0:T(8,128)(2,1)S(1)}, u32[]{:S(2)}, u32[]{:S(2)}) collective-permute-start(bf16[288,512]{1,0:T(8,128)(2,1)S(1)} %collective-permute-done.8.kv_a), channel_id=1, source_target_pairs={{0,128},{1,129},{2,130},{3,131},{4,132},{5,133},{6,134},{7,135},{8... | collective-permute-start | bytes 884744 | tf_op jit(solution)/shard_map/ppermute | solution.py:437
  112.6 5.8 %shard_map.79.space_hbm = bf16[288,512]{1,0:T(8,128)(2,1)} custom-call(f32[8,288]{1,0:T(8,128)S(1)} %select_maximum_fusion.gains, bf16[512,1152]{1,0:T(8,128)(2,1)} %copy-done.1, bf16[4,288,1152]{2,1,0:T(8,128)(2,1)} %get-tuple-element.28.weight_hbm), custom_call_target="tpu_custom_call" | custom-call | flops 16000000000 | bytes 1 | tf_op jit(solution)/shard_map/pallas_call | solution.py:343
  118.4 0.0 all-to-all-done.1.timed
  118.5 2.6 %collective-permute-done.10.kv_b = bf16[288,512]{1,0:T(8,128)(2,1)S(1)} collective-permute-done((bf16[288,512]{1,0:T(8,128)(2,1)S(1)}, bf16[288,512]{1,0:T(8,128)(2,1)S(1)}, u32[]{:S(2)}, u32[]{:S(2)}) %collective-permute-start.10) | collective-permute-done | bytes 294944 | tf_op jit(solution)/shard_map/ppermute | solution.py:437
  121.1 2.6 %shard_map.80 = (bf16[256,576]{1,0:T(8,128)(2,1)S(1)}, bf16[256,576]{1,0:T(8,128)(2,1)S(1)}) custom-call(bf16[288,512]{1,0:T(8,128)(2,1)S(1)} %collective-permute-done.8.kv_a, bf16[288,512]{1,0:T(8,128)(2,1)S(1)} %collective-permute-done.10.kv_b, bf16[32,16,144]{2,1,0:T(8,128)(2,1)S(1)} %all-to-all-done.1.timed, bf16[288,512]{1,0:T(8,128)(2,1)} %shard_map.79.space_hbm, ...), custom_call_target="tpu_custom_call" | custom-call | bytes 1 | tf_op jit(solution)/shard_map/pallas_call | solution.py:343
  123.6 4.4 %collective-permute-start.11 = (bf16[256,576]{1,0:T(8,128)(2,1)S(1)}, bf16[256,576]{1,0:T(8,128)(2,1)S(1)}, u32[]{:S(2)}, u32[]{:S(2)}) collective-permute-start(bf16[256,576]{1,0:T(8,128)(2,1)S(1)} %get-tuple-element.31), channel_id=1, source_target_pairs={{0,1},{1,0},{2,3},{3,2},{4,5},{5,4},{6,7},{7,6},{8,9},{9,8},{10,11... | collective-permute-start | bytes 884744 | tf_op jit(solution)/shard_map/ppermute | solution.py:60
  128.1 1.2 collective-permute-done.11.arrived
  129.3 3.7 %shard_map.81 = bf16[256,1152]{1,0:T(8,128)(2,1)} custom-call(bf16[256,1152]{1,0:T(8,128)(2,1)S(1)} %bitcast.11, bf16[256,576]{1,0:T(8,128)(2,1)S(1)} %get-tuple-element.30.own, bf16[256,576]{1,0:T(8,128)(2,1)S(1)} %collective-permute-done.11.arrived, bf16[576,1152]{1,0:T(8,128)(2,1)S(1)} %get-tuple-element.32.w_own, ...), custom_call_target="tpu_custom_call" | custom-call | bytes 1 | tf_op jit(solution)/shard_map/pallas_call | solution.py:343
  (17 shorter events, 0.1 us)
Async XLA Ops:
  2.7 15.6 %copy-start = (bf16[1,256,1152]{2,1,0:T(8,128)(2,1)S(1)}, bf16[1,256,1152]{2,1,0:T(8,128)(2,1)}, u32[]{:S(2)}) copy-start(bf16[1,256,1152]{2,1,0:T(8,128)(2,1)} %param.7) | copy-start | bytes 1769476
  2.7 18.0 %copy-start.5 = (f32[1152]{0:T(1024)S(1)}, f32[1152]{0:T(1024)}, u32[]{:S(2)}) copy-start(f32[1152]{0:T(1024)} %param.10) | copy-start | bytes 13828
  2.7 18.1 %copy-start.6 = (f32[1152]{0:T(1024)S(1)}, f32[1152]{0:T(1024)}, u32[]{:S(2)}) copy-start(f32[1152]{0:T(1024)} %param.11) | copy-start | bytes 13828
  2.7 18.4 %copy-start.7 = (f32[1152]{0:T(1024)S(1)}, f32[1152]{0:T(1024)}, u32[]{:S(2)}) copy-start(f32[1152]{0:T(1024)} %param.9) | copy-start | bytes 13828
  2.7 19.6 %copy-start.3 = (f32[8,1152]{1,0:T(8,128)S(1)}, f32[8,1152]{1,0:T(8,128)}, u32[]{:S(2)}) copy-start(f32[8,1152]{1,0:T(8,128)} %embed_hbm.1) | copy-start | bytes 110596
  2.7 49.5 %all-to-all-start = ((bf16[64,80,128]{2,1,0:T(8,128)(2,1)}), bf16[64,80,128]{2,1,0:T(8,128)(2,1)S(1)}, u32[]{:S(2)}, u32[]{:S(2)}) async-start(bf16[64,80,128]{2,1,0:T(8,128)(2,1)} %shard_map.74), calls=%async_computation | async-start | bytes 2621440 | tf_op jit(solution)/shard_map/all_to_all | solution.py:404
  18.3 4.0 %collective-permute-start = (bf16[256,1152]{1,0:T(8,128)(2,1)S(1)}, bf16[256,1152]{1,0:T(8,128)(2,1)S(1)}, u32[]{:S(2)}, u32[]{:S(2)}) collective-permute-start(bf16[256,1152]{1,0:T(8,128)(2,1)S(1)} %bitcast.9), channel_id=1, source_target_pairs={{0,1},{1,0},{2,3},{3,2},{4,5},{5,4},{6,7},{7,6},{8,9},{9,8},{10,11... | collective-permute-start | bytes 1769480 | tf_op jit(solution)/shard_map/ppermute | solution.py:60
  23.1 1.0 copy-start.1
  52.2 33.8 %copy-start.2 = (bf16[512,1152]{1,0:T(8,128)(2,1)S(1)}, bf16[512,1152]{1,0:T(8,128)(2,1)}, u32[]{:S(2)}) copy-start(bf16[512,1152]{1,0:T(8,128)(2,1)} %copy-done.1) | copy-start | bytes 3538948
  53.9 16.1 %collective-permute-start.1 = (bf16[288,1152]{1,0:T(8,128)(2,1)}, bf16[288,1152]{1,0:T(8,128)(2,1)S(1)}, u32[]{:S(2)}, u32[]{:S(2)}) collective-permute-start(bf16[288,1152]{1,0:T(8,128)(2,1)} %get-tuple-element.21), channel_id=1, source_target_pairs={{0,384},{1,129},{2,386},{3,131},{4,388},{5,133},{6,390},{7,135},{8... | collective-permute-start | bytes 1990664 | tf_op jit(solution)/shard_map/ppermute | solution.py:423
  57.0 16.4 %collective-permute-start.2 = (bf16[288,1152]{1,0:T(8,128)(2,1)}, bf16[288,1152]{1,0:T(8,128)(2,1)S(1)}, u32[]{:S(2)}, u32[]{:S(2)}) collective-permute-start(bf16[288,1152]{1,0:T(8,128)(2,1)} %get-tuple-element.21), channel_id=1, source_target_pairs={{0,112},{1,17},{2,114},{3,19},{4,116},{5,21},{6,118},{7,23},{8,120... | collective-permute-start | bytes 1990664 | tf_op jit(solution)/shard_map/ppermute | solution.py:423
  60.1 15.2 %collective-permute-start.3 = (bf16[288,1152]{1,0:T(8,128)(2,1)}, bf16[288,1152]{1,0:T(8,128)(2,1)S(1)}, u32[]{:S(2)}, u32[]{:S(2)}) collective-permute-start(bf16[288,1152]{1,0:T(8,128)(2,1)} %get-tuple-element.21), channel_id=1, source_target_pairs={{0,128},{1,385},{2,130},{3,387},{4,132},{5,389},{6,134},{7,391},{8... | collective-permute-start | bytes 1990664 | tf_op jit(solution)/shard_map/ppermute | solution.py:423
  63.5 16.7 %collective-permute-start.4 = (bf16[288,1152]{1,0:T(8,128)(2,1)}, bf16[288,1152]{1,0:T(8,128)(2,1)S(1)}, u32[]{:S(2)}, u32[]{:S(2)}) collective-permute-start(bf16[288,1152]{1,0:T(8,128)(2,1)} %get-tuple-element.21), channel_id=1, source_target_pairs={{0,14},{1,3},{2,0},{3,5},{4,2},{5,7},{6,4},{7,9},{8,6},{9,11},{10,... | collective-permute-start | bytes 1990664 | tf_op jit(solution)/shard_map/ppermute | solution.py:423
  66.7 13.5 %collective-permute-start.5 = (bf16[288,1152]{1,0:T(8,128)(2,1)}, bf16[288,1152]{1,0:T(8,128)(2,1)S(1)}, u32[]{:S(2)}, u32[]{:S(2)}) collective-permute-start(bf16[288,1152]{1,0:T(8,128)(2,1)} %get-tuple-element.21), channel_id=1, source_target_pairs={{0,16},{1,113},{2,18},{3,115},{4,20},{5,117},{6,22},{7,119},{8,24}... | collective-permute-start | bytes 1990664 | tf_op jit(solution)/shard_map/ppermute | solution.py:423
  70.0 14.8 %collective-permute-start.7 = (bf16[288,1152]{1,0:T(8,128)(2,1)}, bf16[288,1152]{1,0:T(8,128)(2,1)S(1)}, u32[]{:S(2)}, u32[]{:S(2)}) collective-permute-start(bf16[288,1152]{1,0:T(8,128)(2,1)} %get-tuple-element.21), channel_id=1, source_target_pairs={{0,2},{1,15},{2,4},{3,1},{4,6},{5,3},{6,8},{7,5},{8,10},{9,7},{10,... | collective-permute-start | bytes 1990664 | tf_op jit(solution)/shard_map/ppermute | solution.py:423
  73.4 12.6 %collective-permute-start.6 = (bf16[288,1152]{1,0:T(8,128)(2,1)S(1)}, bf16[288,1152]{1,0:T(8,128)(2,1)S(1)}, u32[]{:S(2)}, u32[]{:S(2)}) collective-permute-start(bf16[288,1152]{1,0:T(8,128)(2,1)S(1)} %collective-permute-done.1.refs_1_), channel_id=1, source_target_pairs={{0,384},{1,129},{2,386},{3,131},{4,388},{5,133},{6,390},{7,135},{8... | collective-permute-start | bytes 1990664 | tf_op jit(solution)/shard_map/ppermute | solution.py:421
  75.3 21.6 %collective-permute-start.9 = (bf16[256,1152]{1,0:T(8,128)(2,1)}, bf16[256,1152]{1,0:T(8,128)(2,1)S(1)}, u32[]{:S(2)}, u32[]{:S(2)}) collective-permute-start(bf16[256,1152]{1,0:T(8,128)(2,1)} %get-tuple-element.23.own), channel_id=1, source_target_pairs={{0,1},{1,0},{2,3},{3,2},{4,5},{5,4},{6,7},{7,6},{8,9},{9,8},{10,11... | collective-permute-start | bytes 1769480 | tf_op jit(solution)/shard_map/ppermute | solution.py:60
  86.0 10.9 %copy-start.4 = (bf16[256,1152]{1,0:T(8,128)(2,1)S(1)}, bf16[256,1152]{1,0:T(8,128)(2,1)}, u32[]{:S(2)}) copy-start(bf16[256,1152]{1,0:T(8,128)(2,1)} %get-tuple-element.23.own) | copy-start | bytes 1769476
  90.0 20.6 %collective-permute-start.8 = (bf16[288,512]{1,0:T(8,128)(2,1)}, bf16[288,512]{1,0:T(8,128)(2,1)S(1)}, u32[]{:S(2)}, u32[]{:S(2)}) collective-permute-start(bf16[288,512]{1,0:T(8,128)(2,1)} %get-tuple-element.22), channel_id=1, source_target_pairs={{0,64},{1,65},{2,66},{3,67},{4,68},{5,69},{6,70},{7,71},{8,72},{9,... | collective-permute-start | bytes 884744 | tf_op jit(solution)/shard_map/ppermute | solution.py:435
  100.6 17.9 %all-to-all-start.1 = ((bf16[32,16,144]{2,1,0:T(8,128)(2,1)}), bf16[32,16,144]{2,1,0:T(8,128)(2,1)S(1)}, u32[]{:S(2)}, u32[]{:S(2)}) async-start(bf16[32,16,144]{2,1,0:T(8,128)(2,1)} %shard_map.78), calls=%async_computation.1 | async-start | bytes 524288 | tf_op jit(solution)/shard_map/all_to_all | solution.py:451
  105.2 24.1 %collective-permute-start.12 = (bf16[576,1152]{1,0:T(8,128)(2,1)S(1)}, bf16[576,1152]{1,0:T(8,128)(2,1)}, u32[]{:S(2)}, u32[]{:S(2)}) collective-permute-start(bf16[576,1152]{1,0:T(8,128)(2,1)S(1)} %get-tuple-element.32.w_own), channel_id=1, source_target_pairs={{0,1},{1,0},{2,3},{3,2},{4,5},{5,4},{6,7},{7,6},{8,9},{9,8},{10,11... | collective-permute-start | bytes 3981320 | tf_op jit(solution)/shard_map/ppermute | solution.py:60
  110.6 10.5 %collective-permute-start.10 = (bf16[288,512]{1,0:T(8,128)(2,1)S(1)}, bf16[288,512]{1,0:T(8,128)(2,1)S(1)}, u32[]{:S(2)}, u32[]{:S(2)}) collective-permute-start(bf16[288,512]{1,0:T(8,128)(2,1)S(1)} %collective-permute-done.8.kv_a), channel_id=1, source_target_pairs={{0,128},{1,129},{2,130},{3,131},{4,132},{5,133},{6,134},{7,135},{8... | collective-permute-start | bytes 884744 | tf_op jit(solution)/shard_map/ppermute | solution.py:437
  123.6 5.7 %collective-permute-start.11 = (bf16[256,576]{1,0:T(8,128)(2,1)S(1)}, bf16[256,576]{1,0:T(8,128)(2,1)S(1)}, u32[]{:S(2)}, u32[]{:S(2)}) collective-permute-start(bf16[256,576]{1,0:T(8,128)(2,1)S(1)} %get-tuple-element.31), channel_id=1, source_target_pairs={{0,1},{1,0},{2,3},{3,2},{4,5},{5,4},{6,7},{7,6},{8,9},{9,8},{10,11... | collective-permute-start | bytes 884744 | tf_op jit(solution)/shard_map/ppermute | solution.py:60

commit v13 on v11

--- a/solution.py
+++ b/solution.py
@@ -142,23 +142,24 @@
         wide[2, at + 5 : at + 10, :32] = rows[36:41, 32:64]
         wide[2, at + 10 : at + 14, :32] = rows[37:41, 64:96]
         wide[2, at + 14 : at + 18, :32] = rows[37:41, 96:]
-        if source % 2 == 1:
-            pair = [got[source - 1].astype(F32), rows]
-            tiles = []
-            for tile in range(9):
-                start = 44 + tile * 4
-                tiles.append(jnp.concatenate([one[start : start + 4] for one in pair], 0))
-            tokens[source * 4 - 4 : source * 4 + 4] = jnp.concatenate(tiles, 1).astype(BF16)
     block[:128] = wide[0].T.astype(BF16)
     block[128:256] = wide[1].T.astype(BF16)
     block[256:] = wide[2].T[:32].astype(BF16)
     stores = [
         pltpu.make_async_copy(block, block_out, sem.at[0]),
-        pltpu.make_async_copy(tokens, tokens_out, sem.at[1]),
-        pltpu.make_async_copy(block, own_out, sem.at[2]),
+        pltpu.make_async_copy(block, own_out, sem.at[1]),
+        pltpu.make_async_copy(tokens, tokens_out, sem.at[2]),
     ]
-    for store in stores:
+    for store in stores[:2]:
         store.start()
+    for source in range(0, 64, 2):
+        pair = [got[source + i].astype(F32) for i in range(2)]
+        tiles = []
+        for tile in range(9):
+            start = 44 + tile * 4
+            tiles.append(jnp.concatenate([one[start : start + 4] for one in pair], 0))
+        tokens[source * 4 : source * 4 + 8] = jnp.concatenate(tiles, 1).astype(BF16)
+    stores[2].start()
     for store in stores:
         store.wait()
 
@@ -222,14 +223,16 @@
     blocks, (q_out, kv_t, w_out, early, late, q_t, weight, sem) = refs[:8], refs[8:]
     slots = {0: weight.at[0], 4: weight.at[1], 1: early.at[0], 5: early.at[1]}
     slots.update({colour: late.at[place] for place, colour in enumerate(LATE)})
-    for colour, slot in slots.items():
-        start_fetch(blocks, colour, slot, sem.at[colour])
+    for colour in (0, 4):
+        start_fetch(blocks, colour, slots[colour], sem.at[colour])
+    for colour in (0, 4):
+        wait_fetch(blocks, slots[colour], sem.at[colour])
+    for colour in (1, 5) + LATE:
+        start_fetch(blocks, colour, slots[colour], sem.at[colour])
     parts = [block.at[pl.ds(0, PAIR)] for block in blocks]
     thirds = [w_out.at[pl.ds(colour * PAIR, PAIR)] for colour in range(4)]
     for colour in range(4):
         start_fetch(parts, colour, thirds[colour], sem.at[8 + colour])
-    for colour in (0, 4):
-        wait_fetch(blocks, slots[colour], sem.at[colour])
     q, k, v = project_pair(normed, weight[0, PAIR:], weight[1], gains[...].T[:, :1])
     kv_t[...] = jnp.concatenate([k, v], 0).astype(BF16)
     q_t[...] = q.astype(BF16)
@@ -242,9 +245,7 @@
     store.wait()
 
 
-def time_kernel(gains, normed, weight, late, out, late_out, sem):
-    store = pltpu.make_async_copy(late, late_out, sem)
-    store.start()
+def time_kernel(gains, normed, weight, out):
     q, k, v = project_pair(normed, weight[0, PAIR:], weight[1], gains[...].T[:, 1:2])
     row = lax.broadcasted_iota(jnp.int32, (HALF, HALF), 0) % 8
     col = lax.broadcasted_iota(jnp.int32, (HALF, HALF), 1) % 8
@@ -261,7 +262,6 @@
     one = jnp.where(swap, sets[1], sets[0])
     two = jnp.where(swap, sets[0], sets[1])
     out[...] = jnp.concatenate([one, two], 1).reshape(32, 16, PAIR).astype(BF16)
-    store.wait()
 
 
 def space_kernel(gains, normed_hbm, weight_hbm, out, normed, result, weight, sem):
@@ -426,22 +426,14 @@
     time_normed = keep_near(call(norm_kernel, shape(ROWS, D), (time_own, time_other, cam_embed, gain), (), 8 * 10**9))
     q_t, kv_t, w_own, early, late = call(
         cross_project_kernel,
-        (far(PAIR, ROWS), shape(2 * PAIR, ROWS), near(4 * PAIR, D), near(2, QUAD, D), near(4, QUAD, D)),
+        (far(PAIR, ROWS), shape(2 * PAIR, ROWS), near(4 * PAIR, D), near(2, QUAD, D), far(4, QUAD, D)),
         (gains, normed) + blocks,
         [pltpu.VMEM((PAIR, ROWS), BF16), pltpu.VMEM((2, QUAD, D), BF16), pltpu.SemaphoreType.DMA((13,))],
         0,
         8,
     )
     kv_a = lax.ppermute(kv_t, EVERY, ACROSS)
-    w_other = swap_core(w_own)
-    timed, late = call(
-        time_kernel,
-        (shape(32, 16, PAIR), far(4, QUAD, D)),
-        (gains, after(time_normed, kv_t), keep_near(early), keep_near(late)),
-        [pltpu.SemaphoreType.DMA],
-        0,
-        1,
-    )
+    timed = call(time_kernel, shape(32, 16, PAIR), (gains, after(time_normed, kv_t), keep_near(early)))
     kv_b = lax.ppermute(after(kv_a, timed), EVERY, ALONG)
     space = call(
         space_kernel,
@@ -457,6 +449,7 @@
         2,
     )
     returned = lax.all_to_all(timed, CHIP, 0, 0, tiled=True)
+    w_other = swap_core(w_own)
     keep, give, w_other = call(
         cross_kernel,
         (shape(HALF, 4 * PAIR), shape(HALF, 4 * PAIR), near(4 * PAIR, D)),

time: 134 us -> 133 us (level)
  no operation moved by 1% of the time
where the time goes in v13:
time: 133 us
  starting transfers between devices  67.4 us (51%)
  waiting for transfers between devices  39.2 us (29%)
  Pallas kernels  24.2 us (18%)
  local copies, waits for them, and re-layouts  1.41 us (1%)
    all_to_all x1, waiting for transfers between devices, local(): got = lax.all_to_all(pieces, SLAB, 0, 0, tiled=True)  28.1 us
    pallas_call x9, Pallas kernels, call(): pl.pallas_call(kernel, out_shape=out_shapes, in_specs=specs, out_specs=pl...  24.2 us
    ppermute x6, starting transfers between devices, local(): blocks.append(lax.ppermute(block, EVERY, way))  19.5 us
    ppermute x4, starting transfers between devices, swap_core(): return lax.ppermute(block, 'core', [(0, 1), (1, 0)])  16.7 us
    all_to_all x1, starting transfers between devices, local(): got = lax.all_to_all(pieces, SLAB, 0, 0, tiled=True)  15.6 us
    ppermute x1, starting transfers between devices, local(): kv_a = lax.ppermute(kv_t, EVERY, ACROSS)  6.99 us
    all_to_all x1, starting transfers between devices, local(): returned = lax.all_to_all(timed, CHIP, 0, 0, tiled=True)  4.63 us
    ppermute x6, waiting for transfers between devices, local(): blocks.append(lax.ppermute(block, EVERY, way))  4.61 us
  transfers between devices with their start and end apart: 15, of which 7 were waited for; matrix products, arithmetic and copies ran while one was open for 0% of the time, Pallas kernels for 11%

profile of v13, /device:TPU:1, one launch (start us, length us, event | category | flops | bytes accessed | tf_op | source)
XLA Modules:
  0.0 132.8 jit_solution(10639350948671191553)
XLA Ops:
  0.0 2.7 %shard_map.74 = bf16[64,80,128]{2,1,0:T(8,128)(2,1)} custom-call(bf16[18,3456]{1,0:T(8,128)(2,1)} %w_qkv_hbm.1, bf16[18,1152]{1,0:T(8,128)(2,1)} %w_out_hbm.1, bf16[256,1152]{1,0:T(8,128)(2,1)} %bitcast.8), custom_call_target="tpu_custom_call" | custom-call | bytes 1 | tf_op jit(solution)/shard_map/pallas_call | solution.py:343
  2.7 0.0 copy-start
  2.7 0.0 copy-start.5
  2.7 0.0 copy-start.6
  2.7 0.0 copy-start.7
  2.7 0.0 copy-start.3
  2.7 15.6 %all-to-all-start = ((bf16[64,80,128]{2,1,0:T(8,128)(2,1)}), bf16[64,80,128]{2,1,0:T(8,128)(2,1)S(1)}, u32[]{:S(2)}, u32[]{:S(2)}) async-start(bf16[64,80,128]{2,1,0:T(8,128)(2,1)} %shard_map.74), calls=%async_computation | async-start | bytes 2621440 | tf_op jit(solution)/shard_map/all_to_all | solution.py:404
  18.3 2.4 %collective-permute-start = (bf16[256,1152]{1,0:T(8,128)(2,1)S(1)}, bf16[256,1152]{1,0:T(8,128)(2,1)S(1)}, u32[]{:S(2)}, u32[]{:S(2)}) collective-permute-start(bf16[256,1152]{1,0:T(8,128)(2,1)S(1)} %bitcast.9), channel_id=1, source_target_pairs={{0,1},{1,0},{2,3},{3,2},{4,5},{5,4},{6,7},{7,6},{8,9},{9,8},{10,11... | collective-permute-start | bytes 1769480 | tf_op jit(solution)/shard_map/ppermute | solution.py:60
  20.7 0.1 stack_reshape.6
  20.8 0.1 stack_reshape.7
  21.0 0.1 reshape.6
  21.1 0.1 reshape.7
  21.2 1.1 collective-permute-done.other
  22.3 0.8 shard_map.73.normed.normed_hbm
  23.1 1.0 copy-done.1
  24.1 28.1 %all-to-all-done.got = bf16[64,80,128]{2,1,0:T(8,128)(2,1)S(1)} async-done(((bf16[64,80,128]{2,1,0:T(8,128)(2,1)}), bf16[64,80,128]{2,1,0:T(8,128)(2,1)S(1)}, u32[]{:S(2)}, u32[]{:S(2)}) %all-to-all-start) | async-done | bytes 1310752 | tf_op jit(solution)/shard_map/all_to_all | solution.py:404
  52.2 1.7 %shard_map.75 = (bf16[288,1152]{1,0:T(8,128)(2,1)S(1)}, bf16[288,1152]{1,0:T(8,128)(2,1)}, bf16[256,1152]{1,0:T(8,128)(2,1)}) custom-call(bf16[64,80,128]{2,1,0:T(8,128)(2,1)S(1)} %all-to-all-done.got), custom_call_target="tpu_custom_call" | custom-call | bytes 1 | tf_op jit(solution)/shard_map/pallas_call | solution.py:343
  54.0 3.1 %collective-permute-start.1 = (bf16[288,1152]{1,0:T(8,128)(2,1)}, bf16[288,1152]{1,0:T(8,128)(2,1)S(1)}, u32[]{:S(2)}, u32[]{:S(2)}) collective-permute-start(bf16[288,1152]{1,0:T(8,128)(2,1)} %get-tuple-element.22), channel_id=1, source_target_pairs={{0,384},{1,129},{2,386},{3,131},{4,388},{5,133},{6,390},{7,135},{8... | collective-permute-start | bytes 1990664 | tf_op jit(solution)/shard_map/ppermute | solution.py:423
  57.1 3.1 %collective-permute-start.2 = (bf16[288,1152]{1,0:T(8,128)(2,1)}, bf16[288,1152]{1,0:T(8,128)(2,1)S(1)}, u32[]{:S(2)}, u32[]{:S(2)}) collective-permute-start(bf16[288,1152]{1,0:T(8,128)(2,1)} %get-tuple-element.22), channel_id=1, source_target_pairs={{0,112},{1,17},{2,114},{3,19},{4,116},{5,21},{6,118},{7,23},{8,120... | collective-permute-start | bytes 1990664 | tf_op jit(solution)/shard_map/ppermute | solution.py:423
  60.2 3.4 %collective-permute-start.3 = (bf16[288,1152]{1,0:T(8,128)(2,1)}, bf16[288,1152]{1,0:T(8,128)(2,1)S(1)}, u32[]{:S(2)}, u32[]{:S(2)}) collective-permute-start(bf16[288,1152]{1,0:T(8,128)(2,1)} %get-tuple-element.22), channel_id=1, source_target_pairs={{0,128},{1,385},{2,130},{3,387},{4,132},{5,389},{6,134},{7,391},{8... | collective-permute-start | bytes 1990664 | tf_op jit(solution)/shard_map/ppermute | solution.py:423
  63.6 3.2 %collective-permute-start.4 = (bf16[288,1152]{1,0:T(8,128)(2,1)}, bf16[288,1152]{1,0:T(8,128)(2,1)S(1)}, u32[]{:S(2)}, u32[]{:S(2)}) collective-permute-start(bf16[288,1152]{1,0:T(8,128)(2,1)} %get-tuple-element.22), channel_id=1, source_target_pairs={{0,14},{1,3},{2,0},{3,5},{4,2},{5,7},{6,4},{7,9},{8,6},{9,11},{10,... | collective-permute-start | bytes 1990664 | tf_op jit(solution)/shard_map/ppermute | solution.py:423
  66.8 3.3 %collective-permute-start.5 = (bf16[288,1152]{1,0:T(8,128)(2,1)}, bf16[288,1152]{1,0:T(8,128)(2,1)S(1)}, u32[]{:S(2)}, u32[]{:S(2)}) collective-permute-start(bf16[288,1152]{1,0:T(8,128)(2,1)} %get-tuple-element.22), channel_id=1, source_target_pairs={{0,16},{1,113},{2,18},{3,115},{4,20},{5,117},{6,22},{7,119},{8,24}... | collective-permute-start | bytes 1990664 | tf_op jit(solution)/shard_map/ppermute | solution.py:423
  70.1 0.0 collective-permute-done.1.refs_1_
  70.1 3.4 %collective-permute-start.7 = (bf16[288,1152]{1,0:T(8,128)(2,1)}, bf16[288,1152]{1,0:T(8,128)(2,1)S(1)}, u32[]{:S(2)}, u32[]{:S(2)}) collective-permute-start(bf16[288,1152]{1,0:T(8,128)(2,1)} %get-tuple-element.22), channel_id=1, source_target_pairs={{0,2},{1,15},{2,4},{3,1},{4,6},{5,3},{6,8},{7,5},{8,10},{9,7},{10,... | collective-permute-start | bytes 1990664 | tf_op jit(solution)/shard_map/ppermute | solution.py:423
  73.5 0.0 collective-permute-done.2.refs_2_
  73.5 1.9 %collective-permute-start.6 = (bf16[288,1152]{1,0:T(8,128)(2,1)S(1)}, bf16[288,1152]{1,0:T(8,128)(2,1)S(1)}, u32[]{:S(2)}, u32[]{:S(2)}) collective-permute-start(bf16[288,1152]{1,0:T(8,128)(2,1)S(1)} %collective-permute-done.1.refs_1_), channel_id=1, source_target_pairs={{0,384},{1,129},{2,386},{3,131},{4,388},{5,133},{6,390},{7,135},{8... | collective-permute-start | bytes 1990664 | tf_op jit(solution)/shard_map/ppermute | solution.py:421
  75.4 0.0 collective-permute-done.3.refs_3_
  75.4 4.9 %collective-permute-start.9 = (bf16[256,1152]{1,0:T(8,128)(2,1)}, bf16[256,1152]{1,0:T(8,128)(2,1)S(1)}, u32[]{:S(2)}, u32[]{:S(2)}) collective-permute-start(bf16[256,1152]{1,0:T(8,128)(2,1)} %get-tuple-element.24.own), channel_id=1, source_target_pairs={{0,1},{1,0},{2,3},{3,2},{4,5},{5,4},{6,7},{7,6},{8,9},{9,8},{10,11... | collective-permute-start | bytes 1769480 | tf_op jit(solution)/shard_map/ppermute | solution.py:60
  80.3 0.0 collective-permute-done.4.refs_4_
  80.3 0.0 collective-permute-done.5.refs_5_
  80.3 4.6 %collective-permute-done.7.refs_7_ = bf16[288,1152]{1,0:T(8,128)(2,1)S(1)} collective-permute-done((bf16[288,1152]{1,0:T(8,128)(2,1)}, bf16[288,1152]{1,0:T(8,128)(2,1)S(1)}, u32[]{:S(2)}, u32[]{:S(2)}) %collective-permute-start.7) | collective-permute-done | bytes 663584 | tf_op jit(solution)/shard_map/ppermute | solution.py:423
  84.9 1.2 collective-permute-done.6.refs_6_
  86.1 3.9 %shard_map.76 = (bf16[144,512]{1,0:T(8,128)(2,1)}, bf16[288,512]{1,0:T(8,128)(2,1)}, bf16[576,1152]{1,0:T(8,128)(2,1)S(1)}, bf16[2,288,1152]{2,1,0:T(8,128)(2,1)S(1)}, bf16[4,288,1152]{2,1,0:T(8,128)(2,1)}) custom-call(f32[8,288]{1,0:T(8,128)S(1)} %select_maximum_fusion.gains, bf16[512,1152]{1,0:T(8,128)(2,1)S(1)} %copy-done.2, ...), custom_call_target="tpu_custom_call" | custom-call | bytes 1 | tf_op jit(solution)/shard_map/pallas_call | solution.py:343
  90.0 7.0 %collective-permute-start.8 = (bf16[288,512]{1,0:T(8,128)(2,1)}, bf16[288,512]{1,0:T(8,128)(2,1)S(1)}, u32[]{:S(2)}, u32[]{:S(2)}) collective-permute-start(bf16[288,512]{1,0:T(8,128)(2,1)} %get-tuple-element.23), channel_id=1, source_target_pairs={{0,64},{1,65},{2,66},{3,67},{4,68},{5,69},{6,70},{7,71},{8,72},{9,... | collective-permute-start | bytes 884744 | tf_op jit(solution)/shard_map/ppermute | solution.py:435
  97.1 0.0 collective-permute-done.9.other
  97.1 0.8 shard_map.77.normed
  97.9 2.8 %shard_map.78 = bf16[32,16,144]{2,1,0:T(8,128)(2,1)} custom-call(f32[8,288]{1,0:T(8,128)S(1)} %select_maximum_fusion.gains, bf16[512,1152]{1,0:T(8,128)(2,1)S(1)} %shard_map.77.normed, bf16[2,288,1152]{2,1,0:T(8,128)(2,1)S(1)} %get-tuple-element.26.weight), custom_call_target="tpu_custom_call" | custom-call | bytes 1 | tf_op jit(solution)/shard_map/pallas_call | solution.py:343
  100.7 4.6 %all-to-all-start.1 = ((bf16[32,16,144]{2,1,0:T(8,128)(2,1)}), bf16[32,16,144]{2,1,0:T(8,128)(2,1)S(1)}, u32[]{:S(2)}, u32[]{:S(2)}) async-start(bf16[32,16,144]{2,1,0:T(8,128)(2,1)} %shard_map.78), calls=%async_computation.1 | async-start | bytes 524288 | tf_op jit(solution)/shard_map/all_to_all | solution.py:451
  105.3 5.1 %collective-permute-start.11 = (bf16[576,1152]{1,0:T(8,128)(2,1)S(1)}, bf16[576,1152]{1,0:T(8,128)(2,1)}, u32[]{:S(2)}, u32[]{:S(2)}) collective-permute-start(bf16[576,1152]{1,0:T(8,128)(2,1)S(1)} %get-tuple-element.31.w_own), channel_id=1, source_target_pairs={{0,1},{1,0},{2,3},{3,2},{4,5},{5,4},{6,7},{7,6},{8,9},{9,8},{10,11... | collective-permute-start | bytes 3981320 | tf_op jit(solution)/shard_map/ppermute | solution.py:60
  110.4 0.2 collective-permute-done.8.kv_a
  110.6 2.1 %collective-permute-start.10 = (bf16[288,512]{1,0:T(8,128)(2,1)S(1)}, bf16[288,512]{1,0:T(8,128)(2,1)S(1)}, u32[]{:S(2)}, u32[]{:S(2)}) collective-permute-start(bf16[288,512]{1,0:T(8,128)(2,1)S(1)} %collective-permute-done.8.kv_a), channel_id=1, source_target_pairs={{0,128},{1,129},{2,130},{3,131},{4,132},{5,133},{6,134},{7,135},{8... | collective-permute-start | bytes 884744 | tf_op jit(solution)/shard_map/ppermute | solution.py:437
  112.7 5.8 %shard_map.79.space_hbm = bf16[288,512]{1,0:T(8,128)(2,1)} custom-call(f32[8,288]{1,0:T(8,128)S(1)} %select_maximum_fusion.gains, bf16[512,1152]{1,0:T(8,128)(2,1)} %copy-done.1, bf16[4,288,1152]{2,1,0:T(8,128)(2,1)} %get-tuple-element.29.weight_hbm), custom_call_target="tpu_custom_call" | custom-call | flops 16000000000 | bytes 1 | tf_op jit(solution)/shard_map/pallas_call | solution.py:343
  118.5 0.0 all-to-all-done.1.timed
  118.5 2.6 %collective-permute-done.10.kv_b = bf16[288,512]{1,0:T(8,128)(2,1)S(1)} collective-permute-done((bf16[288,512]{1,0:T(8,128)(2,1)S(1)}, bf16[288,512]{1,0:T(8,128)(2,1)S(1)}, u32[]{:S(2)}, u32[]{:S(2)}) %collective-permute-start.10) | collective-permute-done | bytes 294944 | tf_op jit(solution)/shard_map/ppermute | solution.py:437
  121.2 3.0 %shard_map.80 = (bf16[256,576]{1,0:T(8,128)(2,1)S(1)}, bf16[256,576]{1,0:T(8,128)(2,1)S(1)}, bf16[576,1152]{1,0:T(8,128)(2,1)S(1)}) custom-call(bf16[288,512]{1,0:T(8,128)(2,1)S(1)} %collective-permute-done.8.kv_a, bf16[288,512]{1,0:T(8,128)(2,1)S(1)} %collective-permute-done.10.kv_b, bf16[32,16,144]{2,1,0:T(8,128)(2,1)S(1)} %all-to-all-done.1.timed, ...), custom_call_target="tpu_custom_call" | custom-call | bytes 1 | tf_op jit(solution)/shard_map/pallas_call | solution.py:343
  124.1 4.4 %collective-permute-start.12 = (bf16[256,576]{1,0:T(8,128)(2,1)S(1)}, bf16[256,576]{1,0:T(8,128)(2,1)S(1)}, u32[]{:S(2)}, u32[]{:S(2)}) collective-permute-start(bf16[256,576]{1,0:T(8,128)(2,1)S(1)} %get-tuple-element.33), channel_id=1, source_target_pairs={{0,1},{1,0},{2,3},{3,2},{4,5},{5,4},{6,7},{7,6},{8,9},{9,8},{10,11... | collective-permute-start | bytes 884744 | tf_op jit(solution)/shard_map/ppermute | solution.py:60
  128.6 1.2 collective-permute-done.12.arrived
  129.8 2.8 %shard_map.81 = bf16[256,1152]{1,0:T(8,128)(2,1)} custom-call(bf16[256,1152]{1,0:T(8,128)(2,1)S(1)} %bitcast.11, bf16[256,576]{1,0:T(8,128)(2,1)S(1)} %get-tuple-element.32.own, bf16[256,576]{1,0:T(8,128)(2,1)S(1)} %collective-permute-done.12.arrived, bf16[576,1152]{1,0:T(8,128)(2,1)S(1)} %get-tuple-element.31.w_own, ...), custom_call_target="tpu_custom_call" | custom-call | bytes 1 | tf_op jit(solution)/shard_map/pallas_call | solution.py:343
  (17 shorter events, 0.1 us)
Async XLA Ops:
  2.7 15.6 %copy-start = (bf16[1,256,1152]{2,1,0:T(8,128)(2,1)S(1)}, bf16[1,256,1152]{2,1,0:T(8,128)(2,1)}, u32[]{:S(2)}) copy-start(bf16[1,256,1152]{2,1,0:T(8,128)(2,1)} %param.7) | copy-start | bytes 1769476
  2.7 18.0 %copy-start.5 = (f32[1152]{0:T(1024)S(1)}, f32[1152]{0:T(1024)}, u32[]{:S(2)}) copy-start(f32[1152]{0:T(1024)} %param.10) | copy-start | bytes 13828
  2.7 18.1 %copy-start.6 = (f32[1152]{0:T(1024)S(1)}, f32[1152]{0:T(1024)}, u32[]{:S(2)}) copy-start(f32[1152]{0:T(1024)} %param.11) | copy-start | bytes 13828
  2.7 18.4 %copy-start.7 = (f32[1152]{0:T(1024)S(1)}, f32[1152]{0:T(1024)}, u32[]{:S(2)}) copy-start(f32[1152]{0:T(1024)} %param.9) | copy-start | bytes 13828
  2.7 19.6 %copy-start.3 = (f32[8,1152]{1,0:T(8,128)S(1)}, f32[8,1152]{1,0:T(8,128)}, u32[]{:S(2)}) copy-start(f32[8,1152]{1,0:T(8,128)} %embed_hbm.1) | copy-start | bytes 110596
  2.7 49.5 %all-to-all-start = ((bf16[64,80,128]{2,1,0:T(8,128)(2,1)}), bf16[64,80,128]{2,1,0:T(8,128)(2,1)S(1)}, u32[]{:S(2)}, u32[]{:S(2)}) async-start(bf16[64,80,128]{2,1,0:T(8,128)(2,1)} %shard_map.74), calls=%async_computation | async-start | bytes 2621440 | tf_op jit(solution)/shard_map/all_to_all | solution.py:404
  18.3 4.0 %collective-permute-start = (bf16[256,1152]{1,0:T(8,128)(2,1)S(1)}, bf16[256,1152]{1,0:T(8,128)(2,1)S(1)}, u32[]{:S(2)}, u32[]{:S(2)}) collective-permute-start(bf16[256,1152]{1,0:T(8,128)(2,1)S(1)} %bitcast.9), channel_id=1, source_target_pairs={{0,1},{1,0},{2,3},{3,2},{4,5},{5,4},{6,7},{7,6},{8,9},{9,8},{10,11... | collective-permute-start | bytes 1769480 | tf_op jit(solution)/shard_map/ppermute | solution.py:60
  23.1 1.0 copy-start.1
  52.2 33.9 %copy-start.2 = (bf16[512,1152]{1,0:T(8,128)(2,1)S(1)}, bf16[512,1152]{1,0:T(8,128)(2,1)}, u32[]{:S(2)}) copy-start(bf16[512,1152]{1,0:T(8,128)(2,1)} %copy-done.1) | copy-start | bytes 3538948
  54.0 16.1 %collective-permute-start.1 = (bf16[288,1152]{1,0:T(8,128)(2,1)}, bf16[288,1152]{1,0:T(8,128)(2,1)S(1)}, u32[]{:S(2)}, u32[]{:S(2)}) collective-permute-start(bf16[288,1152]{1,0:T(8,128)(2,1)} %get-tuple-element.22), channel_id=1, source_target_pairs={{0,384},{1,129},{2,386},{3,131},{4,388},{5,133},{6,390},{7,135},{8... | collective-permute-start | bytes 1990664 | tf_op jit(solution)/shard_map/ppermute | solution.py:423
  57.1 16.4 %collective-permute-start.2 = (bf16[288,1152]{1,0:T(8,128)(2,1)}, bf16[288,1152]{1,0:T(8,128)(2,1)S(1)}, u32[]{:S(2)}, u32[]{:S(2)}) collective-permute-start(bf16[288,1152]{1,0:T(8,128)(2,1)} %get-tuple-element.22), channel_id=1, source_target_pairs={{0,112},{1,17},{2,114},{3,19},{4,116},{5,21},{6,118},{7,23},{8,120... | collective-permute-start | bytes 1990664 | tf_op jit(solution)/shard_map/ppermute | solution.py:423
  60.2 15.2 %collective-permute-start.3 = (bf16[288,1152]{1,0:T(8,128)(2,1)}, bf16[288,1152]{1,0:T(8,128)(2,1)S(1)}, u32[]{:S(2)}, u32[]{:S(2)}) collective-permute-start(bf16[288,1152]{1,0:T(8,128)(2,1)} %get-tuple-element.22), channel_id=1, source_target_pairs={{0,128},{1,385},{2,130},{3,387},{4,132},{5,389},{6,134},{7,391},{8... | collective-permute-start | bytes 1990664 | tf_op jit(solution)/shard_map/ppermute | solution.py:423
  63.6 16.7 %collective-permute-start.4 = (bf16[288,1152]{1,0:T(8,128)(2,1)}, bf16[288,1152]{1,0:T(8,128)(2,1)S(1)}, u32[]{:S(2)}, u32[]{:S(2)}) collective-permute-start(bf16[288,1152]{1,0:T(8,128)(2,1)} %get-tuple-element.22), channel_id=1, source_target_pairs={{0,14},{1,3},{2,0},{3,5},{4,2},{5,7},{6,4},{7,9},{8,6},{9,11},{10,... | collective-permute-start | bytes 1990664 | tf_op jit(solution)/shard_map/ppermute | solution.py:423
  66.8 13.5 %collective-permute-start.5 = (bf16[288,1152]{1,0:T(8,128)(2,1)}, bf16[288,1152]{1,0:T(8,128)(2,1)S(1)}, u32[]{:S(2)}, u32[]{:S(2)}) collective-permute-start(bf16[288,1152]{1,0:T(8,128)(2,1)} %get-tuple-element.22), channel_id=1, source_target_pairs={{0,16},{1,113},{2,18},{3,115},{4,20},{5,117},{6,22},{7,119},{8,24}... | collective-permute-start | bytes 1990664 | tf_op jit(solution)/shard_map/ppermute | solution.py:423
  70.1 14.8 %collective-permute-start.7 = (bf16[288,1152]{1,0:T(8,128)(2,1)}, bf16[288,1152]{1,0:T(8,128)(2,1)S(1)}, u32[]{:S(2)}, u32[]{:S(2)}) collective-permute-start(bf16[288,1152]{1,0:T(8,128)(2,1)} %get-tuple-element.22), channel_id=1, source_target_pairs={{0,2},{1,15},{2,4},{3,1},{4,6},{5,3},{6,8},{7,5},{8,10},{9,7},{10,... | collective-permute-start | bytes 1990664 | tf_op jit(solution)/shard_map/ppermute | solution.py:423
  73.5 12.6 %collective-permute-start.6 = (bf16[288,1152]{1,0:T(8,128)(2,1)S(1)}, bf16[288,1152]{1,0:T(8,128)(2,1)S(1)}, u32[]{:S(2)}, u32[]{:S(2)}) collective-permute-start(bf16[288,1152]{1,0:T(8,128)(2,1)S(1)} %collective-permute-done.1.refs_1_), channel_id=1, source_target_pairs={{0,384},{1,129},{2,386},{3,131},{4,388},{5,133},{6,390},{7,135},{8... | collective-permute-start | bytes 1990664 | tf_op jit(solution)/shard_map/ppermute | solution.py:421
  75.4 21.6 %collective-permute-start.9 = (bf16[256,1152]{1,0:T(8,128)(2,1)}, bf16[256,1152]{1,0:T(8,128)(2,1)S(1)}, u32[]{:S(2)}, u32[]{:S(2)}) collective-permute-start(bf16[256,1152]{1,0:T(8,128)(2,1)} %get-tuple-element.24.own), channel_id=1, source_target_pairs={{0,1},{1,0},{2,3},{3,2},{4,5},{5,4},{6,7},{7,6},{8,9},{9,8},{10,11... | collective-permute-start | bytes 1769480 | tf_op jit(solution)/shard_map/ppermute | solution.py:60
  86.1 10.9 %copy-start.4 = (bf16[256,1152]{1,0:T(8,128)(2,1)S(1)}, bf16[256,1152]{1,0:T(8,128)(2,1)}, u32[]{:S(2)}) copy-start(bf16[256,1152]{1,0:T(8,128)(2,1)} %get-tuple-element.24.own) | copy-start | bytes 1769476
  90.0 20.6 %collective-permute-start.8 = (bf16[288,512]{1,0:T(8,128)(2,1)}, bf16[288,512]{1,0:T(8,128)(2,1)S(1)}, u32[]{:S(2)}, u32[]{:S(2)}) collective-permute-start(bf16[288,512]{1,0:T(8,128)(2,1)} %get-tuple-element.23), channel_id=1, source_target_pairs={{0,64},{1,65},{2,66},{3,67},{4,68},{5,69},{6,70},{7,71},{8,72},{9,... | collective-permute-start | bytes 884744 | tf_op jit(solution)/shard_map/ppermute | solution.py:435
  100.7 17.8 %all-to-all-start.1 = ((bf16[32,16,144]{2,1,0:T(8,128)(2,1)}), bf16[32,16,144]{2,1,0:T(8,128)(2,1)S(1)}, u32[]{:S(2)}, u32[]{:S(2)}) async-start(bf16[32,16,144]{2,1,0:T(8,128)(2,1)} %shard_map.78), calls=%async_computation.1 | async-start | bytes 524288 | tf_op jit(solution)/shard_map/all_to_all | solution.py:451
  105.3 15.8 %collective-permute-start.11 = (bf16[576,1152]{1,0:T(8,128)(2,1)S(1)}, bf16[576,1152]{1,0:T(8,128)(2,1)}, u32[]{:S(2)}, u32[]{:S(2)}) collective-permute-start(bf16[576,1152]{1,0:T(8,128)(2,1)S(1)} %get-tuple-element.31.w_own), channel_id=1, source_target_pairs={{0,1},{1,0},{2,3},{3,2},{4,5},{5,4},{6,7},{7,6},{8,9},{9,8},{10,11... | collective-permute-start | bytes 3981320 | tf_op jit(solution)/shard_map/ppermute | solution.py:60
  110.6 10.5 %collective-permute-start.10 = (bf16[288,512]{1,0:T(8,128)(2,1)S(1)}, bf16[288,512]{1,0:T(8,128)(2,1)S(1)}, u32[]{:S(2)}, u32[]{:S(2)}) collective-permute-start(bf16[288,512]{1,0:T(8,128)(2,1)S(1)} %collective-permute-done.8.kv_a), channel_id=1, source_target_pairs={{0,128},{1,129},{2,130},{3,131},{4,132},{5,133},{6,134},{7,135},{8... | collective-permute-start | bytes 884744 | tf_op jit(solution)/shard_map/ppermute | solution.py:437
  124.1 5.7 %collective-permute-start.12 = (bf16[256,576]{1,0:T(8,128)(2,1)S(1)}, bf16[256,576]{1,0:T(8,128)(2,1)S(1)}, u32[]{:S(2)}, u32[]{:S(2)}) collective-permute-start(bf16[256,576]{1,0:T(8,128)(2,1)S(1)} %get-tuple-element.33), channel_id=1, source_target_pairs={{0,1},{1,0},{2,3},{3,2},{4,5},{5,4},{6,7},{7,6},{8,9},{9,8},{10,11... | collective-permute-start | bytes 884744 | tf_op jit(solution)/shard_map/ppermute | solution.py:60

commit v14 on v13

--- a/solution.py
+++ b/solution.py
@@ -220,32 +220,31 @@
 
 
 def cross_project_kernel(gains, normed, *refs):
-    blocks, (q_out, kv_t, w_out, early, late, q_t, weight, sem) = refs[:8], refs[8:]
-    slots = {0: weight.at[0], 4: weight.at[1], 1: early.at[0], 5: early.at[1]}
-    slots.update({colour: late.at[place] for place, colour in enumerate(LATE)})
-    for colour in (0, 4):
-        start_fetch(blocks, colour, slots[colour], sem.at[colour])
-    for colour in (0, 4):
-        wait_fetch(blocks, slots[colour], sem.at[colour])
-    for colour in (1, 5) + LATE:
-        start_fetch(blocks, colour, slots[colour], sem.at[colour])
+    blocks, (q_out, kv_t, q_t, weight, sem) = refs[:8], refs[8:]
+    for slot, colour in enumerate((0, 4)):
+        start_fetch(blocks, colour, weight.at[slot], sem.at[slot])
+    for slot in range(2):
+        wait_fetch(blocks, weight.at[slot], sem.at[slot])
+    q, k, v = project_pair(normed, weight[0, PAIR:], weight[1], gains[...].T[:, :1])
+    q_t[...] = q.astype(BF16)
+    store = pltpu.make_async_copy(q_t, q_out, sem.at[2])
+    store.start()
+    kv_t[...] = jnp.concatenate([k, v], 0).astype(BF16)
+    store.wait()
+
+
+def time_kernel(gains, normed, *refs):
+    blocks, (out, w_out, late, weight, sem) = refs[:8], refs[8:]
+    for slot, colour in enumerate((1, 5)):
+        start_fetch(blocks, colour, weight.at[slot], sem.at[slot])
+    for slot in range(2):
+        wait_fetch(blocks, weight.at[slot], sem.at[slot])
+    for place, colour in enumerate(LATE):
+        start_fetch(blocks, colour, late.at[place], sem.at[2 + place])
     parts = [block.at[pl.ds(0, PAIR)] for block in blocks]
     thirds = [w_out.at[pl.ds(colour * PAIR, PAIR)] for colour in range(4)]
     for colour in range(4):
-        start_fetch(parts, colour, thirds[colour], sem.at[8 + colour])
-    q, k, v = project_pair(normed, weight[0, PAIR:], weight[1], gains[...].T[:, :1])
-    kv_t[...] = jnp.concatenate([k, v], 0).astype(BF16)
-    q_t[...] = q.astype(BF16)
-    store = pltpu.make_async_copy(q_t, q_out, sem.at[12])
-    store.start()
-    for colour in (1, 5) + LATE:
-        wait_fetch(blocks, slots[colour], sem.at[colour])
-    for colour in range(4):
-        wait_fetch(parts, thirds[colour], sem.at[8 + colour])
-    store.wait()
-
-
-def time_kernel(gains, normed, weight, out):
+        start_fetch(parts, colour, thirds[colour], sem.at[6 + colour])
     q, k, v = project_pair(normed, weight[0, PAIR:], weight[1], gains[...].T[:, 1:2])
     row = lax.broadcasted_iota(jnp.int32, (HALF, HALF), 0) % 8
     col = lax.broadcasted_iota(jnp.int32, (HALF, HALF), 1) % 8
@@ -262,6 +261,10 @@
     one = jnp.where(swap, sets[1], sets[0])
     two = jnp.where(swap, sets[0], sets[1])
     out[...] = jnp.concatenate([one, two], 1).reshape(32, 16, PAIR).astype(BF16)
+    for place in range(4):
+        wait_fetch(blocks, late.at[place], sem.at[2 + place])
+    for colour in range(4):
+        wait_fetch(parts, thirds[colour], sem.at[6 + colour])
 
 
 def space_kernel(gains, normed_hbm, weight_hbm, out, normed, result, weight, sem):
@@ -424,16 +427,24 @@
     blocks = tuple(blocks)
     time_other = swap_core(time_own)
     time_normed = keep_near(call(norm_kernel, shape(ROWS, D), (time_own, time_other, cam_embed, gain), (), 8 * 10**9))
-    q_t, kv_t, w_own, early, late = call(
+    q_t, kv_t = call(
         cross_project_kernel,
-        (far(PAIR, ROWS), shape(2 * PAIR, ROWS), near(4 * PAIR, D), near(2, QUAD, D), far(4, QUAD, D)),
+        (far(PAIR, ROWS), shape(2 * PAIR, ROWS)),
         (gains, normed) + blocks,
-        [pltpu.VMEM((PAIR, ROWS), BF16), pltpu.VMEM((2, QUAD, D), BF16), pltpu.SemaphoreType.DMA((13,))],
+        [pltpu.VMEM((PAIR, ROWS), BF16), pltpu.VMEM((2, QUAD, D), BF16), pltpu.SemaphoreType.DMA((3,))],
         0,
         8,
     )
     kv_a = lax.ppermute(kv_t, EVERY, ACROSS)
-    timed = call(time_kernel, shape(32, 16, PAIR), (gains, after(time_normed, kv_t), keep_near(early)))
+    timed, w_own, late = call(
+        time_kernel,
+        (shape(32, 16, PAIR), near(4 * PAIR, D), far(4, QUAD, D)),
+        (gains, after(time_normed, kv_t)) + blocks,
+        [pltpu.VMEM((2, QUAD, D), BF16), pltpu.SemaphoreType.DMA((10,))],
+        0,
+        8,
+    )
+    w_other = swap_core(w_own)
     kv_b = lax.ppermute(after(kv_a, timed), EVERY, ALONG)
     space = call(
         space_kernel,
@@ -449,7 +460,6 @@
         2,
     )
     returned = lax.all_to_all(timed, CHIP, 0, 0, tiled=True)
-    w_other = swap_core(w_own)
     keep, give, w_other = call(
         cross_kernel,
         (shape(HALF, 4 * PAIR), shape(HALF, 4 * PAIR), near(4 * PAIR, D)),

time: 133 us -> 135 us (1.015); the launches traced: 133 us -> 133 us
  starting transfers between devices: 67.4 us -> 65.1 us
  waiting for transfers between devices: 39.2 us -> 40.9 us
    ppermute x1, waiting for transfers between devices: 1.21 us -> 4.92 us  [local(): blocks.append(lax.ppermute(blocks[1], EVERY, X_NEXT))]
    ppermute x6, waiting for transfers between devices: 4.61 us -> 1.6 us  [local(): blocks.append(lax.ppermute(block, EVERY, way))]
    ppermute x4, starting transfers between devices: 16.7 us -> 14.8 us  [swap_core(): return lax.ppermute(block, 'core', [(0, 1), (1, 0)])]
    all_to_all x1, waiting for transfers between devices: 0.01 us -> 1.49 us  [local(): returned = lax.all_to_all(timed, CHIP, 0, 0, tiled=True)]
where the time goes in v14:
time: 135 us; the launch traced here: 133 us
  starting transfers between devices  65.1 us (48%)
  waiting for transfers between devices  40.9 us (30%)
  Pallas kernels  24.2 us (18%)
  local copies, waits for them, and re-layouts  2.27 us (2%)
    all_to_all x1, waiting for transfers between devices, local(): got = lax.all_to_all(pieces, SLAB, 0, 0, tiled=True)  27.3 us
    pallas_call x9, Pallas kernels, call(): pl.pallas_call(kernel, out_shape=out_shapes, in_specs=specs, out_specs=pl...  24.2 us
    ppermute x6, starting transfers between devices, local(): blocks.append(lax.ppermute(block, EVERY, way))  18.6 us
    all_to_all x1, starting transfers between devices, local(): got = lax.all_to_all(pieces, SLAB, 0, 0, tiled=True)  15.6 us
    ppermute x4, starting transfers between devices, swap_core(): return lax.ppermute(block, 'core', [(0, 1), (1, 0)])  14.8 us
    ppermute x1, starting transfers between devices, local(): kv_a = lax.ppermute(kv_t, EVERY, ACROSS)  6.42 us
    all_to_all x1, starting transfers between devices, local(): returned = lax.all_to_all(timed, CHIP, 0, 0, tiled=True)  5.74 us
    ppermute x1, waiting for transfers between devices, local(): blocks.append(lax.ppermute(blocks[1], EVERY, X_NEXT))  4.92 us
  transfers between devices with their start and end apart: 15, of which 7 were waited for; matrix products, arithmetic and copies ran while one was open for 0% of the time, Pallas kernels for 11%

profile of v14, /device:TPU:1, one launch (start us, length us, event | category | flops | bytes accessed | tf_op | source)
XLA Modules:
  0.0 133.0 jit_solution(2289948055073791896)
XLA Ops:
  0.0 2.7 %shard_map.74 = bf16[64,80,128]{2,1,0:T(8,128)(2,1)} custom-call(bf16[18,3456]{1,0:T(8,128)(2,1)} %w_qkv_hbm.1, bf16[18,1152]{1,0:T(8,128)(2,1)} %w_out_hbm.1, bf16[256,1152]{1,0:T(8,128)(2,1)} %bitcast.8), custom_call_target="tpu_custom_call" | custom-call | bytes 1 | tf_op jit(solution)/shard_map/pallas_call | solution.py:346
  2.7 0.0 copy-start
  2.7 0.0 copy-start.6
  2.7 0.0 copy-start.7
  2.7 0.0 copy-start.8
  2.7 0.0 copy-start.2
  2.8 15.6 %all-to-all-start = ((bf16[64,80,128]{2,1,0:T(8,128)(2,1)}), bf16[64,80,128]{2,1,0:T(8,128)(2,1)S(1)}, u32[]{:S(2)}, u32[]{:S(2)}) async-start(bf16[64,80,128]{2,1,0:T(8,128)(2,1)} %shard_map.74), calls=%async_computation | async-start | bytes 2621440 | tf_op jit(solution)/shard_map/all_to_all | solution.py:407
  18.3 2.4 %collective-permute-start = (bf16[256,1152]{1,0:T(8,128)(2,1)S(1)}, bf16[256,1152]{1,0:T(8,128)(2,1)S(1)}, u32[]{:S(2)}, u32[]{:S(2)}) collective-permute-start(bf16[256,1152]{1,0:T(8,128)(2,1)S(1)} %bitcast.9), channel_id=1, source_target_pairs={{0,1},{1,0},{2,3},{3,2},{4,5},{5,4},{6,7},{7,6},{8,9},{9,8},{10,11... | collective-permute-start | bytes 1769480 | tf_op jit(solution)/shard_map/ppermute | solution.py:60
  20.7 0.1 stack_reshape.6
  20.8 0.1 stack_reshape.7
  21.0 0.1 reshape.7
  21.1 0.1 reshape.6
  21.2 1.1 collective-permute-done.other
  22.3 0.8 copy-done.4
  23.1 1.1 copy-done.5
  24.2 0.8 shard_map.73.normed.normed_hbm
  25.0 27.3 %all-to-all-done.got = bf16[64,80,128]{2,1,0:T(8,128)(2,1)S(1)} async-done(((bf16[64,80,128]{2,1,0:T(8,128)(2,1)}), bf16[64,80,128]{2,1,0:T(8,128)(2,1)S(1)}, u32[]{:S(2)}, u32[]{:S(2)}) %all-to-all-start) | async-done | bytes 1310752 | tf_op jit(solution)/shard_map/all_to_all | solution.py:407
  52.2 1.7 %shard_map.75 = (bf16[288,1152]{1,0:T(8,128)(2,1)S(1)}, bf16[288,1152]{1,0:T(8,128)(2,1)}, bf16[256,1152]{1,0:T(8,128)(2,1)}) custom-call(bf16[64,80,128]{2,1,0:T(8,128)(2,1)S(1)} %all-to-all-done.got), custom_call_target="tpu_custom_call" | custom-call | bytes 1 | tf_op jit(solution)/shard_map/pallas_call | solution.py:346
  54.0 2.1 %collective-permute-start.7 = (bf16[288,1152]{1,0:T(8,128)(2,1)}, bf16[288,1152]{1,0:T(8,128)(2,1)S(1)}, u32[]{:S(2)}, u32[]{:S(2)}) collective-permute-start(bf16[288,1152]{1,0:T(8,128)(2,1)} %get-tuple-element.22), channel_id=1, source_target_pairs={{0,2},{1,15},{2,4},{3,1},{4,6},{5,3},{6,8},{7,5},{8,10},{9,7},{10,... | collective-permute-start | bytes 1990664 | tf_op jit(solution)/shard_map/ppermute | solution.py:426
  56.1 3.1 %collective-permute-start.1 = (bf16[288,1152]{1,0:T(8,128)(2,1)}, bf16[288,1152]{1,0:T(8,128)(2,1)S(1)}, u32[]{:S(2)}, u32[]{:S(2)}) collective-permute-start(bf16[288,1152]{1,0:T(8,128)(2,1)} %get-tuple-element.22), channel_id=1, source_target_pairs={{0,384},{1,129},{2,386},{3,131},{4,388},{5,133},{6,390},{7,135},{8... | collective-permute-start | bytes 1990664 | tf_op jit(solution)/shard_map/ppermute | solution.py:426
  59.2 6.1 %collective-permute-start.5 = (bf16[288,1152]{1,0:T(8,128)(2,1)}, bf16[288,1152]{1,0:T(8,128)(2,1)S(1)}, u32[]{:S(2)}, u32[]{:S(2)}) collective-permute-start(bf16[288,1152]{1,0:T(8,128)(2,1)} %get-tuple-element.22), channel_id=1, source_target_pairs={{0,16},{1,113},{2,18},{3,115},{4,20},{5,117},{6,22},{7,119},{8,24}... | collective-permute-start | bytes 1990664 | tf_op jit(solution)/shard_map/ppermute | solution.py:426
  65.4 1.9 %collective-permute-start.4 = (bf16[288,1152]{1,0:T(8,128)(2,1)}, bf16[288,1152]{1,0:T(8,128)(2,1)S(1)}, u32[]{:S(2)}, u32[]{:S(2)}) collective-permute-start(bf16[288,1152]{1,0:T(8,128)(2,1)} %get-tuple-element.22), channel_id=1, source_target_pairs={{0,14},{1,3},{2,0},{3,5},{4,2},{5,7},{6,4},{7,9},{8,6},{9,11},{10,... | collective-permute-start | bytes 1990664 | tf_op jit(solution)/shard_map/ppermute | solution.py:426
  67.3 3.4 %collective-permute-start.3 = (bf16[288,1152]{1,0:T(8,128)(2,1)}, bf16[288,1152]{1,0:T(8,128)(2,1)S(1)}, u32[]{:S(2)}, u32[]{:S(2)}) collective-permute-start(bf16[288,1152]{1,0:T(8,128)(2,1)} %get-tuple-element.22), channel_id=1, source_target_pairs={{0,128},{1,385},{2,130},{3,387},{4,132},{5,389},{6,134},{7,391},{8... | collective-permute-start | bytes 1990664 | tf_op jit(solution)/shard_map/ppermute | solution.py:426
  70.7 0.0 collective-permute-done.7.refs_7_
  70.7 1.9 %collective-permute-start.2 = (bf16[288,1152]{1,0:T(8,128)(2,1)}, bf16[288,1152]{1,0:T(8,128)(2,1)S(1)}, u32[]{:S(2)}, u32[]{:S(2)}) collective-permute-start(bf16[288,1152]{1,0:T(8,128)(2,1)} %get-tuple-element.22), channel_id=1, source_target_pairs={{0,112},{1,17},{2,114},{3,19},{4,116},{5,21},{6,118},{7,23},{8,120... | collective-permute-start | bytes 1990664 | tf_op jit(solution)/shard_map/ppermute | solution.py:426
  72.6 0.0 collective-permute-done.1.refs_1_
  72.6 1.9 %collective-permute-start.6 = (bf16[288,1152]{1,0:T(8,128)(2,1)S(1)}, bf16[288,1152]{1,0:T(8,128)(2,1)S(1)}, u32[]{:S(2)}, u32[]{:S(2)}) collective-permute-start(bf16[288,1152]{1,0:T(8,128)(2,1)S(1)} %collective-permute-done.1.refs_1_), channel_id=1, source_target_pairs={{0,384},{1,129},{2,386},{3,131},{4,388},{5,133},{6,390},{7,135},{8... | collective-permute-start | bytes 1990664 | tf_op jit(solution)/shard_map/ppermute | solution.py:424
  74.6 0.0 collective-permute-done.5.refs_5_
  74.6 7.6 %collective-permute-start.9 = (bf16[256,1152]{1,0:T(8,128)(2,1)}, bf16[256,1152]{1,0:T(8,128)(2,1)S(1)}, u32[]{:S(2)}, u32[]{:S(2)}) collective-permute-start(bf16[256,1152]{1,0:T(8,128)(2,1)} %get-tuple-element.24.own), channel_id=1, source_target_pairs={{0,1},{1,0},{2,3},{3,2},{4,5},{5,4},{6,7},{7,6},{8,9},{9,8},{10,11... | collective-permute-start | bytes 1769480 | tf_op jit(solution)/shard_map/ppermute | solution.py:60
  82.2 0.0 collective-permute-done.4.refs_4_
  82.2 0.0 collective-permute-done.3.refs_3_
  82.2 1.6 %collective-permute-done.2.refs_2_ = bf16[288,1152]{1,0:T(8,128)(2,1)S(1)} collective-permute-done((bf16[288,1152]{1,0:T(8,128)(2,1)}, bf16[288,1152]{1,0:T(8,128)(2,1)S(1)}, u32[]{:S(2)}, u32[]{:S(2)}) %collective-permute-start.2) | collective-permute-done | bytes 663584 | tf_op jit(solution)/shard_map/ppermute | solution.py:426
  83.8 4.9 %collective-permute-done.6.refs_6_ = bf16[288,1152]{1,0:T(8,128)(2,1)S(1)} collective-permute-done((bf16[288,1152]{1,0:T(8,128)(2,1)S(1)}, bf16[288,1152]{1,0:T(8,128)(2,1)S(1)}, u32[]{:S(2)}, u32[]{:S(2)}) %collective-permute-start.6) | collective-permute-done | bytes 663584 | tf_op jit(solution)/shard_map/ppermute | solution.py:424
  88.7 2.6 %shard_map.76 = (bf16[144,512]{1,0:T(8,128)(2,1)}, bf16[288,512]{1,0:T(8,128)(2,1)}) custom-call(f32[8,288]{1,0:T(8,128)S(1)} %select_maximum_fusion.gains, bf16[512,1152]{1,0:T(8,128)(2,1)S(1)} %shard_map.73.normed.normed_hbm, bf16[288,1152]{1,0:T(8,128)(2,1)S(1)} %get-tuple-element.21.refs_0_, bf16[288,1152]{1,0:T(8,128)(2,1)S(1)} %collective-permute-done.1.refs_1_, ...), custom_call_target="tpu_custom_call" | custom-call | bytes 1 | tf_op jit(solution)/shard_map/pallas_call | solution.py:346
  91.4 6.4 %collective-permute-start.8 = (bf16[288,512]{1,0:T(8,128)(2,1)}, bf16[288,512]{1,0:T(8,128)(2,1)S(1)}, u32[]{:S(2)}, u32[]{:S(2)}) collective-permute-start(bf16[288,512]{1,0:T(8,128)(2,1)} %get-tuple-element.23), channel_id=1, source_target_pairs={{0,64},{1,65},{2,66},{3,67},{4,68},{5,69},{6,70},{7,71},{8,72},{9,... | collective-permute-start | bytes 884744 | tf_op jit(solution)/shard_map/ppermute | solution.py:438
  97.8 0.8 shard_map.77.normed
  98.6 4.1 %shard_map.78 = (bf16[32,16,144]{2,1,0:T(8,128)(2,1)}, bf16[576,1152]{1,0:T(8,128)(2,1)S(1)}, bf16[4,288,1152]{2,1,0:T(8,128)(2,1)}) custom-call(f32[8,288]{1,0:T(8,128)S(1)} %select_maximum_fusion.gains, bf16[512,1152]{1,0:T(8,128)(2,1)S(1)} %shard_map.77.normed, bf16[288,1152]{1,0:T(8,128)(2,1)S(1)} %get-tuple-element.21.refs_0_, ...), custom_call_target="tpu_custom_call" | custom-call | bytes 1 | tf_op jit(solution)/shard_map/pallas_call | solution.py:346
  102.7 5.7 %all-to-all-start.1 = ((bf16[32,16,144]{2,1,0:T(8,128)(2,1)}), bf16[32,16,144]{2,1,0:T(8,128)(2,1)S(1)}, u32[]{:S(2)}, u32[]{:S(2)}) async-start(bf16[32,16,144]{2,1,0:T(8,128)(2,1)} %get-tuple-element.26), calls=%async_computation.1 | async-start | bytes 524288 | tf_op jit(solution)/shard_map/all_to_all | solution.py:462
  108.5 2.2 %collective-permute-start.11 = (bf16[576,1152]{1,0:T(8,128)(2,1)S(1)}, bf16[576,1152]{1,0:T(8,128)(2,1)}, u32[]{:S(2)}, u32[]{:S(2)}) collective-permute-start(bf16[576,1152]{1,0:T(8,128)(2,1)S(1)} %get-tuple-element.31.w_own), channel_id=1, source_target_pairs={{0,1},{1,0},{2,3},{3,2},{4,5},{5,4},{6,7},{7,6},{8,9},{9,8},{10,11... | collective-permute-start | bytes 3981320 | tf_op jit(solution)/shard_map/ppermute | solution.py:60
  110.7 2.1 %collective-permute-start.10 = (bf16[288,512]{1,0:T(8,128)(2,1)S(1)}, bf16[288,512]{1,0:T(8,128)(2,1)S(1)}, u32[]{:S(2)}, u32[]{:S(2)}) collective-permute-start(bf16[288,512]{1,0:T(8,128)(2,1)S(1)} %collective-permute-done.8.kv_a), channel_id=1, source_target_pairs={{0,128},{1,129},{2,130},{3,131},{4,132},{5,133},{6,134},{7,135},{8... | collective-permute-start | bytes 884744 | tf_op jit(solution)/shard_map/ppermute | solution.py:448
  112.8 5.8 %shard_map.79.space_hbm = bf16[288,512]{1,0:T(8,128)(2,1)} custom-call(f32[8,288]{1,0:T(8,128)S(1)} %select_maximum_fusion.gains, bf16[512,1152]{1,0:T(8,128)(2,1)} %copy-done.1, bf16[4,288,1152]{2,1,0:T(8,128)(2,1)} %get-tuple-element.29.weight_hbm), custom_call_target="tpu_custom_call" | custom-call | flops 16000000000 | bytes 1 | tf_op jit(solution)/shard_map/pallas_call | solution.py:346
  118.6 1.5 %all-to-all-done.1.timed = bf16[32,16,144]{2,1,0:T(8,128)(2,1)S(1)} async-done(((bf16[32,16,144]{2,1,0:T(8,128)(2,1)}), bf16[32,16,144]{2,1,0:T(8,128)(2,1)S(1)}, u32[]{:S(2)}, u32[]{:S(2)}) %all-to-all-start.1) | async-done | bytes 147488 | tf_op jit(solution)/shard_map/all_to_all | solution.py:462
  120.1 3.2 %collective-permute-done.10.kv_b = bf16[288,512]{1,0:T(8,128)(2,1)S(1)} collective-permute-done((bf16[288,512]{1,0:T(8,128)(2,1)S(1)}, bf16[288,512]{1,0:T(8,128)(2,1)S(1)}, u32[]{:S(2)}, u32[]{:S(2)}) %collective-permute-start.10) | collective-permute-done | bytes 294944 | tf_op jit(solution)/shard_map/ppermute | solution.py:448
  123.3 0.0 collective-permute-done.11.w_hbm
  123.3 3.0 %shard_map.80 = (bf16[256,576]{1,0:T(8,128)(2,1)S(1)}, bf16[256,576]{1,0:T(8,128)(2,1)S(1)}, bf16[576,1152]{1,0:T(8,128)(2,1)S(1)}) custom-call(bf16[288,512]{1,0:T(8,128)(2,1)S(1)} %collective-permute-done.8.kv_a, bf16[288,512]{1,0:T(8,128)(2,1)S(1)} %collective-permute-done.10.kv_b, bf16[32,16,144]{2,1,0:T(8,128)(2,1)S(1)} %all-to-all-done.1.timed, ...), custom_call_target="tpu_custom_call" | custom-call | bytes 1 | tf_op jit(solution)/shard_map/pallas_call | solution.py:346
  126.3 2.6 %collective-permute-start.12 = (bf16[256,576]{1,0:T(8,128)(2,1)S(1)}, bf16[256,576]{1,0:T(8,128)(2,1)S(1)}, u32[]{:S(2)}, u32[]{:S(2)}) collective-permute-start(bf16[256,576]{1,0:T(8,128)(2,1)S(1)} %get-tuple-element.33), channel_id=1, source_target_pairs={{0,1},{1,0},{2,3},{3,2},{4,5},{5,4},{6,7},{7,6},{8,9},{9,8},{10,11... | collective-permute-start | bytes 884744 | tf_op jit(solution)/shard_map/ppermute | solution.py:60
  128.9 1.2 collective-permute-done.12.arrived
  130.1 2.8 %shard_map.81 = bf16[256,1152]{1,0:T(8,128)(2,1)} custom-call(bf16[256,1152]{1,0:T(8,128)(2,1)S(1)} %bitcast.11, bf16[256,576]{1,0:T(8,128)(2,1)S(1)} %get-tuple-element.32.own, bf16[256,576]{1,0:T(8,128)(2,1)S(1)} %collective-permute-done.12.arrived, bf16[576,1152]{1,0:T(8,128)(2,1)S(1)} %get-tuple-element.31.w_own, ...), custom_call_target="tpu_custom_call" | custom-call | bytes 1 | tf_op jit(solution)/shard_map/pallas_call | solution.py:346
  (19 shorter events, 0.1 us)
Async XLA Ops:
  2.7 15.6 %copy-start = (bf16[1,256,1152]{2,1,0:T(8,128)(2,1)S(1)}, bf16[1,256,1152]{2,1,0:T(8,128)(2,1)}, u32[]{:S(2)}) copy-start(bf16[1,256,1152]{2,1,0:T(8,128)(2,1)} %param.7) | copy-start | bytes 1769476
  2.7 18.0 %copy-start.6 = (f32[1152]{0:T(1024)S(1)}, f32[1152]{0:T(1024)}, u32[]{:S(2)}) copy-start(f32[1152]{0:T(1024)} %param.9) | copy-start | bytes 13828
  2.7 18.0 %copy-start.7 = (f32[1152]{0:T(1024)S(1)}, f32[1152]{0:T(1024)}, u32[]{:S(2)}) copy-start(f32[1152]{0:T(1024)} %param.10) | copy-start | bytes 13828
  2.7 18.1 %copy-start.8 = (f32[1152]{0:T(1024)S(1)}, f32[1152]{0:T(1024)}, u32[]{:S(2)}) copy-start(f32[1152]{0:T(1024)} %param.11) | copy-start | bytes 13828
  2.7 20.4 %copy-start.2 = (f32[8,1152]{1,0:T(8,128)S(1)}, f32[8,1152]{1,0:T(8,128)}, u32[]{:S(2)}) copy-start(f32[8,1152]{1,0:T(8,128)} %embed_hbm.1) | copy-start | bytes 110596
  2.8 49.5 %all-to-all-start = ((bf16[64,80,128]{2,1,0:T(8,128)(2,1)}), bf16[64,80,128]{2,1,0:T(8,128)(2,1)S(1)}, u32[]{:S(2)}, u32[]{:S(2)}) async-start(bf16[64,80,128]{2,1,0:T(8,128)(2,1)} %shard_map.74), calls=%async_computation | async-start | bytes 2621440 | tf_op jit(solution)/shard_map/all_to_all | solution.py:407
  18.3 4.0 %collective-permute-start = (bf16[256,1152]{1,0:T(8,128)(2,1)S(1)}, bf16[256,1152]{1,0:T(8,128)(2,1)S(1)}, u32[]{:S(2)}, u32[]{:S(2)}) collective-permute-start(bf16[256,1152]{1,0:T(8,128)(2,1)S(1)} %bitcast.9), channel_id=1, source_target_pairs={{0,1},{1,0},{2,3},{3,2},{4,5},{5,4},{6,7},{7,6},{8,9},{9,8},{10,11... | collective-permute-start | bytes 1769480 | tf_op jit(solution)/shard_map/ppermute | solution.py:60
  22.3 0.8 copy-start.4
  23.1 1.1 copy-start.5
  25.0 66.4 %copy-start.1 = (bf16[512,1152]{1,0:T(8,128)(2,1)}, bf16[512,1152]{1,0:T(8,128)(2,1)S(1)}, u32[]{:S(2)}) copy-start(bf16[512,1152]{1,0:T(8,128)(2,1)S(1)} %shard_map.73.normed.normed_hbm) | copy-start | bytes 3538948
  54.0 16.7 %collective-permute-start.7 = (bf16[288,1152]{1,0:T(8,128)(2,1)}, bf16[288,1152]{1,0:T(8,128)(2,1)S(1)}, u32[]{:S(2)}, u32[]{:S(2)}) collective-permute-start(bf16[288,1152]{1,0:T(8,128)(2,1)} %get-tuple-element.22), channel_id=1, source_target_pairs={{0,2},{1,15},{2,4},{3,1},{4,6},{5,3},{6,8},{7,5},{8,10},{9,7},{10,... | collective-permute-start | bytes 1990664 | tf_op jit(solution)/shard_map/ppermute | solution.py:426
  56.1 16.5 %collective-permute-start.1 = (bf16[288,1152]{1,0:T(8,128)(2,1)}, bf16[288,1152]{1,0:T(8,128)(2,1)S(1)}, u32[]{:S(2)}, u32[]{:S(2)}) collective-permute-start(bf16[288,1152]{1,0:T(8,128)(2,1)} %get-tuple-element.22), channel_id=1, source_target_pairs={{0,384},{1,129},{2,386},{3,131},{4,388},{5,133},{6,390},{7,135},{8... | collective-permute-start | bytes 1990664 | tf_op jit(solution)/shard_map/ppermute | solution.py:426
  59.2 15.3 %collective-permute-start.5 = (bf16[288,1152]{1,0:T(8,128)(2,1)}, bf16[288,1152]{1,0:T(8,128)(2,1)S(1)}, u32[]{:S(2)}, u32[]{:S(2)}) collective-permute-start(bf16[288,1152]{1,0:T(8,128)(2,1)} %get-tuple-element.22), channel_id=1, source_target_pairs={{0,16},{1,113},{2,18},{3,115},{4,20},{5,117},{6,22},{7,119},{8,24}... | collective-permute-start | bytes 1990664 | tf_op jit(solution)/shard_map/ppermute | solution.py:426
  65.4 16.8 %collective-permute-start.4 = (bf16[288,1152]{1,0:T(8,128)(2,1)}, bf16[288,1152]{1,0:T(8,128)(2,1)S(1)}, u32[]{:S(2)}, u32[]{:S(2)}) collective-permute-start(bf16[288,1152]{1,0:T(8,128)(2,1)} %get-tuple-element.22), channel_id=1, source_target_pairs={{0,14},{1,3},{2,0},{3,5},{4,2},{5,7},{6,4},{7,9},{8,6},{9,11},{10,... | collective-permute-start | bytes 1990664 | tf_op jit(solution)/shard_map/ppermute | solution.py:426
  67.3 14.9 %collective-permute-start.3 = (bf16[288,1152]{1,0:T(8,128)(2,1)}, bf16[288,1152]{1,0:T(8,128)(2,1)S(1)}, u32[]{:S(2)}, u32[]{:S(2)}) collective-permute-start(bf16[288,1152]{1,0:T(8,128)(2,1)} %get-tuple-element.22), channel_id=1, source_target_pairs={{0,128},{1,385},{2,130},{3,387},{4,132},{5,389},{6,134},{7,391},{8... | collective-permute-start | bytes 1990664 | tf_op jit(solution)/shard_map/ppermute | solution.py:426
  70.7 13.1 %collective-permute-start.2 = (bf16[288,1152]{1,0:T(8,128)(2,1)}, bf16[288,1152]{1,0:T(8,128)(2,1)S(1)}, u32[]{:S(2)}, u32[]{:S(2)}) collective-permute-start(bf16[288,1152]{1,0:T(8,128)(2,1)} %get-tuple-element.22), channel_id=1, source_target_pairs={{0,112},{1,17},{2,114},{3,19},{4,116},{5,21},{6,118},{7,23},{8,120... | collective-permute-start | bytes 1990664 | tf_op jit(solution)/shard_map/ppermute | solution.py:426
  72.6 16.1 %collective-permute-start.6 = (bf16[288,1152]{1,0:T(8,128)(2,1)S(1)}, bf16[288,1152]{1,0:T(8,128)(2,1)S(1)}, u32[]{:S(2)}, u32[]{:S(2)}) collective-permute-start(bf16[288,1152]{1,0:T(8,128)(2,1)S(1)} %collective-permute-done.1.refs_1_), channel_id=1, source_target_pairs={{0,384},{1,129},{2,386},{3,131},{4,388},{5,133},{6,390},{7,135},{8... | collective-permute-start | bytes 1990664 | tf_op jit(solution)/shard_map/ppermute | solution.py:424
  74.6 23.2 %collective-permute-start.9 = (bf16[256,1152]{1,0:T(8,128)(2,1)}, bf16[256,1152]{1,0:T(8,128)(2,1)S(1)}, u32[]{:S(2)}, u32[]{:S(2)}) collective-permute-start(bf16[256,1152]{1,0:T(8,128)(2,1)} %get-tuple-element.24.own), channel_id=1, source_target_pairs={{0,1},{1,0},{2,3},{3,2},{4,5},{5,4},{6,7},{7,6},{8,9},{9,8},{10,11... | collective-permute-start | bytes 1769480 | tf_op jit(solution)/shard_map/ppermute | solution.py:60
  88.7 9.1 %copy-start.3 = (bf16[256,1152]{1,0:T(8,128)(2,1)S(1)}, bf16[256,1152]{1,0:T(8,128)(2,1)}, u32[]{:S(2)}) copy-start(bf16[256,1152]{1,0:T(8,128)(2,1)} %get-tuple-element.24.own) | copy-start | bytes 1769476
  91.4 19.4 %collective-permute-start.8 = (bf16[288,512]{1,0:T(8,128)(2,1)}, bf16[288,512]{1,0:T(8,128)(2,1)S(1)}, u32[]{:S(2)}, u32[]{:S(2)}) collective-permute-start(bf16[288,512]{1,0:T(8,128)(2,1)} %get-tuple-element.23), channel_id=1, source_target_pairs={{0,64},{1,65},{2,66},{3,67},{4,68},{5,69},{6,70},{7,71},{8,72},{9,... | collective-permute-start | bytes 884744 | tf_op jit(solution)/shard_map/ppermute | solution.py:438
  102.7 17.3 %all-to-all-start.1 = ((bf16[32,16,144]{2,1,0:T(8,128)(2,1)}), bf16[32,16,144]{2,1,0:T(8,128)(2,1)S(1)}, u32[]{:S(2)}, u32[]{:S(2)}) async-start(bf16[32,16,144]{2,1,0:T(8,128)(2,1)} %get-tuple-element.26), calls=%async_computation.1 | async-start | bytes 524288 | tf_op jit(solution)/shard_map/all_to_all | solution.py:462
  108.5 14.8 %collective-permute-start.11 = (bf16[576,1152]{1,0:T(8,128)(2,1)S(1)}, bf16[576,1152]{1,0:T(8,128)(2,1)}, u32[]{:S(2)}, u32[]{:S(2)}) collective-permute-start(bf16[576,1152]{1,0:T(8,128)(2,1)S(1)} %get-tuple-element.31.w_own), channel_id=1, source_target_pairs={{0,1},{1,0},{2,3},{3,2},{4,5},{5,4},{6,7},{7,6},{8,9},{9,8},{10,11... | collective-permute-start | bytes 3981320 | tf_op jit(solution)/shard_map/ppermute | solution.py:60
  110.7 12.6 %collective-permute-start.10 = (bf16[288,512]{1,0:T(8,128)(2,1)S(1)}, bf16[288,512]{1,0:T(8,128)(2,1)S(1)}, u32[]{:S(2)}, u32[]{:S(2)}) collective-permute-start(bf16[288,512]{1,0:T(8,128)(2,1)S(1)} %collective-permute-done.8.kv_a), channel_id=1, source_target_pairs={{0,128},{1,129},{2,130},{3,131},{4,132},{5,133},{6,134},{7,135},{8... | collective-permute-start | bytes 884744 | tf_op jit(solution)/shard_map/ppermute | solution.py:448
  126.3 3.8 %collective-permute-start.12 = (bf16[256,576]{1,0:T(8,128)(2,1)S(1)}, bf16[256,576]{1,0:T(8,128)(2,1)S(1)}, u32[]{:S(2)}, u32[]{:S(2)}) collective-permute-start(bf16[256,576]{1,0:T(8,128)(2,1)S(1)} %get-tuple-element.33), channel_id=1, source_target_pairs={{0,1},{1,0},{2,3},{3,2},{4,5},{5,4},{6,7},{7,6},{8,9},{9,8},{10,11... | collective-permute-start | bytes 884744 | tf_op jit(solution)/shard_map/ppermute | solution.py:60

commit v15 on v13

--- a/solution.py
+++ b/solution.py
@@ -41,7 +41,7 @@
     return 1 if core else -1
 
 
-TURNS = (0, 2, 1, 6, 3, 7, 4, 5)
+TURNS = (0, 2, 1, 3, 7, 6, 4, 5)
 
 
 def bring(offset):
@@ -416,7 +416,7 @@
         ],
     )
     blocks = [keep_near(own_block)]
-    for way in (X_NEXT, Y_NEXT, X_LAST, Z_NEXT, Y_LAST, None, Z_LAST):
+    for way in (X_NEXT, Y_NEXT, Z_NEXT, Y_LAST, X_LAST, None, Z_LAST):
         if way is None:
             blocks.append(lax.ppermute(blocks[1], EVERY, X_NEXT))
         else:
@@ -427,13 +427,13 @@
     q_t, kv_t, w_own, early, late = call(
         cross_project_kernel,
         (far(PAIR, ROWS), shape(2 * PAIR, ROWS), near(4 * PAIR, D), near(2, QUAD, D), far(4, QUAD, D)),
-        (gains, normed) + blocks,
+        (gains, after(normed, time_normed)) + blocks,
         [pltpu.VMEM((PAIR, ROWS), BF16), pltpu.VMEM((2, QUAD, D), BF16), pltpu.SemaphoreType.DMA((13,))],
         0,
         8,
     )
     kv_a = lax.ppermute(kv_t, EVERY, ACROSS)
-    timed = call(time_kernel, shape(32, 16, PAIR), (gains, after(time_normed, kv_t), keep_near(early)))
+    timed = call(time_kernel, shape(32, 16, PAIR), (gains, time_normed, keep_near(early)))
     kv_b = lax.ppermute(after(kv_a, timed), EVERY, ALONG)
     space = call(
         space_kernel,

time: 133 us -> 134 us (level)
  waiting for transfers between devices: 39.2 us -> 43.2 us
  starting transfers between devices: 67.4 us -> 63.8 us
    ppermute x1, waiting for transfers between devices: 2.64 us -> 4.78 us  [local(): kv_b = lax.ppermute(after(kv_a, timed), EVERY, ALONG)]
    ppermute x4, starting transfers between devices: 16.7 us -> 14.7 us  [swap_core(): return lax.ppermute(block, 'core', [(0, 1), (1, 0)])]
    ppermute x6, starting transfers between devices: 19.5 us -> 17.7 us  [local(): blocks.append(lax.ppermute(block, EVERY, way))]
    ppermute x6, waiting for transfers between devices: 4.61 us -> 6.26 us  [local(): blocks.append(lax.ppermute(block, EVERY, way))]
  transfers between devices with their start and end apart: 15 -> 15, of which waited for: 7 -> 7; matrix products, arithmetic and copies ran while one was open for 0% -> 0% of each run, Pallas kernels for 11% -> 8%
where the time goes in v15:
time: 134 us
  starting transfers between devices  63.8 us (48%)
  waiting for transfers between devices  43.2 us (32%)
  Pallas kernels  23.5 us (18%)
  local copies, waits for them, and re-layouts  2.46 us (2%)
    all_to_all x1, waiting for transfers between devices, local(): got = lax.all_to_all(pieces, SLAB, 0, 0, tiled=True)  28.1 us
    pallas_call x9, Pallas kernels, call(): pl.pallas_call(kernel, out_shape=out_shapes, in_specs=specs, out_specs=pl...  23.5 us
    ppermute x6, starting transfers between devices, local(): blocks.append(lax.ppermute(block, EVERY, way))  17.7 us
    all_to_all x1, starting transfers between devices, local(): got = lax.all_to_all(pieces, SLAB, 0, 0, tiled=True)  15.6 us
    ppermute x4, starting transfers between devices, swap_core(): return lax.ppermute(block, 'core', [(0, 1), (1, 0)])  14.7 us
    ppermute x1, starting transfers between devices, local(): kv_a = lax.ppermute(kv_t, EVERY, ACROSS)  6.44 us
    ppermute x6, waiting for transfers between devices, local(): blocks.append(lax.ppermute(block, EVERY, way))  6.26 us
    ppermute x1, waiting for transfers between devices, local(): kv_b = lax.ppermute(after(kv_a, timed), EVERY, ALONG)  4.78 us
  transfers between devices with their start and end apart: 15, of which 7 were waited for; matrix products, arithmetic and copies ran while one was open for 0% of the time, Pallas kernels for 8%

profile of v15, /device:TPU:1, one launch (start us, length us, event | category | flops | bytes accessed | tf_op | source)
XLA Modules:
  0.0 133.6 jit_solution(8071404977474799913)
XLA Ops:
  0.0 2.7 %shard_map.74 = bf16[64,80,128]{2,1,0:T(8,128)(2,1)} custom-call(bf16[18,3456]{1,0:T(8,128)(2,1)} %w_qkv_hbm.1, bf16[18,1152]{1,0:T(8,128)(2,1)} %w_out_hbm.1, bf16[256,1152]{1,0:T(8,128)(2,1)} %bitcast.8), custom_call_target="tpu_custom_call" | custom-call | bytes 1 | tf_op jit(solution)/shard_map/pallas_call | solution.py:343
  2.7 0.0 copy-start
  2.7 0.0 copy-start.5
  2.7 0.0 copy-start.6
  2.7 0.0 copy-start.7
  2.7 0.0 copy-start.3
  2.7 15.6 %all-to-all-start = ((bf16[64,80,128]{2,1,0:T(8,128)(2,1)}), bf16[64,80,128]{2,1,0:T(8,128)(2,1)S(1)}, u32[]{:S(2)}, u32[]{:S(2)}) async-start(bf16[64,80,128]{2,1,0:T(8,128)(2,1)} %shard_map.74), calls=%async_computation | async-start | bytes 2621440 | tf_op jit(solution)/shard_map/all_to_all | solution.py:404
  18.3 2.4 %collective-permute-start = (bf16[256,1152]{1,0:T(8,128)(2,1)S(1)}, bf16[256,1152]{1,0:T(8,128)(2,1)S(1)}, u32[]{:S(2)}, u32[]{:S(2)}) collective-permute-start(bf16[256,1152]{1,0:T(8,128)(2,1)S(1)} %bitcast.9), channel_id=1, source_target_pairs={{0,1},{1,0},{2,3},{3,2},{4,5},{5,4},{6,7},{7,6},{8,9},{9,8},{10,11... | collective-permute-start | bytes 1769480 | tf_op jit(solution)/shard_map/ppermute | solution.py:60
  20.7 0.1 stack_reshape.6
  20.8 0.1 stack_reshape.7
  21.0 0.1 reshape.7
  21.1 0.1 reshape.6
  21.2 1.1 collective-permute-done.other
  22.3 0.8 shard_map.73.normed.normed_hbm
  23.1 1.0 copy-done.1
  24.1 28.1 %all-to-all-done.got = bf16[64,80,128]{2,1,0:T(8,128)(2,1)S(1)} async-done(((bf16[64,80,128]{2,1,0:T(8,128)(2,1)}), bf16[64,80,128]{2,1,0:T(8,128)(2,1)S(1)}, u32[]{:S(2)}, u32[]{:S(2)}) %all-to-all-start) | async-done | bytes 1310752 | tf_op jit(solution)/shard_map/all_to_all | solution.py:404
  52.2 1.7 %shard_map.75 = (bf16[288,1152]{1,0:T(8,128)(2,1)S(1)}, bf16[288,1152]{1,0:T(8,128)(2,1)}, bf16[256,1152]{1,0:T(8,128)(2,1)}) custom-call(bf16[64,80,128]{2,1,0:T(8,128)(2,1)S(1)} %all-to-all-done.got), custom_call_target="tpu_custom_call" | custom-call | bytes 1 | tf_op jit(solution)/shard_map/pallas_call | solution.py:343
  54.0 2.1 %collective-permute-start.8 = (bf16[288,1152]{1,0:T(8,128)(2,1)}, bf16[288,1152]{1,0:T(8,128)(2,1)S(1)}, u32[]{:S(2)}, u32[]{:S(2)}) collective-permute-start(bf16[288,1152]{1,0:T(8,128)(2,1)} %get-tuple-element.24), channel_id=1, source_target_pairs={{0,2},{1,15},{2,4},{3,1},{4,6},{5,3},{6,8},{7,5},{8,10},{9,7},{10,... | collective-permute-start | bytes 1990664 | tf_op jit(solution)/shard_map/ppermute | solution.py:423
  56.1 3.1 %collective-permute-start.2 = (bf16[288,1152]{1,0:T(8,128)(2,1)}, bf16[288,1152]{1,0:T(8,128)(2,1)S(1)}, u32[]{:S(2)}, u32[]{:S(2)}) collective-permute-start(bf16[288,1152]{1,0:T(8,128)(2,1)} %get-tuple-element.24), channel_id=1, source_target_pairs={{0,384},{1,129},{2,386},{3,131},{4,388},{5,133},{6,390},{7,135},{8... | collective-permute-start | bytes 1990664 | tf_op jit(solution)/shard_map/ppermute | solution.py:423
  59.2 4.1 %collective-permute-start.1 = (bf16[256,1152]{1,0:T(8,128)(2,1)}, bf16[256,1152]{1,0:T(8,128)(2,1)S(1)}, u32[]{:S(2)}, u32[]{:S(2)}) collective-permute-start(bf16[256,1152]{1,0:T(8,128)(2,1)} %get-tuple-element.21.own), channel_id=1, source_target_pairs={{0,1},{1,0},{2,3},{3,2},{4,5},{5,4},{6,7},{7,6},{8,9},{9,8},{10,11... | collective-permute-start | bytes 1769480 | tf_op jit(solution)/shard_map/ppermute | solution.py:60
  63.4 2.5 %collective-permute-start.6 = (bf16[288,1152]{1,0:T(8,128)(2,1)}, bf16[288,1152]{1,0:T(8,128)(2,1)S(1)}, u32[]{:S(2)}, u32[]{:S(2)}) collective-permute-start(bf16[288,1152]{1,0:T(8,128)(2,1)} %get-tuple-element.24), channel_id=1, source_target_pairs={{0,128},{1,385},{2,130},{3,387},{4,132},{5,389},{6,134},{7,391},{8... | collective-permute-start | bytes 1990664 | tf_op jit(solution)/shard_map/ppermute | solution.py:423
  65.8 5.5 %collective-permute-start.5 = (bf16[288,1152]{1,0:T(8,128)(2,1)}, bf16[288,1152]{1,0:T(8,128)(2,1)S(1)}, u32[]{:S(2)}, u32[]{:S(2)}) collective-permute-start(bf16[288,1152]{1,0:T(8,128)(2,1)} %get-tuple-element.24), channel_id=1, source_target_pairs={{0,16},{1,113},{2,18},{3,115},{4,20},{5,117},{6,22},{7,119},{8,24}... | collective-permute-start | bytes 1990664 | tf_op jit(solution)/shard_map/ppermute | solution.py:423
  71.4 0.0 collective-permute-done.1.other
  71.4 2.6 %collective-permute-start.4 = (bf16[288,1152]{1,0:T(8,128)(2,1)}, bf16[288,1152]{1,0:T(8,128)(2,1)S(1)}, u32[]{:S(2)}, u32[]{:S(2)}) collective-permute-start(bf16[288,1152]{1,0:T(8,128)(2,1)} %get-tuple-element.24), channel_id=1, source_target_pairs={{0,14},{1,3},{2,0},{3,5},{4,2},{5,7},{6,4},{7,9},{8,6},{9,11},{10,... | collective-permute-start | bytes 1990664 | tf_op jit(solution)/shard_map/ppermute | solution.py:423
  74.0 0.0 collective-permute-done.8.refs_7_
  74.0 1.9 %collective-permute-start.3 = (bf16[288,1152]{1,0:T(8,128)(2,1)}, bf16[288,1152]{1,0:T(8,128)(2,1)S(1)}, u32[]{:S(2)}, u32[]{:S(2)}) collective-permute-start(bf16[288,1152]{1,0:T(8,128)(2,1)} %get-tuple-element.24), channel_id=1, source_target_pairs={{0,112},{1,17},{2,114},{3,19},{4,116},{5,21},{6,118},{7,23},{8,120... | collective-permute-start | bytes 1990664 | tf_op jit(solution)/shard_map/ppermute | solution.py:423
  75.9 0.0 collective-permute-done.2.refs_1_
  75.9 2.8 %collective-permute-start.7 = (bf16[288,1152]{1,0:T(8,128)(2,1)S(1)}, bf16[288,1152]{1,0:T(8,128)(2,1)S(1)}, u32[]{:S(2)}, u32[]{:S(2)}) collective-permute-start(bf16[288,1152]{1,0:T(8,128)(2,1)S(1)} %collective-permute-done.2.refs_1_), channel_id=1, source_target_pairs={{0,384},{1,129},{2,386},{3,131},{4,388},{5,133},{6,390},{7,135},{8... | collective-permute-start | bytes 1990664 | tf_op jit(solution)/shard_map/ppermute | solution.py:421
  78.8 0.0 copy-start.4
  78.8 1.1 copy-done.4
  79.8 0.8 shard_map.76.normed
  80.6 0.0 collective-permute-done.6.refs_5_
  80.6 3.6 %collective-permute-done.4.refs_3_ = bf16[288,1152]{1,0:T(8,128)(2,1)S(1)} collective-permute-done((bf16[288,1152]{1,0:T(8,128)(2,1)}, bf16[288,1152]{1,0:T(8,128)(2,1)S(1)}, u32[]{:S(2)}, u32[]{:S(2)}) %collective-permute-start.4) | collective-permute-done | bytes 663584 | tf_op jit(solution)/shard_map/ppermute | solution.py:423
  84.2 2.7 %collective-permute-done.3.refs_2_ = bf16[288,1152]{1,0:T(8,128)(2,1)S(1)} collective-permute-done((bf16[288,1152]{1,0:T(8,128)(2,1)}, bf16[288,1152]{1,0:T(8,128)(2,1)S(1)}, u32[]{:S(2)}, u32[]{:S(2)}) %collective-permute-start.3) | collective-permute-done | bytes 663584 | tf_op jit(solution)/shard_map/ppermute | solution.py:423
  86.9 1.7 %collective-permute-done.7.refs_6_ = bf16[288,1152]{1,0:T(8,128)(2,1)S(1)} collective-permute-done((bf16[288,1152]{1,0:T(8,128)(2,1)S(1)}, bf16[288,1152]{1,0:T(8,128)(2,1)S(1)}, u32[]{:S(2)}, u32[]{:S(2)}) %collective-permute-start.7) | collective-permute-done | bytes 663584 | tf_op jit(solution)/shard_map/ppermute | solution.py:421
  88.6 3.2 %shard_map.77 = (bf16[144,512]{1,0:T(8,128)(2,1)}, bf16[288,512]{1,0:T(8,128)(2,1)S(1)}, bf16[576,1152]{1,0:T(8,128)(2,1)S(1)}, bf16[2,288,1152]{2,1,0:T(8,128)(2,1)S(1)}, bf16[4,288,1152]{2,1,0:T(8,128)(2,1)}) custom-call(f32[8,288]{1,0:T(8,128)S(1)} %select_maximum_fusion.gains, bf16[512,1152]{1,0:T(8,128)(2,1)S(1)} %copy-done.2, ...), custom_call_target="tpu_custom_call" | custom-call | bytes 1 | tf_op jit(solution)/shard_map/pallas_call | solution.py:343
  91.8 6.4 %collective-permute-start.9 = (bf16[288,512]{1,0:T(8,128)(2,1)S(1)}, bf16[288,512]{1,0:T(8,128)(2,1)S(1)}, u32[]{:S(2)}, u32[]{:S(2)}) collective-permute-start(bf16[288,512]{1,0:T(8,128)(2,1)S(1)} %get-tuple-element.25), channel_id=1, source_target_pairs={{0,64},{1,65},{2,66},{3,67},{4,68},{5,69},{6,70},{7,71},{8,72},{9,... | collective-permute-start | bytes 884744 | tf_op jit(solution)/shard_map/ppermute | solution.py:435
  98.2 2.8 %shard_map.78 = bf16[32,16,144]{2,1,0:T(8,128)(2,1)} custom-call(f32[8,288]{1,0:T(8,128)S(1)} %select_maximum_fusion.gains, bf16[512,1152]{1,0:T(8,128)(2,1)S(1)} %shard_map.76.normed, bf16[2,288,1152]{2,1,0:T(8,128)(2,1)S(1)} %get-tuple-element.26.weight), custom_call_target="tpu_custom_call" | custom-call | bytes 1 | tf_op jit(solution)/shard_map/pallas_call | solution.py:343
  101.0 4.5 %all-to-all-start.1 = ((bf16[32,16,144]{2,1,0:T(8,128)(2,1)}), bf16[32,16,144]{2,1,0:T(8,128)(2,1)S(1)}, u32[]{:S(2)}, u32[]{:S(2)}) async-start(bf16[32,16,144]{2,1,0:T(8,128)(2,1)} %shard_map.78), calls=%async_computation.1 | async-start | bytes 524288 | tf_op jit(solution)/shard_map/all_to_all | solution.py:451
  105.5 5.7 %collective-permute-start.11 = (bf16[576,1152]{1,0:T(8,128)(2,1)S(1)}, bf16[576,1152]{1,0:T(8,128)(2,1)}, u32[]{:S(2)}, u32[]{:S(2)}) collective-permute-start(bf16[576,1152]{1,0:T(8,128)(2,1)S(1)} %get-tuple-element.31.w_own), channel_id=1, source_target_pairs={{0,1},{1,0},{2,3},{3,2},{4,5},{5,4},{6,7},{7,6},{8,9},{9,8},{10,11... | collective-permute-start | bytes 3981320 | tf_op jit(solution)/shard_map/ppermute | solution.py:60
  111.2 2.1 %collective-permute-start.10 = (bf16[288,512]{1,0:T(8,128)(2,1)S(1)}, bf16[288,512]{1,0:T(8,128)(2,1)S(1)}, u32[]{:S(2)}, u32[]{:S(2)}) collective-permute-start(bf16[288,512]{1,0:T(8,128)(2,1)S(1)} %collective-permute-done.9.kv_a), channel_id=1, source_target_pairs={{0,128},{1,129},{2,130},{3,131},{4,132},{5,133},{6,134},{7,135},{8... | collective-permute-start | bytes 884744 | tf_op jit(solution)/shard_map/ppermute | solution.py:437
  113.3 5.8 %shard_map.79.space_hbm = bf16[288,512]{1,0:T(8,128)(2,1)} custom-call(f32[8,288]{1,0:T(8,128)S(1)} %select_maximum_fusion.gains, bf16[512,1152]{1,0:T(8,128)(2,1)} %copy-done.1, bf16[4,288,1152]{2,1,0:T(8,128)(2,1)} %get-tuple-element.29.weight_hbm), custom_call_target="tpu_custom_call" | custom-call | flops 16000000000 | bytes 1 | tf_op jit(solution)/shard_map/pallas_call | solution.py:343
  119.1 0.0 all-to-all-done.1.timed
  119.1 4.8 %collective-permute-done.10.kv_b = bf16[288,512]{1,0:T(8,128)(2,1)S(1)} collective-permute-done((bf16[288,512]{1,0:T(8,128)(2,1)S(1)}, bf16[288,512]{1,0:T(8,128)(2,1)S(1)}, u32[]{:S(2)}, u32[]{:S(2)}) %collective-permute-start.10) | collective-permute-done | bytes 294944 | tf_op jit(solution)/shard_map/ppermute | solution.py:437
  123.9 3.0 %shard_map.80 = (bf16[256,576]{1,0:T(8,128)(2,1)S(1)}, bf16[256,576]{1,0:T(8,128)(2,1)S(1)}, bf16[576,1152]{1,0:T(8,128)(2,1)S(1)}) custom-call(bf16[288,512]{1,0:T(8,128)(2,1)S(1)} %collective-permute-done.9.kv_a, bf16[288,512]{1,0:T(8,128)(2,1)S(1)} %collective-permute-done.10.kv_b, bf16[32,16,144]{2,1,0:T(8,128)(2,1)S(1)} %all-to-all-done.1.timed, ...), custom_call_target="tpu_custom_call" | custom-call | bytes 1 | tf_op jit(solution)/shard_map/pallas_call | solution.py:343
  126.9 2.5 %collective-permute-start.12 = (bf16[256,576]{1,0:T(8,128)(2,1)S(1)}, bf16[256,576]{1,0:T(8,128)(2,1)S(1)}, u32[]{:S(2)}, u32[]{:S(2)}) collective-permute-start(bf16[256,576]{1,0:T(8,128)(2,1)S(1)} %get-tuple-element.33), channel_id=1, source_target_pairs={{0,1},{1,0},{2,3},{3,2},{4,5},{5,4},{6,7},{7,6},{8,9},{9,8},{10,11... | collective-permute-start | bytes 884744 | tf_op jit(solution)/shard_map/ppermute | solution.py:60
  129.4 1.2 collective-permute-done.12.arrived
  130.6 2.8 %shard_map.81 = bf16[256,1152]{1,0:T(8,128)(2,1)} custom-call(bf16[256,1152]{1,0:T(8,128)(2,1)S(1)} %bitcast.11, bf16[256,576]{1,0:T(8,128)(2,1)S(1)} %get-tuple-element.32.own, bf16[256,576]{1,0:T(8,128)(2,1)S(1)} %collective-permute-done.12.arrived, bf16[576,1152]{1,0:T(8,128)(2,1)S(1)} %get-tuple-element.31.w_own, ...), custom_call_target="tpu_custom_call" | custom-call | bytes 1 | tf_op jit(solution)/shard_map/pallas_call | solution.py:343
  (17 shorter events, 0.1 us)
Async XLA Ops:
  2.7 15.6 %copy-start = (bf16[1,256,1152]{2,1,0:T(8,128)(2,1)S(1)}, bf16[1,256,1152]{2,1,0:T(8,128)(2,1)}, u32[]{:S(2)}) copy-start(bf16[1,256,1152]{2,1,0:T(8,128)(2,1)} %param.7) | copy-start | bytes 1769476
  2.7 18.0 %copy-start.5 = (f32[1152]{0:T(1024)S(1)}, f32[1152]{0:T(1024)}, u32[]{:S(2)}) copy-start(f32[1152]{0:T(1024)} %param.9) | copy-start | bytes 13828
  2.7 18.0 %copy-start.6 = (f32[1152]{0:T(1024)S(1)}, f32[1152]{0:T(1024)}, u32[]{:S(2)}) copy-start(f32[1152]{0:T(1024)} %param.10) | copy-start | bytes 13828
  2.7 18.1 %copy-start.7 = (f32[1152]{0:T(1024)S(1)}, f32[1152]{0:T(1024)}, u32[]{:S(2)}) copy-start(f32[1152]{0:T(1024)} %param.11) | copy-start | bytes 13828
  2.7 19.6 %copy-start.3 = (f32[8,1152]{1,0:T(8,128)S(1)}, f32[8,1152]{1,0:T(8,128)}, u32[]{:S(2)}) copy-start(f32[8,1152]{1,0:T(8,128)} %embed_hbm.1) | copy-start | bytes 110596
  2.7 49.5 %all-to-all-start = ((bf16[64,80,128]{2,1,0:T(8,128)(2,1)}), bf16[64,80,128]{2,1,0:T(8,128)(2,1)S(1)}, u32[]{:S(2)}, u32[]{:S(2)}) async-start(bf16[64,80,128]{2,1,0:T(8,128)(2,1)} %shard_map.74), calls=%async_computation | async-start | bytes 2621440 | tf_op jit(solution)/shard_map/all_to_all | solution.py:404
  18.3 4.0 %collective-permute-start = (bf16[256,1152]{1,0:T(8,128)(2,1)S(1)}, bf16[256,1152]{1,0:T(8,128)(2,1)S(1)}, u32[]{:S(2)}, u32[]{:S(2)}) collective-permute-start(bf16[256,1152]{1,0:T(8,128)(2,1)S(1)} %bitcast.9), channel_id=1, source_target_pairs={{0,1},{1,0},{2,3},{3,2},{4,5},{5,4},{6,7},{7,6},{8,9},{9,8},{10,11... | collective-permute-start | bytes 1769480 | tf_op jit(solution)/shard_map/ppermute | solution.py:60
  23.1 1.0 copy-start.1
  54.0 20.0 %collective-permute-start.8 = (bf16[288,1152]{1,0:T(8,128)(2,1)}, bf16[288,1152]{1,0:T(8,128)(2,1)S(1)}, u32[]{:S(2)}, u32[]{:S(2)}) collective-permute-start(bf16[288,1152]{1,0:T(8,128)(2,1)} %get-tuple-element.24), channel_id=1, source_target_pairs={{0,2},{1,15},{2,4},{3,1},{4,6},{5,3},{6,8},{7,5},{8,10},{9,7},{10,... | collective-permute-start | bytes 1990664 | tf_op jit(solution)/shard_map/ppermute | solution.py:423
  56.1 19.8 %collective-permute-start.2 = (bf16[288,1152]{1,0:T(8,128)(2,1)}, bf16[288,1152]{1,0:T(8,128)(2,1)S(1)}, u32[]{:S(2)}, u32[]{:S(2)}) collective-permute-start(bf16[288,1152]{1,0:T(8,128)(2,1)} %get-tuple-element.24), channel_id=1, source_target_pairs={{0,384},{1,129},{2,386},{3,131},{4,388},{5,133},{6,390},{7,135},{8... | collective-permute-start | bytes 1990664 | tf_op jit(solution)/shard_map/ppermute | solution.py:423
  59.2 29.3 %copy-start.2 = (bf16[512,1152]{1,0:T(8,128)(2,1)S(1)}, bf16[512,1152]{1,0:T(8,128)(2,1)}, u32[]{:S(2)}) copy-start(bf16[512,1152]{1,0:T(8,128)(2,1)} %copy-done.1) | copy-start | bytes 3538948
  59.2 12.1 %collective-permute-start.1 = (bf16[256,1152]{1,0:T(8,128)(2,1)}, bf16[256,1152]{1,0:T(8,128)(2,1)S(1)}, u32[]{:S(2)}, u32[]{:S(2)}) collective-permute-start(bf16[256,1152]{1,0:T(8,128)(2,1)} %get-tuple-element.21.own), channel_id=1, source_target_pairs={{0,1},{1,0},{2,3},{3,2},{4,5},{5,4},{6,7},{7,6},{8,9},{9,8},{10,11... | collective-permute-start | bytes 1769480 | tf_op jit(solution)/shard_map/ppermute | solution.py:60
  63.4 17.2 %collective-permute-start.6 = (bf16[288,1152]{1,0:T(8,128)(2,1)}, bf16[288,1152]{1,0:T(8,128)(2,1)S(1)}, u32[]{:S(2)}, u32[]{:S(2)}) collective-permute-start(bf16[288,1152]{1,0:T(8,128)(2,1)} %get-tuple-element.24), channel_id=1, source_target_pairs={{0,128},{1,385},{2,130},{3,387},{4,132},{5,389},{6,134},{7,391},{8... | collective-permute-start | bytes 1990664 | tf_op jit(solution)/shard_map/ppermute | solution.py:423
  65.8 14.8 %collective-permute-start.5 = (bf16[288,1152]{1,0:T(8,128)(2,1)}, bf16[288,1152]{1,0:T(8,128)(2,1)S(1)}, u32[]{:S(2)}, u32[]{:S(2)}) collective-permute-start(bf16[288,1152]{1,0:T(8,128)(2,1)} %get-tuple-element.24), channel_id=1, source_target_pairs={{0,16},{1,113},{2,18},{3,115},{4,20},{5,117},{6,22},{7,119},{8,24}... | collective-permute-start | bytes 1990664 | tf_op jit(solution)/shard_map/ppermute | solution.py:423
  71.4 12.8 %collective-permute-start.4 = (bf16[288,1152]{1,0:T(8,128)(2,1)}, bf16[288,1152]{1,0:T(8,128)(2,1)S(1)}, u32[]{:S(2)}, u32[]{:S(2)}) collective-permute-start(bf16[288,1152]{1,0:T(8,128)(2,1)} %get-tuple-element.24), channel_id=1, source_target_pairs={{0,14},{1,3},{2,0},{3,5},{4,2},{5,7},{6,4},{7,9},{8,6},{9,11},{10,... | collective-permute-start | bytes 1990664 | tf_op jit(solution)/shard_map/ppermute | solution.py:423
  74.0 12.9 %collective-permute-start.3 = (bf16[288,1152]{1,0:T(8,128)(2,1)}, bf16[288,1152]{1,0:T(8,128)(2,1)S(1)}, u32[]{:S(2)}, u32[]{:S(2)}) collective-permute-start(bf16[288,1152]{1,0:T(8,128)(2,1)} %get-tuple-element.24), channel_id=1, source_target_pairs={{0,112},{1,17},{2,114},{3,19},{4,116},{5,21},{6,118},{7,23},{8,120... | collective-permute-start | bytes 1990664 | tf_op jit(solution)/shard_map/ppermute | solution.py:423
  75.9 12.6 %collective-permute-start.7 = (bf16[288,1152]{1,0:T(8,128)(2,1)S(1)}, bf16[288,1152]{1,0:T(8,128)(2,1)S(1)}, u32[]{:S(2)}, u32[]{:S(2)}) collective-permute-start(bf16[288,1152]{1,0:T(8,128)(2,1)S(1)} %collective-permute-done.2.refs_1_), channel_id=1, source_target_pairs={{0,384},{1,129},{2,386},{3,131},{4,388},{5,133},{6,390},{7,135},{8... | collective-permute-start | bytes 1990664 | tf_op jit(solution)/shard_map/ppermute | solution.py:421
  78.8 1.1 copy-start.4
  91.8 19.5 %collective-permute-start.9 = (bf16[288,512]{1,0:T(8,128)(2,1)S(1)}, bf16[288,512]{1,0:T(8,128)(2,1)S(1)}, u32[]{:S(2)}, u32[]{:S(2)}) collective-permute-start(bf16[288,512]{1,0:T(8,128)(2,1)S(1)} %get-tuple-element.25), channel_id=1, source_target_pairs={{0,64},{1,65},{2,66},{3,67},{4,68},{5,69},{6,70},{7,71},{8,72},{9,... | collective-permute-start | bytes 884744 | tf_op jit(solution)/shard_map/ppermute | solution.py:435
  101.0 18.1 %all-to-all-start.1 = ((bf16[32,16,144]{2,1,0:T(8,128)(2,1)}), bf16[32,16,144]{2,1,0:T(8,128)(2,1)S(1)}, u32[]{:S(2)}, u32[]{:S(2)}) async-start(bf16[32,16,144]{2,1,0:T(8,128)(2,1)} %shard_map.78), calls=%async_computation.1 | async-start | bytes 524288 | tf_op jit(solution)/shard_map/all_to_all | solution.py:451
  105.5 18.4 %collective-permute-start.11 = (bf16[576,1152]{1,0:T(8,128)(2,1)S(1)}, bf16[576,1152]{1,0:T(8,128)(2,1)}, u32[]{:S(2)}, u32[]{:S(2)}) collective-permute-start(bf16[576,1152]{1,0:T(8,128)(2,1)S(1)} %get-tuple-element.31.w_own), channel_id=1, source_target_pairs={{0,1},{1,0},{2,3},{3,2},{4,5},{5,4},{6,7},{7,6},{8,9},{9,8},{10,11... | collective-permute-start | bytes 3981320 | tf_op jit(solution)/shard_map/ppermute | solution.py:60
  111.2 12.7 %collective-permute-start.10 = (bf16[288,512]{1,0:T(8,128)(2,1)S(1)}, bf16[288,512]{1,0:T(8,128)(2,1)S(1)}, u32[]{:S(2)}, u32[]{:S(2)}) collective-permute-start(bf16[288,512]{1,0:T(8,128)(2,1)S(1)} %collective-permute-done.9.kv_a), channel_id=1, source_target_pairs={{0,128},{1,129},{2,130},{3,131},{4,132},{5,133},{6,134},{7,135},{8... | collective-permute-start | bytes 884744 | tf_op jit(solution)/shard_map/ppermute | solution.py:437
  126.9 3.7 %collective-permute-start.12 = (bf16[256,576]{1,0:T(8,128)(2,1)S(1)}, bf16[256,576]{1,0:T(8,128)(2,1)S(1)}, u32[]{:S(2)}, u32[]{:S(2)}) collective-permute-start(bf16[256,576]{1,0:T(8,128)(2,1)S(1)} %get-tuple-element.33), channel_id=1, source_target_pairs={{0,1},{1,0},{2,3},{3,2},{4,5},{5,4},{6,7},{7,6},{8,9},{9,8},{10,11... | collective-permute-start | bytes 884744 | tf_op jit(solution)/shard_map/ppermute | solution.py:60
